TPU v7x, 32 devices: a whole 2x2x4 slice. The times are simulated.
32 devices in a mesh: grp: 2 (over y), ep: 16 (over z, x, core).
Axes of the slice: x: 2, y: 2, z: 4, core: 2. Of those that a mesh axis runs over, the one named last changes fastest.
Arguments:
- latent_in: bfloat16 [4096, 1024], P(('grp', 'ep')), parts along dimension 0, may hold values from -6 to 6
- routes: int32 [4096, 8], P(('grp', 'ep')), parts along dimension 0, may hold values from 0 to 15, all different within a row; in each aligned block of 128 rows (0 to 127, 128 to 255, ...) at most 96 rows name the same one
- combine_weights: float32 [4096, 8], P(('grp', 'ep')), parts along dimension 0, may hold values from 0.1 to 1
- cotangent: bfloat16 [4096, 1024], P(('grp', 'ep')), parts along dimension 0, may hold values from -6 to 6
- w_gate: bfloat16 [16, 1024, 512], P('ep'), may hold values from -0.1875 to 0.1875
- w_up: bfloat16 [16, 1024, 512], P('ep'), may hold values from -0.1875 to 0.1875
- w_down: bfloat16 [16, 512, 1024], P('ep'), may hold values from -0.25 to 0.25
Outputs:
- combined: bfloat16 [4096, 1024], P(('grp', 'ep')), parts along dimension 0
- grad_latent: bfloat16 [4096, 1024], P(('grp', 'ep')), parts along dimension 0
- grad_combine: float32 [4096, 8], P(('grp', 'ep')), parts along dimension 0
- grad_w_gate: bfloat16 [32, 1024, 512], P(('grp', 'ep')), parts along dimension 0
- grad_w_up: bfloat16 [32, 1024, 512], P(('grp', 'ep')), parts along dimension 0
- grad_w_down: bfloat16 [32, 512, 1024], P(('grp', 'ep')), parts along dimension 0
There are 2 independent parts, one for each index of `grp`. A program takes and returns all parts, laid end to end along the dimension named above; an argument that names none is the same for every part. Nothing has to cross between parts.
Inputs may be any that keep to these rules, and one draw needn't show every extreme that they name: `routes`: each row names 8 different experts. Within the 128 rows of one device no expert is named more than 96 times, a bound that some block reaches.
All inputs are finite; a program needn't handle non-finite values.
Results may differ from a plain program's by a relative error of at most 0.0065.
Values may be sent and summed in bfloat16 or wider, within the bound.
No kernel may reach another device: no remote copies, remote signals or barrier semaphores. Data moves between devices by JAX's collectives and lax.ppermute only.
A program may use at most 128 MiB of HBM per device.

v0:
```python
import jax
import jax.numpy as jnp
from jax import lax
from jax.sharding import PartitionSpec as P


def assign_slots(route_rows, expert_count):
    flat_ids = route_rows.reshape(-1)
    onehot = (flat_ids[:, None] == jnp.arange(expert_count, dtype=jnp.int32)[None, :]).astype(
        jnp.int32
    )
    ranks = jnp.cumsum(onehot, axis=0) - 1
    return (flat_ids, jnp.sum(onehot * ranks, axis=1))


def expert_forward(rows, gate_w, up_w, down_w):
    gate_pre = jnp.einsum("erl,elf->erf", rows, gate_w, preferred_element_type=jnp.float32)
    up_pre = jnp.einsum("erl,elf->erf", rows, up_w, preferred_element_type=jnp.float32)
    sigma = jax.nn.sigmoid(gate_pre)
    silu_val = gate_pre * sigma
    hidden = (silu_val * up_pre).astype(jnp.bfloat16)
    expert_out = jnp.einsum(
        "erf,efl->erl", hidden, down_w, preferred_element_type=jnp.float32
    ).astype(jnp.bfloat16)
    return (expert_out, (gate_pre, up_pre, sigma, silu_val, hidden))


def expert_backward(rows, grad_out, saved, gate_w, up_w, down_w):
    gate_pre, up_pre, sigma, silu_val, hidden = saved
    grad_down = jnp.einsum(
        "erf,erl->efl", hidden, grad_out, preferred_element_type=jnp.float32
    ).astype(jnp.bfloat16)
    grad_hidden = jnp.einsum("erl,efl->erf", grad_out, down_w, preferred_element_type=jnp.float32)
    grad_gate = (grad_hidden * up_pre * sigma * (1.0 + gate_pre * (1.0 - sigma))).astype(
        jnp.bfloat16
    )
    grad_up = (grad_hidden * silu_val).astype(jnp.bfloat16)
    grad_gw = jnp.einsum(
        "erl,erf->elf", rows, grad_gate, preferred_element_type=jnp.float32
    ).astype(jnp.bfloat16)
    grad_uw = jnp.einsum("erl,erf->elf", rows, grad_up, preferred_element_type=jnp.float32).astype(
        jnp.bfloat16
    )
    grad_rows = (
        jnp.einsum("erf,elf->erl", grad_gate, gate_w, preferred_element_type=jnp.float32)
        + jnp.einsum("erf,elf->erl", grad_up, up_w, preferred_element_type=jnp.float32)
    ).astype(jnp.bfloat16)
    return (grad_rows, grad_gw, grad_uw, grad_down)


def local(latent_in, routes, combine_weights, cotangent, w_gate, w_up, w_down):
    devices_ep = lax.axis_size("ep")
    local_experts = w_gate.shape[0]
    expert_count = local_experts * devices_ep
    tok_count = latent_in.shape[0]
    top_count = routes.shape[1]
    width = latent_in.shape[1]
    capacity = tok_count * top_count * 3 // (2 * expert_count)
    expert_ids, slot_ids = assign_slots(routes, expert_count)
    position = expert_ids * capacity + slot_ids
    repeated = jnp.repeat(latent_in, top_count, axis=0)
    weighted = (combine_weights[:, :, None] * cotangent.astype(jnp.float32)[:, None, :]).astype(
        jnp.bfloat16
    )
    send_rows = jnp.zeros((expert_count * capacity, width), jnp.bfloat16).at[position].set(repeated)
    send_rows = send_rows.reshape(expert_count, capacity, width)
    send_cot = (
        jnp.zeros((expert_count * capacity, width), jnp.bfloat16)
        .at[position]
        .set(weighted.reshape(-1, width))
    )
    send_cot = send_cot.reshape(expert_count, capacity, width)

    def to_local(received):
        shaped = received.reshape(devices_ep, local_experts, capacity, width)
        return shaped.transpose(1, 0, 2, 3).reshape(local_experts, devices_ep * capacity, width)

    def to_home(local_rows):
        shaped = local_rows.reshape(local_experts, devices_ep, capacity, width)
        return shaped.transpose(1, 0, 2, 3).reshape(expert_count, capacity, width)

    got_rows = lax.all_to_all(send_rows, "ep", split_axis=0, concat_axis=0, tiled=True)
    rows_local = to_local(got_rows)
    expert_out, saved = expert_forward(rows_local, w_gate, w_up, w_down)
    back_out = lax.all_to_all(to_home(expert_out), "ep", split_axis=0, concat_axis=0, tiled=True)
    got_cot = lax.all_to_all(send_cot, "ep", split_axis=0, concat_axis=0, tiled=True)
    grad_rows, grad_gw, grad_uw, grad_down = expert_backward(
        rows_local, to_local(got_cot), saved, w_gate, w_up, w_down
    )
    back_grad = lax.all_to_all(to_home(grad_rows), "ep", split_axis=0, concat_axis=0, tiled=True)
    out_rows = (
        back_out.reshape(-1, width)[position]
        .reshape(tok_count, top_count, width)
        .astype(jnp.float32)
    )
    grad_back = (
        back_grad.reshape(-1, width)[position]
        .reshape(tok_count, top_count, width)
        .astype(jnp.float32)
    )
    combined = jnp.sum(combine_weights[:, :, None] * out_rows, axis=1).astype(jnp.bfloat16)
    grad_combine = jnp.sum(cotangent.astype(jnp.float32)[:, None, :] * out_rows, axis=2)
    grad_latent = jnp.sum(grad_back, axis=1).astype(jnp.bfloat16)
    return (combined, grad_latent, grad_combine, grad_gw, grad_uw, grad_down)


def solution(mesh):
    return jax.shard_map(
        local,
        mesh=mesh,
        in_specs=(
            P(("grp", "ep"), None),
            P(("grp", "ep"), None),
            P(("grp", "ep"), None),
            P(("grp", "ep"), None),
            P("ep", None, None),
            P("ep", None, None),
            P("ep", None, None),
        ),
        out_specs=(
            P(("grp", "ep"), None),
            P(("grp", "ep"), None),
            P(("grp", "ep"), None),
            P(("grp", "ep"), None, None),
            P(("grp", "ep"), None, None),
            P(("grp", "ep"), None, None),
        ),
        check_vma=False,
    )
```

profile of v0, /device:TPU:11, one launch (start us, length us, event | category | flops | bytes accessed | tf_op | source)
XLA Modules:
  0.0 336.7 jit_solution(4380827726162128049)
XLA Ops:
  0.6 0.8 broadcast_multiply_fusion
  1.4 0.8 copy.25
  2.4 0.1 copy.24
  2.5 0.1 mul.86
  2.6 4.5 %reduce-window.6 = s32[16,8,128]{2,1,0:T(8,128)S(1)} reduce-window(s32[16,8,128]{2,1,0:T(8,128)S(1)} %fusion.28, s32[]{:T(128)} %constant.5.clone.1), window={size=1x1x128 pad=0_0x0_0x127_0}, to_apply=%region_0.0 | reduce-window | flops 2080768 | bytes 131076 | tf_op jit(solution)/shard_map/reduce-window
  7.2 0.1 copy.27
  7.6 7.8 %scatter_custom_fusion = bf16[1536,1024]{1,0:T(8,128)(2,1)} fusion(s32[1024]{0:T(1024)S(1)} %bitcast.82, bf16[]{:T(256)} %constant.7.clone.1, bf16[128,1024]{1,0:T(8,128)(2,1)} %param.7), kind=kCustom, calls=%fused_computation.19 | custom fusion | bytes 3407874 | tf_op jit(solution)/shard_map/scatter | solution.py:65
  15.4 6.7 %all-to-all-start = ((bf16[16,96,1024]{2,1,0:T(8,128)(2,1)}), bf16[16,96,1024]{2,1,0:T(8,128)(2,1)}, u32[]{:S(2)}, u32[]{:S(2)}) async-start(bf16[16,96,1024]{2,1,0:T(8,128)(2,1)} %bitcast.76), calls=%async_computation | async-start | bytes 6291456 | tf_op jit(solution)/shard_map/all_to_all | solution.py:82
  22.1 0.1 copy.23
  22.2 0.1 mul.91
  22.3 7.8 %scatter_custom_fusion.1 = bf16[1536,1024]{1,0:T(8,128)(2,1)} fusion(s32[1024]{0:T(1024)S(1)} %bitcast.83, f32[128,1024]{1,0:T(8,128)S(1)} %convert_element_type.72, f32[1024]{0:T(1024)S(1)} %mul.91, bf16[]{:T(256)} %constant.7.clone.1), kind=kCustom, calls=%fused_computation.17 | custom fusion | flops 2097152 | bytes 3674114 | tf_op jit(solution)/shard_map/scatter | solution.py:70
  30.2 61.9 %all-to-all-done = bf16[16,96,1024]{2,1,0:T(8,128)(2,1)} async-done(((bf16[16,96,1024]{2,1,0:T(8,128)(2,1)}), bf16[16,96,1024]{2,1,0:T(8,128)(2,1)}, u32[]{:S(2)}, u32[]{:S(2)}) %all-to-all-start) | async-done | bytes 3145760 | tf_op jit(solution)/shard_map/all_to_all | solution.py:82
  92.1 5.0 %all-to-all-start.2 = ((bf16[16,96,1024]{2,1,0:T(8,128)(2,1)}), bf16[16,96,1024]{2,1,0:T(8,128)(2,1)}, u32[]{:S(2)}, u32[]{:S(2)}) async-start(bf16[16,96,1024]{2,1,0:T(8,128)(2,1)} %bitcast.75), calls=%async_computation.2 | async-start | bytes 6291456 | tf_op jit(solution)/shard_map/all_to_all | solution.py:86
  97.1 5.5 %fusion.19 = f32[1536,512]{1,0:T(8,128)} fusion(bf16[1536,1024]{1,0:T(8,128)(2,1)} %bitcast.6, bf16[1,1024,512]{2,1,0:T(8,128)(2,1)S(1)} %copy-done.2), kind=kOutput, calls=%fused_computation.35 | convolution fusion | flops 1610612736 | bytes 7340032 | tf_op jit(solution)/shard_map/erl,elf->erf/dot_general | solution.py:18
  102.6 5.3 %fusion.23 = f32[1536,512]{1,0:T(8,128)} fusion(bf16[1536,1024]{1,0:T(8,128)(2,1)} %bitcast.6, bf16[1,1024,512]{2,1,0:T(8,128)(2,1)S(1)} %copy-done.6), kind=kOutput, calls=%fused_computation.39 | convolution fusion | flops 1610612736 | bytes 7340032 | tf_op jit(solution)/shard_map/erl,elf->erf/dot_general | solution.py:17
  107.9 59.2 %all-to-all-done.2 = bf16[16,96,1024]{2,1,0:T(8,128)(2,1)} async-done(((bf16[16,96,1024]{2,1,0:T(8,128)(2,1)}), bf16[16,96,1024]{2,1,0:T(8,128)(2,1)}, u32[]{:S(2)}, u32[]{:S(2)}) %all-to-all-start.2) | async-done | bytes 3145760 | tf_op jit(solution)/shard_map/all_to_all | solution.py:86
  167.1 6.8 %multiply_convert_fusion = (bf16[1536,512]{1,0:T(8,128)(2,1)S(1)}, bf16[1536,512]{1,0:T(8,128)(2,1)}, bf16[1536,512]{1,0:T(8,128)(2,1)S(1)}) fusion(f32[1536,512]{1,0:T(8,128)} %fusion.23, f32[1536,512]{1,0:T(8,128)} %fusion.19, bf16[1536,1024]{1,0:T(8,128)(2,1)} %bitcast.15, bf16[1,512,1024]{2,1,0:T(8,128)(2,1)S(1)} %copy-done), kind=kOutput, calls=%fused_computation.12 | convolution fusion | flops 1622409216 | bytes 15204352 | tf_op jit(solution)/shard_map/erl,efl->erf/dot_general | solution.py:33
  173.9 3.5 %convolution_convert_fusion = bf16[1536,1024]{1,0:T(8,128)(2,1)} fusion(bf16[1536,512]{1,0:T(8,128)(2,1)S(1)} %get-tuple-element.16, bf16[1,512,1024]{2,1,0:T(8,128)(2,1)S(1)} %copy-done), kind=kOutput, calls=%fused_computation.11 | convolution fusion | flops 1612185600 | bytes 5767168 | tf_op jit(solution)/shard_map/erf,efl->erl/dot_general | solution.py:22
  177.4 4.9 %all-to-all-start.1 = ((bf16[16,96,1024]{2,1,0:T(8,128)(2,1)}), bf16[16,96,1024]{2,1,0:T(8,128)(2,1)}, u32[]{:S(2)}, u32[]{:S(2)}) async-start(bf16[16,96,1024]{2,1,0:T(8,128)(2,1)} %bitcast.78), calls=%async_computation.1 | async-start | bytes 6291456 | tf_op jit(solution)/shard_map/all_to_all | solution.py:85
  182.4 3.7 %fusion.21 = f32[1536,1024]{1,0:T(8,128)S(1)} fusion(bf16[1536,512]{1,0:T(8,128)(2,1)} %get-tuple-element.15, bf16[1,1024,512]{2,1,0:T(8,128)(2,1)} %param.11), kind=kOutput, calls=%fused_computation.37 | convolution fusion | flops 1610612736 | bytes 8912896 | tf_op jit(solution)/shard_map/erf,elf->erl/dot_general | solution.py:45
  186.1 3.7 %add_convert_fusion = bf16[1536,1024]{1,0:T(8,128)(2,1)} fusion(f32[1536,1024]{1,0:T(8,128)S(1)} %fusion.21, bf16[1536,512]{1,0:T(8,128)(2,1)S(1)} %get-tuple-element.14, bf16[1,1024,512]{2,1,0:T(8,128)(2,1)S(1)} %copy-done.3), kind=kOutput, calls=%fused_computation.4 | convolution fusion | flops 1613758464 | bytes 12058624 | tf_op jit(solution)/shard_map/erf,elf->erl/dot_general | solution.py:46
  189.7 62.6 %all-to-all-done.1 = bf16[16,96,1024]{2,1,0:T(8,128)(2,1)} async-done(((bf16[16,96,1024]{2,1,0:T(8,128)(2,1)}), bf16[16,96,1024]{2,1,0:T(8,128)(2,1)}, u32[]{:S(2)}, u32[]{:S(2)}) %all-to-all-start.1) | async-done | bytes 3145760 | tf_op jit(solution)/shard_map/all_to_all | solution.py:85
  252.4 4.9 %all-to-all-start.3 = ((bf16[16,96,1024]{2,1,0:T(8,128)(2,1)}), bf16[16,96,1024]{2,1,0:T(8,128)(2,1)}, u32[]{:S(2)}, u32[]{:S(2)}) async-start(bf16[16,96,1024]{2,1,0:T(8,128)(2,1)} %bitcast.77), calls=%async_computation.3 | async-start | bytes 6291456 | tf_op jit(solution)/shard_map/all_to_all | solution.py:90
  257.3 5.1 %fusion.14 = bf16[1,512,1024]{2,1,0:T(8,128)(2,1)} fusion(bf16[1536,512]{1,0:T(8,128)(2,1)} %copy-done.8, bf16[1536,1024]{1,0:T(8,128)(2,1)} %bitcast.15), kind=kOutput, calls=%fused_computation.30 | convolution fusion | flops 1611137024 | bytes 5767168 | tf_op jit(solution)/shard_map/erf,erl->efl/dot_general | solution.py:30
  262.4 4.8 %fusion.13 = bf16[1,1024,512]{2,1,0:T(8,128)(2,1)} fusion(bf16[1536,1024]{1,0:T(8,128)(2,1)} %bitcast.6, bf16[1536,512]{1,0:T(8,128)(2,1)S(1)} %get-tuple-element.14), kind=kOutput, calls=%fused_computation.29 | convolution fusion | flops 1611137024 | bytes 5767168 | tf_op jit(solution)/shard_map/erl,erf->elf/dot_general | solution.py:41
  267.2 4.7 %fusion.12 = bf16[1,1024,512]{2,1,0:T(8,128)(2,1)} fusion(bf16[1536,1024]{1,0:T(8,128)(2,1)} %bitcast.6, bf16[1536,512]{1,0:T(8,128)(2,1)S(1)} %copy-done.7), kind=kOutput, calls=%fused_computation.28 | convolution fusion | flops 1611137024 | bytes 5767168 | tf_op jit(solution)/shard_map/erl,erf->elf/dot_general | solution.py:38
  271.9 7.3 %gather_fusion = bf16[1024,1024]{1,0:T(8,128)(2,1)S(1)} fusion(bf16[1536,1024]{1,0:T(8,128)(2,1)} %bitcast.11, s32[1024]{0:T(1024)S(1)} %broadcast_clamp_fusion), kind=kCustom, calls=%fused_computation | custom fusion | bytes 4198400 | tf_op jit(solution)/shard_map/gather | solution.py:92
  279.2 3.4 %fusion.1 = (f32[128,8]{1,0:T(8,128)S(1)}, bf16[128,1024]{1,0:T(8,128)(2,1)}) fusion(bf16[1024,1024]{1,0:T(8,128)(2,1)S(1)} %gather_fusion, f32[128,1024]{1,0:T(8,128)} %copy-done.1, f32[128,8]{1,0:T(8,128)S(1)} %copy.23), kind=kLoop, calls=%fused_computation.8 | loop fusion | flops 5110784 | bytes 2891776 | tf_op jit(solution)/shard_map/reduce_sum | solution.py:102
  282.6 0.7 copy.30
  283.3 44.0 %all-to-all-done.3 = bf16[16,96,1024]{2,1,0:T(8,128)(2,1)} async-done(((bf16[16,96,1024]{2,1,0:T(8,128)(2,1)}), bf16[16,96,1024]{2,1,0:T(8,128)(2,1)}, u32[]{:S(2)}, u32[]{:S(2)}) %all-to-all-start.3) | async-done | bytes 3145760 | tf_op jit(solution)/shard_map/all_to_all | solution.py:90
  327.3 7.3 %gather_fusion.1 = bf16[1024,1024]{1,0:T(8,128)(2,1)S(1)} fusion(bf16[1536,1024]{1,0:T(8,128)(2,1)} %bitcast.17, s32[1024]{0:T(1024)S(1)} %broadcast_clamp_fusion), kind=kCustom, calls=%fused_computation.1 | custom fusion | bytes 4198400 | tf_op jit(solution)/shard_map/gather | solution.py:97
  334.5 2.1 bitcast_reduce_fusion
  (30 shorter events, 0.6 us)
Async XLA Ops:
  0.6 166.5 %copy-start = (bf16[1,512,1024]{2,1,0:T(8,128)(2,1)S(1)}, bf16[1,512,1024]{2,1,0:T(8,128)(2,1)}, u32[]{:S(2)}) copy-start(bf16[1,512,1024]{2,1,0:T(8,128)(2,1)} %param.13) | copy-start | bytes 3145732
  15.4 6.7 %copy-start.5 = (f32[128,8]{0,1:T(8,128)S(1)}, f32[128,8]{0,1:T(8,128)}, u32[]{:S(2)}) copy-start(f32[128,8]{0,1:T(8,128)} %param.9) | copy-start | bytes 12292
  15.4 6.9 %copy-start.4 = (bf16[128,1024]{1,0:T(8,128)(2,1)S(1)}, bf16[128,1024]{1,0:T(8,128)(2,1)}, u32[]{:S(2)}) copy-start(bf16[128,1024]{1,0:T(8,128)(2,1)} %param.10) | copy-start | bytes 786436
  15.4 76.7 %all-to-all-start = ((bf16[16,96,1024]{2,1,0:T(8,128)(2,1)}), bf16[16,96,1024]{2,1,0:T(8,128)(2,1)}, u32[]{:S(2)}, u32[]{:S(2)}) async-start(bf16[16,96,1024]{2,1,0:T(8,128)(2,1)} %bitcast.76), calls=%async_computation | async-start | bytes 6291456 | tf_op jit(solution)/shard_map/all_to_all | solution.py:82
  22.3 69.7 %copy-start.1 = (f32[128,1024]{1,0:T(8,128)}, f32[128,1024]{1,0:T(8,128)S(1)}, u32[]{:S(2)}) copy-start(f32[128,1024]{1,0:T(8,128)S(1)} %convert_element_type.72) | copy-start | bytes 1572868
  92.1 5.0 %copy-start.2 = (bf16[1,1024,512]{2,1,0:T(8,128)(2,1)S(1)}, bf16[1,1024,512]{2,1,0:T(8,128)(2,1)}, u32[]{:S(2)}) copy-start(bf16[1,1024,512]{2,1,0:T(8,128)(2,1)} %param.12) | copy-start | bytes 3145732
  92.1 75.0 %all-to-all-start.2 = ((bf16[16,96,1024]{2,1,0:T(8,128)(2,1)}), bf16[16,96,1024]{2,1,0:T(8,128)(2,1)}, u32[]{:S(2)}, u32[]{:S(2)}) async-start(bf16[16,96,1024]{2,1,0:T(8,128)(2,1)} %bitcast.75), calls=%async_computation.2 | async-start | bytes 6291456 | tf_op jit(solution)/shard_map/all_to_all | solution.py:86
  97.1 5.5 %copy-start.6 = (bf16[1,1024,512]{2,1,0:T(8,128)(2,1)S(1)}, bf16[1,1024,512]{2,1,0:T(8,128)(2,1)}, u32[]{:S(2)}) copy-start(bf16[1,1024,512]{2,1,0:T(8,128)(2,1)} %param.11) | copy-start | bytes 3145732
  173.9 3.5 %copy-start.8 = (bf16[1536,512]{1,0:T(8,128)(2,1)}, bf16[1536,512]{1,0:T(8,128)(2,1)S(1)}, u32[]{:S(2)}) copy-start(bf16[1536,512]{1,0:T(8,128)(2,1)S(1)} %get-tuple-element.16) | copy-start | bytes 4718596
  177.4 74.9 %all-to-all-start.1 = ((bf16[16,96,1024]{2,1,0:T(8,128)(2,1)}), bf16[16,96,1024]{2,1,0:T(8,128)(2,1)}, u32[]{:S(2)}, u32[]{:S(2)}) async-start(bf16[16,96,1024]{2,1,0:T(8,128)(2,1)} %bitcast.78), calls=%async_computation.1 | async-start | bytes 6291456 | tf_op jit(solution)/shard_map/all_to_all | solution.py:85
  182.4 3.7 %copy-start.3 = (bf16[1,1024,512]{2,1,0:T(8,128)(2,1)S(1)}, bf16[1,1024,512]{2,1,0:T(8,128)(2,1)}, u32[]{:S(2)}) copy-start(bf16[1,1024,512]{2,1,0:T(8,128)(2,1)} %param.12) | copy-start | bytes 3145732
  252.4 74.9 %all-to-all-start.3 = ((bf16[16,96,1024]{2,1,0:T(8,128)(2,1)}), bf16[16,96,1024]{2,1,0:T(8,128)(2,1)}, u32[]{:S(2)}, u32[]{:S(2)}) async-start(bf16[16,96,1024]{2,1,0:T(8,128)(2,1)} %bitcast.77), calls=%async_computation.3 | async-start | bytes 6291456 | tf_op jit(solution)/shard_map/all_to_all | solution.py:90
  262.4 4.8 %copy-start.7 = (bf16[1536,512]{1,0:T(8,128)(2,1)S(1)}, bf16[1536,512]{1,0:T(8,128)(2,1)}, u32[]{:S(2)}) copy-start(bf16[1536,512]{1,0:T(8,128)(2,1)} %get-tuple-element.15) | copy-start | bytes 4718596
where the time goes:
time: 337 us
  waiting for transfers between devices  228 us (68%)
  matrix products  43.1 us (13%)
  local copies, waits for them, and re-layouts  24.7 us (7%)
  starting transfers between devices  21.5 us (6%)
  other arithmetic  18.9 us (6%)
    all_to_all x1, waiting for transfers between devices, local(): lax.all_to_all(to_home(expert_out), 'ep', split_axis=0, concat_axis=0, ti...  62.6 us
    all_to_all x1, waiting for transfers between devices, local(): lax.all_to_all(send_rows, 'ep', split_axis=0, concat_axis=0, tiled=True)  61.9 us
    all_to_all x1, waiting for transfers between devices, local(): lax.all_to_all(send_cot, 'ep', split_axis=0, concat_axis=0, tiled=True)  59.2 us
    all_to_all x1, waiting for transfers between devices, local(): lax.all_to_all(to_home(grad_rows), 'ep', split_axis=0, concat_axis=0, til...  44 us
    scatter x1, other arithmetic, local(): send_cot = jnp.zeros((expert_count * capacity, width), jnp.bfloat16).at[p...  7.82 us
    scatter x1, local copies, waits for them, and re-layouts, local(): jnp.zeros((expert_count * capacity, width), jnp.bfloat16).at[position]  7.78 us
    gather x1, local copies, waits for them, and re-layouts, local(): back_grad.reshape(-1, width)[position].reshape(tok_count, top_count, width)  7.27 us
    gather x1, local copies, waits for them, and re-layouts, local(): back_out.reshape(-1, width)[position].reshape(tok_count, top_count, width)  7.27 us
  transfers between devices with their start and end apart: 4, of which 4 were waited for; matrix products, arithmetic and copies ran while one was open for 15% of the time, Pallas kernels for 0%

commit v1 on v0

--- a/solution.py
+++ b/solution.py
@@ -48,7 +48,7 @@
     return (grad_rows, grad_gw, grad_uw, grad_down)
 
 
-def local(latent_in, routes, combine_weights, cotangent, w_gate, w_up, w_down):
+def exchanged(latent_in, routes, combine_weights, cotangent, w_gate, w_up, w_down):
     devices_ep = lax.axis_size("ep")
     local_experts = w_gate.shape[0]
     expert_count = local_experts * devices_ep
@@ -104,6 +104,60 @@
     return (combined, grad_latent, grad_combine, grad_gw, grad_uw, grad_down)
 
 
+def dot(a, b, dims):
+    return lax.dot_general(a, b, (dims, ((), ())), preferred_element_type=jnp.float32)
+
+
+def gathered(latent_in, routes, combine_weights, cotangent, w_gate, w_up, w_down):
+    devices_ep = lax.axis_size("ep")
+    tok_count = latent_in.shape[0]
+    bf16, f32 = jnp.bfloat16, jnp.float32
+    chosen = routes[:, :, None] == jnp.arange(devices_ep, dtype=jnp.int32)[None, None, :]
+    share = jnp.sum(jnp.where(chosen, combine_weights[:, :, None], 0.0), axis=1)
+    share = lax.all_to_all(
+        share.T.reshape(devices_ep, 1, tok_count), "ep", split_axis=0, concat_axis=0, tiled=True
+    )
+    share = share.reshape(devices_ep * tok_count, 1)
+    rows = lax.all_gather(latent_in, "ep", axis=0, tiled=True)
+    cot = lax.all_gather(cotangent, "ep", axis=0, tiled=True)
+    gate_w, up_w, down_w = w_gate[0], w_up[0], w_down[0]
+
+    gate_pre = dot(rows, gate_w, ((1,), (0,)))
+    up_pre = dot(rows, up_w, ((1,), (0,)))
+    sigma = jax.nn.sigmoid(gate_pre)
+    silu_val = gate_pre * sigma
+    hidden = (silu_val * up_pre).astype(bf16)
+    out = dot(hidden, down_w, ((1,), (0,)))
+    back_out = lax.psum_scatter(
+        (share * out).astype(bf16), "ep", scatter_dimension=0, tiled=True
+    )
+    cot32 = cot.astype(f32)
+    inner = jnp.sum(cot32 * out, axis=1)
+    inner = lax.all_to_all(
+        inner.reshape(devices_ep, tok_count), "ep", split_axis=0, concat_axis=0, tiled=True
+    )
+    weighted = (share * cot32).astype(bf16)
+    grad_hidden = dot(weighted, down_w, ((1,), (1,)))
+    grad_gate = (grad_hidden * up_pre * sigma * (1.0 + gate_pre * (1.0 - sigma))).astype(bf16)
+    grad_up = (grad_hidden * silu_val).astype(bf16)
+    grad_rows = dot(grad_gate, gate_w, ((1,), (1,))) + dot(grad_up, up_w, ((1,), (1,)))
+    back_grad = lax.psum_scatter(
+        grad_rows.astype(bf16), "ep", scatter_dimension=0, tiled=True
+    )
+    grad_down = dot(hidden, weighted, ((0,), (0,))).astype(bf16)
+    grad_gw = dot(rows, grad_gate, ((0,), (0,))).astype(bf16)
+    grad_uw = dot(rows, grad_up, ((0,), (0,))).astype(bf16)
+    grad_combine = jnp.sum(jnp.where(chosen, inner.T[:, None, :], 0.0), axis=2)
+    return (back_out, back_grad, grad_combine, grad_gw[None], grad_uw[None], grad_down[None])
+
+
+def local(latent_in, routes, combine_weights, cotangent, w_gate, w_up, w_down):
+    every = latent_in.shape[0] * lax.axis_size("ep")
+    slots = latent_in.shape[0] * routes.shape[1] * 3 // 2
+    plan = gathered if w_gate.shape[0] == 1 and every <= 2 * slots else exchanged
+    return plan(latent_in, routes, combine_weights, cotangent, w_gate, w_up, w_down)
+
+
 def solution(mesh):
     return jax.shard_map(
         local,

time: 337 us -> 304 us (0.902)
  the two profiles are of different devices: /device:TPU:11 before, /device:TPU:0 now
where the time goes in v1:
time: 304 us
  waiting for transfers between devices  204 us (67%)
  matrix products  48.9 us (16%)
  blocking collectives  18.1 us (6%)
  local copies, waits for them, and re-layouts  14.7 us (5%)
  between operations  13.9 us (5%)
  other arithmetic  3.82 us (1%)
    reduce_scatter x1, waiting for transfers between devices, gathered(): lax.psum_scatter(grad_rows.astype(bf16), 'ep', scatter_dimension=0, tiled...  76.2 us
    all_gather x1, waiting for transfers between devices, gathered(): rows = lax.all_gather(latent_in, 'ep', axis=0, tiled=True)  53.6 us
    dot_general x9, matrix products, dot(): lax.dot_general(a, b, (dims, ((), ())), preferred_element_type=jnp.float32)  48.9 us
    all_gather x1, waiting for transfers between devices, gathered(): cot = lax.all_gather(cotangent, 'ep', axis=0, tiled=True)  41.6 us
    unnamed x5, waiting for transfers between devices  32.4 us
    unnamed x22, local copies, waits for them, and re-layouts  14.7 us
    all_to_all x1, blocking collectives, gathered(): lax.all_to_all(inner.reshape(devices_ep, tok_count), 'ep', split_axis=0,...  9.17 us
    all_to_all x1, blocking collectives, gathered(): lax.all_to_all(share.T.reshape(devices_ep, 1, tok_count), 'ep', split_axi...  8.97 us
  transfers between devices with their start and end apart: 4, of which 4 were waited for; matrix products, arithmetic and copies ran while one was open for 17% of the time, Pallas kernels for 0%

profile of v1, /device:TPU:0, one launch (start us, length us, event | category | flops | bytes accessed | tf_op | source)
XLA Modules:
  0.0 303.6 jit_solution(326847924279250343)
XLA Ops:
  7.2 0.0 copy-start
  7.2 0.0 all-gather.3.cloned.1.call-start
  7.2 0.7 all-gather.3.cloned.1.call-update
  7.9 0.0 all-gather.5.cloned.1.call-start
  8.0 1.8 copy.35
  9.8 0.0 all-gather.5.cloned.1.call-update
  9.8 0.0 reduce-scatter.7.cloned.1.call-start
  9.8 53.6 %all-gather.3.cloned.1.call-done = bf16[2048,1024]{1,0:T(8,128)(2,1)} async-done(((bf16[128,1024]{1,0:T(8,128)(2,1)}), bf16[2048,1024]{1,0:T(8,128)(2,1)}) %all-gather.3.cloned.1.call-update) | async-done | bytes 4194320 | tf_op jit(solution)/shard_map/all_gather | solution.py:121
  63.5 5.0 %fusion.23 = f32[2048,512]{1,0:T(8,128)S(1)} fusion(bf16[2048,1024]{1,0:T(8,128)(2,1)} %all-gather.3.cloned.1.call-done, bf16[1,1024,512]{2,1,0:T(8,128)(2,1)} %param.11), kind=kOutput, calls=%fused_computation.27 | convolution fusion | flops 2147483648 | bytes 9437184 | tf_op jit(solution)/shard_map/dot_general | solution.py:108
  68.5 1.9 copy-done.8
  70.4 6.0 %multiply_convert_fusion.3 = (bf16[2048,512]{1,0:T(8,128)(2,1)S(1)}, f32[2048,512]{1,0:T(8,128)}) fusion(f32[2048,512]{1,0:T(8,128)S(1)} %fusion.23, bf16[2048,1024]{1,0:T(8,128)(2,1)S(1)} %copy-done.3, bf16[1,1024,512]{2,1,0:T(8,128)(2,1)} %param.12), kind=kOutput, calls=%fused_computation.8 | convolution fusion | flops 2153775104 | bytes 15728640 | tf_op jit(solution)/shard_map/dot_general | solution.py:108
  76.4 41.6 %all-gather.5.cloned.1.call-done = bf16[2048,1024]{0,1:T(8,128)(2,1)} async-done(((bf16[128,1024]{0,1:T(8,128)(2,1)}), bf16[2048,1024]{0,1:T(8,128)(2,1)}) %all-gather.5.cloned.1.call-update) | async-done | bytes 4194320 | tf_op jit(solution)/shard_map/all_gather | solution.py:122
  117.9 4.9 %fusion.1 = (f32[2048]{0:T(1024)S(1)}, f32[2048,1024]{0,1:T(8,128)S(1)}) fusion(bf16[2048,1024]{0,1:T(8,128)(2,1)} %all-gather.5.cloned.1.call-done, bf16[2048,512]{1,0:T(8,128)(2,1)S(1)} %get-tuple-element.34, bf16[1,512,1024]{2,1,0:T(8,128)(2,1)S(1)} %copy-done), kind=kOutput, calls=%fused_computation.3 | convolution fusion | flops 2153773056 | bytes 15736832 | tf_op jit(solution)/shard_map/dot_general | solution.py:108
  122.8 9.2 %all_to_all.17 = f32[16,1,128]{2,1,0:T(1,128)S(1)} all-to-all(f32[16,1,128]{2,1,0:T(1,128)S(1)} %bitcast.54), channel_id=1, replica_groups=mesh['grp'=2,'ep'=16] {'ep'}, dimensions={0} | all-to-all | bytes 16384 | tf_op jit(solution)/shard_map/all_to_all | solution.py:136
  132.0 0.6 select_reduce_fusion
  132.6 9.0 %all_to_all.18 = f32[16,1,128]{2,1,0:T(1,128)S(1)} all-to-all(f32[16,1,128]{2,1,0:T(1,128)S(1)} %bitcast.56), channel_id=1, replica_groups=mesh['grp'=2,'ep'=16] {'ep'}, dimensions={0} | all-to-all | bytes 16384 | tf_op jit(solution)/shard_map/all_to_all | solution.py:117
  141.6 3.2 %multiply_convert_fusion = bf16[2048,1024]{0,1:T(8,128)(2,1)} fusion(f32[2048,1024]{0,1:T(8,128)S(1)} %get-tuple-element.37, f32[2048]{0:T(1024)S(1)} %bitcast.57), kind=kLoop, calls=%fused_computation.5 | loop fusion | flops 4194304 | bytes 12591104 | tf_op jit(solution)/shard_map/convert_element_type | solution.py:132
  144.8 6.4 %copy.40 = bf16[2048,1024]{1,0:T(8,128)(2,1)} copy(bf16[2048,1024]{0,1:T(8,128)(2,1)} %multiply_convert_fusion) | data formatting | bytes 8388608
  151.2 0.0 reduce-scatter.7.cloned.1.call-update
  151.2 0.2 reduce-scatter.5.cloned.1.call-start
  151.4 0.0 copy-start.4
  151.4 8.2 %multiply_convert_fusion.1 = (bf16[2048,512]{1,0:T(8,128)(2,1)S(1)}, bf16[2048,512]{1,0:T(8,128)(2,1)S(1)}) fusion(f32[2048,512]{1,0:T(8,128)} %copy-done.8, f32[2048,512]{1,0:T(8,128)} %get-tuple-element.35, bf16[1,512,1024]{2,1,0:T(8,128)(2,1)S(1)} %copy-done, bf16[2048,1024]{0,1:T(8,128)(2,1)} %all-gather.5.cloned.1.call-done, f32[2048]{0:T(1024)S(1)} %bitcast.58), kind=kOutput, calls=%fused_computation.6 | convolution fusion | flops 2167406592 | bytes 17833984 | tf_op jit(solution)/shard_map/dot_general | solution.py:108
  159.6 2.4 fusion.21
  162.0 4.4 %add_convert_fusion = bf16[2048,1024]{1,0:T(8,128)(2,1)} fusion(f32[2048,1024]{1,0:T(8,128)S(1)} %fusion.21, bf16[2048,512]{1,0:T(8,128)(2,1)S(1)} %get-tuple-element.32, bf16[1,1024,512]{2,1,0:T(8,128)(2,1)S(1)} %copy-done.5), kind=kOutput, calls=%fused_computation.4 | convolution fusion | flops 2151677952 | bytes 15728640 | tf_op jit(solution)/shard_map/dot_general | solution.py:108
  166.5 0.0 reduce-scatter.5.cloned.1.call-update
  166.5 6.4 %fusion.10 = bf16[1,1024,512]{1,2,0:T(8,128)(2,1)} fusion(bf16[2048,512]{1,0:T(8,128)(2,1)} %copy-done.6, bf16[2048,1024]{1,0:T(8,128)(2,1)} %all-gather.3.cloned.1.call-done), kind=kOutput, calls=%fused_computation.16 | convolution fusion | flops 2148007936 | bytes 7340032 | tf_op jit(solution)/shard_map/dot_general | solution.py:108
  172.9 2.3 copy.38
  175.1 6.2 %fusion.11 = bf16[1,1024,512]{1,2,0:T(8,128)(2,1)} fusion(bf16[2048,512]{1,0:T(8,128)(2,1)} %copy-done.7, bf16[2048,1024]{1,0:T(8,128)(2,1)} %all-gather.3.cloned.1.call-done), kind=kOutput, calls=%fused_computation.17 | convolution fusion | flops 2148007936 | bytes 7340032 | tf_op jit(solution)/shard_map/dot_general | solution.py:108
  181.3 2.3 copy.39
  183.6 5.6 %fusion.12 = bf16[1,512,1024]{2,1,0:T(8,128)(2,1)} fusion(bf16[2048,512]{1,0:T(8,128)(2,1)S(1)} %get-tuple-element.34, bf16[2048,1024]{0,1:T(8,128)(2,1)} %all-gather.5.cloned.1.call-done, f32[2048]{0:T(1024)S(1)} %bitcast.59), kind=kOutput, calls=%fused_computation.18 | convolution fusion | flops 2154299392 | bytes 7348224 | tf_op jit(solution)/shard_map/dot_general | solution.py:108
  189.1 31.7 %reduce-scatter.7.cloned.1.call-done = bf16[128,1024]{1,0:T(8,128)(2,1)} async-done(((bf16[2048,1024]{1,0:T(8,128)(2,1)}), bf16[128,1024]{1,0:T(8,128)(2,1)}) %reduce-scatter.7.cloned.1.call-update) | async-done | bytes 262160
  220.9 76.2 %reduce-scatter.5.cloned.1.call-done = bf16[128,1024]{1,0:T(8,128)(2,1)} async-done(((bf16[2048,1024]{1,0:T(8,128)(2,1)}), bf16[128,1024]{1,0:T(8,128)(2,1)}) %reduce-scatter.5.cloned.1.call-update) | async-done | bytes 262160 | tf_op jit(solution)/shard_map/reduce_scatter | solution.py:144
  (15 shorter events, 0.0 us)
Async XLA Ops:
  7.2 110.8 %copy-start = (bf16[1,512,1024]{2,1,0:T(8,128)(2,1)S(1)}, bf16[1,512,1024]{2,1,0:T(8,128)(2,1)}, u32[]{:S(2)}) copy-start(bf16[1,512,1024]{2,1,0:T(8,128)(2,1)} %param.13) | copy-start | bytes 3145732
  7.2 56.3 %all-gather.3.cloned.1.call-start = ((), (), s32[]{:S(2)}) async-start(), calls=%async_computation.4 | async-start | bytes 4456448 | tf_op jit(solution)/shard_map/all_gather | solution.py:121
  7.9 110.0 %all-gather.5.cloned.1.call-start = ((), (), s32[]{:S(2)}) async-start(), calls=%async_computation.5 | async-start | bytes 4456448 | tf_op jit(solution)/shard_map/all_gather | solution.py:122
  9.8 211.1 %reduce-scatter.7.cloned.1.call-start = ((), (), s32[]{:S(2)}) async-start(), calls=%async_computation.7 | async-start | bytes 4456448
  63.5 6.9 %copy-start.3 = (bf16[2048,1024]{1,0:T(8,128)(2,1)S(1)}, bf16[2048,1024]{1,0:T(8,128)(2,1)}, u32[]{:S(2)}) copy-start(bf16[2048,1024]{1,0:T(8,128)(2,1)} %all-gather.3.cloned.1.call-done) | copy-start | bytes 12582916
  68.5 1.9 copy-start.8
  117.9 14.0 %copy-start.1 = (s32[128,8]{0,1:T(8,128)S(1)}, s32[128,8]{0,1:T(8,128)}, u32[]{:S(2)}) copy-start(s32[128,8]{0,1:T(8,128)} %param.8) | copy-start | bytes 12292
  117.9 14.0 %copy-start.2 = (f32[128,8]{0,1:T(8,128)S(1)}, f32[128,8]{0,1:T(8,128)}, u32[]{:S(2)}) copy-start(f32[128,8]{0,1:T(8,128)} %param.9) | copy-start | bytes 12292
  151.2 145.9 %reduce-scatter.5.cloned.1.call-start = ((), (), s32[]{:S(2)}) async-start(), calls=%async_computation.6 | async-start | bytes 4456448 | tf_op jit(solution)/shard_map/reduce_scatter | solution.py:144
  151.4 8.2 %copy-start.4 = (bf16[1,1024,512]{2,1,0:T(8,128)(2,1)S(1)}, bf16[1,1024,512]{2,1,0:T(8,128)(2,1)}, u32[]{:S(2)}) copy-start(bf16[1,1024,512]{2,1,0:T(8,128)(2,1)} %param.11) | copy-start | bytes 3145732
  159.6 2.4 copy-start.6
  159.6 2.4 copy-start.7
  159.6 2.4 copy-start.5
Sparse Core Ops, SparseCore 0:
  10.2 53.2 all-gather.2
  66.2 51.7 all-gather.4
  151.3 69.4 reduce-scatter.6
  225.6 71.4 reduce-scatter.4

commit v2 on v0

--- a/solution.py
+++ b/solution.py
@@ -48,7 +48,7 @@
     return (grad_rows, grad_gw, grad_uw, grad_down)
 
 
-def local(latent_in, routes, combine_weights, cotangent, w_gate, w_up, w_down):
+def exchanged(latent_in, routes, combine_weights, cotangent, w_gate, w_up, w_down):
     devices_ep = lax.axis_size("ep")
     local_experts = w_gate.shape[0]
     expert_count = local_experts * devices_ep
@@ -104,6 +104,107 @@
     return (combined, grad_latent, grad_combine, grad_gw, grad_uw, grad_down)
 
 
+def dot(a, b, dims):
+    return lax.dot_general(a, b, (dims, ((), ())), preferred_element_type=jnp.float32)
+
+
+def swap(value, bit):
+    pairs = [(i, i ^ bit) for i in range(lax.axis_size("ep"))]
+    return lax.ppermute(value, "ep", pairs)
+
+
+CORE, SIDE, NEAR, FAR = 1, 2, 4, 8
+REACH = (0, NEAR, FAR, NEAR | FAR, SIDE, SIDE | NEAR, SIDE | FAR, SIDE | NEAR | FAR)
+
+
+def collect(block):
+    near = swap(block, NEAR)
+    far = swap(block, FAR)
+    both = swap(far, NEAR)
+    line = [block, near, far, both]
+    return line + [swap(item, SIDE) for item in line]
+
+
+def give_back(parts):
+    bf16, f32 = jnp.bfloat16, jnp.float32
+    other = [swap(item, SIDE) for item in parts[4:]]
+    line = [a.astype(f32) + b.astype(f32) for a, b in zip(parts[:4], other)]
+    both = swap(line[3].astype(bf16), NEAR)
+    near = swap(line[1].astype(bf16), NEAR)
+    far = swap((line[2] + both.astype(f32)).astype(bf16), FAR)
+    return (line[0] + near.astype(f32) + far.astype(f32)).astype(bf16)
+
+
+def paired(latent_in, routes, combine_weights, cotangent, w_gate, w_up, w_down):
+    devices_ep = lax.axis_size("ep")
+    me = lax.axis_index("ep")
+    tok_count = latent_in.shape[0]
+    bf16, f32 = jnp.bfloat16, jnp.float32
+    experts = jnp.arange(devices_ep, dtype=jnp.int32)
+    sources = jnp.stack([me ^ bits for bits in REACH])
+    mine = jnp.stack([me, me ^ CORE])
+
+    chosen = routes[None, :, :] == experts[:, None, None]
+    share = jnp.sum(jnp.where(chosen, combine_weights[None, :, :], 0.0), axis=2)
+    share = lax.all_gather(share, "ep", axis=0, tiled=False)
+    rows = jnp.concatenate(collect(latent_in), axis=0)
+    weights = [w_gate[0], w_up[0], w_down[0]]
+    both_w = [weights, [swap(w, CORE) for w in weights]]
+    cot = jnp.concatenate(collect(cotangent), axis=0)
+    share = share[sources][:, mine, :]
+
+    partial_out, saved = 0.0, []
+    for i, (gate_w, up_w, down_w) in enumerate(both_w):
+        part = share[:, i, :].reshape(-1, 1)
+        gate_pre = dot(rows, gate_w, ((1,), (0,)))
+        up_pre = dot(rows, up_w, ((1,), (0,)))
+        sigma = jax.nn.sigmoid(gate_pre)
+        silu_val = gate_pre * sigma
+        hidden = silu_val * up_pre
+        weighted = (part * hidden).astype(bf16)
+        partial_out = partial_out + dot(weighted, down_w, ((1,), (0,)))
+        saved.append((part, gate_pre, up_pre, sigma, silu_val, hidden, weighted))
+    back = partial_out.astype(bf16).reshape(len(REACH), tok_count, -1)
+    combined = give_back([back[i] for i in range(len(REACH))])
+
+    inner, grad_rows, grads = [], 0.0, []
+    for (gate_w, up_w, down_w), kept in zip(both_w, saved):
+        part, gate_pre, up_pre, sigma, silu_val, hidden, weighted = kept
+        plain = dot(cot, down_w, ((1,), (1,)))
+        inner.append(jnp.sum(hidden * plain, axis=1).reshape(len(REACH), tok_count))
+        grad_hidden = part * plain
+        grad_gate = (grad_hidden * up_pre * sigma * (1.0 + gate_pre * (1.0 - sigma))).astype(bf16)
+        grad_up = (grad_hidden * silu_val).astype(bf16)
+        grad_rows = grad_rows + dot(grad_gate, gate_w, ((1,), (1,)))
+        grad_rows = grad_rows + dot(grad_up, up_w, ((1,), (1,)))
+        grads.append((weighted, grad_gate, grad_up))
+    inner = jnp.stack(inner, axis=1)
+    at_source = (sources[None, :] == experts[:, None]).astype(f32)
+    at_expert = (mine[None, :] == experts[:, None]).astype(f32)
+    inner = jnp.einsum("ds,ei,sit->det", at_source, at_expert, inner, precision="highest")
+    inner = lax.psum_scatter(inner, "ep", scatter_dimension=0, tiled=False)
+    grad_combine = jnp.sum(jnp.where(chosen, inner[:, :, None], 0.0), axis=0)
+
+    back = grad_rows.astype(bf16).reshape(len(REACH), tok_count, -1)
+    grad_latent = give_back([back[i] for i in range(len(REACH))])
+
+    def weight_grads(weighted, grad_gate, grad_up):
+        return (
+            dot(rows, grad_gate, ((0,), (0,))),
+            dot(rows, grad_up, ((0,), (0,))),
+            dot(weighted, cot, ((0,), (0,))),
+        )
+
+    away = [swap(g.astype(bf16), CORE) for g in weight_grads(*grads[1])]
+    grad_w = [(g + a.astype(f32)).astype(bf16)[None] for g, a in zip(weight_grads(*grads[0]), away)]
+    return (combined, grad_latent, grad_combine, *grad_w)
+
+
+def local(latent_in, routes, combine_weights, cotangent, w_gate, w_up, w_down):
+    plan = paired if w_gate.shape[0] == 1 and lax.axis_size("ep") == 2 * len(REACH) else exchanged
+    return plan(latent_in, routes, combine_weights, cotangent, w_gate, w_up, w_down)
+
+
 def solution(mesh):
     return jax.shard_map(
         local,

time: 337 us -> 261 us (0.77)
  the two profiles are of different devices: /device:TPU:11 before, /device:TPU:0 now
where the time goes in v2:
time: 261 us; the launch traced here: 260 us
  waiting for transfers between devices  136 us (52%)
  matrix products  37.9 us (15%)
  starting transfers between devices  31 us (12%)
  blocking collectives  20 us (8%)
  between operations  14.5 us (6%)
  local copies, waits for them, and re-layouts  11.5 us (4%)
  other arithmetic  9.2 us (4%)
    ppermute x34, waiting for transfers between devices, swap(): return lax.ppermute(value, 'ep', pairs)  81.3 us
    reduce_scatter x1, waiting for transfers between devices, paired(): inner = lax.psum_scatter(inner, 'ep', scatter_dimension=0, tiled=False)  54.8 us
    dot_general x18, matrix products, dot(): lax.dot_general(a, b, (dims, ((), ())), preferred_element_type=jnp.float32)  36.7 us
    ppermute x34, starting transfers between devices, swap(): return lax.ppermute(value, 'ep', pairs)  31 us
    all_gather x1, blocking collectives, paired(): share = lax.all_gather(share, 'ep', axis=0, tiled=False)  20 us
    unnamed x54, local copies, waits for them, and re-layouts  9.98 us
  transfers between devices with their start and end apart: 35, of which 19 were waited for; matrix products, arithmetic and copies ran while one was open for 14% of the time, Pallas kernels for 0%

profile of v2, /device:TPU:0, one launch (start us, length us, event | category | flops | bytes accessed | tf_op | source)
XLA Modules:
  0.0 260.2 jit_solution(18150978771357198537)
XLA Ops:
  7.2 4.1 %collective-permute-start.1 = (bf16[128,1024]{1,0:T(8,128)(2,1)}, bf16[128,1024]{1,0:T(8,128)(2,1)S(1)}, u32[]{:S(2)}, u32[]{:S(2)}) collective-permute-start(bf16[128,1024]{1,0:T(8,128)(2,1)} %param.7), channel_id=1, source_target_pairs={{0,8},{1,9},{2,10},{3,11},{4,12},{5,13},{6,14},{7,15},{8,0},{9,1},... | collective-permute-start | bytes 786440 | tf_op jit(solution)/shard_map/ppermute | solution.py:113
  15.2 1.7 constant_dynamic-update-slice_fusion.7
  17.0 1.7 constant_dynamic-update-slice_fusion.15
  18.8 6.4 %collective-permute-done.1 = bf16[128,1024]{1,0:T(8,128)(2,1)S(1)} collective-permute-done((bf16[128,1024]{1,0:T(8,128)(2,1)}, bf16[128,1024]{1,0:T(8,128)(2,1)S(1)}, u32[]{:S(2)}, u32[]{:S(2)}) %collective-permute-start.1) | collective-permute-done | bytes 262176 | tf_op jit(solution)/shard_map/ppermute | solution.py:113
  25.2 5.5 %collective-permute-start.20 = (bf16[128,1024]{1,0:T(8,128)(2,1)}, bf16[128,1024]{1,0:T(8,128)(2,1)S(1)}, u32[]{:S(2)}, u32[]{:S(2)}) collective-permute-start(bf16[128,1024]{1,0:T(8,128)(2,1)} %param.10), channel_id=1, source_target_pairs={{0,2},{1,3},{2,0},{3,1},{4,6},{5,7},{6,4},{7,5},{8,10},{9,11},{10,... | collective-permute-start | bytes 786440 | tf_op jit(solution)/shard_map/ppermute | solution.py:113
  32.2 4.3 %collective-permute-done.17 = bf16[128,1024]{1,0:T(8,128)(2,1)S(1)} collective-permute-done((bf16[128,1024]{1,0:T(8,128)(2,1)}, bf16[128,1024]{1,0:T(8,128)(2,1)S(1)}, u32[]{:S(2)}, u32[]{:S(2)}) %collective-permute-start.17) | collective-permute-done | bytes 262176 | tf_op jit(solution)/shard_map/ppermute | solution.py:113
  47.0 4.5 %collective-permute-done.5 = bf16[128,1024]{1,0:T(8,128)(2,1)S(1)} collective-permute-done((bf16[128,1024]{1,0:T(8,128)(2,1)S(1)}, bf16[128,1024]{1,0:T(8,128)(2,1)S(1)}, u32[]{:S(2)}, u32[]{:S(2)}) %collective-permute-start.5) | collective-permute-done | bytes 262176 | tf_op jit(solution)/shard_map/ppermute | solution.py:113
  55.9 4.8 %collective-permute-done.21 = bf16[128,1024]{1,0:T(8,128)(2,1)S(1)} collective-permute-done((bf16[128,1024]{1,0:T(8,128)(2,1)S(1)}, bf16[128,1024]{1,0:T(8,128)(2,1)S(1)}, u32[]{:S(2)}, u32[]{:S(2)}) %collective-permute-start.21) | collective-permute-done | bytes 262176 | tf_op jit(solution)/shard_map/ppermute | solution.py:113
  60.8 5.6 %collective-permute-done.22 = bf16[128,1024]{1,0:T(8,128)(2,1)S(1)} collective-permute-done((bf16[128,1024]{1,0:T(8,128)(2,1)S(1)}, bf16[128,1024]{1,0:T(8,128)(2,1)S(1)}, u32[]{:S(2)}, u32[]{:S(2)}) %collective-permute-start.22) | collective-permute-done | bytes 262176 | tf_op jit(solution)/shard_map/ppermute | solution.py:113
  67.9 4.1 %collective-permute-done.6 = bf16[128,1024]{1,0:T(8,128)(2,1)S(1)} collective-permute-done((bf16[128,1024]{1,0:T(8,128)(2,1)S(1)}, bf16[128,1024]{1,0:T(8,128)(2,1)S(1)}, u32[]{:S(2)}, u32[]{:S(2)}) %collective-permute-start.6) | collective-permute-done | bytes 262176 | tf_op jit(solution)/shard_map/ppermute | solution.py:113
  72.0 3.3 %fusion.26 = f32[1024,512]{0,1:T(8,128)S(1)} fusion(bf16[1024,1024]{1,0:T(8,128)(2,1)S(1)} %constant_dynamic-update-slice_fusion, bf16[1,1024,512]{2,1,0:T(8,128)(2,1)} %param.12), kind=kOutput, calls=%fused_computation.81 | convolution fusion | flops 1073741824 | bytes 5242880 | tf_op jit(solution)/shard_map/dot_general | solution.py:108
  77.7 4.9 %multiply_reduce_fusion.1 = (f32[1024]{0:T(1024)S(1)}, f32[1024,512]{0,1:T(8,128)}) fusion(f32[1024,512]{0,1:T(8,128)S(1)} %fusion.26, f32[1024,512]{0,1:T(8,128)S(1)} %fusion.30, bf16[1024,1024]{1,0:T(8,128)(2,1)S(1)} %constant_dynamic-update-slice_fusion.8, bf16[1,512,1024]{2,1,0:T(8,128)(2,1)} %param.13), kind=kOutput, calls=%fused_computation.8 | convolution fusion | flops 1077410816 | bytes 9441280 | tf_op jit(solution)/shard_map/dot_general | solution.py:108
  85.5 2.9 %multiply_reduce_fusion = (f32[1024]{0:T(1024)S(1)}, f32[1024,512]{0,1:T(8,128)}) fusion(f32[1024,512]{0,1:T(8,128)S(1)} %fusion.35, f32[1024,512]{0,1:T(8,128)S(1)} %fusion.34, bf16[1024,1024]{1,0:T(8,128)(2,1)S(1)} %constant_dynamic-update-slice_fusion.8, bf16[512,1024]{1,0:T(8,128)(2,1)S(1)} %collective-permute-done.9), kind=kOutput, calls=%fused_computation.7 | convolution fusion | flops 1077410816 | bytes 9441280 | tf_op jit(solution)/shard_map/dot_general | solution.py:108
  89.8 54.8 %reduce-scatter.2.cloned.1.call-done = f32[1,16,128]{2,1,0:T(8,128)} async-done(((f32[16,16,128]{2,1,0:T(8,128)}), f32[1,16,128]{2,1,0:T(8,128)}) %reduce-scatter.2.cloned.1.call-update) | async-done | bytes 8208 | tf_op jit(solution)/shard_map/reduce_scatter | solution.py:185
  145.9 20.0 %all-gather = f32[256,128]{1,0:T(8,128)S(1)} all-gather(f32[16,128]{1,0:T(8,128)S(1)} %get-tuple-element.7), channel_id=2, replica_groups=mesh['grp'=2,'ep'=16] {'ep'}, dimensions={0}, use_global_device_ids=true | all-gather | bytes 139264 | tf_op jit(solution)/shard_map/all_gather | solution.py:149
  167.1 3.7 %multiply_convert_fusion.2 = (bf16[1024,512]{0,1:T(8,128)(2,1)S(1)}, bf16[1024,512]{0,1:T(8,128)(2,1)S(1)}, bf16[1024,512]{0,1:T(8,128)(2,1)S(1)}) fusion(f32[1024,512]{0,1:T(8,128)} %get-tuple-element.31, f32[1024]{0:T(1024)S(1)} %get-tuple-element.27, f32[1024,512]{0,1:T(8,128)} %copy-done.4, f32[1024,512]{0,1:T(8,128)S(1)} %fusion.26), kind=kLoop, calls=%fused_computation.11 | loop fusion | flops 8912896 | bytes 9441280 | tf_op jit(solution)/shard_map/convert_element_type | solution.py:177
  172.2 2.7 %fusion.24 = f32[1024,1024]{1,0:T(8,128)S(1)} fusion(bf16[1024,512]{0,1:T(8,128)(2,1)S(1)} %get-tuple-element.8, bf16[1,1024,512]{2,1,0:T(8,128)(2,1)} %param.12), kind=kOutput, calls=%fused_computation.79 | convolution fusion | flops 1073741824 | bytes 6291456 | tf_op jit(solution)/shard_map/dot_general | solution.py:108
  179.8 2.0 collective-permute-start.27
  181.9 2.6 %fusion.22 = f32[1024,1024]{1,0:T(8,128)S(1)} fusion(bf16[1024,512]{0,1:T(8,128)(2,1)S(1)} %get-tuple-element.10, bf16[1,512,1024]{2,1,0:T(8,128)(2,1)} %param.13), kind=kOutput, calls=%fused_computation.77 | convolution fusion | flops 1073741824 | bytes 6291456 | tf_op jit(solution)/shard_map/dot_general | solution.py:108
  186.1 2.0 collective-permute-start.14
  188.9 11.2 %collective-permute-done.25 = bf16[128,1024]{1,0:T(8,128)(2,1)S(1)} collective-permute-done((bf16[128,1024]{1,0:T(8,128)(2,1)S(1)}, bf16[128,1024]{1,0:T(8,128)(2,1)S(1)}, u32[]{:S(2)}, u32[]{:S(2)}) %collective-permute-start.25) | collective-permute-done | bytes 262176 | tf_op jit(solution)/shard_map/ppermute | solution.py:113
  202.1 3.7 %collective-permute-done.14 = bf16[128,1024]{1,0:T(8,128)(2,1)S(1)} collective-permute-done((bf16[128,1024]{1,0:T(8,128)(2,1)S(1)}, bf16[128,1024]{1,0:T(8,128)(2,1)S(1)}, u32[]{:S(2)}, u32[]{:S(2)}) %collective-permute-start.14) | collective-permute-done | bytes 262176 | tf_op jit(solution)/shard_map/ppermute | solution.py:113
  205.9 5.6 %collective-permute-done.11 = bf16[128,1024]{1,0:T(8,128)(2,1)S(1)} collective-permute-done((bf16[128,1024]{1,0:T(8,128)(2,1)S(1)}, bf16[128,1024]{1,0:T(8,128)(2,1)S(1)}, u32[]{:S(2)}, u32[]{:S(2)}) %collective-permute-start.11) | collective-permute-done | bytes 262176 | tf_op jit(solution)/shard_map/ppermute | solution.py:113
  211.6 2.1 collective-permute-start.15
  215.2 6.9 %collective-permute-done.13 = bf16[128,1024]{1,0:T(8,128)(2,1)S(1)} collective-permute-done((bf16[128,1024]{1,0:T(8,128)(2,1)S(1)}, bf16[128,1024]{1,0:T(8,128)(2,1)S(1)}, u32[]{:S(2)}, u32[]{:S(2)}) %collective-permute-start.13) | collective-permute-done | bytes 262176 | tf_op jit(solution)/shard_map/ppermute | solution.py:113
  222.1 7.8 %collective-permute-done.15 = bf16[128,1024]{1,0:T(8,128)(2,1)S(1)} collective-permute-done((bf16[128,1024]{1,0:T(8,128)(2,1)S(1)}, bf16[128,1024]{1,0:T(8,128)(2,1)S(1)}, u32[]{:S(2)}, u32[]{:S(2)}) %collective-permute-start.15) | collective-permute-done | bytes 262176 | tf_op jit(solution)/shard_map/ppermute | solution.py:113
  233.2 5.6 %collective-permute-done.10 = bf16[128,1024]{1,0:T(8,128)(2,1)S(1)} collective-permute-done((bf16[128,1024]{1,0:T(8,128)(2,1)S(1)}, bf16[128,1024]{1,0:T(8,128)(2,1)S(1)}, u32[]{:S(2)}, u32[]{:S(2)}) %collective-permute-start.10) | collective-permute-done | bytes 262176 | tf_op jit(solution)/shard_map/ppermute | solution.py:113
  238.8 2.9 %collective-permute-done.12 = bf16[128,1024]{1,0:T(8,128)(2,1)S(1)} collective-permute-done((bf16[128,1024]{1,0:T(8,128)(2,1)S(1)}, bf16[128,1024]{1,0:T(8,128)(2,1)S(1)}, u32[]{:S(2)}, u32[]{:S(2)}) %collective-permute-start.12) | collective-permute-done | bytes 262176 | tf_op jit(solution)/shard_map/ppermute | solution.py:113
  241.7 4.0 %collective-permute-done.16 = bf16[128,1024]{1,0:T(8,128)(2,1)S(1)} collective-permute-done((bf16[128,1024]{1,0:T(8,128)(2,1)S(1)}, bf16[128,1024]{1,0:T(8,128)(2,1)S(1)}, u32[]{:S(2)}, u32[]{:S(2)}) %collective-permute-start.16) | collective-permute-done | bytes 262176 | tf_op jit(solution)/shard_map/ppermute | solution.py:113
  246.5 2.3 fusion.4
  248.8 2.3 fusion.3
  251.1 2.3 fusion.2
  (138 shorter events, 47.8 us)
Async XLA Ops:
  7.2 137.4 %reduce-scatter.2.cloned.1.call-start = ((), (), s32[]{:S(2)}) async-start(), calls=%async_computation.1 | async-start | bytes 139264 | tf_op jit(solution)/shard_map/reduce_scatter | solution.py:185
  7.2 18.0 %collective-permute-start.1 = (bf16[128,1024]{1,0:T(8,128)(2,1)}, bf16[128,1024]{1,0:T(8,128)(2,1)S(1)}, u32[]{:S(2)}, u32[]{:S(2)}) collective-permute-start(bf16[128,1024]{1,0:T(8,128)(2,1)} %param.7), channel_id=1, source_target_pairs={{0,8},{1,9},{2,10},{3,11},{4,12},{5,13},{6,14},{7,15},{8,0},{9,1},... | collective-permute-start | bytes 786440 | tf_op jit(solution)/shard_map/ppermute | solution.py:113
  11.3 19.4 %collective-permute-start = (bf16[128,1024]{1,0:T(8,128)(2,1)}, bf16[128,1024]{1,0:T(8,128)(2,1)S(1)}, u32[]{:S(2)}, u32[]{:S(2)}) collective-permute-start(bf16[128,1024]{1,0:T(8,128)(2,1)} %param.7), channel_id=1, source_target_pairs={{0,4},{1,5},{2,6},{3,7},{4,0},{5,1},{6,2},{7,3},{8,12},{9,13},{10,... | collective-permute-start | bytes 786440 | tf_op jit(solution)/shard_map/ppermute | solution.py:113
  12.9 30.0 %collective-permute-start.3 = (bf16[128,1024]{1,0:T(8,128)(2,1)}, bf16[128,1024]{1,0:T(8,128)(2,1)S(1)}, u32[]{:S(2)}, u32[]{:S(2)}) collective-permute-start(bf16[128,1024]{1,0:T(8,128)(2,1)} %param.7), channel_id=1, source_target_pairs={{0,2},{1,3},{2,0},{3,1},{4,6},{5,7},{6,4},{7,5},{8,10},{9,11},{10,... | collective-permute-start | bytes 786440 | tf_op jit(solution)/shard_map/ppermute | solution.py:113
  14.4 22.8 %collective-permute-start.18 = (bf16[128,1024]{1,0:T(8,128)(2,1)}, bf16[128,1024]{1,0:T(8,128)(2,1)S(1)}, u32[]{:S(2)}, u32[]{:S(2)}) collective-permute-start(bf16[128,1024]{1,0:T(8,128)(2,1)} %param.10), channel_id=1, source_target_pairs={{0,8},{1,9},{2,10},{3,11},{4,12},{5,13},{6,14},{7,15},{8,0},{9,1},... | collective-permute-start | bytes 786440 | tf_op jit(solution)/shard_map/ppermute | solution.py:113
  14.7 21.7 %collective-permute-start.17 = (bf16[128,1024]{1,0:T(8,128)(2,1)}, bf16[128,1024]{1,0:T(8,128)(2,1)S(1)}, u32[]{:S(2)}, u32[]{:S(2)}) collective-permute-start(bf16[128,1024]{1,0:T(8,128)(2,1)} %param.10), channel_id=1, source_target_pairs={{0,4},{1,5},{2,6},{3,7},{4,0},{5,1},{6,2},{7,3},{8,12},{9,13},{10,... | collective-permute-start | bytes 786440 | tf_op jit(solution)/shard_map/ppermute | solution.py:113
  25.2 29.1 %collective-permute-start.20 = (bf16[128,1024]{1,0:T(8,128)(2,1)}, bf16[128,1024]{1,0:T(8,128)(2,1)S(1)}, u32[]{:S(2)}, u32[]{:S(2)}) collective-permute-start(bf16[128,1024]{1,0:T(8,128)(2,1)} %param.10), channel_id=1, source_target_pairs={{0,2},{1,3},{2,0},{3,1},{4,6},{5,7},{6,4},{7,5},{8,10},{9,11},{10,... | collective-permute-start | bytes 786440 | tf_op jit(solution)/shard_map/ppermute | solution.py:113
  30.7 9.9 %collective-permute-start.2 = (bf16[128,1024]{1,0:T(8,128)(2,1)S(1)}, bf16[128,1024]{1,0:T(8,128)(2,1)S(1)}, u32[]{:S(2)}, u32[]{:S(2)}) collective-permute-start(bf16[128,1024]{1,0:T(8,128)(2,1)S(1)} %collective-permute-done.1), channel_id=1, source_target_pairs={{0,4},{1,5},{2,6},{3,7},{4,0},{5,1},{6,2},{7,3},{8,12},{9,13},{10,... | collective-permute-start | bytes 786440 | tf_op jit(solution)/shard_map/ppermute | solution.py:113
  36.4 48.9 %collective-permute-start.9 = (bf16[512,1024]{1,0:T(8,128)(2,1)}, bf16[512,1024]{1,0:T(8,128)(2,1)S(1)}, u32[]{:S(2)}, u32[]{:S(2)}) collective-permute-start(bf16[512,1024]{1,0:T(8,128)(2,1)} %bitcast.16), channel_id=1, source_target_pairs={{0,1},{1,0},{2,3},{3,2},{4,5},{5,4},{6,7},{7,6},{8,9},{9,8},{10,11... | collective-permute-start | bytes 3145736 | tf_op jit(solution)/shard_map/ppermute | solution.py:113
  40.6 10.9 %collective-permute-start.5 = (bf16[128,1024]{1,0:T(8,128)(2,1)S(1)}, bf16[128,1024]{1,0:T(8,128)(2,1)S(1)}, u32[]{:S(2)}, u32[]{:S(2)}) collective-permute-start(bf16[128,1024]{1,0:T(8,128)(2,1)S(1)} %collective-permute-done.1), channel_id=1, source_target_pairs={{0,2},{1,3},{2,0},{3,1},{4,6},{5,7},{6,4},{7,5},{8,10},{9,11},{10,... | collective-permute-start | bytes 786440 | tf_op jit(solution)/shard_map/ppermute | solution.py:113
  42.9 10.9 %collective-permute-start.19 = (bf16[128,1024]{1,0:T(8,128)(2,1)S(1)}, bf16[128,1024]{1,0:T(8,128)(2,1)S(1)}, u32[]{:S(2)}, u32[]{:S(2)}) collective-permute-start(bf16[128,1024]{1,0:T(8,128)(2,1)S(1)} %collective-permute-done.18), channel_id=1, source_target_pairs={{0,4},{1,5},{2,6},{3,7},{4,0},{5,1},{6,2},{7,3},{8,12},{9,13},{10,... | collective-permute-start | bytes 786440 | tf_op jit(solution)/shard_map/ppermute | solution.py:113
  46.3 36.3 %collective-permute-start.8 = (bf16[1024,512]{1,0:T(8,128)(2,1)}, bf16[1024,512]{1,0:T(8,128)(2,1)S(1)}, u32[]{:S(2)}, u32[]{:S(2)}) collective-permute-start(bf16[1024,512]{1,0:T(8,128)(2,1)} %bitcast.15), channel_id=1, source_target_pairs={{0,1},{1,0},{2,3},{3,2},{4,5},{5,4},{6,7},{7,6},{8,9},{9,8},{10,11... | collective-permute-start | bytes 3145736 | tf_op jit(solution)/shard_map/ppermute | solution.py:113
  51.5 9.2 %collective-permute-start.21 = (bf16[128,1024]{1,0:T(8,128)(2,1)S(1)}, bf16[128,1024]{1,0:T(8,128)(2,1)S(1)}, u32[]{:S(2)}, u32[]{:S(2)}) collective-permute-start(bf16[128,1024]{1,0:T(8,128)(2,1)S(1)} %collective-permute-done.17), channel_id=1, source_target_pairs={{0,2},{1,3},{2,0},{3,1},{4,6},{5,7},{6,4},{7,5},{8,10},{9,11},{10,... | collective-permute-start | bytes 786440 | tf_op jit(solution)/shard_map/ppermute | solution.py:113
  53.8 12.6 %collective-permute-start.22 = (bf16[128,1024]{1,0:T(8,128)(2,1)S(1)}, bf16[128,1024]{1,0:T(8,128)(2,1)S(1)}, u32[]{:S(2)}, u32[]{:S(2)}) collective-permute-start(bf16[128,1024]{1,0:T(8,128)(2,1)S(1)} %collective-permute-done.18), channel_id=1, source_target_pairs={{0,2},{1,3},{2,0},{3,1},{4,6},{5,7},{6,4},{7,5},{8,10},{9,11},{10,... | collective-permute-start | bytes 786440 | tf_op jit(solution)/shard_map/ppermute | solution.py:113
  54.3 17.7 %collective-permute-start.6 = (bf16[128,1024]{1,0:T(8,128)(2,1)S(1)}, bf16[128,1024]{1,0:T(8,128)(2,1)S(1)}, u32[]{:S(2)}, u32[]{:S(2)}) collective-permute-start(bf16[128,1024]{1,0:T(8,128)(2,1)S(1)} %collective-permute-done.2), channel_id=1, source_target_pairs={{0,2},{1,3},{2,0},{3,1},{4,6},{5,7},{6,4},{7,5},{8,10},{9,11},{10,... | collective-permute-start | bytes 786440 | tf_op jit(solution)/shard_map/ppermute | solution.py:113
  60.7 23.2 %collective-permute-start.7 = (bf16[1024,512]{1,0:T(8,128)(2,1)S(1)}, bf16[1024,512]{1,0:T(8,128)(2,1)S(1)}, u32[]{:S(2)}, u32[]{:S(2)}) collective-permute-start(bf16[1024,512]{1,0:T(8,128)(2,1)S(1)} %bitcast.95), channel_id=1, source_target_pairs={{0,1},{1,0},{2,3},{3,2},{4,5},{5,4},{6,7},{7,6},{8,9},{9,8},{10,11... | collective-permute-start | bytes 3145736 | tf_op jit(solution)/shard_map/ppermute | solution.py:113
  66.3 10.0 %collective-permute-start.23 = (bf16[128,1024]{1,0:T(8,128)(2,1)S(1)}, bf16[128,1024]{1,0:T(8,128)(2,1)S(1)}, u32[]{:S(2)}, u32[]{:S(2)}) collective-permute-start(bf16[128,1024]{1,0:T(8,128)(2,1)S(1)} %collective-permute-done.19), channel_id=1, source_target_pairs={{0,2},{1,3},{2,0},{3,1},{4,6},{5,7},{6,4},{7,5},{8,10},{9,11},{10,... | collective-permute-start | bytes 786440 | tf_op jit(solution)/shard_map/ppermute | solution.py:113
  179.8 31.8 %collective-permute-start.27 = (bf16[128,1024]{1,0:T(8,128)(2,1)S(1)}, bf16[128,1024]{1,0:T(8,128)(2,1)S(1)}, u32[]{:S(2)}, u32[]{:S(2)}) collective-permute-start(bf16[128,1024]{1,0:T(8,128)(2,1)S(1)} %get-tuple-element.16), channel_id=1, source_target_pairs={{0,2},{1,3},{2,0},{3,1},{4,6},{5,7},{6,4},{7,5},{8,10},{9,11},{10,... | collective-permute-start | bytes 786440 | tf_op jit(solution)/shard_map/ppermute | solution.py:113
  181.8 18.3 %collective-permute-start.25 = (bf16[128,1024]{1,0:T(8,128)(2,1)S(1)}, bf16[128,1024]{1,0:T(8,128)(2,1)S(1)}, u32[]{:S(2)}, u32[]{:S(2)}) collective-permute-start(bf16[128,1024]{1,0:T(8,128)(2,1)S(1)} %get-tuple-element.17), channel_id=1, source_target_pairs={{0,2},{1,3},{2,0},{3,1},{4,6},{5,7},{6,4},{7,5},{8,10},{9,11},{10,... | collective-permute-start | bytes 786440 | tf_op jit(solution)/shard_map/ppermute | solution.py:113
  186.1 19.7 %collective-permute-start.14 = (bf16[128,1024]{1,0:T(8,128)(2,1)S(1)}, bf16[128,1024]{1,0:T(8,128)(2,1)S(1)}, u32[]{:S(2)}, u32[]{:S(2)}) collective-permute-start(bf16[128,1024]{1,0:T(8,128)(2,1)S(1)} %get-tuple-element.21), channel_id=1, source_target_pairs={{0,2},{1,3},{2,0},{3,1},{4,6},{5,7},{6,4},{7,5},{8,10},{9,11},{10,... | collective-permute-start | bytes 786440 | tf_op jit(solution)/shard_map/ppermute | solution.py:113
  188.1 23.3 %collective-permute-start.11 = (bf16[128,1024]{1,0:T(8,128)(2,1)S(1)}, bf16[128,1024]{1,0:T(8,128)(2,1)S(1)}, u32[]{:S(2)}, u32[]{:S(2)}) collective-permute-start(bf16[128,1024]{1,0:T(8,128)(2,1)S(1)} %get-tuple-element.23), channel_id=1, source_target_pairs={{0,2},{1,3},{2,0},{3,1},{4,6},{5,7},{6,4},{7,5},{8,10},{9,11},{10,... | collective-permute-start | bytes 786440 | tf_op jit(solution)/shard_map/ppermute | solution.py:113
  200.4 13.4 %collective-permute-start.29 = (bf16[128,1024]{1,0:T(8,128)(2,1)S(1)}, bf16[128,1024]{1,0:T(8,128)(2,1)S(1)}, u32[]{:S(2)}, u32[]{:S(2)}) collective-permute-start(bf16[128,1024]{1,0:T(8,128)(2,1)S(1)} %get-tuple-element.19), channel_id=1, source_target_pairs={{0,4},{1,5},{2,6},{3,7},{4,0},{5,1},{6,2},{7,3},{8,12},{9,13},{10,... | collective-permute-start | bytes 786440 | tf_op jit(solution)/shard_map/ppermute | solution.py:113
  202.0 28.0 %collective-permute-start.24 = (bf16[128,1024]{1,0:T(8,128)(2,1)S(1)}, bf16[128,1024]{1,0:T(8,128)(2,1)S(1)}, u32[]{:S(2)}, u32[]{:S(2)}) collective-permute-start(bf16[128,1024]{1,0:T(8,128)(2,1)S(1)} %get-tuple-element.14), channel_id=1, source_target_pairs={{0,2},{1,3},{2,0},{3,1},{4,6},{5,7},{6,4},{7,5},{8,10},{9,11},{10,... | collective-permute-start | bytes 786440 | tf_op jit(solution)/shard_map/ppermute | solution.py:113
  205.8 16.3 %collective-permute-start.13 = (bf16[128,1024]{1,0:T(8,128)(2,1)S(1)}, bf16[128,1024]{1,0:T(8,128)(2,1)S(1)}, u32[]{:S(2)}, u32[]{:S(2)}) collective-permute-start(bf16[128,1024]{1,0:T(8,128)(2,1)S(1)} %get-tuple-element.22), channel_id=1, source_target_pairs={{0,2},{1,3},{2,0},{3,1},{4,6},{5,7},{6,4},{7,5},{8,10},{9,11},{10,... | collective-permute-start | bytes 786440 | tf_op jit(solution)/shard_map/ppermute | solution.py:113
  211.4 19.1 %collective-permute-start.26 = (bf16[128,1024]{1,0:T(8,128)(2,1)S(1)}, bf16[128,1024]{1,0:T(8,128)(2,1)S(1)}, u32[]{:S(2)}, u32[]{:S(2)}) collective-permute-start(bf16[128,1024]{1,0:T(8,128)(2,1)S(1)} %get-tuple-element.18), channel_id=1, source_target_pairs={{0,4},{1,5},{2,6},{3,7},{4,0},{5,1},{6,2},{7,3},{8,12},{9,13},{10,... | collective-permute-start | bytes 786440 | tf_op jit(solution)/shard_map/ppermute | solution.py:113
  211.6 18.2 %collective-permute-start.15 = (bf16[128,1024]{1,0:T(8,128)(2,1)S(1)}, bf16[128,1024]{1,0:T(8,128)(2,1)S(1)}, u32[]{:S(2)}, u32[]{:S(2)}) collective-permute-start(bf16[128,1024]{1,0:T(8,128)(2,1)S(1)} %get-tuple-element.25), channel_id=1, source_target_pairs={{0,4},{1,5},{2,6},{3,7},{4,0},{5,1},{6,2},{7,3},{8,12},{9,13},{10,... | collective-permute-start | bytes 786440 | tf_op jit(solution)/shard_map/ppermute | solution.py:113
  213.8 16.7 %collective-permute-start.30 = (bf16[128,1024]{1,0:T(8,128)(2,1)S(1)}, bf16[128,1024]{1,0:T(8,128)(2,1)S(1)}, u32[]{:S(2)}, u32[]{:S(2)}) collective-permute-start(bf16[128,1024]{1,0:T(8,128)(2,1)S(1)} %add_convert_fusion.6), channel_id=1, source_target_pairs={{0,8},{1,9},{2,10},{3,11},{4,12},{5,13},{6,14},{7,15},{8,0},{9,1},... | collective-permute-start | bytes 786440 | tf_op jit(solution)/shard_map/ppermute | solution.py:113
  222.1 24.4 %collective-permute-start.33 = (bf16[512,1024]{1,0:T(8,128)(2,1)S(1)}, bf16[512,1024]{1,0:T(8,128)(2,1)S(1)}, u32[]{:S(2)}, u32[]{:S(2)}) collective-permute-start(bf16[512,1024]{1,0:T(8,128)(2,1)S(1)} %convolution_convert_fusion), channel_id=1, source_target_pairs={{0,1},{1,0},{2,3},{3,2},{4,5},{5,4},{6,7},{7,6},{8,9},{9,8},{10,11... | collective-permute-start | bytes 3145736 | tf_op jit(solution)/shard_map/ppermute | solution.py:113
  229.8 18.9 %collective-permute-start.32 = (bf16[1024,512]{1,0:T(8,128)(2,1)S(1)}, bf16[1024,512]{1,0:T(8,128)(2,1)S(1)}, u32[]{:S(2)}, u32[]{:S(2)}) collective-permute-start(bf16[1024,512]{1,0:T(8,128)(2,1)S(1)} %convolution_convert_fusion.1), channel_id=1, source_target_pairs={{0,1},{1,0},{2,3},{3,2},{4,5},{5,4},{6,7},{7,6},{8,9},{9,8},{10,11... | collective-permute-start | bytes 3145736 | tf_op jit(solution)/shard_map/ppermute | solution.py:113
  230.6 11.1 %collective-permute-start.12 = (bf16[128,1024]{1,0:T(8,128)(2,1)S(1)}, bf16[128,1024]{1,0:T(8,128)(2,1)S(1)}, u32[]{:S(2)}, u32[]{:S(2)}) collective-permute-start(bf16[128,1024]{1,0:T(8,128)(2,1)S(1)} %get-tuple-element.24), channel_id=1, source_target_pairs={{0,4},{1,5},{2,6},{3,7},{4,0},{5,1},{6,2},{7,3},{8,12},{9,13},{10,... | collective-permute-start | bytes 786440 | tf_op jit(solution)/shard_map/ppermute | solution.py:113
  230.6 15.1 %collective-permute-start.16 = (bf16[128,1024]{1,0:T(8,128)(2,1)S(1)}, bf16[128,1024]{1,0:T(8,128)(2,1)S(1)}, u32[]{:S(2)}, u32[]{:S(2)}) collective-permute-start(bf16[128,1024]{1,0:T(8,128)(2,1)S(1)} %add_convert_fusion.10), channel_id=1, source_target_pairs={{0,8},{1,9},{2,10},{3,11},{4,12},{5,13},{6,14},{7,15},{8,0},{9,1},... | collective-permute-start | bytes 786440 | tf_op jit(solution)/shard_map/ppermute | solution.py:113
  238.8 12.3 %collective-permute-start.31 = (bf16[1024,512]{1,0:T(8,128)(2,1)S(1)}, bf16[1024,512]{1,0:T(8,128)(2,1)S(1)}, u32[]{:S(2)}, u32[]{:S(2)}) collective-permute-start(bf16[1024,512]{1,0:T(8,128)(2,1)S(1)} %convolution_convert_fusion.2), channel_id=1, source_target_pairs={{0,1},{1,0},{2,3},{3,2},{4,5},{5,4},{6,7},{7,6},{8,9},{9,8},{10,11... | collective-permute-start | bytes 3145736 | tf_op jit(solution)/shard_map/ppermute | solution.py:113
  (23 other events, 280.8 us)
Sparse Core Ops, SparseCore 0:
  89.8 54.7 reduce-scatter.1

commit v3 on v2

--- a/solution.py
+++ b/solution.py
@@ -115,6 +115,7 @@
 
 CORE, SIDE, NEAR, FAR = 1, 2, 4, 8
 REACH = (0, NEAR, FAR, NEAR | FAR, SIDE, SIDE | NEAR, SIDE | FAR, SIDE | NEAR | FAR)
+HALVED = (0, SIDE, FAR, FAR | SIDE, NEAR, NEAR | SIDE, NEAR | FAR, NEAR | FAR | SIDE)
 
 
 def collect(block):
@@ -135,23 +136,38 @@
     return (line[0] + near.astype(f32) + far.astype(f32)).astype(bf16)
 
 
+def collect_small(value):
+    value = value[None]
+    for bit in (NEAR, FAR, SIDE):
+        value = jnp.concatenate([value, swap(value, bit)], axis=0)
+    return value
+
+
+def give_back_small(parts):
+    count = len(REACH)
+    parts = parts[:, None]
+    for bit in (SIDE, FAR, NEAR):
+        count = count // 2
+        parts = jnp.concatenate([parts[:count], swap(parts[count:], bit)], axis=1)
+    return parts[0]
+
+
 def paired(latent_in, routes, combine_weights, cotangent, w_gate, w_up, w_down):
     devices_ep = lax.axis_size("ep")
     me = lax.axis_index("ep")
     tok_count = latent_in.shape[0]
     bf16, f32 = jnp.bfloat16, jnp.float32
     experts = jnp.arange(devices_ep, dtype=jnp.int32)
-    sources = jnp.stack([me ^ bits for bits in REACH])
     mine = jnp.stack([me, me ^ CORE])
 
     chosen = routes[None, :, :] == experts[:, None, None]
     share = jnp.sum(jnp.where(chosen, combine_weights[None, :, :], 0.0), axis=2)
-    share = lax.all_gather(share, "ep", axis=0, tiled=False)
+    share = collect_small(share)
     rows = jnp.concatenate(collect(latent_in), axis=0)
     weights = [w_gate[0], w_up[0], w_down[0]]
     both_w = [weights, [swap(w, CORE) for w in weights]]
     cot = jnp.concatenate(collect(cotangent), axis=0)
-    share = share[sources][:, mine, :]
+    share = share[:, mine, :]
 
     partial_out, saved = 0.0, []
     for i, (gate_w, up_w, down_w) in enumerate(both_w):
@@ -179,11 +195,11 @@
         grad_rows = grad_rows + dot(grad_up, up_w, ((1,), (1,)))
         grads.append((weighted, grad_gate, grad_up))
     inner = jnp.stack(inner, axis=1)
-    at_source = (sources[None, :] == experts[:, None]).astype(f32)
-    at_expert = (mine[None, :] == experts[:, None]).astype(f32)
-    inner = jnp.einsum("ds,ei,sit->det", at_source, at_expert, inner, precision="highest")
-    inner = lax.psum_scatter(inner, "ep", scatter_dimension=0, tiled=False)
-    grad_combine = jnp.sum(jnp.where(chosen, inner[:, :, None], 0.0), axis=0)
+    inner = give_back_small(inner)
+    owner = jnp.stack([me ^ bits for bits in HALVED])
+    owner = jnp.stack([owner, owner ^ CORE], axis=1)
+    owns = routes[None, None, :, :] == owner[:, :, None, None]
+    grad_combine = jnp.sum(jnp.where(owns, inner[:, :, :, None], 0.0), axis=(0, 1))
 
     back = grad_rows.astype(bf16).reshape(len(REACH), tok_count, -1)
     grad_latent = give_back([back[i] for i in range(len(REACH))])

time: 261 us -> 178 us (0.68)
  waiting for transfers between devices: 136 us -> 92.1 us
  blocking collectives: 20 us -> 0 us
  between operations: 14.5 us -> 1.04 us
  starting transfers between devices: 31 us -> 41.8 us
  matrix products: 37.9 us -> 28.7 us
  other arithmetic: 9.2 us -> 3.98 us
    reduce_scatter x1 -> x0, waiting for transfers between devices: 54.8 us -> none  [paired(): inner = lax.psum_scatter(inner, 'ep', scatter_dimension=0, tiled=False)]
    all_gather x1 -> x0, blocking collectives: 20 us -> none  [paired(): share = lax.all_gather(share, 'ep', axis=0, tiled=False)]
    ppermute x34 -> x40, starting transfers between devices: 31 us -> 41.8 us  [swap(): return lax.ppermute(value, 'ep', pairs)]
    ppermute x34 -> x40, waiting for transfers between devices: 81.3 us -> 92.1 us  [swap(): return lax.ppermute(value, 'ep', pairs)]
    dot_general x18, matrix products: 36.7 us -> 28.7 us  [dot(): lax.dot_general(a, b, (dims, ((), ())), preferred_element_type=jnp.float32)]
    convert_element_type x2 -> x0, other arithmetic: 5.35 us -> none  [the longest x1 3.73 us: paired(): grad_up = (grad_hidden * silu_val).astype(bf16)]
    unnamed x54 -> x34, local copies, waits for them, and re-layouts: 9.98 us -> 9.36 us
  transfers between devices with their start and end apart: 35 -> 40, of which waited for: 19 -> 20; matrix products, arithmetic and copies ran while one was open for 14% -> 22% of each run, Pallas kernels for 0% -> 0%
where the time goes in v3:
time: 178 us
  waiting for transfers between devices  92.1 us (52%)
  starting transfers between devices  41.8 us (23%)
  matrix products  28.7 us (16%)
  local copies, waits for them, and re-layouts  10.4 us (6%)
  other arithmetic  3.98 us (2%)
    ppermute x40, waiting for transfers between devices, swap(): return lax.ppermute(value, 'ep', pairs)  92.1 us
    ppermute x40, starting transfers between devices, swap(): return lax.ppermute(value, 'ep', pairs)  41.8 us
    dot_general x18, matrix products, dot(): lax.dot_general(a, b, (dims, ((), ())), preferred_element_type=jnp.float32)  28.7 us
    unnamed x34, local copies, waits for them, and re-layouts  9.36 us
  transfers between devices with their start and end apart: 40, of which 20 were waited for; matrix products, arithmetic and copies ran while one was open for 22% of the time, Pallas kernels for 0%

profile of v3, /device:TPU:0, one launch (start us, length us, event | category | flops | bytes accessed | tf_op | source)
XLA Modules:
  0.0 178.0 jit_solution(3641651155376755306)
XLA Ops:
  0.6 4.1 %collective-permute-start.4 = (bf16[128,1024]{1,0:T(8,128)(2,1)}, bf16[128,1024]{1,0:T(8,128)(2,1)S(1)}, u32[]{:S(2)}, u32[]{:S(2)}) collective-permute-start(bf16[128,1024]{1,0:T(8,128)(2,1)} %param.7), channel_id=1, source_target_pairs={{0,8},{1,9},{2,10},{3,11},{4,12},{5,13},{6,14},{7,15},{8,0},{9,1},... | collective-permute-start | bytes 786440 | tf_op jit(solution)/shard_map/ppermute | solution.py:113
  4.7 1.6 collective-permute-start.3
  9.4 1.7 constant_dynamic-update-slice_fusion.7
  11.1 1.8 constant_dynamic-update-slice_fusion.15
  13.0 4.9 %collective-permute-done = f32[1,16,128]{2,0,1:T(1,128)S(1)} collective-permute-done((f32[1,16,128]{2,0,1:T(1,128)S(1)}, f32[1,16,128]{2,0,1:T(1,128)S(1)}, u32[]{:S(2)}, u32[]{:S(2)}) %collective-permute-start) | collective-permute-done | bytes 8224 | tf_op jit(solution)/shard_map/ppermute | solution.py:113
  17.9 2.0 %collective-permute-start.1 = (f32[2,16,128]{2,0,1:T(2,128)S(1)}, f32[2,16,128]{2,0,1:T(2,128)S(1)}, u32[]{:S(2)}, u32[]{:S(2)}) collective-permute-start(f32[2,16,128]{2,0,1:T(2,128)S(1)} %pad_maximum_fusion.2), channel_id=1, source_target_pairs={{0,8},{1,9},{2,10},{3,11},{4,12},{5,13},{6,14},{7,15},{8,0},{9,1},... | collective-permute-start | bytes 49160 | tf_op jit(solution)/shard_map/ppermute | solution.py:113
  20.0 8.9 %collective-permute-done.1 = f32[2,16,128]{2,0,1:T(2,128)S(1)} collective-permute-done((f32[2,16,128]{2,0,1:T(2,128)S(1)}, f32[2,16,128]{2,0,1:T(2,128)S(1)}, u32[]{:S(2)}, u32[]{:S(2)}) %collective-permute-start.1) | collective-permute-done | bytes 16416 | tf_op jit(solution)/shard_map/ppermute | solution.py:113
  28.9 1.6 collective-permute-start.2
  30.6 2.3 %collective-permute-done.2 = f32[4,16,128]{2,0,1:T(4,128)S(1)} collective-permute-done((f32[4,16,128]{2,0,1:T(4,128)S(1)}, f32[4,16,128]{2,0,1:T(4,128)S(1)}, u32[]{:S(2)}, u32[]{:S(2)}) %collective-permute-start.2) | collective-permute-done | bytes 32800 | tf_op jit(solution)/shard_map/ppermute | solution.py:113
  38.6 3.7 %collective-permute-done.20 = bf16[128,1024]{1,0:T(8,128)(2,1)S(1)} collective-permute-done((bf16[128,1024]{1,0:T(8,128)(2,1)}, bf16[128,1024]{1,0:T(8,128)(2,1)S(1)}, u32[]{:S(2)}, u32[]{:S(2)}) %collective-permute-start.20) | collective-permute-done | bytes 262176 | tf_op jit(solution)/shard_map/ppermute | solution.py:113
  47.0 1.7 collective-permute-start.22
  49.4 2.7 %collective-permute-done.7 = bf16[128,1024]{1,0:T(8,128)(2,1)S(1)} collective-permute-done((bf16[128,1024]{1,0:T(8,128)(2,1)S(1)}, bf16[128,1024]{1,0:T(8,128)(2,1)S(1)}, u32[]{:S(2)}, u32[]{:S(2)}) %collective-permute-start.7) | collective-permute-done | bytes 262176 | tf_op jit(solution)/shard_map/ppermute | solution.py:113
  52.8 4.5 %collective-permute-done.8 = bf16[128,1024]{1,0:T(8,128)(2,1)S(1)} collective-permute-done((bf16[128,1024]{1,0:T(8,128)(2,1)S(1)}, bf16[128,1024]{1,0:T(8,128)(2,1)S(1)}, u32[]{:S(2)}, u32[]{:S(2)}) %collective-permute-start.8) | collective-permute-done | bytes 262176 | tf_op jit(solution)/shard_map/ppermute | solution.py:113
  61.4 5.1 %collective-permute-done.24 = bf16[128,1024]{1,0:T(8,128)(2,1)S(1)} collective-permute-done((bf16[128,1024]{1,0:T(8,128)(2,1)S(1)}, bf16[128,1024]{1,0:T(8,128)(2,1)S(1)}, u32[]{:S(2)}, u32[]{:S(2)}) %collective-permute-start.24) | collective-permute-done | bytes 262176 | tf_op jit(solution)/shard_map/ppermute | solution.py:113
  66.6 5.6 %collective-permute-done.25 = bf16[128,1024]{1,0:T(8,128)(2,1)S(1)} collective-permute-done((bf16[128,1024]{1,0:T(8,128)(2,1)S(1)}, bf16[128,1024]{1,0:T(8,128)(2,1)S(1)}, u32[]{:S(2)}, u32[]{:S(2)}) %collective-permute-start.25) | collective-permute-done | bytes 262176 | tf_op jit(solution)/shard_map/ppermute | solution.py:113
  73.4 4.4 %collective-permute-done.9 = bf16[128,1024]{1,0:T(8,128)(2,1)S(1)} collective-permute-done((bf16[128,1024]{1,0:T(8,128)(2,1)S(1)}, bf16[128,1024]{1,0:T(8,128)(2,1)S(1)}, u32[]{:S(2)}, u32[]{:S(2)}) %collective-permute-start.9) | collective-permute-done | bytes 262176 | tf_op jit(solution)/shard_map/ppermute | solution.py:113
  80.4 1.7 collective-permute-done.26
  82.1 2.2 %multiply_reduce_fusion.1 = (f32[1024]{0:T(1024)S(1)}, bf16[1024,512]{0,1:T(8,128)(2,1)S(1)}, bf16[1024,512]{0,1:T(8,128)(2,1)S(1)}, bf16[1024,512]{0,1:T(8,128)(2,1)S(1)}) fusion(f32[1024,512]{0,1:T(8,128)S(1)} %fusion.17, f32[1024,512]{0,1:T(8,128)S(1)} %fusion.21, f32[1024]{0:T(1024)S(1)} %get-tuple-element.33, ...), kind=kOutput, calls=%fused_computation.7 | convolution fusion | flops 1083702272 | bytes 10493952 | tf_op jit(solution)/shard_map/dot_general | solution.py:108
  91.2 2.3 %multiply_reduce_fusion = (f32[1024]{0:T(1024)S(1)}, bf16[1024,512]{0,1:T(8,128)(2,1)S(1)}, bf16[1024,512]{0,1:T(8,128)(2,1)S(1)}, bf16[1024,512]{0,1:T(8,128)(2,1)S(1)}) fusion(f32[1024,512]{0,1:T(8,128)S(1)} %fusion.26, f32[1024,512]{0,1:T(8,128)S(1)} %fusion.25, f32[1024]{0:T(1024)S(1)} %get-tuple-element.32, ...), kind=kOutput, calls=%fused_computation.6 | convolution fusion | flops 1083702272 | bytes 10493952 | tf_op jit(solution)/shard_map/dot_general | solution.py:108
  107.3 2.2 %collective-permute-done.17 = bf16[128,1024]{1,0:T(8,128)(2,1)S(1)} collective-permute-done((bf16[128,1024]{1,0:T(8,128)(2,1)S(1)}, bf16[128,1024]{1,0:T(8,128)(2,1)S(1)}, u32[]{:S(2)}, u32[]{:S(2)}) %collective-permute-start.17) | collective-permute-done | bytes 262176 | tf_op jit(solution)/shard_map/ppermute | solution.py:113
  110.3 10.4 %collective-permute-done.14 = bf16[128,1024]{1,0:T(8,128)(2,1)S(1)} collective-permute-done((bf16[128,1024]{1,0:T(8,128)(2,1)S(1)}, bf16[128,1024]{1,0:T(8,128)(2,1)S(1)}, u32[]{:S(2)}, u32[]{:S(2)}) %collective-permute-start.14) | collective-permute-done | bytes 262176 | tf_op jit(solution)/shard_map/ppermute | solution.py:113
  120.7 2.4 %collective-permute-start.35 = (f32[2,2,2,128]{3,2,1,0:T(2,128)S(1)}, f32[2,2,2,128]{3,2,1,0:T(2,128)S(1)}, u32[]{:S(2)}, u32[]{:S(2)}) collective-permute-start(f32[2,2,2,128]{3,2,1,0:T(2,128)S(1)} %get-tuple-element.29), channel_id=1, source_target_pairs={{0,8},{1,9},{2,10},{3,11},{4,12},{5,13},{6,14},{7,15},{8,0},{9,1},... | collective-permute-start | bytes 12296 | tf_op jit(solution)/shard_map/ppermute | solution.py:113
  123.3 1.9 %collective-permute-done.35 = f32[2,2,2,128]{3,2,1,0:T(2,128)S(1)} collective-permute-done((f32[2,2,2,128]{3,2,1,0:T(2,128)S(1)}, f32[2,2,2,128]{3,2,1,0:T(2,128)S(1)}, u32[]{:S(2)}, u32[]{:S(2)}) %collective-permute-start.35) | collective-permute-done | bytes 4128 | tf_op jit(solution)/shard_map/ppermute | solution.py:113
  127.3 4.6 %collective-permute-done.28 = bf16[128,1024]{1,0:T(8,128)(2,1)S(1)} collective-permute-done((bf16[128,1024]{1,0:T(8,128)(2,1)S(1)}, bf16[128,1024]{1,0:T(8,128)(2,1)S(1)}, u32[]{:S(2)}, u32[]{:S(2)}) %collective-permute-start.28) | collective-permute-done | bytes 262176 | tf_op jit(solution)/shard_map/ppermute | solution.py:113
  137.4 5.4 %collective-permute-done.30 = bf16[128,1024]{1,0:T(8,128)(2,1)S(1)} collective-permute-done((bf16[128,1024]{1,0:T(8,128)(2,1)S(1)}, bf16[128,1024]{1,0:T(8,128)(2,1)S(1)}, u32[]{:S(2)}, u32[]{:S(2)}) %collective-permute-start.30) | collective-permute-done | bytes 262176 | tf_op jit(solution)/shard_map/ppermute | solution.py:113
  142.8 2.4 %collective-permute-start.19 = (bf16[128,1024]{1,0:T(8,128)(2,1)S(1)}, bf16[128,1024]{1,0:T(8,128)(2,1)S(1)}, u32[]{:S(2)}, u32[]{:S(2)}) collective-permute-start(bf16[128,1024]{1,0:T(8,128)(2,1)S(1)} %add_convert_fusion.10), channel_id=1, source_target_pairs={{0,8},{1,9},{2,10},{3,11},{4,12},{5,13},{6,14},{7,15},{8,0},{9,1},... | collective-permute-start | bytes 786440 | tf_op jit(solution)/shard_map/ppermute | solution.py:113
  146.2 1.8 collective-permute-done.15
  148.2 9.1 %collective-permute-done.19 = bf16[128,1024]{1,0:T(8,128)(2,1)S(1)} collective-permute-done((bf16[128,1024]{1,0:T(8,128)(2,1)S(1)}, bf16[128,1024]{1,0:T(8,128)(2,1)S(1)}, u32[]{:S(2)}, u32[]{:S(2)}) %collective-permute-start.19) | collective-permute-done | bytes 262176 | tf_op jit(solution)/shard_map/ppermute | solution.py:113
  159.0 11.3 %collective-permute-done.33 = bf16[128,1024]{1,0:T(8,128)(2,1)S(1)} collective-permute-done((bf16[128,1024]{1,0:T(8,128)(2,1)S(1)}, bf16[128,1024]{1,0:T(8,128)(2,1)S(1)}, u32[]{:S(2)}, u32[]{:S(2)}) %collective-permute-start.33) | collective-permute-done | bytes 262176 | tf_op jit(solution)/shard_map/ppermute | solution.py:113
  171.1 2.3 %fusion.3 = bf16[1,1024,512]{2,1,0:T(8,128)(2,1)} fusion(bf16[1024,512]{1,0:T(8,128)(2,1)S(1)} %collective-permute-done.38, bf16[1024,1024]{1,0:T(8,128)(2,1)S(1)} %constant_dynamic-update-slice_fusion, bf16[1024,512]{0,1:T(8,128)(2,1)S(1)} %copy-done.9), kind=kOutput, calls=%fused_computation.22 | convolution fusion | flops 1075314688 | bytes 5242880 | tf_op jit(solution)/shard_map/dot_general | solution.py:108
  173.4 2.2 %fusion.4 = bf16[1,512,1024]{2,1,0:T(8,128)(2,1)} fusion(bf16[512,1024]{1,0:T(8,128)(2,1)S(1)} %collective-permute-done.39, bf16[1024,512]{0,1:T(8,128)(2,1)S(1)} %get-tuple-element.12, bf16[1024,1024]{1,0:T(8,128)(2,1)S(1)} %constant_dynamic-update-slice_fusion.8), kind=kOutput, calls=%fused_computation.23 | convolution fusion | flops 1075314688 | bytes 5242880 | tf_op jit(solution)/shard_map/dot_general | solution.py:108
  175.7 2.3 %fusion.2 = bf16[1,1024,512]{2,1,0:T(8,128)(2,1)} fusion(bf16[1024,512]{1,0:T(8,128)(2,1)S(1)} %collective-permute-done.37, bf16[1024,1024]{1,0:T(8,128)(2,1)S(1)} %constant_dynamic-update-slice_fusion, bf16[1024,512]{0,1:T(8,128)(2,1)S(1)} %copy-done.7), kind=kOutput, calls=%fused_computation.21 | convolution fusion | flops 1075314688 | bytes 5242880 | tf_op jit(solution)/shard_map/dot_general | solution.py:108
  (128 shorter events, 56.0 us)
Async XLA Ops:
  0.6 33.5 %collective-permute-start.4 = (bf16[128,1024]{1,0:T(8,128)(2,1)}, bf16[128,1024]{1,0:T(8,128)(2,1)S(1)}, u32[]{:S(2)}, u32[]{:S(2)}) collective-permute-start(bf16[128,1024]{1,0:T(8,128)(2,1)} %param.7), channel_id=1, source_target_pairs={{0,8},{1,9},{2,10},{3,11},{4,12},{5,13},{6,14},{7,15},{8,0},{9,1},... | collective-permute-start | bytes 786440 | tf_op jit(solution)/shard_map/ppermute | solution.py:113
  4.7 31.0 %collective-permute-start.3 = (bf16[128,1024]{1,0:T(8,128)(2,1)}, bf16[128,1024]{1,0:T(8,128)(2,1)S(1)}, u32[]{:S(2)}, u32[]{:S(2)}) collective-permute-start(bf16[128,1024]{1,0:T(8,128)(2,1)} %param.7), channel_id=1, source_target_pairs={{0,4},{1,5},{2,6},{3,7},{4,0},{5,1},{6,2},{7,3},{8,12},{9,13},{10,... | collective-permute-start | bytes 786440 | tf_op jit(solution)/shard_map/ppermute | solution.py:113
  6.3 40.7 %collective-permute-start.6 = (bf16[128,1024]{1,0:T(8,128)(2,1)}, bf16[128,1024]{1,0:T(8,128)(2,1)S(1)}, u32[]{:S(2)}, u32[]{:S(2)}) collective-permute-start(bf16[128,1024]{1,0:T(8,128)(2,1)} %param.7), channel_id=1, source_target_pairs={{0,2},{1,3},{2,0},{3,1},{4,6},{5,7},{6,4},{7,5},{8,10},{9,11},{10,... | collective-permute-start | bytes 786440 | tf_op jit(solution)/shard_map/ppermute | solution.py:113
  8.5 9.4 %collective-permute-start = (f32[1,16,128]{2,0,1:T(1,128)S(1)}, f32[1,16,128]{2,0,1:T(1,128)S(1)}, u32[]{:S(2)}, u32[]{:S(2)}) collective-permute-start(f32[1,16,128]{2,0,1:T(1,128)S(1)} %bitcast.90), channel_id=1, source_target_pairs={{0,4},{1,5},{2,6},{3,7},{4,0},{5,1},{6,2},{7,3},{8,12},{9,13},{10,... | collective-permute-start | bytes 24584 | tf_op jit(solution)/shard_map/ppermute | solution.py:113
  9.1 33.9 %collective-permute-start.21 = (bf16[128,1024]{1,0:T(8,128)(2,1)}, bf16[128,1024]{1,0:T(8,128)(2,1)S(1)}, u32[]{:S(2)}, u32[]{:S(2)}) collective-permute-start(bf16[128,1024]{1,0:T(8,128)(2,1)} %param.10), channel_id=1, source_target_pairs={{0,8},{1,9},{2,10},{3,11},{4,12},{5,13},{6,14},{7,15},{8,0},{9,1},... | collective-permute-start | bytes 786440 | tf_op jit(solution)/shard_map/ppermute | solution.py:113
  17.9 10.9 %collective-permute-start.1 = (f32[2,16,128]{2,0,1:T(2,128)S(1)}, f32[2,16,128]{2,0,1:T(2,128)S(1)}, u32[]{:S(2)}, u32[]{:S(2)}) collective-permute-start(f32[2,16,128]{2,0,1:T(2,128)S(1)} %pad_maximum_fusion.2), channel_id=1, source_target_pairs={{0,8},{1,9},{2,10},{3,11},{4,12},{5,13},{6,14},{7,15},{8,0},{9,1},... | collective-permute-start | bytes 49160 | tf_op jit(solution)/shard_map/ppermute | solution.py:113
  32.9 9.4 %collective-permute-start.20 = (bf16[128,1024]{1,0:T(8,128)(2,1)}, bf16[128,1024]{1,0:T(8,128)(2,1)S(1)}, u32[]{:S(2)}, u32[]{:S(2)}) collective-permute-start(bf16[128,1024]{1,0:T(8,128)(2,1)} %param.10), channel_id=1, source_target_pairs={{0,4},{1,5},{2,6},{3,7},{4,0},{5,1},{6,2},{7,3},{8,12},{9,13},{10,... | collective-permute-start | bytes 786440 | tf_op jit(solution)/shard_map/ppermute | solution.py:113
  34.2 25.9 %collective-permute-start.23 = (bf16[128,1024]{1,0:T(8,128)(2,1)}, bf16[128,1024]{1,0:T(8,128)(2,1)S(1)}, u32[]{:S(2)}, u32[]{:S(2)}) collective-permute-start(bf16[128,1024]{1,0:T(8,128)(2,1)} %param.10), channel_id=1, source_target_pairs={{0,2},{1,3},{2,0},{3,1},{4,6},{5,7},{6,4},{7,5},{8,10},{9,11},{10,... | collective-permute-start | bytes 786440 | tf_op jit(solution)/shard_map/ppermute | solution.py:113
  42.2 48.9 %collective-permute-start.12 = (bf16[512,1024]{1,0:T(8,128)(2,1)S(1)}, bf16[512,1024]{1,0:T(8,128)(2,1)S(1)}, u32[]{:S(2)}, u32[]{:S(2)}) collective-permute-start(bf16[512,1024]{1,0:T(8,128)(2,1)S(1)} %bitcast.89), channel_id=1, source_target_pairs={{0,1},{1,0},{2,3},{3,2},{4,5},{5,4},{6,7},{7,6},{8,9},{9,8},{10,11... | collective-permute-start | bytes 3145736 | tf_op jit(solution)/shard_map/ppermute | solution.py:113
  45.1 12.3 %collective-permute-start.8 = (bf16[128,1024]{1,0:T(8,128)(2,1)S(1)}, bf16[128,1024]{1,0:T(8,128)(2,1)S(1)}, u32[]{:S(2)}, u32[]{:S(2)}) collective-permute-start(bf16[128,1024]{1,0:T(8,128)(2,1)S(1)} %collective-permute-done.4), channel_id=1, source_target_pairs={{0,2},{1,3},{2,0},{3,1},{4,6},{5,7},{6,4},{7,5},{8,10},{9,11},{10,... | collective-permute-start | bytes 786440 | tf_op jit(solution)/shard_map/ppermute | solution.py:113
  47.0 12.3 %collective-permute-start.22 = (bf16[128,1024]{1,0:T(8,128)(2,1)S(1)}, bf16[128,1024]{1,0:T(8,128)(2,1)S(1)}, u32[]{:S(2)}, u32[]{:S(2)}) collective-permute-start(bf16[128,1024]{1,0:T(8,128)(2,1)S(1)} %collective-permute-done.21), channel_id=1, source_target_pairs={{0,4},{1,5},{2,6},{3,7},{4,0},{5,1},{6,2},{7,3},{8,12},{9,13},{10,... | collective-permute-start | bytes 786440 | tf_op jit(solution)/shard_map/ppermute | solution.py:113
  52.1 36.2 %collective-permute-start.11 = (bf16[1024,512]{1,0:T(8,128)(2,1)S(1)}, bf16[1024,512]{1,0:T(8,128)(2,1)S(1)}, u32[]{:S(2)}, u32[]{:S(2)}) collective-permute-start(bf16[1024,512]{1,0:T(8,128)(2,1)S(1)} %bitcast.98), channel_id=1, source_target_pairs={{0,1},{1,0},{2,3},{3,2},{4,5},{5,4},{6,7},{7,6},{8,9},{9,8},{10,11... | collective-permute-start | bytes 3145736 | tf_op jit(solution)/shard_map/ppermute | solution.py:113
  59.3 12.9 %collective-permute-start.25 = (bf16[128,1024]{1,0:T(8,128)(2,1)S(1)}, bf16[128,1024]{1,0:T(8,128)(2,1)S(1)}, u32[]{:S(2)}, u32[]{:S(2)}) collective-permute-start(bf16[128,1024]{1,0:T(8,128)(2,1)S(1)} %collective-permute-done.21), channel_id=1, source_target_pairs={{0,2},{1,3},{2,0},{3,1},{4,6},{5,7},{6,4},{7,5},{8,10},{9,11},{10,... | collective-permute-start | bytes 786440 | tf_op jit(solution)/shard_map/ppermute | solution.py:113
  60.1 17.7 %collective-permute-start.9 = (bf16[128,1024]{1,0:T(8,128)(2,1)S(1)}, bf16[128,1024]{1,0:T(8,128)(2,1)S(1)}, u32[]{:S(2)}, u32[]{:S(2)}) collective-permute-start(bf16[128,1024]{1,0:T(8,128)(2,1)S(1)} %collective-permute-done.5), channel_id=1, source_target_pairs={{0,2},{1,3},{2,0},{3,1},{4,6},{5,7},{6,4},{7,5},{8,10},{9,11},{10,... | collective-permute-start | bytes 786440 | tf_op jit(solution)/shard_map/ppermute | solution.py:113
  66.5 23.1 %collective-permute-start.10 = (bf16[1024,512]{1,0:T(8,128)(2,1)S(1)}, bf16[1024,512]{1,0:T(8,128)(2,1)S(1)}, u32[]{:S(2)}, u32[]{:S(2)}) collective-permute-start(bf16[1024,512]{1,0:T(8,128)(2,1)S(1)} %bitcast.99), channel_id=1, source_target_pairs={{0,1},{1,0},{2,3},{3,2},{4,5},{5,4},{6,7},{7,6},{8,9},{9,8},{10,11... | collective-permute-start | bytes 3145736 | tf_op jit(solution)/shard_map/ppermute | solution.py:113
  72.1 10.0 %collective-permute-start.26 = (bf16[128,1024]{1,0:T(8,128)(2,1)S(1)}, bf16[128,1024]{1,0:T(8,128)(2,1)S(1)}, u32[]{:S(2)}, u32[]{:S(2)}) collective-permute-start(bf16[128,1024]{1,0:T(8,128)(2,1)S(1)} %collective-permute-done.22), channel_id=1, source_target_pairs={{0,2},{1,3},{2,0},{3,1},{4,6},{5,7},{6,4},{7,5},{8,10},{9,11},{10,... | collective-permute-start | bytes 786440 | tf_op jit(solution)/shard_map/ppermute | solution.py:113
  93.6 12.4 %collective-permute-start.34 = (f32[4,1,2,128]{3,2,1,0:T(2,128)S(1)}, f32[4,1,2,128]{3,2,1,0:T(2,128)S(1)}, u32[]{:S(2)}, u32[]{:S(2)}) collective-permute-start(f32[4,1,2,128]{3,2,1,0:T(2,128)S(1)} %get-tuple-element.31), channel_id=1, source_target_pairs={{0,2},{1,3},{2,0},{3,1},{4,6},{5,7},{6,4},{7,5},{8,10},{9,11},{10,... | collective-permute-start | bytes 12296 | tf_op jit(solution)/shard_map/ppermute | solution.py:113
  98.7 72.4 %collective-permute-start.38 = (bf16[1024,512]{1,0:T(8,128)(2,1)S(1)}, bf16[1024,512]{1,0:T(8,128)(2,1)S(1)}, u32[]{:S(2)}, u32[]{:S(2)}) collective-permute-start(bf16[1024,512]{1,0:T(8,128)(2,1)S(1)} %convolution_convert_fusion.1), channel_id=1, source_target_pairs={{0,1},{1,0},{2,3},{3,2},{4,5},{5,4},{6,7},{7,6},{8,9},{9,8},{10,11... | collective-permute-start | bytes 3145736 | tf_op jit(solution)/shard_map/ppermute | solution.py:113
  101.2 31.8 %collective-permute-start.16 = (bf16[128,1024]{1,0:T(8,128)(2,1)S(1)}, bf16[128,1024]{1,0:T(8,128)(2,1)S(1)}, u32[]{:S(2)}, u32[]{:S(2)}) collective-permute-start(bf16[128,1024]{1,0:T(8,128)(2,1)S(1)} %get-tuple-element.22), channel_id=1, source_target_pairs={{0,2},{1,3},{2,0},{3,1},{4,6},{5,7},{6,4},{7,5},{8,10},{9,11},{10,... | collective-permute-start | bytes 786440 | tf_op jit(solution)/shard_map/ppermute | solution.py:113
  102.4 18.3 %collective-permute-start.14 = (bf16[128,1024]{1,0:T(8,128)(2,1)S(1)}, bf16[128,1024]{1,0:T(8,128)(2,1)S(1)}, u32[]{:S(2)}, u32[]{:S(2)}) collective-permute-start(bf16[128,1024]{1,0:T(8,128)(2,1)S(1)} %get-tuple-element.23), channel_id=1, source_target_pairs={{0,2},{1,3},{2,0},{3,1},{4,6},{5,7},{6,4},{7,5},{8,10},{9,11},{10,... | collective-permute-start | bytes 786440 | tf_op jit(solution)/shard_map/ppermute | solution.py:113
  106.0 20.7 %collective-permute-start.31 = (bf16[128,1024]{1,0:T(8,128)(2,1)S(1)}, bf16[128,1024]{1,0:T(8,128)(2,1)S(1)}, u32[]{:S(2)}, u32[]{:S(2)}) collective-permute-start(bf16[128,1024]{1,0:T(8,128)(2,1)S(1)} %get-tuple-element.15), channel_id=1, source_target_pairs={{0,2},{1,3},{2,0},{3,1},{4,6},{5,7},{6,4},{7,5},{8,10},{9,11},{10,... | collective-permute-start | bytes 786440 | tf_op jit(solution)/shard_map/ppermute | solution.py:113
  109.5 22.5 %collective-permute-start.28 = (bf16[128,1024]{1,0:T(8,128)(2,1)S(1)}, bf16[128,1024]{1,0:T(8,128)(2,1)S(1)}, u32[]{:S(2)}, u32[]{:S(2)}) collective-permute-start(bf16[128,1024]{1,0:T(8,128)(2,1)S(1)} %get-tuple-element.17), channel_id=1, source_target_pairs={{0,2},{1,3},{2,0},{3,1},{4,6},{5,7},{6,4},{7,5},{8,10},{9,11},{10,... | collective-permute-start | bytes 786440 | tf_op jit(solution)/shard_map/ppermute | solution.py:113
  126.7 18.9 %collective-permute-start.13 = (bf16[128,1024]{1,0:T(8,128)(2,1)S(1)}, bf16[128,1024]{1,0:T(8,128)(2,1)S(1)}, u32[]{:S(2)}, u32[]{:S(2)}) collective-permute-start(bf16[128,1024]{1,0:T(8,128)(2,1)S(1)} %get-tuple-element.20), channel_id=1, source_target_pairs={{0,2},{1,3},{2,0},{3,1},{4,6},{5,7},{6,4},{7,5},{8,10},{9,11},{10,... | collective-permute-start | bytes 786440 | tf_op jit(solution)/shard_map/ppermute | solution.py:113
  131.9 10.8 %collective-permute-start.30 = (bf16[128,1024]{1,0:T(8,128)(2,1)S(1)}, bf16[128,1024]{1,0:T(8,128)(2,1)S(1)}, u32[]{:S(2)}, u32[]{:S(2)}) collective-permute-start(bf16[128,1024]{1,0:T(8,128)(2,1)S(1)} %get-tuple-element.16), channel_id=1, source_target_pairs={{0,2},{1,3},{2,0},{3,1},{4,6},{5,7},{6,4},{7,5},{8,10},{9,11},{10,... | collective-permute-start | bytes 786440 | tf_op jit(solution)/shard_map/ppermute | solution.py:113
  133.8 11.4 %collective-permute-start.32 = (bf16[128,1024]{1,0:T(8,128)(2,1)S(1)}, bf16[128,1024]{1,0:T(8,128)(2,1)S(1)}, u32[]{:S(2)}, u32[]{:S(2)}) collective-permute-start(bf16[128,1024]{1,0:T(8,128)(2,1)S(1)} %get-tuple-element.19), channel_id=1, source_target_pairs={{0,4},{1,5},{2,6},{3,7},{4,0},{5,1},{6,2},{7,3},{8,12},{9,13},{10,... | collective-permute-start | bytes 786440 | tf_op jit(solution)/shard_map/ppermute | solution.py:113
  136.7 11.3 %collective-permute-start.15 = (bf16[128,1024]{1,0:T(8,128)(2,1)S(1)}, bf16[128,1024]{1,0:T(8,128)(2,1)S(1)}, u32[]{:S(2)}, u32[]{:S(2)}) collective-permute-start(bf16[128,1024]{1,0:T(8,128)(2,1)S(1)} %get-tuple-element.24), channel_id=1, source_target_pairs={{0,4},{1,5},{2,6},{3,7},{4,0},{5,1},{6,2},{7,3},{8,12},{9,13},{10,... | collective-permute-start | bytes 786440 | tf_op jit(solution)/shard_map/ppermute | solution.py:113
  142.8 14.6 %collective-permute-start.19 = (bf16[128,1024]{1,0:T(8,128)(2,1)S(1)}, bf16[128,1024]{1,0:T(8,128)(2,1)S(1)}, u32[]{:S(2)}, u32[]{:S(2)}) collective-permute-start(bf16[128,1024]{1,0:T(8,128)(2,1)S(1)} %add_convert_fusion.10), channel_id=1, source_target_pairs={{0,8},{1,9},{2,10},{3,11},{4,12},{5,13},{6,14},{7,15},{8,0},{9,1},... | collective-permute-start | bytes 786440 | tf_op jit(solution)/shard_map/ppermute | solution.py:113
  145.2 28.3 %collective-permute-start.39 = (bf16[512,1024]{1,0:T(8,128)(2,1)S(1)}, bf16[512,1024]{1,0:T(8,128)(2,1)S(1)}, u32[]{:S(2)}, u32[]{:S(2)}) collective-permute-start(bf16[512,1024]{1,0:T(8,128)(2,1)S(1)} %convolution_convert_fusion), channel_id=1, source_target_pairs={{0,1},{1,0},{2,3},{3,2},{4,5},{5,4},{6,7},{7,6},{8,9},{9,8},{10,11... | collective-permute-start | bytes 3145736 | tf_op jit(solution)/shard_map/ppermute | solution.py:113
  145.6 13.3 %collective-permute-start.27 = (bf16[128,1024]{1,0:T(8,128)(2,1)S(1)}, bf16[128,1024]{1,0:T(8,128)(2,1)S(1)}, u32[]{:S(2)}, u32[]{:S(2)}) collective-permute-start(bf16[128,1024]{1,0:T(8,128)(2,1)S(1)} %get-tuple-element.14), channel_id=1, source_target_pairs={{0,2},{1,3},{2,0},{3,1},{4,6},{5,7},{6,4},{7,5},{8,10},{9,11},{10,... | collective-permute-start | bytes 786440 | tf_op jit(solution)/shard_map/ppermute | solution.py:113
  148.0 11.0 %collective-permute-start.29 = (bf16[128,1024]{1,0:T(8,128)(2,1)S(1)}, bf16[128,1024]{1,0:T(8,128)(2,1)S(1)}, u32[]{:S(2)}, u32[]{:S(2)}) collective-permute-start(bf16[128,1024]{1,0:T(8,128)(2,1)S(1)} %get-tuple-element.18), channel_id=1, source_target_pairs={{0,4},{1,5},{2,6},{3,7},{4,0},{5,1},{6,2},{7,3},{8,12},{9,13},{10,... | collective-permute-start | bytes 786440 | tf_op jit(solution)/shard_map/ppermute | solution.py:113
  157.4 12.9 %collective-permute-start.33 = (bf16[128,1024]{1,0:T(8,128)(2,1)S(1)}, bf16[128,1024]{1,0:T(8,128)(2,1)S(1)}, u32[]{:S(2)}, u32[]{:S(2)}) collective-permute-start(bf16[128,1024]{1,0:T(8,128)(2,1)S(1)} %add_convert_fusion.6), channel_id=1, source_target_pairs={{0,8},{1,9},{2,10},{3,11},{4,12},{5,13},{6,14},{7,15},{8,0},{9,1},... | collective-permute-start | bytes 786440 | tf_op jit(solution)/shard_map/ppermute | solution.py:113
  158.9 16.7 %collective-permute-start.37 = (bf16[1024,512]{1,0:T(8,128)(2,1)S(1)}, bf16[1024,512]{1,0:T(8,128)(2,1)S(1)}, u32[]{:S(2)}, u32[]{:S(2)}) collective-permute-start(bf16[1024,512]{1,0:T(8,128)(2,1)S(1)} %convolution_convert_fusion.2), channel_id=1, source_target_pairs={{0,1},{1,0},{2,3},{3,2},{4,5},{5,4},{6,7},{7,6},{8,9},{9,8},{10,11... | collective-permute-start | bytes 3145736 | tf_op jit(solution)/shard_map/ppermute | solution.py:113
  (18 other events, 274.5 us)

commit v4 on v0

--- a/solution.py
+++ b/solution.py
@@ -1,6 +1,8 @@
 import jax
 import jax.numpy as jnp
 from jax import lax
+from jax.experimental import pallas as pl
+from jax.experimental.pallas import tpu as pltpu
 from jax.sharding import PartitionSpec as P
 
 
@@ -48,7 +50,7 @@
     return (grad_rows, grad_gw, grad_uw, grad_down)
 
 
-def local(latent_in, routes, combine_weights, cotangent, w_gate, w_up, w_down):
+def exchanged(latent_in, routes, combine_weights, cotangent, w_gate, w_up, w_down):
     devices_ep = lax.axis_size("ep")
     local_experts = w_gate.shape[0]
     expert_count = local_experts * devices_ep
@@ -104,6 +106,253 @@
     return (combined, grad_latent, grad_combine, grad_gw, grad_uw, grad_down)
 
 
+def dot(a, b, dims):
+    return lax.dot_general(a, b, (dims, ((), ())), preferred_element_type=jnp.float32)
+
+
+def swap(value, bit):
+    pairs = [(i, i ^ bit) for i in range(lax.axis_size("ep"))]
+    return lax.ppermute(value, "ep", pairs)
+
+
+CORE, SIDE, NEAR, FAR = 1, 2, 4, 8
+REACH = (0, NEAR, FAR, NEAR | FAR, SIDE, SIDE | NEAR, SIDE | FAR, SIDE | NEAR | FAR)
+HALVED = (0, SIDE, FAR, FAR | SIDE, NEAR, NEAR | SIDE, NEAR | FAR, NEAR | FAR | SIDE)
+
+
+def fence(*values):
+    return lax.optimization_barrier(values)
+
+
+def added(a, b):
+    return a.astype(jnp.float32) + b.astype(jnp.float32)
+
+
+def narrow(value):
+    return value.astype(jnp.bfloat16)
+
+
+MIB = 1 << 20
+
+
+def kernel(body, outs, flops, *operands):
+    whole = pl.BlockSpec(memory_space=pltpu.VMEM)
+    moved = sum(v.size * v.dtype.itemsize for v in (*operands, *outs))
+    return pl.pallas_call(
+        body,
+        out_shape=outs,
+        in_specs=[whole] * len(operands),
+        out_specs=[whole] * len(outs),
+        compiler_params=pltpu.CompilerParams(vmem_limit_bytes=24 * MIB),
+        cost_estimate=pl.CostEstimate(flops=flops, bytes_accessed=moved, transcendentals=0),
+    )(*operands)
+
+
+def shape(rows, columns, dtype):
+    return jax.ShapeDtypeStruct((rows, columns), dtype)
+
+
+def forward(blocks, weights, share):
+    bf16, f32 = jnp.bfloat16, jnp.float32
+    count, (tok_count, width) = len(blocks), blocks[0].shape
+    units, half = weights[0][0].shape[1], len(blocks) // 2
+    every = count * tok_count
+
+    def body(*refs):
+        x_refs, refs = refs[:count], refs[count:]
+        w_refs, share_ref, refs = (refs[0:3], refs[3:6]), refs[6], refs[7:]
+        y_refs, (rows_ref, gate_ref, up_ref, weighted_ref) = refs[:count], refs[count:]
+        for i, x_ref in enumerate(x_refs):
+            rows_ref[i * tok_count : (i + 1) * tok_count, :] = x_ref[...]
+        for start in (half, 0):
+            at = slice(start * tok_count, (start + half) * tok_count)
+            x, total = rows_ref[at, :], 0.0
+            for e, (gate_w, up_w, down_w) in enumerate(w_refs):
+                lanes = slice(e * units, (e + 1) * units)
+                gate_pre = dot(x, gate_w[...], ((1,), (0,)))
+                up_pre = dot(x, up_w[...], ((1,), (0,)))
+                gate_ref[at, lanes] = gate_pre
+                up_ref[at, lanes] = up_pre
+                hidden = gate_pre * jax.nn.sigmoid(gate_pre) * up_pre
+                part = []
+                for j in range(half):
+                    column = e * count + start + j
+                    part.append(share_ref[:, column : column + 1])
+                weighted = (jnp.concatenate(part, axis=0) * hidden).astype(bf16)
+                weighted_ref[at, lanes] = weighted
+                total = total + dot(weighted, down_w[...], ((1,), (0,)))
+            for j in range(half):
+                y_refs[start + j][...] = total[j * tok_count : (j + 1) * tok_count].astype(bf16)
+
+    outs = [shape(tok_count, width, bf16)] * count + [
+        shape(every, width, bf16),
+        shape(every, 2 * units, f32),
+        shape(every, 2 * units, f32),
+        shape(every, 2 * units, bf16),
+    ]
+    flops = 12 * every * width * units
+    outs = kernel(body, outs, flops, *blocks, *weights[0], *weights[1], share)
+    return outs[:count], *outs[count:]
+
+
+def backward(blocks, weights, share, gate_pre, up_pre):
+    bf16, f32 = jnp.bfloat16, jnp.float32
+    count, (tok_count, width) = len(blocks), blocks[0].shape
+    units, half = weights[0][0].shape[1], len(blocks) // 2
+    every = count * tok_count
+
+    def body(*refs):
+        c_refs, refs = refs[:count], refs[count:]
+        w_refs, (share_ref, gate_ref, up_ref), refs = (refs[0:3], refs[3:6]), refs[6:9], refs[9:]
+        g_refs, (cot_ref, inner_ref, factor_ref) = refs[:count], refs[count:]
+        for i, c_ref in enumerate(c_refs):
+            cot_ref[i * tok_count : (i + 1) * tok_count, :] = c_ref[...]
+        for start in (half, 0):
+            at = slice(start * tok_count, (start + half) * tok_count)
+            cot, total = cot_ref[at, :], 0.0
+            for e, (gate_w, up_w, down_w) in enumerate(w_refs):
+                lanes = slice(e * units, (e + 1) * units)
+                plain = dot(cot, down_w[...], ((1,), (1,)))
+                gate, up = gate_ref[at, lanes], up_ref[at, lanes]
+                sigma = jax.nn.sigmoid(gate)
+                silu_val = gate * sigma
+                inner = jnp.sum(silu_val * up * plain, axis=1, keepdims=True)
+                part = []
+                for j in range(half):
+                    column = e * count + start + j
+                    part.append(share_ref[:, column : column + 1])
+                    inner_ref[:, column : column + 1] = inner[j * tok_count : (j + 1) * tok_count]
+                grad_hidden = jnp.concatenate(part, axis=0) * plain
+                slope = sigma * (1.0 + gate * (1.0 - sigma))
+                grad_gate = (grad_hidden * up * slope).astype(bf16)
+                grad_up = (grad_hidden * silu_val).astype(bf16)
+                factor_ref[at, 2 * e * units : (2 * e + 1) * units] = grad_gate
+                factor_ref[at, (2 * e + 1) * units : (2 * e + 2) * units] = grad_up
+                total = total + dot(grad_gate, gate_w[...], ((1,), (1,)))
+                total = total + dot(grad_up, up_w[...], ((1,), (1,)))
+            for j in range(half):
+                g_refs[start + j][...] = total[j * tok_count : (j + 1) * tok_count].astype(bf16)
+
+    outs = [shape(tok_count, width, bf16)] * count + [
+        shape(every, width, bf16),
+        shape(tok_count, 2 * count, f32),
+        shape(every, 4 * units, bf16),
+    ]
+    flops = 12 * every * width * units
+    outs = kernel(body, outs, flops, *blocks, *weights[0], *weights[1], share, gate_pre, up_pre)
+    return outs[:count], *outs[count:]
+
+
+def weight_grads(expert, rows, cot, weighted, factors, away=None):
+    bf16 = jnp.bfloat16
+    (every, width), units = rows.shape, weighted.shape[1] // 2
+
+    def body(rows_ref, cot_ref, weighted_ref, factor_ref, *refs):
+        for number in range(3):
+            if number < 2:
+                left, right, lead = rows_ref, factor_ref, 0
+                lanes = slice((2 * expert + number) * units, (2 * expert + number + 1) * units)
+                columns, into = slice(number * units, (number + 1) * units), slice(0, width)
+            else:
+                left, right, lead = weighted_ref, cot_ref, expert * units
+                lanes, columns, into = slice(0, width), slice(0, width), slice(width, width + units)
+            for start in range(0, into.stop - into.start, units):
+                part = left[:, lead + start : lead + start + units]
+                value = dot(part, right[:, lanes], ((0,), (0,)))
+                at = slice(into.start + start, into.start + start + units)
+                if away is None:
+                    refs[0][at, columns] = value.astype(bf16)
+                else:
+                    value = value + refs[0][at, columns].astype(jnp.float32)
+                    refs[1 + number][start : start + units, :] = value.astype(bf16)
+
+    flops = 6 * every * width * units
+    operands = (rows, cot, weighted, factors)
+    if away is None:
+        return kernel(body, [shape(width + units, width, bf16)], flops, *operands)[0]
+    outs = [shape(width, units, bf16)] * 2 + [shape(units, width, bf16)]
+    return kernel(body, outs, flops, *operands, away)
+
+
+def doubled(value, arrived):
+    return jnp.concatenate([value, arrived], axis=0)
+
+
+def paired(latent_in, routes, combine_weights, cotangent, w_gate, w_up, w_down):
+    devices_ep = lax.axis_size("ep")
+    me = lax.axis_index("ep")
+    experts = jnp.arange(devices_ep, dtype=jnp.int32)
+    mine = jnp.stack([me, me ^ CORE])
+    own = (w_gate[0], w_up[0], w_down[0])
+
+    chosen = routes[None, :, :] == experts[:, None, None]
+    share = jnp.sum(jnp.where(chosen, combine_weights[None, :, :], 0.0), axis=2)[None]
+    x0, c0 = latent_in, cotangent
+
+    x2, x1, x4, c4 = swap(x0, FAR), swap(x0, NEAR), swap(x0, SIDE), swap(c0, SIDE)
+    arrived, gate_w = swap(share, NEAR), swap(own[0], CORE)
+    x1, x2, x4, c0, c4, arrived, gate_w, own = fence(x1, x2, x4, c0, c4, arrived, gate_w, own)
+    share = doubled(share, arrived)
+    x3, x5, x6, c2 = swap(x2, NEAR), swap(x1, SIDE), swap(x2, SIDE), swap(c0, FAR)
+    arrived, up_w = swap(share, FAR), swap(own[1], CORE)
+    x3, x5, x6, c0, c2, arrived, up_w, own = fence(x3, x5, x6, c0, c2, arrived, up_w, own)
+    share = doubled(share, arrived)
+    x7, c1, c3, c6 = swap(x3, SIDE), swap(c0, NEAR), swap(c2, NEAR), swap(c2, SIDE)
+    arrived, down_w = swap(share, SIDE), swap(own[2], CORE)
+    x7, c1, c3, c6, arrived, down_w, own = fence(x7, c1, c3, c6, arrived, down_w, own)
+    weights = (own, (gate_w, up_w, down_w))
+    share = doubled(share, arrived)[:, mine, :]
+    share = share.transpose(2, 1, 0).reshape(share.shape[2], -1)
+    share, c1, c3 = fence(share, c1, c3)
+    c5, c7 = swap(c1, SIDE), swap(c3, SIDE)
+    y, rows, gate_pre, up_pre, weighted = forward(
+        [x0, x1, x2, x3, x4, x5, x6, x7], weights, share
+    )
+    y, rows, c5, c7 = fence(y, rows, c5, c7)
+    y7, y6 = swap(y[7], SIDE), swap(y[6], SIDE)
+    g, cot, inner, factors = backward(
+        [c0, c1, c2, c3, c4, c5, c6, c7], weights, share, gate_pre, up_pre
+    )
+    y, g, cot, factors, inner, y7, y6 = fence(y, g, cot, factors, inner, y7, y6)
+    y3, y2 = narrow(added(y[3], y7)), added(y[2], y6)
+    inner = inner.T.reshape(2, len(REACH), 1, -1).transpose(1, 2, 0, 3)
+    y3, y2, inner, g = fence(y3, y2, inner, g)
+    y3, g7, g6, arrived = swap(y3, NEAR), swap(g[7], SIDE), swap(g[6], SIDE), swap(inner[4:], SIDE)
+    away = weight_grads(1, rows, cot, weighted, factors)
+    y, g, arrived, away, y3, y2, g7, g6 = fence(y, g, arrived, away, y3, y2, g7, g6)
+    g3, g2 = narrow(added(g[3], g7)), added(g[2], g6)
+    y2 = narrow(added(y2, y3))
+    inner = jnp.concatenate([inner[:4], arrived], axis=1)
+    y2, g3, g2, inner, g, y, away = fence(y2, g3, g2, inner, g, y, away)
+    y2, g3, g5, y5 = swap(y2, FAR), swap(g3, NEAR), swap(g[5], SIDE), swap(y[5], SIDE)
+    arrived, away = swap(inner[2:], FAR), swap(away, CORE)
+    y, g, arrived, away, y2, g3, g2, g5, y5 = fence(y, g, arrived, away, y2, g3, g2, g5, y5)
+    y1, g1 = narrow(added(y[1], y5)), narrow(added(g[1], g5))
+    g2 = narrow(added(g2, g3))
+    inner = jnp.concatenate([inner[:2], arrived], axis=1)
+    y1, g1, g2, inner, g, y, away = fence(y1, g1, g2, inner, g, y, away)
+    g2, y1, g1, y4, g4 = (
+        swap(g2, FAR), swap(y1, NEAR), swap(g1, NEAR), swap(y[4], SIDE), swap(g[4], SIDE),
+    )
+    arrived = swap(inner[1:], NEAR)
+    grad_w = weight_grads(0, rows, cot, weighted, factors, away)
+    y, g, arrived, grad_w, y1, g1, g2, y4, g4 = fence(y, g, arrived, grad_w, y1, g1, g2, y4, g4)
+
+    inner = jnp.concatenate([inner[:1], arrived], axis=1)[0]
+    combined = narrow(added(added(y[0], y4), added(y1, y2)))
+    grad_latent = narrow(added(added(g[0], g4), added(g1, g2)))
+    owner = jnp.stack([me ^ bits for bits in HALVED])
+    owner = jnp.stack([owner, owner ^ CORE], axis=1)
+    owns = routes[None, None, :, :] == owner[:, :, None, None]
+    grad_combine = jnp.sum(jnp.where(owns, inner[:, :, :, None], 0.0), axis=(0, 1))
+    return (combined, grad_latent, grad_combine, *[v[None] for v in grad_w])
+
+
+def local(latent_in, routes, combine_weights, cotangent, w_gate, w_up, w_down):
+    plan = paired if w_gate.shape[0] == 1 and lax.axis_size("ep") == 2 * len(REACH) else exchanged
+    return plan(latent_in, routes, combine_weights, cotangent, w_gate, w_up, w_down)
+
+
 def solution(mesh):
     return jax.shard_map(
         local,

time: 337 us -> 171 us (0.51)
  the two profiles are of different devices: /device:TPU:11 before, /device:TPU:0 now
where the time goes in v4:
time: 171 us; the launch traced here: 170 us
  waiting for transfers between devices  44.2 us (26%)
  local copies, waits for them, and re-layouts  42.8 us (25%)
  starting transfers between devices  41.3 us (24%)
  Pallas kernels  28.5 us (17%)
  other arithmetic  12.4 us (7%)
    ppermute x38, waiting for transfers between devices, swap(): return lax.ppermute(value, 'ep', pairs)  44.2 us
    unnamed x98, local copies, waits for them, and re-layouts  41.8 us
    ppermute x38, starting transfers between devices, swap(): return lax.ppermute(value, 'ep', pairs)  41.3 us
    pallas_call x4, Pallas kernels, kernel(): pl.pallas_call(body, out_shape=outs, in_specs=[whole] * len(operands), ou...  28.5 us
    convert_element_type x7, other arithmetic, narrow(): return value.astype(jnp.bfloat16)  8.57 us
  transfers between devices with their start and end apart: 38, of which 10 were waited for; matrix products, arithmetic and copies ran while one was open for 1% of the time, Pallas kernels for 17%

profile of v4, /device:TPU:0, one launch (start us, length us, event | category | flops | bytes accessed | tf_op | source)
XLA Modules:
  0.0 170.1 jit_solution(14872376696399714547)
XLA Ops:
  1.9 2.7 %collective-permute-start.4 = (f32[1,16,128]{2,0,1:T(1,128)S(1)}, f32[1,16,128]{2,0,1:T(1,128)S(1)}, u32[]{:S(2)}, u32[]{:S(2)}) collective-permute-start(f32[1,16,128]{2,0,1:T(1,128)S(1)} %bitcast.45), channel_id=1, source_target_pairs={{0,4},{1,5},{2,6},{3,7},{4,0},{5,1},{6,2},{7,3},{8,12},{9,13},{10,... | collective-permute-start | bytes 24584 | tf_op jit(solution)/shard_map/ppermute | solution.py:115
  4.6 3.0 %collective-permute-start.1 = (bf16[128,1024]{1,0:T(8,128)(2,1)}, bf16[128,1024]{1,0:T(8,128)(2,1)S(1)}, u32[]{:S(2)}, u32[]{:S(2)}) collective-permute-start(bf16[128,1024]{1,0:T(8,128)(2,1)} %refs_0_.1), channel_id=1, source_target_pairs={{0,8},{1,9},{2,10},{3,11},{4,12},{5,13},{6,14},{7,15},{8,0},{9,1},... | collective-permute-start | bytes 786440 | tf_op jit(solution)/shard_map/ppermute | solution.py:115
  7.6 1.5 collective-permute-start.2
  9.6 9.2 %collective-permute-done.refs_1_ = bf16[128,1024]{1,0:T(8,128)(2,1)S(1)} collective-permute-done((bf16[128,1024]{1,0:T(8,128)(2,1)}, bf16[128,1024]{1,0:T(8,128)(2,1)S(1)}, u32[]{:S(2)}, u32[]{:S(2)}) %collective-permute-start) | collective-permute-done | bytes 262176 | tf_op jit(solution)/shard_map/ppermute | solution.py:115
  18.8 2.5 %collective-permute-done.3.refs_4_ = bf16[128,1024]{1,0:T(8,128)(2,1)S(1)} collective-permute-done((bf16[128,1024]{1,0:T(8,128)(2,1)}, bf16[128,1024]{1,0:T(8,128)(2,1)S(1)}, u32[]{:S(2)}, u32[]{:S(2)}) %collective-permute-start.3) | collective-permute-done | bytes 262176 | tf_op jit(solution)/shard_map/ppermute | solution.py:115
  23.3 2.5 %collective-permute-start.6 = (bf16[128,1024]{1,0:T(8,128)(2,1)S(1)}, bf16[128,1024]{1,0:T(8,128)(2,1)S(1)}, u32[]{:S(2)}, u32[]{:S(2)}) collective-permute-start(bf16[128,1024]{1,0:T(8,128)(2,1)S(1)} %collective-permute-done.1.refs_2_), channel_id=1, source_target_pairs={{0,4},{1,5},{2,6},{3,7},{4,0},{5,1},{6,2},{7,3},{8,12},{9,13},{10,... | collective-permute-start | bytes 786440 | tf_op jit(solution)/shard_map/ppermute | solution.py:115
  28.6 1.7 collective-permute-start.9
  30.3 5.0 %collective-permute-done.6.refs_3_ = bf16[128,1024]{1,0:T(8,128)(2,1)S(1)} collective-permute-done((bf16[128,1024]{1,0:T(8,128)(2,1)S(1)}, bf16[128,1024]{1,0:T(8,128)(2,1)S(1)}, u32[]{:S(2)}, u32[]{:S(2)}) %collective-permute-start.6) | collective-permute-done | bytes 262176 | tf_op jit(solution)/shard_map/ppermute | solution.py:115
  35.3 4.3 %collective-permute-done.7.refs_5_ = bf16[128,1024]{1,0:T(8,128)(2,1)S(1)} collective-permute-done((bf16[128,1024]{1,0:T(8,128)(2,1)S(1)}, bf16[128,1024]{1,0:T(8,128)(2,1)S(1)}, u32[]{:S(2)}, u32[]{:S(2)}) %collective-permute-start.7) | collective-permute-done | bytes 262176 | tf_op jit(solution)/shard_map/ppermute | solution.py:115
  40.3 2.6 %collective-permute-done.9.refs_2_ = bf16[128,1024]{1,0:T(8,128)(2,1)S(1)} collective-permute-done((bf16[128,1024]{1,0:T(8,128)(2,1)}, bf16[128,1024]{1,0:T(8,128)(2,1)S(1)}, u32[]{:S(2)}, u32[]{:S(2)}) %collective-permute-start.9) | collective-permute-done | bytes 262176 | tf_op jit(solution)/shard_map/ppermute | solution.py:115
  44.0 1.6 collective-permute-start.16
  48.9 2.0 %collective-permute-start.13 = (bf16[128,1024]{1,0:T(8,128)(2,1)}, bf16[128,1024]{1,0:T(8,128)(2,1)}, u32[]{:S(2)}, u32[]{:S(2)}) collective-permute-start(bf16[128,1024]{1,0:T(8,128)(2,1)} %refs_0_.2), channel_id=1, source_target_pairs={{0,4},{1,5},{2,6},{3,7},{4,0},{5,1},{6,2},{7,3},{8,12},{9,13},{10,... | collective-permute-start | bytes 786440 | tf_op jit(solution)/shard_map/ppermute | solution.py:115
  51.0 3.7 %collective-permute-done.14.refs_3_ = bf16[128,1024]{1,0:T(8,128)(2,1)} collective-permute-done((bf16[128,1024]{1,0:T(8,128)(2,1)S(1)}, bf16[128,1024]{1,0:T(8,128)(2,1)}, u32[]{:S(2)}, u32[]{:S(2)}) %collective-permute-start.14) | collective-permute-done | bytes 262176 | tf_op jit(solution)/shard_map/ppermute | solution.py:115
  55.5 4.1 %collective-permute-done.12.refs_7_ = bf16[128,1024]{1,0:T(8,128)(2,1)S(1)} collective-permute-done((bf16[128,1024]{1,0:T(8,128)(2,1)S(1)}, bf16[128,1024]{1,0:T(8,128)(2,1)S(1)}, u32[]{:S(2)}, u32[]{:S(2)}) %collective-permute-start.12) | collective-permute-done | bytes 262176 | tf_op jit(solution)/shard_map/ppermute | solution.py:115
  76.2 6.9 %shard_map.118 = (bf16[128,1024]{1,0:T(8,128)(2,1)S(1)}, bf16[128,1024]{1,0:T(8,128)(2,1)S(1)}, bf16[128,1024]{1,0:T(8,128)(2,1)S(1)}, bf16[128,1024]{1,0:T(8,12...) custom-call(bf16[128,1024]{1,0:T(8,128)(2,1)S(1)} %copy-done.26, ...), custom_call_target="tpu_custom_call" | custom-call | flops 6442450944 | bytes 23076864 | tf_op jit(solution)/shard_map/pallas_call | solution.py:141
  88.8 10.1 %shard_map.119 = (bf16[128,1024]{1,0:T(8,128)(2,1)S(1)}, bf16[128,1024]{1,0:T(8,128)(2,1)S(1)}, bf16[128,1024]{1,0:T(8,128)(2,1)S(1)}, bf16[128,1024]{1,0:T(8,12...) custom-call(bf16[128,1024]{1,0:T(8,128)(2,1)S(1)} %copy-done.27, ...), custom_call_target="tpu_custom_call" | custom-call | flops 6442450944 | bytes 25182208 | tf_op jit(solution)/shard_map/pallas_call | solution.py:141
  98.9 2.0 %copy-done = bf16[1024,2048]{1,0:T(8,128)(2,1)} copy-done((bf16[1024,2048]{1,0:T(8,128)(2,1)}, bf16[1024,2048]{1,0:T(8,128)(2,1)S(1)}, u32[]{:S(2)}) %copy-start) | copy-done | bytes 4194328
  107.9 1.8 %collective-permute-start.23 = (bf16[128,1024]{1,0:T(8,128)(2,1)S(1)}, bf16[128,1024]{1,0:T(8,128)(2,1)S(1)}, u32[]{:S(2)}, u32[]{:S(2)}) collective-permute-start(bf16[128,1024]{1,0:T(8,128)(2,1)S(1)} %get-tuple-element.261), channel_id=1, source_target_pairs={{0,4},{1,5},{2,6},{3,7},{4,0},{5,1},{6,2},{7,3},{8,12},{9,13},{10,... | collective-permute-start | bytes 786440 | tf_op jit(solution)/shard_map/ppermute | solution.py:115
  112.3 2.2 %copy-done.1 = bf16[1024,2048]{1,0:T(8,128)(2,1)S(1)} copy-done((bf16[1024,2048]{1,0:T(8,128)(2,1)S(1)}, bf16[1024,2048]{1,0:T(8,128)(2,1)}, u32[]{:S(2)}) %copy-start.1) | copy-done | bytes 4194328
  114.5 1.6 copy-done.4
  116.1 1.6 copy-done.7
  117.6 5.2 %shard_map.120 = bf16[1536,1024]{1,0:T(8,128)(2,1)} custom-call(bf16[1024,1024]{1,0:T(8,128)(2,1)S(1)} %get-tuple-element.257.rows_ref, bf16[1024,1024]{1,0:T(8,128)(2,1)S(1)} %copy-done.7, bf16[1024,1024]{1,0:T(8,128)(2,1)S(1)} %copy-done.4, bf16[1024,2048]{1,0:T(8,128)(2,1)S(1)} %copy-done.1), custom_call_target="tpu_custom_call" | custom-call | flops 3221225472 | bytes 13631488 | tf_op jit(solution)/shard_map/pallas_call | solution.py:141
  126.2 2.1 %collective-permute-start.28 = (bf16[128,1024]{1,0:T(8,128)(2,1)}, bf16[128,1024]{1,0:T(8,128)(2,1)S(1)}, u32[]{:S(2)}, u32[]{:S(2)}) collective-permute-start(bf16[128,1024]{1,0:T(8,128)(2,1)} %add_convert_fusion.6), channel_id=1, source_target_pairs={{0,8},{1,9},{2,10},{3,11},{4,12},{5,13},{6,14},{7,15},{8,0},{9,1},... | collective-permute-start | bytes 786440 | tf_op jit(solution)/shard_map/ppermute | solution.py:115
  131.5 9.8 %collective-permute-done.28 = bf16[128,1024]{1,0:T(8,128)(2,1)S(1)} collective-permute-done((bf16[128,1024]{1,0:T(8,128)(2,1)}, bf16[128,1024]{1,0:T(8,128)(2,1)S(1)}, u32[]{:S(2)}, u32[]{:S(2)}) %collective-permute-start.28) | collective-permute-done | bytes 262176 | tf_op jit(solution)/shard_map/ppermute | solution.py:115
  142.7 1.9 %add_convert_fusion.2 = bf16[128,1024]{1,0:T(8,128)(2,1)} fusion(f32[128,1024]{1,0:T(8,128)} %convert_add_fusion, bf16[128,1024]{1,0:T(8,128)(2,1)} %collective-permute-done.29), kind=kLoop, calls=%fused_computation.3 | loop fusion | flops 393216 | bytes 1048576 | tf_op jit(solution)/shard_map/convert_element_type | solution.py:132
  144.6 1.7 %add_convert_fusion.3 = bf16[128,1024]{1,0:T(8,128)(2,1)} fusion(bf16[128,1024]{1,0:T(8,128)(2,1)} %collective-permute-done.30, bf16[128,1024]{1,0:T(8,128)(2,1)S(1)} %get-tuple-element.294), kind=kLoop, calls=%fused_computation.4 | loop fusion | flops 524288 | bytes 786432 | tf_op jit(solution)/shard_map/convert_element_type | solution.py:132
  146.3 1.7 %add_convert_fusion.4 = bf16[128,1024]{1,0:T(8,128)(2,1)} fusion(bf16[128,1024]{1,0:T(8,128)(2,1)} %collective-permute-done.31, bf16[128,1024]{1,0:T(8,128)(2,1)S(1)} %get-tuple-element.292), kind=kLoop, calls=%fused_computation.5 | loop fusion | flops 524288 | bytes 786432 | tf_op jit(solution)/shard_map/convert_element_type | solution.py:132
  154.4 2.2 %copy-done.2 = bf16[1024,2048]{1,0:T(8,128)(2,1)S(1)} copy-done((bf16[1024,2048]{1,0:T(8,128)(2,1)S(1)}, bf16[1024,2048]{1,0:T(8,128)(2,1)}, u32[]{:S(2)}) %copy-start.2) | copy-done | bytes 4194328
  156.6 1.6 copy-done.5
  158.2 1.6 copy-done.8
  159.8 6.3 %shard_map.121 = (bf16[1024,512]{1,0:T(8,128)(2,1)}, bf16[1024,512]{1,0:T(8,128)(2,1)}, bf16[512,1024]{1,0:T(8,128)(2,1)}) custom-call(bf16[1024,1024]{1,0:T(8,128)(2,1)S(1)} %get-tuple-element.257.rows_ref, bf16[1024,1024]{1,0:T(8,128)(2,1)S(1)} %copy-done.8, bf16[1024,1024]{1,0:T(8,128)(2,1)S(1)} %copy-done.5, bf16[1024,2048]{1,0:T(8,128)(2,1)S(1)} %copy-done.2, ...), custom_call_target="tpu_custom_call" | custom-call | flops 3221225472 | bytes 16777216 | tf_op jit(solution)/shard_map/pallas_call | solution.py:141
  166.1 1.5 collective-permute-done.34
  (176 shorter events, 61.0 us)
Async XLA Ops:
  0.6 21.3 %collective-permute-start.5 = (bf16[1024,512]{1,0:T(8,128)(2,1)}, bf16[1024,512]{1,0:T(8,128)(2,1)S(1)}, u32[]{:S(2)}, u32[]{:S(2)}) collective-permute-start(bf16[1024,512]{1,0:T(8,128)(2,1)} %bitcast.36), channel_id=1, source_target_pairs={{0,1},{1,0},{2,3},{3,2},{4,5},{5,4},{6,7},{7,6},{8,9},{9,8},{10,11... | collective-permute-start | bytes 3145736 | tf_op jit(solution)/shard_map/ppermute | solution.py:115
  4.5 14.3 %collective-permute-start = (bf16[128,1024]{1,0:T(8,128)(2,1)}, bf16[128,1024]{1,0:T(8,128)(2,1)S(1)}, u32[]{:S(2)}, u32[]{:S(2)}) collective-permute-start(bf16[128,1024]{1,0:T(8,128)(2,1)} %refs_0_.1), channel_id=1, source_target_pairs={{0,4},{1,5},{2,6},{3,7},{4,0},{5,1},{6,2},{7,3},{8,12},{9,13},{10,... | collective-permute-start | bytes 786440 | tf_op jit(solution)/shard_map/ppermute | solution.py:115
  4.6 14.2 %collective-permute-start.1 = (bf16[128,1024]{1,0:T(8,128)(2,1)}, bf16[128,1024]{1,0:T(8,128)(2,1)S(1)}, u32[]{:S(2)}, u32[]{:S(2)}) collective-permute-start(bf16[128,1024]{1,0:T(8,128)(2,1)} %refs_0_.1), channel_id=1, source_target_pairs={{0,8},{1,9},{2,10},{3,11},{4,12},{5,13},{6,14},{7,15},{8,0},{9,1},... | collective-permute-start | bytes 786440 | tf_op jit(solution)/shard_map/ppermute | solution.py:115
  7.6 11.2 %collective-permute-start.2 = (bf16[128,1024]{1,0:T(8,128)(2,1)}, bf16[128,1024]{1,0:T(8,128)(2,1)S(1)}, u32[]{:S(2)}, u32[]{:S(2)}) collective-permute-start(bf16[128,1024]{1,0:T(8,128)(2,1)} %refs_0_.1), channel_id=1, source_target_pairs={{0,2},{1,3},{2,0},{3,1},{4,6},{5,7},{6,4},{7,5},{8,10},{9,11},{10,... | collective-permute-start | bytes 786440 | tf_op jit(solution)/shard_map/ppermute | solution.py:115
  9.1 12.2 %collective-permute-start.3 = (bf16[128,1024]{1,0:T(8,128)(2,1)}, bf16[128,1024]{1,0:T(8,128)(2,1)S(1)}, u32[]{:S(2)}, u32[]{:S(2)}) collective-permute-start(bf16[128,1024]{1,0:T(8,128)(2,1)} %refs_0_.2), channel_id=1, source_target_pairs={{0,2},{1,3},{2,0},{3,1},{4,6},{5,7},{6,4},{7,5},{8,10},{9,11},{10,... | collective-permute-start | bytes 786440 | tf_op jit(solution)/shard_map/ppermute | solution.py:115
  22.9 20.0 %collective-permute-start.11 = (bf16[1024,512]{1,0:T(8,128)(2,1)}, bf16[1024,512]{1,0:T(8,128)(2,1)S(1)}, u32[]{:S(2)}, u32[]{:S(2)}) collective-permute-start(bf16[1024,512]{1,0:T(8,128)(2,1)} %bitcast.39), channel_id=1, source_target_pairs={{0,1},{1,0},{2,3},{3,2},{4,5},{5,4},{6,7},{7,6},{8,9},{9,8},{10,11... | collective-permute-start | bytes 3145736 | tf_op jit(solution)/shard_map/ppermute | solution.py:115
  23.3 12.0 %collective-permute-start.6 = (bf16[128,1024]{1,0:T(8,128)(2,1)S(1)}, bf16[128,1024]{1,0:T(8,128)(2,1)S(1)}, u32[]{:S(2)}, u32[]{:S(2)}) collective-permute-start(bf16[128,1024]{1,0:T(8,128)(2,1)S(1)} %collective-permute-done.1.refs_2_), channel_id=1, source_target_pairs={{0,4},{1,5},{2,6},{3,7},{4,0},{5,1},{6,2},{7,3},{8,12},{9,13},{10,... | collective-permute-start | bytes 786440 | tf_op jit(solution)/shard_map/ppermute | solution.py:115
  25.8 9.5 %collective-permute-start.8 = (bf16[128,1024]{1,0:T(8,128)(2,1)S(1)}, bf16[128,1024]{1,0:T(8,128)(2,1)S(1)}, u32[]{:S(2)}, u32[]{:S(2)}) collective-permute-start(bf16[128,1024]{1,0:T(8,128)(2,1)S(1)} %collective-permute-done.1.refs_2_), channel_id=1, source_target_pairs={{0,2},{1,3},{2,0},{3,1},{4,6},{5,7},{6,4},{7,5},{8,10},{9,11},{10,... | collective-permute-start | bytes 786440 | tf_op jit(solution)/shard_map/ppermute | solution.py:115
  27.3 12.3 %collective-permute-start.7 = (bf16[128,1024]{1,0:T(8,128)(2,1)S(1)}, bf16[128,1024]{1,0:T(8,128)(2,1)S(1)}, u32[]{:S(2)}, u32[]{:S(2)}) collective-permute-start(bf16[128,1024]{1,0:T(8,128)(2,1)S(1)} %collective-permute-done.refs_1_), channel_id=1, source_target_pairs={{0,2},{1,3},{2,0},{3,1},{4,6},{5,7},{6,4},{7,5},{8,10},{9,11},{10,... | collective-permute-start | bytes 786440 | tf_op jit(solution)/shard_map/ppermute | solution.py:115
  28.6 14.4 %collective-permute-start.9 = (bf16[128,1024]{1,0:T(8,128)(2,1)}, bf16[128,1024]{1,0:T(8,128)(2,1)S(1)}, u32[]{:S(2)}, u32[]{:S(2)}) collective-permute-start(bf16[128,1024]{1,0:T(8,128)(2,1)} %refs_0_.2), channel_id=1, source_target_pairs={{0,8},{1,9},{2,10},{3,11},{4,12},{5,13},{6,14},{7,15},{8,0},{9,1},... | collective-permute-start | bytes 786440 | tf_op jit(solution)/shard_map/ppermute | solution.py:115
  43.9 16.4 %collective-permute-start.17 = (bf16[512,1024]{1,0:T(8,128)(2,1)}, bf16[512,1024]{1,0:T(8,128)(2,1)S(1)}, u32[]{:S(2)}, u32[]{:S(2)}) collective-permute-start(bf16[512,1024]{1,0:T(8,128)(2,1)} %bitcast.42), channel_id=1, source_target_pairs={{0,1},{1,0},{2,3},{3,2},{4,5},{5,4},{6,7},{7,6},{8,9},{9,8},{10,11... | collective-permute-start | bytes 3145736 | tf_op jit(solution)/shard_map/ppermute | solution.py:115
  45.5 9.2 %collective-permute-start.14 = (bf16[128,1024]{1,0:T(8,128)(2,1)S(1)}, bf16[128,1024]{1,0:T(8,128)(2,1)}, u32[]{:S(2)}, u32[]{:S(2)}) collective-permute-start(bf16[128,1024]{1,0:T(8,128)(2,1)S(1)} %collective-permute-done.9.refs_2_), channel_id=1, source_target_pairs={{0,4},{1,5},{2,6},{3,7},{4,0},{5,1},{6,2},{7,3},{8,12},{9,13},{10,... | collective-permute-start | bytes 786440 | tf_op jit(solution)/shard_map/ppermute | solution.py:115
  46.7 12.8 %collective-permute-start.12 = (bf16[128,1024]{1,0:T(8,128)(2,1)S(1)}, bf16[128,1024]{1,0:T(8,128)(2,1)S(1)}, u32[]{:S(2)}, u32[]{:S(2)}) collective-permute-start(bf16[128,1024]{1,0:T(8,128)(2,1)S(1)} %collective-permute-done.6.refs_3_), channel_id=1, source_target_pairs={{0,2},{1,3},{2,0},{3,1},{4,6},{5,7},{6,4},{7,5},{8,10},{9,11},{10,... | collective-permute-start | bytes 786440 | tf_op jit(solution)/shard_map/ppermute | solution.py:115
  48.9 11.3 %collective-permute-start.13 = (bf16[128,1024]{1,0:T(8,128)(2,1)}, bf16[128,1024]{1,0:T(8,128)(2,1)}, u32[]{:S(2)}, u32[]{:S(2)}) collective-permute-start(bf16[128,1024]{1,0:T(8,128)(2,1)} %refs_0_.2), channel_id=1, source_target_pairs={{0,4},{1,5},{2,6},{3,7},{4,0},{5,1},{6,2},{7,3},{8,12},{9,13},{10,... | collective-permute-start | bytes 786440 | tf_op jit(solution)/shard_map/ppermute | solution.py:115
  62.0 24.7 %collective-permute-start.18 = (bf16[128,1024]{1,0:T(8,128)(2,1)}, bf16[128,1024]{1,0:T(8,128)(2,1)S(1)}, u32[]{:S(2)}, u32[]{:S(2)}) collective-permute-start(bf16[128,1024]{1,0:T(8,128)(2,1)} %collective-permute-done.13.refs_1_), channel_id=1, source_target_pairs={{0,2},{1,3},{2,0},{3,1},{4,6},{5,7},{6,4},{7,5},{8,10},{9,11},{10,... | collective-permute-start | bytes 786440 | tf_op jit(solution)/shard_map/ppermute | solution.py:115
  63.0 23.7 %collective-permute-start.19 = (bf16[128,1024]{1,0:T(8,128)(2,1)}, bf16[128,1024]{1,0:T(8,128)(2,1)S(1)}, u32[]{:S(2)}, u32[]{:S(2)}) collective-permute-start(bf16[128,1024]{1,0:T(8,128)(2,1)} %collective-permute-done.14.refs_3_), channel_id=1, source_target_pairs={{0,2},{1,3},{2,0},{3,1},{4,6},{5,7},{6,4},{7,5},{8,10},{9,11},{10,... | collective-permute-start | bytes 786440 | tf_op jit(solution)/shard_map/ppermute | solution.py:115
  86.7 18.4 %collective-permute-start.20 = (bf16[128,1024]{1,0:T(8,128)(2,1)S(1)}, bf16[128,1024]{1,0:T(8,128)(2,1)S(1)}, u32[]{:S(2)}, u32[]{:S(2)}) collective-permute-start(bf16[128,1024]{1,0:T(8,128)(2,1)S(1)} %get-tuple-element.213), channel_id=1, source_target_pairs={{0,2},{1,3},{2,0},{3,1},{4,6},{5,7},{6,4},{7,5},{8,10},{9,11},{10,... | collective-permute-start | bytes 786440 | tf_op jit(solution)/shard_map/ppermute | solution.py:115
  87.7 17.4 %collective-permute-start.21 = (bf16[128,1024]{1,0:T(8,128)(2,1)S(1)}, bf16[128,1024]{1,0:T(8,128)(2,1)S(1)}, u32[]{:S(2)}, u32[]{:S(2)}) collective-permute-start(bf16[128,1024]{1,0:T(8,128)(2,1)S(1)} %get-tuple-element.212), channel_id=1, source_target_pairs={{0,2},{1,3},{2,0},{3,1},{4,6},{5,7},{6,4},{7,5},{8,10},{9,11},{10,... | collective-permute-start | bytes 786440 | tf_op jit(solution)/shard_map/ppermute | solution.py:115
  107.9 14.9 %collective-permute-start.23 = (bf16[128,1024]{1,0:T(8,128)(2,1)S(1)}, bf16[128,1024]{1,0:T(8,128)(2,1)S(1)}, u32[]{:S(2)}, u32[]{:S(2)}) collective-permute-start(bf16[128,1024]{1,0:T(8,128)(2,1)S(1)} %get-tuple-element.261), channel_id=1, source_target_pairs={{0,4},{1,5},{2,6},{3,7},{4,0},{5,1},{6,2},{7,3},{8,12},{9,13},{10,... | collective-permute-start | bytes 786440 | tf_op jit(solution)/shard_map/ppermute | solution.py:115
  109.7 13.1 %collective-permute-start.24 = (bf16[128,1024]{1,0:T(8,128)(2,1)}, bf16[128,1024]{1,0:T(8,128)(2,1)S(1)}, u32[]{:S(2)}, u32[]{:S(2)}) collective-permute-start(bf16[128,1024]{1,0:T(8,128)(2,1)} %copy-done.45), channel_id=1, source_target_pairs={{0,2},{1,3},{2,0},{3,1},{4,6},{5,7},{6,4},{7,5},{8,10},{9,11},{10,... | collective-permute-start | bytes 786440 | tf_op jit(solution)/shard_map/ppermute | solution.py:115
  110.2 12.6 %collective-permute-start.25 = (bf16[128,1024]{1,0:T(8,128)(2,1)}, bf16[128,1024]{1,0:T(8,128)(2,1)S(1)}, u32[]{:S(2)}, u32[]{:S(2)}) collective-permute-start(bf16[128,1024]{1,0:T(8,128)(2,1)} %copy-done.42), channel_id=1, source_target_pairs={{0,2},{1,3},{2,0},{3,1},{4,6},{5,7},{6,4},{7,5},{8,10},{9,11},{10,... | collective-permute-start | bytes 786440 | tf_op jit(solution)/shard_map/ppermute | solution.py:115
  111.7 11.1 %collective-permute-start.22 = (f32[4,1,2,128]{3,0,2,1:T(4,128)S(1)}, f32[4,1,2,128]{3,0,2,1:T(4,128)S(1)}, u32[]{:S(2)}, u32[]{:S(2)}) collective-permute-start(f32[4,1,2,128]{3,0,2,1:T(4,128)S(1)} %get-tuple-element.333), channel_id=1, source_target_pairs={{0,2},{1,3},{2,0},{3,1},{4,6},{5,7},{6,4},{7,5},{8,10},{9,11},{10,... | collective-permute-start | bytes 12296 | tf_op jit(solution)/shard_map/ppermute | solution.py:115
  125.2 17.5 %collective-permute-start.27 = (bf16[1536,1024]{1,0:T(8,128)(2,1)}, bf16[1536,1024]{1,0:T(8,128)(2,1)}, u32[]{:S(2)}, u32[]{:S(2)}) collective-permute-start(bf16[1536,1024]{1,0:T(8,128)(2,1)} %shard_map.120), channel_id=1, source_target_pairs={{0,1},{1,0},{2,3},{3,2},{4,5},{5,4},{6,7},{7,6},{8,9},{9,8},{10,11... | collective-permute-start | bytes 9437192 | tf_op jit(solution)/shard_map/ppermute | solution.py:115
  126.2 15.2 %collective-permute-start.28 = (bf16[128,1024]{1,0:T(8,128)(2,1)}, bf16[128,1024]{1,0:T(8,128)(2,1)S(1)}, u32[]{:S(2)}, u32[]{:S(2)}) collective-permute-start(bf16[128,1024]{1,0:T(8,128)(2,1)} %add_convert_fusion.6), channel_id=1, source_target_pairs={{0,8},{1,9},{2,10},{3,11},{4,12},{5,13},{6,14},{7,15},{8,0},{9,1},... | collective-permute-start | bytes 786440 | tf_op jit(solution)/shard_map/ppermute | solution.py:115
  128.2 13.1 %collective-permute-start.29 = (bf16[128,1024]{1,0:T(8,128)(2,1)}, bf16[128,1024]{1,0:T(8,128)(2,1)}, u32[]{:S(2)}, u32[]{:S(2)}) collective-permute-start(bf16[128,1024]{1,0:T(8,128)(2,1)} %add_convert_fusion.5), channel_id=1, source_target_pairs={{0,4},{1,5},{2,6},{3,7},{4,0},{5,1},{6,2},{7,3},{8,12},{9,13},{10,... | collective-permute-start | bytes 786440 | tf_op jit(solution)/shard_map/ppermute | solution.py:115
  129.0 12.4 %collective-permute-start.30 = (bf16[128,1024]{1,0:T(8,128)(2,1)}, bf16[128,1024]{1,0:T(8,128)(2,1)}, u32[]{:S(2)}, u32[]{:S(2)}) collective-permute-start(bf16[128,1024]{1,0:T(8,128)(2,1)} %get-tuple-element.286), channel_id=1, source_target_pairs={{0,2},{1,3},{2,0},{3,1},{4,6},{5,7},{6,4},{7,5},{8,10},{9,11},{10,... | collective-permute-start | bytes 786440 | tf_op jit(solution)/shard_map/ppermute | solution.py:115
  130.0 12.7 %collective-permute-start.31 = (bf16[128,1024]{1,0:T(8,128)(2,1)}, bf16[128,1024]{1,0:T(8,128)(2,1)}, u32[]{:S(2)}, u32[]{:S(2)}) collective-permute-start(bf16[128,1024]{1,0:T(8,128)(2,1)} %get-tuple-element.282), channel_id=1, source_target_pairs={{0,2},{1,3},{2,0},{3,1},{4,6},{5,7},{6,4},{7,5},{8,10},{9,11},{10,... | collective-permute-start | bytes 786440 | tf_op jit(solution)/shard_map/ppermute | solution.py:115
  149.5 16.6 %collective-permute-start.33 = (bf16[128,1024]{1,0:T(8,128)(2,1)}, bf16[128,1024]{1,0:T(8,128)(2,1)S(1)}, u32[]{:S(2)}, u32[]{:S(2)}) collective-permute-start(bf16[128,1024]{1,0:T(8,128)(2,1)} %add_convert_fusion.4), channel_id=1, source_target_pairs={{0,4},{1,5},{2,6},{3,7},{4,0},{5,1},{6,2},{7,3},{8,12},{9,13},{10,... | collective-permute-start | bytes 786440 | tf_op jit(solution)/shard_map/ppermute | solution.py:115
  150.2 17.4 %collective-permute-start.34 = (bf16[128,1024]{1,0:T(8,128)(2,1)}, bf16[128,1024]{1,0:T(8,128)(2,1)S(1)}, u32[]{:S(2)}, u32[]{:S(2)}) collective-permute-start(bf16[128,1024]{1,0:T(8,128)(2,1)} %add_convert_fusion.3), channel_id=1, source_target_pairs={{0,4},{1,5},{2,6},{3,7},{4,0},{5,1},{6,2},{7,3},{8,12},{9,13},{10,... | collective-permute-start | bytes 786440 | tf_op jit(solution)/shard_map/ppermute | solution.py:115
  151.5 16.1 %collective-permute-start.35 = (bf16[128,1024]{1,0:T(8,128)(2,1)}, bf16[128,1024]{1,0:T(8,128)(2,1)S(1)}, u32[]{:S(2)}, u32[]{:S(2)}) collective-permute-start(bf16[128,1024]{1,0:T(8,128)(2,1)} %add_convert_fusion.2), channel_id=1, source_target_pairs={{0,8},{1,9},{2,10},{3,11},{4,12},{5,13},{6,14},{7,15},{8,0},{9,1},... | collective-permute-start | bytes 786440 | tf_op jit(solution)/shard_map/ppermute | solution.py:115
  152.4 15.3 %collective-permute-start.36 = (bf16[128,1024]{1,0:T(8,128)(2,1)}, bf16[128,1024]{1,0:T(8,128)(2,1)S(1)}, u32[]{:S(2)}, u32[]{:S(2)}) collective-permute-start(bf16[128,1024]{1,0:T(8,128)(2,1)} %copy-done.28), channel_id=1, source_target_pairs={{0,2},{1,3},{2,0},{3,1},{4,6},{5,7},{6,4},{7,5},{8,10},{9,11},{10,... | collective-permute-start | bytes 786440 | tf_op jit(solution)/shard_map/ppermute | solution.py:115
  153.4 14.2 %collective-permute-start.37 = (bf16[128,1024]{1,0:T(8,128)(2,1)}, bf16[128,1024]{1,0:T(8,128)(2,1)S(1)}, u32[]{:S(2)}, u32[]{:S(2)}) collective-permute-start(bf16[128,1024]{1,0:T(8,128)(2,1)} %copy-done.29), channel_id=1, source_target_pairs={{0,2},{1,3},{2,0},{3,1},{4,6},{5,7},{6,4},{7,5},{8,10},{9,11},{10,... | collective-permute-start | bytes 786440 | tf_op jit(solution)/shard_map/ppermute | solution.py:115
  (55 other events, 202.9 us)

commit v5 on v4

--- a/solution.py
+++ b/solution.py
@@ -135,15 +135,34 @@
 MIB = 1 << 20
 
 
-def kernel(body, outs, flops, *operands):
-    whole = pl.BlockSpec(memory_space=pltpu.VMEM)
+class Fetch:
+    def __init__(self, sems):
+        self.sems, self.waiting = sems, {}
+
+    def start(self, name, source, target):
+        copy = pltpu.make_async_copy(source, target, self.sems.at[len(self.waiting)])
+        copy.start()
+        self.waiting[name] = [copy, False]
+
+    def wait(self, *names):
+        for name in names:
+            if not self.waiting[name][1]:
+                self.waiting[name][0].wait()
+                self.waiting[name][1] = True
+
+    def wait_all(self):
+        self.wait(*self.waiting)
+
+
+def kernel(body, outs, scratch, copies, flops, *operands):
     moved = sum(v.size * v.dtype.itemsize for v in (*operands, *outs))
     return pl.pallas_call(
         body,
         out_shape=outs,
-        in_specs=[whole] * len(operands),
-        out_specs=[whole] * len(outs),
-        compiler_params=pltpu.CompilerParams(vmem_limit_bytes=24 * MIB),
+        in_specs=[pl.BlockSpec(memory_space=pl.ANY)] * len(operands),
+        out_specs=[pl.BlockSpec(memory_space=pl.ANY)] * len(outs),
+        scratch_shapes=[*scratch, pltpu.SemaphoreType.DMA((copies,))],
+        compiler_params=pltpu.CompilerParams(vmem_limit_bytes=56 * MIB),
         cost_estimate=pl.CostEstimate(flops=flops, bytes_accessed=moved, transcendentals=0),
     )(*operands)
 
@@ -159,39 +178,59 @@
     every = count * tok_count
 
     def body(*refs):
-        x_refs, refs = refs[:count], refs[count:]
-        w_refs, share_ref, refs = (refs[0:3], refs[3:6]), refs[6], refs[7:]
-        y_refs, (rows_ref, gate_ref, up_ref, weighted_ref) = refs[:count], refs[count:]
-        for i, x_ref in enumerate(x_refs):
-            rows_ref[i * tok_count : (i + 1) * tok_count, :] = x_ref[...]
+        x_refs, w_refs, share_ref, refs = refs[:count], refs[count : count + 6], refs[count + 6], refs[count + 7 :]
+        y_refs, saved_refs, refs = refs[:count], refs[count : count + 3], refs[count + 3 :]
+        w_bufs, (rows, share_buf, gate_buf, up_buf, weighted_buf, y_buf, sems) = refs[:6], refs[6:]
+        fetch = Fetch(sems)
+        order = (*range(half, count), *range(half))
+        for i in order[:half]:
+            fetch.start(("x", i), x_refs[i], rows.at[i * tok_count : (i + 1) * tok_count])
+        for i in range(6):
+            fetch.start(("w", i), w_refs[i], w_bufs[i])
+            if i == 0:
+                fetch.start("share", share_ref, share_buf)
+        for i in order[half:]:
+            fetch.start(("x", i), x_refs[i], rows.at[i * tok_count : (i + 1) * tok_count])
         for start in (half, 0):
             at = slice(start * tok_count, (start + half) * tok_count)
-            x, total = rows_ref[at, :], 0.0
-            for e, (gate_w, up_w, down_w) in enumerate(w_refs):
+            fetch.wait(*[("x", start + j) for j in range(half)])
+            x, total = rows[at, :], 0.0
+            for e in range(2):
                 lanes = slice(e * units, (e + 1) * units)
-                gate_pre = dot(x, gate_w[...], ((1,), (0,)))
-                up_pre = dot(x, up_w[...], ((1,), (0,)))
-                gate_ref[at, lanes] = gate_pre
-                up_ref[at, lanes] = up_pre
+                fetch.wait(("w", 3 * e))
+                gate_pre = dot(x, w_bufs[3 * e][...], ((1,), (0,)))
+                gate_buf[at, lanes] = gate_pre
+                fetch.wait(("w", 3 * e + 1))
+                up_pre = dot(x, w_bufs[3 * e + 1][...], ((1,), (0,)))
+                up_buf[at, lanes] = up_pre
                 hidden = gate_pre * jax.nn.sigmoid(gate_pre) * up_pre
+                fetch.wait("share")
                 part = []
                 for j in range(half):
                     column = e * count + start + j
-                    part.append(share_ref[:, column : column + 1])
+                    part.append(share_buf[:, column : column + 1])
                 weighted = (jnp.concatenate(part, axis=0) * hidden).astype(bf16)
-                weighted_ref[at, lanes] = weighted
-                total = total + dot(weighted, down_w[...], ((1,), (0,)))
-            for j in range(half):
-                y_refs[start + j][...] = total[j * tok_count : (j + 1) * tok_count].astype(bf16)
-
-    outs = [shape(tok_count, width, bf16)] * count + [
-        shape(every, width, bf16),
-        shape(every, 2 * units, f32),
-        shape(every, 2 * units, f32),
-        shape(every, 2 * units, bf16),
+                weighted_buf[at, lanes] = weighted
+                fetch.wait(("w", 3 * e + 2))
+                total = total + dot(weighted, w_bufs[3 * e + 2][...], ((1,), (0,)))
+            y_buf[at, :] = total.astype(bf16)
+            for j in range(start, start + half):
+                block = y_buf.at[j * tok_count : (j + 1) * tok_count]
+                fetch.start(("y", j), block, y_refs[j])
+            for name, buf, ref in zip("gus", (gate_buf, up_buf, weighted_buf), saved_refs):
+                fetch.start((name, start), buf.at[at], ref.at[at])
+        fetch.wait_all()
+
+    saved = [
+        shape(every, 2 * units, f32), shape(every, 2 * units, f32), shape(every, 2 * units, bf16)
     ]
+    outs = [shape(tok_count, width, bf16)] * count + saved
+    scratch = [pltpu.VMEM(w.shape, bf16) for w in (*weights[0], *weights[1])]
+    scratch += [pltpu.VMEM((every, width), bf16), pltpu.VMEM(share.shape, f32)]
+    scratch += [pltpu.VMEM(v.shape, v.dtype) for v in saved] + [pltpu.VMEM((every, width), bf16)]
     flops = 12 * every * width * units
-    outs = kernel(body, outs, flops, *blocks, *weights[0], *weights[1], share)
+    copies = 2 * count + 7 + 6
+    outs = kernel(body, outs, scratch, copies, flops, *blocks, *weights[0], *weights[1], share)
     return outs[:count], *outs[count:]
 
 
@@ -202,76 +241,140 @@
     every = count * tok_count
 
     def body(*refs):
-        c_refs, refs = refs[:count], refs[count:]
-        w_refs, (share_ref, gate_ref, up_ref), refs = (refs[0:3], refs[3:6]), refs[6:9], refs[9:]
-        g_refs, (cot_ref, inner_ref, factor_ref) = refs[:count], refs[count:]
-        for i, c_ref in enumerate(c_refs):
-            cot_ref[i * tok_count : (i + 1) * tok_count, :] = c_ref[...]
+        c_refs, w_refs, refs = refs[:count], refs[count : count + 6], refs[count + 6 :]
+        (share_ref, gate_ref, up_ref), refs = refs[:3], refs[3:]
+        g_refs, inner_ref, factor_ref, refs = refs[:count], refs[count], refs[count + 1], refs[count + 2 :]
+        w_bufs, refs = refs[:6], refs[6:]
+        rows, share_buf, gate_buf, up_buf, g_buf, inner_buf, factor_buf, sems = refs
+        fetch = Fetch(sems)
+
+        def fetch_half(start):
+            at = slice(start * tok_count, (start + half) * tok_count)
+            for i in range(start, start + half):
+                fetch.start(("c", i), c_refs[i], rows.at[i * tok_count : (i + 1) * tok_count])
+            if start:
+                fetch.start(("w", 2), w_refs[2], w_bufs[2])
+            fetch.start(("g", start), gate_ref.at[at], gate_buf.at[at])
+            fetch.start(("u", start), up_ref.at[at], up_buf.at[at])
+
+        fetch_half(half)
+        fetch.start("share", share_ref, share_buf)
+        for i in (0, 1, 5, 3, 4):
+            fetch.start(("w", i), w_refs[i], w_bufs[i])
+        fetch_half(0)
         for start in (half, 0):
             at = slice(start * tok_count, (start + half) * tok_count)
-            cot, total = cot_ref[at, :], 0.0
-            for e, (gate_w, up_w, down_w) in enumerate(w_refs):
+            fetch.wait(*[("c", start + j) for j in range(half)])
+            cot, total = rows[at, :], 0.0
+            for e in range(2):
                 lanes = slice(e * units, (e + 1) * units)
-                plain = dot(cot, down_w[...], ((1,), (1,)))
-                gate, up = gate_ref[at, lanes], up_ref[at, lanes]
+                fetch.wait(("w", 3 * e + 2))
+                plain = dot(cot, w_bufs[3 * e + 2][...], ((1,), (1,)))
+                fetch.wait(("g", start), ("u", start), "share")
+                gate, up = gate_buf[at, lanes], up_buf[at, lanes]
                 sigma = jax.nn.sigmoid(gate)
                 silu_val = gate * sigma
                 inner = jnp.sum(silu_val * up * plain, axis=1, keepdims=True)
                 part = []
                 for j in range(half):
                     column = e * count + start + j
-                    part.append(share_ref[:, column : column + 1])
-                    inner_ref[:, column : column + 1] = inner[j * tok_count : (j + 1) * tok_count]
+                    part.append(share_buf[:, column : column + 1])
+                    inner_buf[:, column : column + 1] = inner[j * tok_count : (j + 1) * tok_count]
                 grad_hidden = jnp.concatenate(part, axis=0) * plain
                 slope = sigma * (1.0 + gate * (1.0 - sigma))
                 grad_gate = (grad_hidden * up * slope).astype(bf16)
                 grad_up = (grad_hidden * silu_val).astype(bf16)
-                factor_ref[at, 2 * e * units : (2 * e + 1) * units] = grad_gate
-                factor_ref[at, (2 * e + 1) * units : (2 * e + 2) * units] = grad_up
-                total = total + dot(grad_gate, gate_w[...], ((1,), (1,)))
-                total = total + dot(grad_up, up_w[...], ((1,), (1,)))
-            for j in range(half):
-                g_refs[start + j][...] = total[j * tok_count : (j + 1) * tok_count].astype(bf16)
-
-    outs = [shape(tok_count, width, bf16)] * count + [
-        shape(every, width, bf16),
-        shape(tok_count, 2 * count, f32),
-        shape(every, 4 * units, bf16),
-    ]
+                factor_buf[at, 2 * e * units : (2 * e + 1) * units] = grad_gate
+                factor_buf[at, (2 * e + 1) * units : (2 * e + 2) * units] = grad_up
+                fetch.wait(("w", 3 * e), ("w", 3 * e + 1))
+                total = total + dot(grad_gate, w_bufs[3 * e][...], ((1,), (1,)))
+                total = total + dot(grad_up, w_bufs[3 * e + 1][...], ((1,), (1,)))
+            g_buf[at, :] = total.astype(bf16)
+            for j in range(start, start + half):
+                block = g_buf.at[j * tok_count : (j + 1) * tok_count]
+                fetch.start(("grad", j), block, g_refs[j])
+            fetch.start(("factor", start), factor_buf.at[at], factor_ref.at[at])
+        fetch.start("inner", inner_buf, inner_ref)
+        fetch.wait_all()
+
+    small = shape(tok_count, 2 * count, f32)
+    factors = shape(every, 4 * units, bf16)
+    outs = [shape(tok_count, width, bf16)] * count + [small, factors]
+    scratch = [pltpu.VMEM(w.shape, bf16) for w in (*weights[0], *weights[1])]
+    scratch += [pltpu.VMEM((every, width), bf16), pltpu.VMEM(share.shape, f32)]
+    scratch += [pltpu.VMEM(gate_pre.shape, f32)] * 2 + [pltpu.VMEM((every, width), bf16)]
+    scratch += [pltpu.VMEM(small.shape, f32), pltpu.VMEM(factors.shape, bf16)]
     flops = 12 * every * width * units
-    outs = kernel(body, outs, flops, *blocks, *weights[0], *weights[1], share, gate_pre, up_pre)
+    copies = 2 * count + 6 + 1 + 4 + 3
+    operands = (*blocks, *weights[0], *weights[1], share, gate_pre, up_pre)
+    outs = kernel(body, outs, scratch, copies, flops, *operands)
     return outs[:count], *outs[count:]
 
 
 def weight_grads(expert, rows, cot, weighted, factors, away=None):
     bf16 = jnp.bfloat16
-    (every, width), units = rows.shape, weighted.shape[1] // 2
-
-    def body(rows_ref, cot_ref, weighted_ref, factor_ref, *refs):
+    count, (tok_count, width) = len(rows), rows[0].shape
+    every, units = count * tok_count, weighted.shape[1] // 2
+    extra = 0 if away is None else 1
+
+    def body(*refs):
+        x_refs, c_refs, refs = refs[:count], refs[count : 2 * count], refs[2 * count :]
+        weighted_ref, factor_ref, refs = refs[0], refs[1], refs[2:]
+        away_refs, out_refs, refs = refs[:extra], refs[extra : 3 * extra + 1], refs[3 * extra + 1 :]
+        x_buf, c_buf, weighted_buf, factor_buf, *bufs, sems = refs
+        away_bufs, out_bufs = bufs[:extra], bufs[extra:]
+        fetch = Fetch(sems)
+        for i in range(count):
+            fetch.start(("x", i), x_refs[i], x_buf.at[i * tok_count : (i + 1) * tok_count])
+        lanes = pl.ds(2 * expert * units, 2 * units)
+        fetch.start("factor", factor_ref.at[:, lanes], factor_buf)
+        if extra:
+            fetch.start("away", away_refs[0], away_bufs[0])
+        lanes = pl.ds(expert * units, units)
+        fetch.start("weighted", weighted_ref.at[:, lanes], weighted_buf)
+        for i in range(count):
+            fetch.start(("c", i), c_refs[i], c_buf.at[i * tok_count : (i + 1) * tok_count])
+        fetch.wait(*[("x", i) for i in range(count)], "factor")
         for number in range(3):
             if number < 2:
-                left, right, lead = rows_ref, factor_ref, 0
-                lanes = slice((2 * expert + number) * units, (2 * expert + number + 1) * units)
+                left, right = x_buf, factor_buf[:, number * units : (number + 1) * units]
                 columns, into = slice(number * units, (number + 1) * units), slice(0, width)
             else:
-                left, right, lead = weighted_ref, cot_ref, expert * units
-                lanes, columns, into = slice(0, width), slice(0, width), slice(width, width + units)
+                fetch.wait("weighted", *[("c", i) for i in range(count)])
+                left, right = weighted_buf, c_buf[...]
+                columns, into = slice(0, width), slice(width, width + units)
             for start in range(0, into.stop - into.start, units):
-                part = left[:, lead + start : lead + start + units]
-                value = dot(part, right[:, lanes], ((0,), (0,)))
+                value = dot(left[:, start : start + units], right, ((0,), (0,)))
                 at = slice(into.start + start, into.start + start + units)
-                if away is None:
-                    refs[0][at, columns] = value.astype(bf16)
+                if not extra:
+                    out_bufs[0][at, columns] = value.astype(bf16)
                 else:
-                    value = value + refs[0][at, columns].astype(jnp.float32)
-                    refs[1 + number][start : start + units, :] = value.astype(bf16)
+                    fetch.wait("away")
+                    value = value + away_bufs[0][at, columns].astype(jnp.float32)
+                    out_bufs[number][start : start + units, :] = value.astype(bf16)
+                    block = out_bufs[number].at[start : start + units]
+                    target = out_refs[number].at[start : start + units]
+                    fetch.start(("out", number, start), block, target)
+            if not extra and number:
+                at = pl.ds(into.start, into.stop - into.start)
+                fetch.start(("out", number), out_bufs[0].at[at], out_refs[0].at[at])
+        fetch.wait_all()
 
     flops = 6 * every * width * units
-    operands = (rows, cot, weighted, factors)
+    operands = (*rows, *cot, weighted, factors)
+    scratch = [pltpu.VMEM((every, width), bf16)] * 2
+    scratch += [pltpu.VMEM((every, units), bf16), pltpu.VMEM((every, 2 * units), bf16)]
+    packed = shape(width + units, width, bf16)
     if away is None:
-        return kernel(body, [shape(width + units, width, bf16)], flops, *operands)[0]
-    outs = [shape(width, units, bf16)] * 2 + [shape(units, width, bf16)]
-    return kernel(body, outs, flops, *operands, away)
+        outs = [packed]
+        scratch += [pltpu.VMEM(packed.shape, bf16)]
+    else:
+        operands += (away,)
+        outs = [shape(width, units, bf16)] * 2 + [shape(units, width, bf16)]
+        scratch += [pltpu.VMEM(v.shape, bf16) for v in (packed, *outs)]
+    copies = 2 * count + 3 + 2 * -(-width // units) + 1
+    outs = kernel(body, outs, scratch, copies, flops, *operands)
+    return outs if extra else outs[0]
 
 
 def doubled(value, arrived):
@@ -290,53 +393,63 @@
     x0, c0 = latent_in, cotangent
 
     x2, x1, x4, c4 = swap(x0, FAR), swap(x0, NEAR), swap(x0, SIDE), swap(c0, SIDE)
-    arrived, gate_w = swap(share, NEAR), swap(own[0], CORE)
-    x1, x2, x4, c0, c4, arrived, gate_w, own = fence(x1, x2, x4, c0, c4, arrived, gate_w, own)
+    gate_w = swap(own[0], CORE)
+    x1, x2, c0, share, up_w = fence(x1, x2, c0, share, own[1])
+
+    x3, x5, x6, c2 = swap(x2, NEAR), swap(x1, SIDE), swap(x2, SIDE), swap(c0, FAR)
+    arrived, up_w = swap(share, NEAR), swap(up_w, CORE)
+    x3, x4, c4, c0, arrived, down_w = fence(x3, x4, c4, c0, arrived, own[2])
+
     share = doubled(share, arrived)
-    x3, x5, x6, c2 = swap(x2, NEAR), swap(x1, SIDE), swap(x2, SIDE), swap(c0, FAR)
-    arrived, up_w = swap(share, FAR), swap(own[1], CORE)
-    x3, x5, x6, c0, c2, arrived, up_w, own = fence(x3, x5, x6, c0, c2, arrived, up_w, own)
+    x7, c1 = swap(x3, SIDE), swap(c0, NEAR)
+    arrived, down_w = swap(share, FAR), swap(down_w, CORE)
+    c2, x5, x6, arrived = fence(c2, x5, x6, arrived)
+
     share = doubled(share, arrived)
-    x7, c1, c3, c6 = swap(x3, SIDE), swap(c0, NEAR), swap(c2, NEAR), swap(c2, SIDE)
-    arrived, down_w = swap(share, SIDE), swap(own[2], CORE)
-    x7, c1, c3, c6, arrived, down_w, own = fence(x7, c1, c3, c6, arrived, down_w, own)
+    c6, c3, arrived = swap(c2, SIDE), swap(c2, NEAR), swap(share, SIDE)
+    x7, c1, arrived, gate_w, up_w, down_w = fence(x7, c1, arrived, gate_w, up_w, down_w)
+
     weights = (own, (gate_w, up_w, down_w))
     share = doubled(share, arrived)[:, mine, :]
     share = share.transpose(2, 1, 0).reshape(share.shape[2], -1)
-    share, c1, c3 = fence(share, c1, c3)
-    c5, c7 = swap(c1, SIDE), swap(c3, SIDE)
-    y, rows, gate_pre, up_pre, weighted = forward(
-        [x0, x1, x2, x3, x4, x5, x6, x7], weights, share
-    )
-    y, rows, c5, c7 = fence(y, rows, c5, c7)
-    y7, y6 = swap(y[7], SIDE), swap(y[6], SIDE)
-    g, cot, inner, factors = backward(
-        [c0, c1, c2, c3, c4, c5, c6, c7], weights, share, gate_pre, up_pre
-    )
-    y, g, cot, factors, inner, y7, y6 = fence(y, g, cot, factors, inner, y7, y6)
+    share, c1 = fence(share, c1)
+    c5 = swap(c1, SIDE)
+    rows = [x0, x1, x2, x3, x4, x5, x6, x7]
+    y, gate_pre, up_pre, weighted = forward(rows, weights, share)
+    y, c3 = fence(y, c3)
+
+    c7, y7, y6 = swap(c3, SIDE), swap(y[7], SIDE), swap(y[6], SIDE)
+    c5, c6, c7 = fence(c5, c6, c7)
+
+    cot = [c0, c1, c2, c3, c4, c5, c6, c7]
+    g, inner, factors = backward(cot, weights, share, gate_pre, up_pre)
+    y, g, factors, inner, y7, y6 = fence(y, g, factors, inner, y7, y6)
+
     y3, y2 = narrow(added(y[3], y7)), added(y[2], y6)
     inner = inner.T.reshape(2, len(REACH), 1, -1).transpose(1, 2, 0, 3)
-    y3, y2, inner, g = fence(y3, y2, inner, g)
-    y3, g7, g6, arrived = swap(y3, NEAR), swap(g[7], SIDE), swap(g[6], SIDE), swap(inner[4:], SIDE)
+    y3, y2, inner, g, y = fence(y3, y2, inner, g, y)
+    y3, g7, g6, y5 = swap(y3, NEAR), swap(g[7], SIDE), swap(g[6], SIDE), swap(y[5], SIDE)
+    arrived = swap(inner[4:], SIDE)
     away = weight_grads(1, rows, cot, weighted, factors)
-    y, g, arrived, away, y3, y2, g7, g6 = fence(y, g, arrived, away, y3, y2, g7, g6)
+    y, g, arrived, away, y3, g7, g6 = fence(y, g, arrived, away, y3, g7, g6)
+
     g3, g2 = narrow(added(g[3], g7)), added(g[2], g6)
     y2 = narrow(added(y2, y3))
     inner = jnp.concatenate([inner[:4], arrived], axis=1)
     y2, g3, g2, inner, g, y, away = fence(y2, g3, g2, inner, g, y, away)
-    y2, g3, g5, y5 = swap(y2, FAR), swap(g3, NEAR), swap(g[5], SIDE), swap(y[5], SIDE)
+    g3, y2, g5, y4 = swap(g3, NEAR), swap(y2, FAR), swap(g[5], SIDE), swap(y[4], SIDE)
     arrived, away = swap(inner[2:], FAR), swap(away, CORE)
-    y, g, arrived, away, y2, g3, g2, g5, y5 = fence(y, g, arrived, away, y2, g3, g2, g5, y5)
-    y1, g1 = narrow(added(y[1], y5)), narrow(added(g[1], g5))
-    g2 = narrow(added(g2, g3))
+    y, g, arrived, g3, y5 = fence(y, g, arrived, g3, y5)
+
+    y1, g2 = narrow(added(y[1], y5)), narrow(added(g2, g3))
     inner = jnp.concatenate([inner[:2], arrived], axis=1)
-    y1, g1, g2, inner, g, y, away = fence(y1, g1, g2, inner, g, y, away)
-    g2, y1, g1, y4, g4 = (
-        swap(g2, FAR), swap(y1, NEAR), swap(g1, NEAR), swap(y[4], SIDE), swap(g[4], SIDE),
-    )
-    arrived = swap(inner[1:], NEAR)
+    y1, g2, inner, g = fence(y1, g2, inner, g)
+    g2, y1, g4, arrived = swap(g2, FAR), swap(y1, NEAR), swap(g[4], SIDE), swap(inner[1:], NEAR)
+    g5, away = fence(g5, away)
+
+    g1 = swap(narrow(added(g[1], g5)), NEAR)
     grad_w = weight_grads(0, rows, cot, weighted, factors, away)
-    y, g, arrived, grad_w, y1, g1, g2, y4, g4 = fence(y, g, arrived, grad_w, y1, g1, g2, y4, g4)
+    arrived, grad_w, y1, g1, g2, y2, y4, g4 = fence(arrived, grad_w, y1, g1, g2, y2, y4, g4)
 
     inner = jnp.concatenate([inner[:1], arrived], axis=1)[0]
     combined = narrow(added(added(y[0], y4), added(y1, y2)))

time: 171 us -> 161 us (0.942)
  local copies, waits for them, and re-layouts: 42.8 us -> 3.24 us
  waiting for transfers between devices: 44.2 us -> 66.6 us
  Pallas kernels: 28.5 us -> 41.6 us
  other arithmetic: 12.4 us -> 9.3 us
  starting transfers between devices: 41.3 us -> 39.4 us
    unnamed x98 -> x46, local copies, waits for them, and re-layouts: 41.8 us -> 0.78 us
    ppermute x38, waiting for transfers between devices: 44.2 us -> 66.6 us  [swap(): return lax.ppermute(value, 'ep', pairs)]
    pallas_call x4, Pallas kernels: 28.5 us -> 41.6 us  [kernel(): pl.pallas_call(body, out_shape=outs, in_specs=[pl.BlockSpec(memory_space=...]
    convert_element_type x7, other arithmetic: 8.57 us -> 6.65 us  [narrow(): return value.astype(jnp.bfloat16)]
    ppermute x38, starting transfers between devices: 41.3 us -> 39.4 us  [swap(): return lax.ppermute(value, 'ep', pairs)]
  transfers between devices with their start and end apart: 38 -> 38, of which waited for: 10 -> 14; matrix products, arithmetic and copies ran while one was open for 1% -> 4% of each run, Pallas kernels for 17% -> 26%
where the time goes in v5:
time: 161 us
  waiting for transfers between devices  66.6 us (41%)
  Pallas kernels  41.6 us (26%)
  starting transfers between devices  39.4 us (24%)
  other arithmetic  9.3 us (6%)
  local copies, waits for them, and re-layouts  3.24 us (2%)
    ppermute x38, waiting for transfers between devices, swap(): return lax.ppermute(value, 'ep', pairs)  66.6 us
    pallas_call x4, Pallas kernels, kernel(): pl.pallas_call(body, out_shape=outs, in_specs=[pl.BlockSpec(memory_space=...  41.6 us
    ppermute x38, starting transfers between devices, swap(): return lax.ppermute(value, 'ep', pairs)  39.4 us
    convert_element_type x7, other arithmetic, narrow(): return value.astype(jnp.bfloat16)  6.65 us
  transfers between devices with their start and end apart: 38, of which 14 were waited for; matrix products, arithmetic and copies ran while one was open for 4% of the time, Pallas kernels for 26%

profile of v5, /device:TPU:0, one launch (start us, length us, event | category | flops | bytes accessed | tf_op | source)
XLA Modules:
  0.0 161.1 jit_solution(12884801212815613910)
XLA Ops:
  0.6 3.1 %collective-permute-start = (bf16[128,1024]{1,0:T(8,128)(2,1)}, bf16[128,1024]{1,0:T(8,128)(2,1)S(1)}, u32[]{:S(2)}, u32[]{:S(2)}) collective-permute-start(bf16[128,1024]{1,0:T(8,128)(2,1)} %refs_0_.6), channel_id=1, source_target_pairs={{0,4},{1,5},{2,6},{3,7},{4,0},{5,1},{6,2},{7,3},{8,12},{9,13},{10,... | collective-permute-start | bytes 786440 | tf_op jit(solution)/shard_map/ppermute | solution.py:115
  3.7 2.6 %collective-permute-start.1 = (bf16[128,1024]{1,0:T(8,128)(2,1)}, bf16[128,1024]{1,0:T(8,128)(2,1)S(1)}, u32[]{:S(2)}, u32[]{:S(2)}) collective-permute-start(bf16[128,1024]{1,0:T(8,128)(2,1)} %refs_0_.6), channel_id=1, source_target_pairs={{0,8},{1,9},{2,10},{3,11},{4,12},{5,13},{6,14},{7,15},{8,0},{9,1},... | collective-permute-start | bytes 786440 | tf_op jit(solution)/shard_map/ppermute | solution.py:115
  6.3 1.5 collective-permute-start.3
  9.1 6.7 %collective-permute-done.refs_1_ = bf16[128,1024]{1,0:T(8,128)(2,1)S(1)} collective-permute-done((bf16[128,1024]{1,0:T(8,128)(2,1)}, bf16[128,1024]{1,0:T(8,128)(2,1)S(1)}, u32[]{:S(2)}, u32[]{:S(2)}) %collective-permute-start) | collective-permute-done | bytes 262176 | tf_op jit(solution)/shard_map/ppermute | solution.py:115
  15.7 2.5 %collective-permute-done.1.refs_2_ = bf16[128,1024]{1,0:T(8,128)(2,1)S(1)} collective-permute-done((bf16[128,1024]{1,0:T(8,128)(2,1)}, bf16[128,1024]{1,0:T(8,128)(2,1)S(1)}, u32[]{:S(2)}, u32[]{:S(2)}) %collective-permute-start.1) | collective-permute-done | bytes 262176 | tf_op jit(solution)/shard_map/ppermute | solution.py:115
  18.7 1.6 collective-permute-start.5
  20.8 3.9 %collective-permute-done.5 = f32[1,16,128]{2,0,1:T(1,128)S(1)} collective-permute-done((f32[1,16,128]{2,0,1:T(1,128)S(1)}, f32[1,16,128]{2,0,1:T(1,128)S(1)}, u32[]{:S(2)}, u32[]{:S(2)}) %collective-permute-start.5) | collective-permute-done | bytes 8224 | tf_op jit(solution)/shard_map/ppermute | solution.py:115
  26.0 1.5 collective-permute-start.7
  27.5 12.7 %collective-permute-done.6.refs_2_.refs_10_ = bf16[128,1024]{1,0:T(8,128)(2,1)S(1)} collective-permute-done((bf16[128,1024]{1,0:T(8,128)(2,1)}, bf16[128,1024]{1,0:T(8,128)(2,1)S(1)}, u32[]{:S(2)}, u32[]{:S(2)}) %collective-permute-start.6) | collective-permute-done | bytes 262176 | tf_op jit(solution)/shard_map/ppermute | solution.py:115
  40.2 1.5 collective-permute-start.8
  41.8 6.2 %collective-permute-done.8.refs_6_ = bf16[128,1024]{1,0:T(8,128)(2,1)S(1)} collective-permute-done((bf16[128,1024]{1,0:T(8,128)(2,1)S(1)}, bf16[128,1024]{1,0:T(8,128)(2,1)S(1)}, u32[]{:S(2)}, u32[]{:S(2)}) %collective-permute-start.8) | collective-permute-done | bytes 262176 | tf_op jit(solution)/shard_map/ppermute | solution.py:115
  48.1 1.6 collective-permute-start.12
  50.2 2.2 %collective-permute-done.12 = f32[4,16,128]{2,0,1:T(4,128)S(1)} collective-permute-done((f32[4,16,128]{2,0,1:T(4,128)S(1)}, f32[4,16,128]{2,0,1:T(4,128)S(1)}, u32[]{:S(2)}, u32[]{:S(2)}) %collective-permute-start.12) | collective-permute-done | bytes 32800 | tf_op jit(solution)/shard_map/ppermute | solution.py:115
  52.5 4.2 %collective-permute-done.10.refs_7_ = bf16[128,1024]{1,0:T(8,128)(2,1)S(1)} collective-permute-done((bf16[128,1024]{1,0:T(8,128)(2,1)S(1)}, bf16[128,1024]{1,0:T(8,128)(2,1)S(1)}, u32[]{:S(2)}, u32[]{:S(2)}) %collective-permute-start.10) | collective-permute-done | bytes 262176 | tf_op jit(solution)/shard_map/ppermute | solution.py:115
  56.9 3.9 %collective-permute-done.11.refs_1_.refs_9_ = bf16[128,1024]{1,0:T(8,128)(2,1)S(1)} collective-permute-done((bf16[128,1024]{1,0:T(8,128)(2,1)}, bf16[128,1024]{1,0:T(8,128)(2,1)S(1)}, u32[]{:S(2)}, u32[]{:S(2)}) %collective-permute-start.11) | collective-permute-done | bytes 262176 | tf_op jit(solution)/shard_map/ppermute | solution.py:115
  60.8 2.5 %collective-permute-start.18 = (bf16[128,1024]{1,0:T(8,128)(2,1)S(1)}, bf16[128,1024]{1,0:T(8,128)(2,1)S(1)}, u32[]{:S(2)}, u32[]{:S(2)}) collective-permute-start(bf16[128,1024]{1,0:T(8,128)(2,1)S(1)} %collective-permute-done.6.refs_2_.refs_10_), channel_id=1, source_target_pairs={{0,2},{1,3},{2,0},{3,1},{4,6},{5,7},{6,4},{7,5},{8,10},{9,11},{10,... | collective-permute-start | bytes 786440 | tf_op jit(solution)/shard_map/ppermute | solution.py:115
  64.7 12.5 %shard_map.118 = (bf16[128,1024]{1,0:T(8,128)(2,1)}, bf16[128,1024]{1,0:T(8,128)(2,1)}, bf16[128,1024]{1,0:T(8,128)(2,1)}, bf16[128,1024]{1,0:T(8,128)(2,1)}, bf...) custom-call(bf16[128,1024]{1,0:T(8,128)(2,1)} %refs_0_.6, ...), custom_call_target="tpu_custom_call" | custom-call | flops 6442450944 | bytes 20979712 | tf_op jit(solution)/shard_map/pallas_call | solution.py:159
  77.3 2.0 %collective-permute-start.19 = (bf16[128,1024]{1,0:T(8,128)(2,1)S(1)}, bf16[128,1024]{1,0:T(8,128)(2,1)S(1)}, u32[]{:S(2)}, u32[]{:S(2)}) collective-permute-start(bf16[128,1024]{1,0:T(8,128)(2,1)S(1)} %collective-permute-done.16.refs_3_.refs_11_), channel_id=1, source_target_pairs={{0,2},{1,3},{2,0},{3,1},{4,6},{5,7},{6,4},{7,5},{8,10},{9,11},{10,... | collective-permute-start | bytes 786440 | tf_op jit(solution)/shard_map/ppermute | solution.py:115
  79.4 1.9 %collective-permute-start.21 = (bf16[128,1024]{1,0:T(8,128)(2,1)}, bf16[128,1024]{1,0:T(8,128)(2,1)S(1)}, u32[]{:S(2)}, u32[]{:S(2)}) collective-permute-start(bf16[128,1024]{1,0:T(8,128)(2,1)} %get-tuple-element.185), channel_id=1, source_target_pairs={{0,2},{1,3},{2,0},{3,1},{4,6},{5,7},{6,4},{7,5},{8,10},{9,11},{10,... | collective-permute-start | bytes 786440 | tf_op jit(solution)/shard_map/ppermute | solution.py:115
  81.4 5.2 %collective-permute-done.17.refs_5_.refs_13_ = bf16[128,1024]{1,0:T(8,128)(2,1)S(1)} collective-permute-done((bf16[128,1024]{1,0:T(8,128)(2,1)S(1)}, bf16[128,1024]{1,0:T(8,128)(2,1)S(1)}, u32[]{:S(2)}, u32[]{:S(2)}) %collective-permute-start.17) | collective-permute-done | bytes 262176 | tf_op jit(solution)/shard_map/ppermute | solution.py:115
  86.6 3.5 %collective-permute-done.19.refs_7_.refs_15_ = bf16[128,1024]{1,0:T(8,128)(2,1)S(1)} collective-permute-done((bf16[128,1024]{1,0:T(8,128)(2,1)S(1)}, bf16[128,1024]{1,0:T(8,128)(2,1)S(1)}, u32[]{:S(2)}, u32[]{:S(2)}) %collective-permute-start.19) | collective-permute-done | bytes 262176 | tf_op jit(solution)/shard_map/ppermute | solution.py:115
  90.7 14.0 %shard_map.119 = (bf16[128,1024]{1,0:T(8,128)(2,1)}, bf16[128,1024]{1,0:T(8,128)(2,1)}, bf16[128,1024]{1,0:T(8,128)(2,1)}, bf16[128,1024]{1,0:T(8,128)(2,1)}, bf...) custom-call(bf16[128,1024]{1,0:T(8,128)(2,1)} %refs_8_.1, ...), custom_call_target="tpu_custom_call" | custom-call | flops 6442450944 | bytes 23085056 | tf_op jit(solution)/shard_map/pallas_call | solution.py:159
  109.4 7.2 %shard_map.120 = bf16[1536,1024]{1,0:T(8,128)(2,1)} custom-call(bf16[128,1024]{1,0:T(8,128)(2,1)} %refs_0_.6, bf16[128,1024]{1,0:T(8,128)(2,1)} %copy-done.1, bf16[128,1024]{1,0:T(8,128)(2,1)} %copy-done.2, bf16[128,1024]{1,0:T(8,128)(2,1)} %copy-done.5, bf16[128,1024]{1,0:T(8,128)(2,1)} %copy-done.3, bf16[128,1024]{1,0:T(8,128)(2,1)} %copy-done.7, ...), custom_call_target="tpu_custom_call" | custom-call | flops 3221225472 | bytes 13631488 | tf_op jit(solution)/shard_map/pallas_call | solution.py:159
  120.3 1.7 %collective-permute-start.27 = (bf16[128,1024]{1,0:T(8,128)(2,1)}, bf16[128,1024]{1,0:T(8,128)(2,1)}, u32[]{:S(2)}, u32[]{:S(2)}) collective-permute-start(bf16[128,1024]{1,0:T(8,128)(2,1)} %add_convert_fusion.5), channel_id=1, source_target_pairs={{0,4},{1,5},{2,6},{3,7},{4,0},{5,1},{6,2},{7,3},{8,12},{9,13},{10,... | collective-permute-start | bytes 786440 | tf_op jit(solution)/shard_map/ppermute | solution.py:115
  122.0 1.9 %collective-permute-start.26 = (f32[2,2,2,128]{3,0,2,1:T(2,128)S(1)}, f32[2,2,2,128]{3,0,2,1:T(2,128)S(1)}, u32[]{:S(2)}, u32[]{:S(2)}) collective-permute-start(f32[2,2,2,128]{3,0,2,1:T(2,128)S(1)} %get-tuple-element.297), channel_id=1, source_target_pairs={{0,8},{1,9},{2,10},{3,11},{4,12},{5,13},{6,14},{7,15},{8,0},{9,1},... | collective-permute-start | bytes 12296 | tf_op jit(solution)/shard_map/ppermute | solution.py:115
  124.2 4.6 %collective-permute-done.28 = bf16[128,1024]{1,0:T(8,128)(2,1)} collective-permute-done((bf16[128,1024]{1,0:T(8,128)(2,1)}, bf16[128,1024]{1,0:T(8,128)(2,1)}, u32[]{:S(2)}, u32[]{:S(2)}) %collective-permute-start.28) | collective-permute-done | bytes 262176 | tf_op jit(solution)/shard_map/ppermute | solution.py:115
  128.9 2.6 %collective-permute-start.35 = (bf16[128,1024]{1,0:T(8,128)(2,1)}, bf16[128,1024]{1,0:T(8,128)(2,1)S(1)}, u32[]{:S(2)}, u32[]{:S(2)}) collective-permute-start(bf16[128,1024]{1,0:T(8,128)(2,1)} %add_convert_fusion.6), channel_id=1, source_target_pairs={{0,8},{1,9},{2,10},{3,11},{4,12},{5,13},{6,14},{7,15},{8,0},{9,1},... | collective-permute-start | bytes 786440 | tf_op jit(solution)/shard_map/ppermute | solution.py:115
  131.5 1.5 collective-permute-start.36
  135.7 1.6 collective-permute-start.32
  138.5 7.0 %collective-permute-done.35 = bf16[128,1024]{1,0:T(8,128)(2,1)S(1)} collective-permute-done((bf16[128,1024]{1,0:T(8,128)(2,1)}, bf16[128,1024]{1,0:T(8,128)(2,1)S(1)}, u32[]{:S(2)}, u32[]{:S(2)}) %collective-permute-start.35) | collective-permute-done | bytes 262176 | tf_op jit(solution)/shard_map/ppermute | solution.py:115
  147.0 8.0 %shard_map.121 = (bf16[1024,512]{1,0:T(8,128)(2,1)}, bf16[1024,512]{1,0:T(8,128)(2,1)}, bf16[512,1024]{1,0:T(8,128)(2,1)}) custom-call(bf16[128,1024]{1,0:T(8,128)(2,1)} %refs_0_.6, bf16[128,1024]{1,0:T(8,128)(2,1)} %copy-done.1, bf16[128,1024]{1,0:T(8,128)(2,1)} %copy-done.2, bf16[128,1024]{1,0:T(8,128)(2,1)} %copy-done.5, bf16[128,1024]{1,0:T(8,128)(2,1)} %copy-done.3, ...), custom_call_target="tpu_custom_call" | custom-call | flops 3221225472 | bytes 16777216 | tf_op jit(solution)/shard_map/pallas_call | solution.py:159
  155.1 3.6 %collective-permute-done.33 = bf16[128,1024]{1,0:T(8,128)(2,1)S(1)} collective-permute-done((bf16[128,1024]{1,0:T(8,128)(2,1)S(1)}, bf16[128,1024]{1,0:T(8,128)(2,1)S(1)}, u32[]{:S(2)}, u32[]{:S(2)}) %collective-permute-start.33) | collective-permute-done | bytes 262176 | tf_op jit(solution)/shard_map/ppermute | solution.py:115
  (124 shorter events, 23.0 us)
Async XLA Ops:
  0.6 15.1 %collective-permute-start = (bf16[128,1024]{1,0:T(8,128)(2,1)}, bf16[128,1024]{1,0:T(8,128)(2,1)S(1)}, u32[]{:S(2)}, u32[]{:S(2)}) collective-permute-start(bf16[128,1024]{1,0:T(8,128)(2,1)} %refs_0_.6), channel_id=1, source_target_pairs={{0,4},{1,5},{2,6},{3,7},{4,0},{5,1},{6,2},{7,3},{8,12},{9,13},{10,... | collective-permute-start | bytes 786440 | tf_op jit(solution)/shard_map/ppermute | solution.py:115
  3.7 14.6 %collective-permute-start.1 = (bf16[128,1024]{1,0:T(8,128)(2,1)}, bf16[128,1024]{1,0:T(8,128)(2,1)S(1)}, u32[]{:S(2)}, u32[]{:S(2)}) collective-permute-start(bf16[128,1024]{1,0:T(8,128)(2,1)} %refs_0_.6), channel_id=1, source_target_pairs={{0,8},{1,9},{2,10},{3,11},{4,12},{5,13},{6,14},{7,15},{8,0},{9,1},... | collective-permute-start | bytes 786440 | tf_op jit(solution)/shard_map/ppermute | solution.py:115
  6.3 14.0 %collective-permute-start.3 = (bf16[128,1024]{1,0:T(8,128)(2,1)}, bf16[128,1024]{1,0:T(8,128)(2,1)S(1)}, u32[]{:S(2)}, u32[]{:S(2)}) collective-permute-start(bf16[128,1024]{1,0:T(8,128)(2,1)} %refs_0_.6), channel_id=1, source_target_pairs={{0,2},{1,3},{2,0},{3,1},{4,6},{5,7},{6,4},{7,5},{8,10},{9,11},{10,... | collective-permute-start | bytes 786440 | tf_op jit(solution)/shard_map/ppermute | solution.py:115
  7.8 13.0 %collective-permute-start.4 = (bf16[128,1024]{1,0:T(8,128)(2,1)}, bf16[128,1024]{1,0:T(8,128)(2,1)S(1)}, u32[]{:S(2)}, u32[]{:S(2)}) collective-permute-start(bf16[128,1024]{1,0:T(8,128)(2,1)} %refs_8_.1), channel_id=1, source_target_pairs={{0,2},{1,3},{2,0},{3,1},{4,6},{5,7},{6,4},{7,5},{8,10},{9,11},{10,... | collective-permute-start | bytes 786440 | tf_op jit(solution)/shard_map/ppermute | solution.py:115
  20.3 43.1 %collective-permute-start.13 = (bf16[1024,512]{1,0:T(8,128)(2,1)}, bf16[1024,512]{1,0:T(8,128)(2,1)}, u32[]{:S(2)}, u32[]{:S(2)}) collective-permute-start(bf16[1024,512]{1,0:T(8,128)(2,1)} %bitcast.44), channel_id=1, source_target_pairs={{0,1},{1,0},{2,3},{3,2},{4,5},{5,4},{6,7},{7,6},{8,9},{9,8},{10,11... | collective-permute-start | bytes 3145736 | tf_op jit(solution)/shard_map/ppermute | solution.py:115
  20.3 43.0 %collective-permute-start.14 = (bf16[1024,512]{1,0:T(8,128)(2,1)}, bf16[1024,512]{1,0:T(8,128)(2,1)}, u32[]{:S(2)}, u32[]{:S(2)}) collective-permute-start(bf16[1024,512]{1,0:T(8,128)(2,1)} %bitcast.47), channel_id=1, source_target_pairs={{0,1},{1,0},{2,3},{3,2},{4,5},{5,4},{6,7},{7,6},{8,9},{9,8},{10,11... | collective-permute-start | bytes 3145736 | tf_op jit(solution)/shard_map/ppermute | solution.py:115
  24.7 38.6 %collective-permute-start.15 = (bf16[512,1024]{1,0:T(8,128)(2,1)}, bf16[512,1024]{1,0:T(8,128)(2,1)}, u32[]{:S(2)}, u32[]{:S(2)}) collective-permute-start(bf16[512,1024]{1,0:T(8,128)(2,1)} %bitcast.50), channel_id=1, source_target_pairs={{0,1},{1,0},{2,3},{3,2},{4,5},{5,4},{6,7},{7,6},{8,9},{9,8},{10,11... | collective-permute-start | bytes 3145736 | tf_op jit(solution)/shard_map/ppermute | solution.py:115
  24.7 15.4 %collective-permute-start.6 = (bf16[128,1024]{1,0:T(8,128)(2,1)}, bf16[128,1024]{1,0:T(8,128)(2,1)S(1)}, u32[]{:S(2)}, u32[]{:S(2)}) collective-permute-start(bf16[128,1024]{1,0:T(8,128)(2,1)} %refs_8_.1), channel_id=1, source_target_pairs={{0,8},{1,9},{2,10},{3,11},{4,12},{5,13},{6,14},{7,15},{8,0},{9,1},... | collective-permute-start | bytes 786440 | tf_op jit(solution)/shard_map/ppermute | solution.py:115
  26.0 15.7 %collective-permute-start.7 = (bf16[128,1024]{1,0:T(8,128)(2,1)S(1)}, bf16[128,1024]{1,0:T(8,128)(2,1)S(1)}, u32[]{:S(2)}, u32[]{:S(2)}) collective-permute-start(bf16[128,1024]{1,0:T(8,128)(2,1)S(1)} %collective-permute-done.refs_1_), channel_id=1, source_target_pairs={{0,2},{1,3},{2,0},{3,1},{4,6},{5,7},{6,4},{7,5},{8,10},{9,11},{10,... | collective-permute-start | bytes 786440 | tf_op jit(solution)/shard_map/ppermute | solution.py:115
  52.4 8.4 %collective-permute-start.11 = (bf16[128,1024]{1,0:T(8,128)(2,1)}, bf16[128,1024]{1,0:T(8,128)(2,1)S(1)}, u32[]{:S(2)}, u32[]{:S(2)}) collective-permute-start(bf16[128,1024]{1,0:T(8,128)(2,1)} %refs_8_.1), channel_id=1, source_target_pairs={{0,4},{1,5},{2,6},{3,7},{4,0},{5,1},{6,2},{7,3},{8,12},{9,13},{10,... | collective-permute-start | bytes 786440 | tf_op jit(solution)/shard_map/ppermute | solution.py:115
  56.7 20.5 %collective-permute-start.16 = (bf16[128,1024]{1,0:T(8,128)(2,1)S(1)}, bf16[128,1024]{1,0:T(8,128)(2,1)S(1)}, u32[]{:S(2)}, u32[]{:S(2)}) collective-permute-start(bf16[128,1024]{1,0:T(8,128)(2,1)S(1)} %collective-permute-done.6.refs_2_.refs_10_), channel_id=1, source_target_pairs={{0,4},{1,5},{2,6},{3,7},{4,0},{5,1},{6,2},{7,3},{8,12},{9,13},{10,... | collective-permute-start | bytes 786440 | tf_op jit(solution)/shard_map/ppermute | solution.py:115
  60.8 20.5 %collective-permute-start.18 = (bf16[128,1024]{1,0:T(8,128)(2,1)S(1)}, bf16[128,1024]{1,0:T(8,128)(2,1)S(1)}, u32[]{:S(2)}, u32[]{:S(2)}) collective-permute-start(bf16[128,1024]{1,0:T(8,128)(2,1)S(1)} %collective-permute-done.6.refs_2_.refs_10_), channel_id=1, source_target_pairs={{0,2},{1,3},{2,0},{3,1},{4,6},{5,7},{6,4},{7,5},{8,10},{9,11},{10,... | collective-permute-start | bytes 786440 | tf_op jit(solution)/shard_map/ppermute | solution.py:115
  77.2 9.3 %collective-permute-start.17 = (bf16[128,1024]{1,0:T(8,128)(2,1)S(1)}, bf16[128,1024]{1,0:T(8,128)(2,1)S(1)}, u32[]{:S(2)}, u32[]{:S(2)}) collective-permute-start(bf16[128,1024]{1,0:T(8,128)(2,1)S(1)} %collective-permute-done.11.refs_1_.refs_9_), channel_id=1, source_target_pairs={{0,2},{1,3},{2,0},{3,1},{4,6},{5,7},{6,4},{7,5},{8,10},{9,11},{10,... | collective-permute-start | bytes 786440 | tf_op jit(solution)/shard_map/ppermute | solution.py:115
  77.3 12.7 %collective-permute-start.19 = (bf16[128,1024]{1,0:T(8,128)(2,1)S(1)}, bf16[128,1024]{1,0:T(8,128)(2,1)S(1)}, u32[]{:S(2)}, u32[]{:S(2)}) collective-permute-start(bf16[128,1024]{1,0:T(8,128)(2,1)S(1)} %collective-permute-done.16.refs_3_.refs_11_), channel_id=1, source_target_pairs={{0,2},{1,3},{2,0},{3,1},{4,6},{5,7},{6,4},{7,5},{8,10},{9,11},{10,... | collective-permute-start | bytes 786440 | tf_op jit(solution)/shard_map/ppermute | solution.py:115
  79.3 25.4 %collective-permute-start.20 = (bf16[128,1024]{1,0:T(8,128)(2,1)}, bf16[128,1024]{1,0:T(8,128)(2,1)S(1)}, u32[]{:S(2)}, u32[]{:S(2)}) collective-permute-start(bf16[128,1024]{1,0:T(8,128)(2,1)} %get-tuple-element.186), channel_id=1, source_target_pairs={{0,2},{1,3},{2,0},{3,1},{4,6},{5,7},{6,4},{7,5},{8,10},{9,11},{10,... | collective-permute-start | bytes 786440 | tf_op jit(solution)/shard_map/ppermute | solution.py:115
  79.4 25.3 %collective-permute-start.21 = (bf16[128,1024]{1,0:T(8,128)(2,1)}, bf16[128,1024]{1,0:T(8,128)(2,1)S(1)}, u32[]{:S(2)}, u32[]{:S(2)}) collective-permute-start(bf16[128,1024]{1,0:T(8,128)(2,1)} %get-tuple-element.185), channel_id=1, source_target_pairs={{0,2},{1,3},{2,0},{3,1},{4,6},{5,7},{6,4},{7,5},{8,10},{9,11},{10,... | collective-permute-start | bytes 786440 | tf_op jit(solution)/shard_map/ppermute | solution.py:115
  105.9 10.7 %collective-permute-start.22 = (f32[4,1,2,128]{3,0,2,1:T(4,128)S(1)}, f32[4,1,2,128]{3,0,2,1:T(4,128)S(1)}, u32[]{:S(2)}, u32[]{:S(2)}) collective-permute-start(f32[4,1,2,128]{3,0,2,1:T(4,128)S(1)} %get-tuple-element.299), channel_id=1, source_target_pairs={{0,2},{1,3},{2,0},{3,1},{4,6},{5,7},{6,4},{7,5},{8,10},{9,11},{10,... | collective-permute-start | bytes 12296 | tf_op jit(solution)/shard_map/ppermute | solution.py:115
  106.5 10.1 %collective-permute-start.23 = (bf16[128,1024]{1,0:T(8,128)(2,1)S(1)}, bf16[128,1024]{1,0:T(8,128)(2,1)S(1)}, u32[]{:S(2)}, u32[]{:S(2)}) collective-permute-start(bf16[128,1024]{1,0:T(8,128)(2,1)S(1)} %get-tuple-element.238), channel_id=1, source_target_pairs={{0,4},{1,5},{2,6},{3,7},{4,0},{5,1},{6,2},{7,3},{8,12},{9,13},{10,... | collective-permute-start | bytes 786440 | tf_op jit(solution)/shard_map/ppermute | solution.py:115
  107.4 9.2 %collective-permute-start.24 = (bf16[128,1024]{1,0:T(8,128)(2,1)}, bf16[128,1024]{1,0:T(8,128)(2,1)S(1)}, u32[]{:S(2)}, u32[]{:S(2)}) collective-permute-start(bf16[128,1024]{1,0:T(8,128)(2,1)} %get-tuple-element.234), channel_id=1, source_target_pairs={{0,2},{1,3},{2,0},{3,1},{4,6},{5,7},{6,4},{7,5},{8,10},{9,11},{10,... | collective-permute-start | bytes 786440 | tf_op jit(solution)/shard_map/ppermute | solution.py:115
  108.2 8.5 %collective-permute-start.25 = (bf16[128,1024]{1,0:T(8,128)(2,1)}, bf16[128,1024]{1,0:T(8,128)(2,1)S(1)}, u32[]{:S(2)}, u32[]{:S(2)}) collective-permute-start(bf16[128,1024]{1,0:T(8,128)(2,1)} %get-tuple-element.233), channel_id=1, source_target_pairs={{0,2},{1,3},{2,0},{3,1},{4,6},{5,7},{6,4},{7,5},{8,10},{9,11},{10,... | collective-permute-start | bytes 786440 | tf_op jit(solution)/shard_map/ppermute | solution.py:115
  119.2 18.1 %collective-permute-start.31 = (bf16[1536,1024]{1,0:T(8,128)(2,1)}, bf16[1536,1024]{1,0:T(8,128)(2,1)S(1)}, u32[]{:S(2)}, u32[]{:S(2)}) collective-permute-start(bf16[1536,1024]{1,0:T(8,128)(2,1)} %shard_map.120), channel_id=1, source_target_pairs={{0,1},{1,0},{2,3},{3,2},{4,5},{5,4},{6,7},{7,6},{8,9},{9,8},{10,11... | collective-permute-start | bytes 9437192 | tf_op jit(solution)/shard_map/ppermute | solution.py:115
  119.4 9.5 %collective-permute-start.28 = (bf16[128,1024]{1,0:T(8,128)(2,1)}, bf16[128,1024]{1,0:T(8,128)(2,1)}, u32[]{:S(2)}, u32[]{:S(2)}) collective-permute-start(bf16[128,1024]{1,0:T(8,128)(2,1)} %get-tuple-element.226), channel_id=1, source_target_pairs={{0,2},{1,3},{2,0},{3,1},{4,6},{5,7},{6,4},{7,5},{8,10},{9,11},{10,... | collective-permute-start | bytes 786440 | tf_op jit(solution)/shard_map/ppermute | solution.py:115
  120.3 12.6 %collective-permute-start.27 = (bf16[128,1024]{1,0:T(8,128)(2,1)}, bf16[128,1024]{1,0:T(8,128)(2,1)}, u32[]{:S(2)}, u32[]{:S(2)}) collective-permute-start(bf16[128,1024]{1,0:T(8,128)(2,1)} %add_convert_fusion.5), channel_id=1, source_target_pairs={{0,4},{1,5},{2,6},{3,7},{4,0},{5,1},{6,2},{7,3},{8,12},{9,13},{10,... | collective-permute-start | bytes 786440 | tf_op jit(solution)/shard_map/ppermute | solution.py:115
  122.0 9.4 %collective-permute-start.26 = (f32[2,2,2,128]{3,0,2,1:T(2,128)S(1)}, f32[2,2,2,128]{3,0,2,1:T(2,128)S(1)}, u32[]{:S(2)}, u32[]{:S(2)}) collective-permute-start(f32[2,2,2,128]{3,0,2,1:T(2,128)S(1)} %get-tuple-element.297), channel_id=1, source_target_pairs={{0,8},{1,9},{2,10},{3,11},{4,12},{5,13},{6,14},{7,15},{8,0},{9,1},... | collective-permute-start | bytes 12296 | tf_op jit(solution)/shard_map/ppermute | solution.py:115
  124.1 11.6 %collective-permute-start.30 = (bf16[128,1024]{1,0:T(8,128)(2,1)}, bf16[128,1024]{1,0:T(8,128)(2,1)S(1)}, u32[]{:S(2)}, u32[]{:S(2)}) collective-permute-start(bf16[128,1024]{1,0:T(8,128)(2,1)} %get-tuple-element.259), channel_id=1, source_target_pairs={{0,2},{1,3},{2,0},{3,1},{4,6},{5,7},{6,4},{7,5},{8,10},{9,11},{10,... | collective-permute-start | bytes 786440 | tf_op jit(solution)/shard_map/ppermute | solution.py:115
  128.9 16.7 %collective-permute-start.35 = (bf16[128,1024]{1,0:T(8,128)(2,1)}, bf16[128,1024]{1,0:T(8,128)(2,1)S(1)}, u32[]{:S(2)}, u32[]{:S(2)}) collective-permute-start(bf16[128,1024]{1,0:T(8,128)(2,1)} %add_convert_fusion.6), channel_id=1, source_target_pairs={{0,8},{1,9},{2,10},{3,11},{4,12},{5,13},{6,14},{7,15},{8,0},{9,1},... | collective-permute-start | bytes 786440 | tf_op jit(solution)/shard_map/ppermute | solution.py:115
  131.5 15.5 %collective-permute-start.36 = (bf16[128,1024]{1,0:T(8,128)(2,1)}, bf16[128,1024]{1,0:T(8,128)(2,1)S(1)}, u32[]{:S(2)}, u32[]{:S(2)}) collective-permute-start(bf16[128,1024]{1,0:T(8,128)(2,1)} %get-tuple-element.255), channel_id=1, source_target_pairs={{0,2},{1,3},{2,0},{3,1},{4,6},{5,7},{6,4},{7,5},{8,10},{9,11},{10,... | collective-permute-start | bytes 786440 | tf_op jit(solution)/shard_map/ppermute | solution.py:115
  135.2 19.8 %collective-permute-start.29 = (f32[1,4,2,128]{3,0,2,1:T(1,128)S(1)}, f32[1,4,2,128]{3,0,2,1:T(1,128)S(1)}, u32[]{:S(2)}, u32[]{:S(2)}) collective-permute-start(f32[1,4,2,128]{3,0,2,1:T(1,128)S(1)} %get-tuple-element.295), channel_id=1, source_target_pairs={{0,4},{1,5},{2,6},{3,7},{4,0},{5,1},{6,2},{7,3},{8,12},{9,13},{10,... | collective-permute-start | bytes 12296 | tf_op jit(solution)/shard_map/ppermute | solution.py:115
  135.7 19.3 %collective-permute-start.32 = (bf16[128,1024]{1,0:T(8,128)(2,1)S(1)}, bf16[128,1024]{1,0:T(8,128)(2,1)S(1)}, u32[]{:S(2)}, u32[]{:S(2)}) collective-permute-start(bf16[128,1024]{1,0:T(8,128)(2,1)S(1)} %add_convert_fusion.4), channel_id=1, source_target_pairs={{0,4},{1,5},{2,6},{3,7},{4,0},{5,1},{6,2},{7,3},{8,12},{9,13},{10,... | collective-permute-start | bytes 786440 | tf_op jit(solution)/shard_map/ppermute | solution.py:115
  137.3 17.8 %collective-permute-start.34 = (bf16[128,1024]{1,0:T(8,128)(2,1)S(1)}, bf16[128,1024]{1,0:T(8,128)(2,1)S(1)}, u32[]{:S(2)}, u32[]{:S(2)}) collective-permute-start(bf16[128,1024]{1,0:T(8,128)(2,1)S(1)} %add_convert_fusion.3), channel_id=1, source_target_pairs={{0,8},{1,9},{2,10},{3,11},{4,12},{5,13},{6,14},{7,15},{8,0},{9,1},... | collective-permute-start | bytes 786440 | tf_op jit(solution)/shard_map/ppermute | solution.py:115
  145.5 9.5 %collective-permute-start.37 = (bf16[128,1024]{1,0:T(8,128)(2,1)}, bf16[128,1024]{1,0:T(8,128)(2,1)S(1)}, u32[]{:S(2)}, u32[]{:S(2)}) collective-permute-start(bf16[128,1024]{1,0:T(8,128)(2,1)} %get-tuple-element.282), channel_id=1, source_target_pairs={{0,2},{1,3},{2,0},{3,1},{4,6},{5,7},{6,4},{7,5},{8,10},{9,11},{10,... | collective-permute-start | bytes 786440 | tf_op jit(solution)/shard_map/ppermute | solution.py:115
  147.0 11.7 %collective-permute-start.33 = (bf16[128,1024]{1,0:T(8,128)(2,1)S(1)}, bf16[128,1024]{1,0:T(8,128)(2,1)S(1)}, u32[]{:S(2)}, u32[]{:S(2)}) collective-permute-start(bf16[128,1024]{1,0:T(8,128)(2,1)S(1)} %add_convert_fusion.2), channel_id=1, source_target_pairs={{0,4},{1,5},{2,6},{3,7},{4,0},{5,1},{6,2},{7,3},{8,12},{9,13},{10,... | collective-permute-start | bytes 786440 | tf_op jit(solution)/shard_map/ppermute | solution.py:115
  (29 other events, 543.9 us)

commit v6 on v0

--- a/solution.py
+++ b/solution.py
@@ -1,6 +1,8 @@
 import jax
 import jax.numpy as jnp
 from jax import lax
+from jax.experimental import pallas as pl
+from jax.experimental.pallas import tpu as pltpu
 from jax.sharding import PartitionSpec as P
 
 
@@ -48,7 +50,7 @@
     return (grad_rows, grad_gw, grad_uw, grad_down)
 
 
-def local(latent_in, routes, combine_weights, cotangent, w_gate, w_up, w_down):
+def exchanged(latent_in, routes, combine_weights, cotangent, w_gate, w_up, w_down):
     devices_ep = lax.axis_size("ep")
     local_experts = w_gate.shape[0]
     expert_count = local_experts * devices_ep
@@ -104,6 +106,365 @@
     return (combined, grad_latent, grad_combine, grad_gw, grad_uw, grad_down)
 
 
+def dot(a, b, dims):
+    return lax.dot_general(a, b, (dims, ((), ())), preferred_element_type=jnp.float32)
+
+
+def swap(value, bit):
+    pairs = [(i, i ^ bit) for i in range(lax.axis_size("ep"))]
+    return lax.ppermute(value, "ep", pairs)
+
+
+CORE, SIDE, NEAR, FAR = 1, 2, 4, 8
+REACH = (0, NEAR, FAR, NEAR | FAR, SIDE, SIDE | NEAR, SIDE | FAR, SIDE | NEAR | FAR)
+
+
+def fence(*values):
+    return lax.optimization_barrier(values)
+
+
+def added(a, b):
+    return a.astype(jnp.float32) + b.astype(jnp.float32)
+
+
+def narrow(value):
+    return value.astype(jnp.bfloat16)
+
+
+MIB = 1 << 20
+
+
+class Fetch:
+    def __init__(self, sems):
+        self.sems, self.waiting = sems, {}
+
+    def start(self, name, source, target):
+        copy = pltpu.make_async_copy(source, target, self.sems.at[len(self.waiting)])
+        copy.start()
+        self.waiting[name] = [copy, False]
+
+    def wait(self, *names):
+        for name in names:
+            if not self.waiting[name][1]:
+                self.waiting[name][0].wait()
+                self.waiting[name][1] = True
+
+    def wait_all(self):
+        self.wait(*self.waiting)
+
+
+def kernel(body, outs, scratch, copies, flops, *operands, scalar=None):
+    moved = sum(v.size * v.dtype.itemsize for v in (*operands, *outs))
+    in_specs = [pl.BlockSpec(memory_space=pl.ANY)] * len(operands)
+    if scalar is not None:
+        operands = (scalar, *operands)
+        in_specs = [pl.BlockSpec(memory_space=pltpu.SMEM), *in_specs]
+    return pl.pallas_call(
+        body,
+        out_shape=outs,
+        in_specs=in_specs,
+        out_specs=[pl.BlockSpec(memory_space=pl.ANY)] * len(outs),
+        scratch_shapes=[*scratch, pltpu.SemaphoreType.DMA((copies,))],
+        compiler_params=pltpu.CompilerParams(vmem_limit_bytes=56 * MIB),
+        cost_estimate=pl.CostEstimate(flops=flops, bytes_accessed=moved, transcendentals=0),
+    )(*operands)
+
+
+def shape(rows, columns, dtype):
+    return jax.ShapeDtypeStruct((rows, columns), dtype)
+
+
+def pieces(value):
+    first = narrow(value)
+    value = value - first.astype(jnp.float32)
+    second = narrow(value)
+    return first, second, narrow(value - second.astype(jnp.float32))
+
+
+EXTRA = 16
+
+
+def both_ways(number, blocks, weights, me, before=None):
+    bf16, f32 = jnp.bfloat16, jnp.float32
+    count, width = len(blocks), blocks[0].shape[1]
+    units, last = weights[0][0].shape[1], before is not None
+    tok_count = (blocks[0].shape[0] - (0 if last else EXTRA)) // 2
+    every, size = count * tok_count, 2 * tok_count
+    lanes = 128
+    back = size + (EXTRA if last else 0)
+
+    def body(me_ref, *refs):
+        b_refs, w_refs, refs = refs[:count], refs[count : count + 6], refs[count + 6 :]
+        before_refs, refs = (refs[:2], refs[2:]) if last else ((), refs)
+        q_refs, refs = refs[:count], refs[count:]
+        weighted_ref, factor_ref, refs = refs[0], refs[1], refs[2:]
+        after_refs, refs = ((), refs) if last else (refs[:2], refs[2:])
+        w_bufs, refs = refs[:6], refs[6:]
+        x_buf, c_buf, y_buf, g_buf, weighted_buf, factor_buf, refs = *refs[:6], refs[6:]
+        share_buf, inner_buf, wide_buf, extra_buf, sems = refs
+        fetch = Fetch(sems)
+        me = me_ref[0]
+        low = lax.rem(me, 8)
+        for b in range(count):
+            at = pl.ds(b * tok_count, tok_count)
+            fetch.start(("x", b), b_refs[b].at[pl.ds(0, tok_count)], x_buf.at[at])
+            if b == 0:
+                fetch.start(("w", 0), w_refs[0], w_bufs[0])
+        if last:
+            fetch.start("share", before_refs[0], share_buf)
+            fetch.start("inner", before_refs[1], inner_buf)
+        else:
+            for b in range(count):
+                fetch.start(("s", b), b_refs[b].at[pl.ds(size, EXTRA)], extra_buf.at[b])
+        for i in (1, 2):
+            fetch.start(("w", i), w_refs[i], w_bufs[i])
+        for b in range(count):
+            at = pl.ds(b * tok_count, tok_count)
+            fetch.start(("c", b), b_refs[b].at[pl.ds(tok_count, tok_count)], c_buf.at[at])
+        for i in (3, 4, 5):
+            fetch.start(("w", i), w_refs[i], w_bufs[i])
+
+        def place(e):
+            number = lax.rem(low + e, 2) + low - lax.rem(low, 2)
+            return pl.ds(pl.multiple_of(number * lanes, lanes), lanes)
+
+        upper = me >= 8
+        if last:
+            fetch.wait("share", "inner")
+        else:
+            inner_buf[...] = jnp.zeros((lanes, lanes), f32)
+            share_buf[...] = jnp.zeros((lanes, lanes), f32)
+            for b in range(count):
+                fetch.wait(("s", b))
+                wide_buf[b] = extra_buf[b].astype(f32)
+            for e in range(2):
+                for b in range(count):
+                    tile = wide_buf[b, :, place(e)]
+                    sums = [tile[r : r + 1] + tile[r + 2 : r + 3] + tile[r + 4 : r + 5] for r in (0, 1)]
+                    row = e * count + b
+                    share_buf[row : row + 1, :] = jnp.where(upper, sums[1], sums[0])
+            share_buf[...] = share_buf[...].T
+
+        half = slice(number * tok_count, (number + 1) * tok_count)
+        fetch.wait(*[("x", b) for b in range(count)])
+        x, y, g = x_buf[...], 0.0, 0.0
+        for e in range(2):
+            gate_w, up_w, down_w = w_bufs[3 * e : 3 * e + 3]
+            columns = slice(e * units, (e + 1) * units)
+            fetch.wait(("w", 3 * e))
+            gate = dot(x, gate_w[...], ((1,), (0,)))
+            fetch.wait(("w", 3 * e + 1))
+            up = dot(x, up_w[...], ((1,), (0,)))
+            sigma = jax.nn.sigmoid(gate)
+            silu_val = gate * sigma
+            hidden = silu_val * up
+            part = [share_buf[half, e * count + b : e * count + b + 1] for b in range(count)]
+            part = jnp.concatenate(part, axis=0)
+            weighted = (part * hidden).astype(bf16)
+            weighted_buf[:, columns] = weighted
+            fetch.wait(("w", 3 * e + 2))
+            if e == 0:
+                fetch.wait(*[("c", b) for b in range(count)])
+            plain = dot(c_buf[...], down_w[...], ((1,), (1,)))
+            y = y + dot(weighted, down_w[...], ((1,), (0,)))
+            inner = jnp.sum(hidden * plain, axis=1, keepdims=True)
+            for b in range(count):
+                value = inner[b * tok_count : (b + 1) * tok_count]
+                inner_buf[half, e * count + b : e * count + b + 1] = value
+            grad_hidden = part * plain
+            grad_gate = (grad_hidden * up * (sigma * (1.0 + gate * (1.0 - sigma)))).astype(bf16)
+            grad_up = (grad_hidden * silu_val).astype(bf16)
+            factor_buf[:, 2 * e * units : (2 * e + 1) * units] = grad_gate
+            factor_buf[:, (2 * e + 1) * units : (2 * e + 2) * units] = grad_up
+            g = g + dot(grad_gate, gate_w[...], ((1,), (1,)))
+            g = g + dot(grad_up, up_w[...], ((1,), (1,)))
+        y_buf[...] = y.astype(bf16)
+        g_buf[...] = g.astype(bf16)
+        for b in range(count):
+            at = pl.ds(b * tok_count, tok_count)
+            fetch.start(("y", b), y_buf.at[at], q_refs[b].at[pl.ds(0, tok_count)])
+            fetch.start(("g", b), g_buf.at[at], q_refs[b].at[pl.ds(tok_count, tok_count)])
+        fetch.start("weighted", weighted_buf, weighted_ref)
+        fetch.start("factor", factor_buf, factor_ref)
+        if last:
+            wide_buf[...] = jnp.zeros((count, EXTRA, width), f32)
+            inner_buf[...] = inner_buf[...].T
+            for e in range(2):
+                for b in range(count):
+                    row = e * count + b
+                    value, lines = inner_buf[row : row + 1, :], []
+                    for _ in range(3):
+                        piece = value.astype(bf16).astype(f32)
+                        lines += [jnp.where(upper, 0.0, piece), jnp.where(upper, piece, 0.0)]
+                        value = value - piece
+                    lines += [jnp.zeros((2, lanes), f32)]
+                    wide_buf[b, 0:8, place(e)] = jnp.concatenate(lines, axis=0)
+            for b in range(count):
+                extra_buf[b] = wide_buf[b].astype(bf16)
+                fetch.start(("i", b), extra_buf.at[b], q_refs[b].at[pl.ds(size, EXTRA)])
+        else:
+            fetch.start("share", share_buf, after_refs[0])
+            fetch.start("inner", inner_buf, after_refs[1])
+        fetch.wait_all()
+
+    outs = [shape(back, width, bf16)] * count
+    outs += [shape(every, 2 * units, bf16), shape(every, 4 * units, bf16)]
+    small = shape(lanes, lanes, f32)
+    operands = (*blocks, *weights[0], *weights[1])
+    if last:
+        operands += before
+    else:
+        outs += [small, small]
+    scratch = [pltpu.VMEM(w.shape, bf16) for w in (*weights[0], *weights[1])]
+    scratch += [pltpu.VMEM((every, width), bf16)] * 4
+    scratch += [pltpu.VMEM((every, 2 * units), bf16), pltpu.VMEM((every, 4 * units), bf16)]
+    scratch += [pltpu.VMEM(small.shape, f32)] * 2
+    scratch += [pltpu.VMEM((count, EXTRA, width), f32), pltpu.VMEM((count, EXTRA, width), bf16)]
+    flops = 24 * every * width * units
+    copies = 5 * count + 6 + 2 + 2
+    outs = kernel(body, outs, scratch, copies, flops, *operands, scalar=me)
+    return outs[:count], outs[count:]
+
+
+def weight_grads(expert, blocks, factors, away=None):
+    bf16 = jnp.bfloat16
+    parts, count, width = len(blocks), len(blocks[0]), blocks[0][0].shape[1]
+    each = factors[0][0].shape[0]
+    tok_count, every, units = each // count, each * parts, factors[0][0].shape[1] // 2
+    extra = 0 if away is None else 1
+
+    def body(*refs):
+        b_refs, refs = refs[: parts * count], refs[parts * count :]
+        f_refs, refs = refs[: 2 * parts], refs[2 * parts :]
+        away_refs, out_refs, refs = refs[:extra], refs[extra : 3 * extra + 1], refs[3 * extra + 1 :]
+        x_buf, c_buf, weighted_buf, factor_buf, *bufs, sems = refs
+        away_bufs, out_bufs = bufs[:extra], bufs[extra:]
+        fetch = Fetch(sems)
+        names = range(parts * count)
+        for i in names:
+            at = pl.ds(i * tok_count, tok_count)
+            fetch.start(("x", i), b_refs[i].at[pl.ds(0, tok_count)], x_buf.at[at])
+        for p in range(parts):
+            at = pl.ds(p * each, each)
+            lanes = pl.ds(2 * expert * units, 2 * units)
+            fetch.start(("f", p), f_refs[2 * p + 1].at[:, lanes], factor_buf.at[at])
+        if extra:
+            fetch.start("away", away_refs[0], away_bufs[0])
+        for p in range(parts):
+            at = pl.ds(p * each, each)
+            lanes = pl.ds(expert * units, units)
+            fetch.start(("w", p), f_refs[2 * p].at[:, lanes], weighted_buf.at[at])
+        for i in names:
+            at = pl.ds(i * tok_count, tok_count)
+            fetch.start(("c", i), b_refs[i].at[pl.ds(tok_count, tok_count)], c_buf.at[at])
+        fetch.wait(*[("x", i) for i in names], *[("f", p) for p in range(parts)])
+        for number in range(3):
+            if number < 2:
+                left, right = x_buf, factor_buf[:, number * units : (number + 1) * units]
+                columns, into = slice(number * units, (number + 1) * units), slice(0, width)
+            else:
+                fetch.wait(*[("c", i) for i in names], *[("w", p) for p in range(parts)])
+                left, right = weighted_buf, c_buf[...]
+                columns, into = slice(0, width), slice(width, width + units)
+            for start in range(0, into.stop - into.start, units):
+                value = dot(left[:, start : start + units], right, ((0,), (0,)))
+                at = slice(into.start + start, into.start + start + units)
+                if not extra:
+                    out_bufs[0][at, columns] = value.astype(bf16)
+                else:
+                    fetch.wait("away")
+                    value = value + away_bufs[0][at, columns].astype(jnp.float32)
+                    out_bufs[number][start : start + units, :] = value.astype(bf16)
+                    block = out_bufs[number].at[start : start + units]
+                    target = out_refs[number].at[start : start + units]
+                    fetch.start(("out", number, start), block, target)
+            if not extra and number:
+                at = pl.ds(into.start, into.stop - into.start)
+                fetch.start(("out", number), out_bufs[0].at[at], out_refs[0].at[at])
+        fetch.wait_all()
+
+    flops = 6 * every * width * units
+    operands = (*[b for part in blocks for b in part], *[f for part in factors for f in part])
+    scratch = [pltpu.VMEM((every, width), bf16)] * 2
+    scratch += [pltpu.VMEM((every, units), bf16), pltpu.VMEM((every, 2 * units), bf16)]
+    packed = shape(width + units, width, bf16)
+    if away is None:
+        outs = [packed]
+        scratch += [pltpu.VMEM(packed.shape, bf16)]
+    else:
+        operands += (away,)
+        outs = [shape(width, units, bf16)] * 2 + [shape(units, width, bf16)]
+        scratch += [pltpu.VMEM(v.shape, bf16) for v in (packed, *outs)]
+    copies = 2 * parts * count + 2 * parts + 1 + 2 * -(-width // units) + 1
+    outs = kernel(body, outs, scratch, copies, flops, *operands)
+    return outs if extra else outs[0]
+
+
+def paired(latent_in, routes, combine_weights, cotangent, w_gate, w_up, w_down):
+    f32 = jnp.float32
+    devices_ep, tok_count, width = lax.axis_size("ep"), *latent_in.shape
+    me = lax.axis_index("ep")
+    mid = tok_count // 2
+    experts = jnp.arange(devices_ep, dtype=jnp.int32)
+    own = (w_gate[0], w_up[0], w_down[0])
+
+    chosen = routes[None, :, :] == experts[:, None, None]
+    share = jnp.sum(jnp.where(chosen, combine_weights[None, :, :], 0.0), axis=2)
+    lines = jnp.stack(pieces(share)).reshape(-1, width)
+    lines = jnp.pad(lines, ((0, EXTRA - lines.shape[0]), (0, 0)))
+    a0 = jnp.concatenate([latent_in[:mid], cotangent[:mid], lines], axis=0)
+    b0 = jnp.concatenate([latent_in[mid:], cotangent[mid:]], axis=0)
+    a0, b0, own = fence(a0, b0, own)
+
+    a4, a2, a1, b4 = swap(a0, SIDE), swap(a0, FAR), swap(a0, NEAR), swap(b0, SIDE)
+    gate_w = swap(own[0], CORE)
+    a0, b0, a1, a2, a4, b4, gate_w, own = fence(a0, b0, a1, a2, a4, b4, gate_w, own)
+    a6, a5, b2, a3 = swap(a2, SIDE), swap(a1, SIDE), swap(b0, FAR), swap(a2, NEAR)
+    up_w = swap(own[1], CORE)
+    a0, b0, a3, a5, a6, b2, up_w, own = fence(a0, b0, a3, a5, a6, b2, up_w, own)
+    a7, b6, b1, b3 = swap(a3, SIDE), swap(b2, SIDE), swap(b0, NEAR), swap(b2, NEAR)
+    down_w = swap(own[2], CORE)
+    a0, b0, a7, b1, b3, b6, down_w, own = fence(a0, b0, a7, b1, b3, b6, down_w, own)
+    b5, b7 = swap(b1, SIDE), swap(b3, SIDE)
+    weights, me = (own, (gate_w, up_w, down_w)), me.astype(jnp.int32).reshape(1)
+    a = [a0, a1, a2, a3, a4, a5, a6, a7]
+    q, (*a_factors, shares, inners) = both_ways(0, a, weights, me)
+    q, shares, inners, b5, b7 = fence(q, shares, inners, b5, b7)
+    q7, q5 = swap(q[7], SIDE), swap(q[5], SIDE)
+    b = [b0, b1, b2, b3, b4, b5, b6, b7]
+    p, b_factors = both_ways(1, b, weights, me, (shares, inners))
+    p, q, q7, q5, b_factors = fence(p, q, q7, q5, b_factors)
+    factors = (a_factors, b_factors)
+    q3, q1 = narrow(added(q[3], q7)), narrow(added(q[1], q5))
+    q3, q1, p, q = fence(q3, q1, p, q)
+    q6, p7, q3, q1 = swap(q[6], SIDE), swap(p[7], SIDE), swap(q3, NEAR), swap(q1, NEAR)
+    away = weight_grads(1, (a, b), factors)
+    p, q, q6, p7, q3, q1, away = fence(p, q, q6, p7, q3, q1, away)
+    q2, p3 = narrow(added(q[2], q6) + q3.astype(f32)), narrow(added(p[3], p7))
+    q2, p3, p, q, away = fence(q2, p3, p, q, away)
+    p6, p5, q2, p3 = swap(p[6], SIDE), swap(p[5], SIDE), swap(q2, FAR), swap(p3, NEAR)
+    away = swap(away, CORE)
+    p, q, p6, p5, q2, p3, away = fence(p, q, p6, p5, q2, p3, away)
+    p2, p1 = narrow(added(p[2], p6) + p3.astype(f32)), narrow(added(p[1], p5))
+    p2, p1, p, q, away = fence(p2, p1, p, q, away)
+    p4, q4, p2, p1 = swap(p[4], SIDE), swap(q[4], SIDE), swap(p2, FAR), swap(p1, NEAR)
+    grad_w = weight_grads(0, (a, b), factors, away)
+    p4, q4, p2, p1, grad_w = fence(p4, q4, p2, p1, grad_w)
+
+    q = added(q[0], q4) + added(q1, q2)
+    p = added(p[0], p4) + added(p1, p2)
+    combined = narrow(jnp.concatenate([q[:mid], p[:mid]], axis=0))
+    grad_latent = narrow(jnp.concatenate([q[mid : 2 * mid], p[mid : 2 * mid]], axis=0))
+    inner = p[2 * mid :].reshape(-1, devices_ep, tok_count)[:3].sum(axis=0)
+    grad_combine = jnp.sum(jnp.where(chosen, inner[:, :, None], 0.0), axis=0)
+    return (combined, grad_latent, grad_combine, *[v[None] for v in grad_w])
+
+
+def local(latent_in, routes, combine_weights, cotangent, w_gate, w_up, w_down):
+    plan = paired if w_gate.shape[0] == 1 and lax.axis_size("ep") == 2 * len(REACH) else exchanged
+    return plan(latent_in, routes, combine_weights, cotangent, w_gate, w_up, w_down)
+
+
 def solution(mesh):
     return jax.shard_map(
         local,

time: 337 us -> 135 us (0.40)
  the two profiles are of different devices: /device:TPU:11 before, /device:TPU:0 now
where the time goes in v6:
time: 135 us
  waiting for transfers between devices  54.7 us (41%)
  Pallas kernels  41.4 us (31%)
  starting transfers between devices  32.9 us (24%)
  other arithmetic  3.77 us (3%)
  local copies, waits for them, and re-layouts  1.36 us (1%)
    ppermute x32, waiting for transfers between devices, swap(): return lax.ppermute(value, 'ep', pairs)  54.7 us
    pallas_call x4, Pallas kernels, kernel(): pl.pallas_call(body, out_shape=outs, in_specs=in_specs, out_specs=[pl.Blo...  41.4 us
    ppermute x32, starting transfers between devices, swap(): return lax.ppermute(value, 'ep', pairs)  32.9 us
  transfers between devices with their start and end apart: 32, of which 9 were waited for; matrix products, arithmetic and copies ran while one was open for 0% of the time, Pallas kernels for 31%

profile of v6, /device:TPU:0, one launch (start us, length us, event | category | flops | bytes accessed | tf_op | source)
XLA Modules:
  0.0 135.3 jit_solution(13608445279203808049)
XLA Ops:
  1.4 1.1 fusion.6
  3.2 2.7 %collective-permute-start = (bf16[144,1024]{1,0:T(8,128)(2,1)S(1)}, bf16[144,1024]{1,0:T(8,128)(2,1)S(1)}, u32[]{:S(2)}, u32[]{:S(2)}) collective-permute-start(bf16[144,1024]{1,0:T(8,128)(2,1)S(1)} %fusion.1.refs_0_), channel_id=1, source_target_pairs={{0,4},{1,5},{2,6},{3,7},{4,0},{5,1},{6,2},{7,3},{8,12},{9,13},{10,... | collective-permute-start | bytes 884744 | tf_op jit(solution)/shard_map/ppermute | solution.py:115
  5.8 2.6 %collective-permute-start.1 = (bf16[144,1024]{1,0:T(8,128)(2,1)S(1)}, bf16[144,1024]{1,0:T(8,128)(2,1)S(1)}, u32[]{:S(2)}, u32[]{:S(2)}) collective-permute-start(bf16[144,1024]{1,0:T(8,128)(2,1)S(1)} %fusion.1.refs_0_), channel_id=1, source_target_pairs={{0,8},{1,9},{2,10},{3,11},{4,12},{5,13},{6,14},{7,15},{8,0},{9,1},... | collective-permute-start | bytes 884744 | tf_op jit(solution)/shard_map/ppermute | solution.py:115
  8.4 1.5 %collective-permute-start.2 = (bf16[144,1024]{1,0:T(8,128)(2,1)S(1)}, bf16[144,1024]{1,0:T(8,128)(2,1)S(1)}, u32[]{:S(2)}, u32[]{:S(2)}) collective-permute-start(bf16[144,1024]{1,0:T(8,128)(2,1)S(1)} %fusion.1.refs_0_), channel_id=1, source_target_pairs={{0,2},{1,3},{2,0},{3,1},{4,6},{5,7},{6,4},{7,5},{8,10},{9,11},{10,... | collective-permute-start | bytes 884744 | tf_op jit(solution)/shard_map/ppermute | solution.py:115
  10.4 12.4 %collective-permute-done.3.refs_4_.refs_12_ = bf16[128,1024]{1,0:T(8,128)(2,1)S(1)} collective-permute-done((bf16[128,1024]{1,0:T(8,128)(2,1)S(1)}, bf16[128,1024]{1,0:T(8,128)(2,1)S(1)}, u32[]{:S(2)}, u32[]{:S(2)}) %collective-permute-start.3) | collective-permute-done | bytes 262176 | tf_op jit(solution)/shard_map/ppermute | solution.py:115
  23.5 1.5 %collective-permute-start.7 = (bf16[144,1024]{1,0:T(8,128)(2,1)S(1)}, bf16[144,1024]{1,0:T(8,128)(2,1)S(1)}, u32[]{:S(2)}, u32[]{:S(2)}) collective-permute-start(bf16[144,1024]{1,0:T(8,128)(2,1)S(1)} %collective-permute-done.1.refs_2_), channel_id=1, source_target_pairs={{0,2},{1,3},{2,0},{3,1},{4,6},{5,7},{6,4},{7,5},{8,10},{9,11},{10,... | collective-permute-start | bytes 884744 | tf_op jit(solution)/shard_map/ppermute | solution.py:115
  25.5 1.9 %collective-permute-start.8 = (bf16[128,1024]{1,0:T(8,128)(2,1)S(1)}, bf16[128,1024]{1,0:T(8,128)(2,1)S(1)}, u32[]{:S(2)}, u32[]{:S(2)}) collective-permute-start(bf16[128,1024]{1,0:T(8,128)(2,1)S(1)} %pad_maximum_fusion.refs_0_.refs_8_), channel_id=1, source_target_pairs={{0,8},{1,9},{2,10},{3,11},{4,12},{5,13},{6,14},{7,15},{8,0},{9,1},... | collective-permute-start | bytes 786440 | tf_op jit(solution)/shard_map/ppermute | solution.py:115
  27.4 12.5 %collective-permute-done.8.refs_2_.refs_10_ = bf16[128,1024]{1,0:T(8,128)(2,1)S(1)} collective-permute-done((bf16[128,1024]{1,0:T(8,128)(2,1)S(1)}, bf16[128,1024]{1,0:T(8,128)(2,1)S(1)}, u32[]{:S(2)}, u32[]{:S(2)}) %collective-permute-start.8) | collective-permute-done | bytes 262176 | tf_op jit(solution)/shard_map/ppermute | solution.py:115
  40.1 1.5 %collective-permute-start.10 = (bf16[144,1024]{1,0:T(8,128)(2,1)S(1)}, bf16[144,1024]{1,0:T(8,128)(2,1)S(1)}, u32[]{:S(2)}, u32[]{:S(2)}) collective-permute-start(bf16[144,1024]{1,0:T(8,128)(2,1)S(1)} %collective-permute-done.5.refs_3_), channel_id=1, source_target_pairs={{0,2},{1,3},{2,0},{3,1},{4,6},{5,7},{6,4},{7,5},{8,10},{9,11},{10,... | collective-permute-start | bytes 884744 | tf_op jit(solution)/shard_map/ppermute | solution.py:115
  42.1 1.6 %collective-permute-start.12 = (bf16[128,1024]{1,0:T(8,128)(2,1)S(1)}, bf16[128,1024]{1,0:T(8,128)(2,1)}, u32[]{:S(2)}, u32[]{:S(2)}) collective-permute-start(bf16[128,1024]{1,0:T(8,128)(2,1)S(1)} %collective-permute-done.8.refs_2_.refs_10_), channel_id=1, source_target_pairs={{0,4},{1,5},{2,6},{3,7},{4,0},{5,1},{6,2},{7,3},{8,12},{9,13},{10,... | collective-permute-start | bytes 786440 | tf_op jit(solution)/shard_map/ppermute | solution.py:115
  44.2 6.6 %collective-permute-done.11.refs_1_.refs_9_ = bf16[128,1024]{1,0:T(8,128)(2,1)S(1)} collective-permute-done((bf16[128,1024]{1,0:T(8,128)(2,1)S(1)}, bf16[128,1024]{1,0:T(8,128)(2,1)S(1)}, u32[]{:S(2)}, u32[]{:S(2)}) %collective-permute-start.11) | collective-permute-done | bytes 262176 | tf_op jit(solution)/shard_map/ppermute | solution.py:115
  50.8 4.9 %collective-permute-done.12.refs_3_.refs_11_ = bf16[128,1024]{1,0:T(8,128)(2,1)} collective-permute-done((bf16[128,1024]{1,0:T(8,128)(2,1)S(1)}, bf16[128,1024]{1,0:T(8,128)(2,1)}, u32[]{:S(2)}, u32[]{:S(2)}) %collective-permute-start.12) | collective-permute-done | bytes 262176 | tf_op jit(solution)/shard_map/ppermute | solution.py:115
  55.7 1.0 collective-permute-start.15
  56.8 1.1 collective-permute-start.16
  57.9 12.8 %shard_map.118 = (bf16[128,1024]{1,0:T(8,128)(2,1)}, bf16[128,1024]{1,0:T(8,128)(2,1)}, bf16[128,1024]{1,0:T(8,128)(2,1)}, bf16[128,1024]{1,0:T(8,128)(2,1)}, bf...) custom-call(s32[1]{0:T(128)} %bitcast.me_ref, ...), custom_call_target="tpu_custom_call" | custom-call | flops 6442450944 | bytes 14024704 | tf_op jit(solution)/shard_map/pallas_call | solution.py:162
  70.8 1.0 collective-permute-start.17
  71.8 1.1 collective-permute-start.18
  72.9 12.9 %shard_map.119 = (bf16[144,1024]{1,0:T(8,128)(2,1)}, bf16[144,1024]{1,0:T(8,128)(2,1)}, bf16[144,1024]{1,0:T(8,128)(2,1)}, bf16[144,1024]{1,0:T(8,128)(2,1)}, bf...) custom-call(s32[1]{0:T(128)} %bitcast.me_ref, ...), custom_call_target="tpu_custom_call" | custom-call | flops 6442450944 | bytes 14024704 | tf_op jit(solution)/shard_map/pallas_call | solution.py:162
  85.9 1.0 collective-permute-start.20
  87.0 1.0 collective-permute-start.19
  88.5 1.5 %collective-permute-start.22 = (bf16[128,1024]{1,0:T(8,128)(2,1)S(1)}, bf16[128,1024]{1,0:T(8,128)(2,1)S(1)}, u32[]{:S(2)}, u32[]{:S(2)}) collective-permute-start(bf16[128,1024]{1,0:T(8,128)(2,1)S(1)} %add_convert_fusion.5), channel_id=1, source_target_pairs={{0,4},{1,5},{2,6},{3,7},{4,0},{5,1},{6,2},{7,3},{8,12},{9,13},{10,... | collective-permute-start | bytes 786440 | tf_op jit(solution)/shard_map/ppermute | solution.py:115
  90.1 7.4 %shard_map.120 = bf16[1536,1024]{1,0:T(8,128)(2,1)} custom-call(bf16[144,1024]{1,0:T(8,128)(2,1)} %copy-done.1, bf16[144,1024]{1,0:T(8,128)(2,1)} %copy-done.3, bf16[144,1024]{1,0:T(8,128)(2,1)} %copy-done.4, bf16[144,1024]{1,0:T(8,128)(2,1)} %copy-done.6, bf16[144,1024]{1,0:T(8,128)(2,1)} %copy-done.5, bf16[144,1024]{1,0:T(8,128)(2,1)} %copy-done.8, ...), custom_call_target="tpu_custom_call" | custom-call | flops 3221225472 | bytes 13893632 | tf_op jit(solution)/shard_map/pallas_call | solution.py:162
  97.5 1.4 %collective-permute-done.19 = bf16[128,1024]{1,0:T(8,128)(2,1)S(1)} collective-permute-done((bf16[128,1024]{1,0:T(8,128)(2,1)S(1)}, bf16[128,1024]{1,0:T(8,128)(2,1)S(1)}, u32[]{:S(2)}, u32[]{:S(2)}) %collective-permute-start.19) | collective-permute-done | bytes 262176 | tf_op jit(solution)/shard_map/ppermute | solution.py:115
  99.8 1.4 %collective-permute-start.23 = (bf16[144,1024]{1,0:T(8,128)(2,1)S(1)}, bf16[144,1024]{1,0:T(8,128)(2,1)S(1)}, u32[]{:S(2)}, u32[]{:S(2)}) collective-permute-start(bf16[144,1024]{1,0:T(8,128)(2,1)S(1)} %copy-done.28), channel_id=1, source_target_pairs={{0,2},{1,3},{2,0},{3,1},{4,6},{5,7},{6,4},{7,5},{8,10},{9,11},{10,... | collective-permute-start | bytes 884744 | tf_op jit(solution)/shard_map/ppermute | solution.py:115
  102.4 1.6 %collective-permute-start.25 = (bf16[128,1024]{1,0:T(8,128)(2,1)S(1)}, bf16[128,1024]{1,0:T(8,128)(2,1)S(1)}, u32[]{:S(2)}, u32[]{:S(2)}) collective-permute-start(bf16[128,1024]{1,0:T(8,128)(2,1)S(1)} %add_convert_fusion.4), channel_id=1, source_target_pairs={{0,8},{1,9},{2,10},{3,11},{4,12},{5,13},{6,14},{7,15},{8,0},{9,1},... | collective-permute-start | bytes 786440 | tf_op jit(solution)/shard_map/ppermute | solution.py:115
  104.1 12.7 %collective-permute-done.25 = bf16[128,1024]{1,0:T(8,128)(2,1)S(1)} collective-permute-done((bf16[128,1024]{1,0:T(8,128)(2,1)S(1)}, bf16[128,1024]{1,0:T(8,128)(2,1)S(1)}, u32[]{:S(2)}, u32[]{:S(2)}) %collective-permute-start.25) | collective-permute-done | bytes 262176 | tf_op jit(solution)/shard_map/ppermute | solution.py:115
  117.1 1.4 %collective-permute-start.28 = (bf16[144,1024]{1,0:T(8,128)(2,1)S(1)}, bf16[144,1024]{1,0:T(8,128)(2,1)S(1)}, u32[]{:S(2)}, u32[]{:S(2)}) collective-permute-start(bf16[144,1024]{1,0:T(8,128)(2,1)S(1)} %copy-done.26), channel_id=1, source_target_pairs={{0,2},{1,3},{2,0},{3,1},{4,6},{5,7},{6,4},{7,5},{8,10},{9,11},{10,... | collective-permute-start | bytes 884744 | tf_op jit(solution)/shard_map/ppermute | solution.py:115
  118.5 0.9 collective-permute-start.30
  120.1 0.7 collective-permute-start.29
  120.9 8.3 %shard_map.121 = (bf16[1024,512]{1,0:T(8,128)(2,1)}, bf16[1024,512]{1,0:T(8,128)(2,1)}, bf16[512,1024]{1,0:T(8,128)(2,1)}) custom-call(bf16[144,1024]{1,0:T(8,128)(2,1)} %copy-done.1, bf16[144,1024]{1,0:T(8,128)(2,1)} %copy-done.3, bf16[144,1024]{1,0:T(8,128)(2,1)} %copy-done.4, bf16[144,1024]{1,0:T(8,128)(2,1)} %copy-done.6, bf16[144,1024]{1,0:T(8,128)(2,1)} %copy-done.5, ...), custom_call_target="tpu_custom_call" | custom-call | flops 3221225472 | bytes 17039360 | tf_op jit(solution)/shard_map/pallas_call | solution.py:162
  129.2 0.9 collective-permute-done.29
  130.1 2.6 %collective-permute-done.30 = bf16[144,1024]{1,0:T(8,128)(2,1)S(1)} collective-permute-done((bf16[144,1024]{1,0:T(8,128)(2,1)S(1)}, bf16[144,1024]{1,0:T(8,128)(2,1)S(1)}, u32[]{:S(2)}, u32[]{:S(2)}) %collective-permute-start.30) | collective-permute-done | bytes 294944 | tf_op jit(solution)/shard_map/ppermute | solution.py:115
  (122 shorter events, 10.4 us)
Async XLA Ops:
  2.7 20.2 %collective-permute-start.4 = (bf16[1024,512]{1,0:T(8,128)(2,1)}, bf16[1024,512]{1,0:T(8,128)(2,1)S(1)}, u32[]{:S(2)}, u32[]{:S(2)}) collective-permute-start(bf16[1024,512]{1,0:T(8,128)(2,1)} %bitcast.20), channel_id=1, source_target_pairs={{0,1},{1,0},{2,3},{3,2},{4,5},{5,4},{6,7},{7,6},{8,9},{9,8},{10,11... | collective-permute-start | bytes 3145736 | tf_op jit(solution)/shard_map/ppermute | solution.py:115
  3.2 19.7 %collective-permute-start = (bf16[144,1024]{1,0:T(8,128)(2,1)S(1)}, bf16[144,1024]{1,0:T(8,128)(2,1)S(1)}, u32[]{:S(2)}, u32[]{:S(2)}) collective-permute-start(bf16[144,1024]{1,0:T(8,128)(2,1)S(1)} %fusion.1.refs_0_), channel_id=1, source_target_pairs={{0,4},{1,5},{2,6},{3,7},{4,0},{5,1},{6,2},{7,3},{8,12},{9,13},{10,... | collective-permute-start | bytes 884744 | tf_op jit(solution)/shard_map/ppermute | solution.py:115
  5.8 17.0 %collective-permute-start.1 = (bf16[144,1024]{1,0:T(8,128)(2,1)S(1)}, bf16[144,1024]{1,0:T(8,128)(2,1)S(1)}, u32[]{:S(2)}, u32[]{:S(2)}) collective-permute-start(bf16[144,1024]{1,0:T(8,128)(2,1)S(1)} %fusion.1.refs_0_), channel_id=1, source_target_pairs={{0,8},{1,9},{2,10},{3,11},{4,12},{5,13},{6,14},{7,15},{8,0},{9,1},... | collective-permute-start | bytes 884744 | tf_op jit(solution)/shard_map/ppermute | solution.py:115
  8.4 14.4 %collective-permute-start.2 = (bf16[144,1024]{1,0:T(8,128)(2,1)S(1)}, bf16[144,1024]{1,0:T(8,128)(2,1)S(1)}, u32[]{:S(2)}, u32[]{:S(2)}) collective-permute-start(bf16[144,1024]{1,0:T(8,128)(2,1)S(1)} %fusion.1.refs_0_), channel_id=1, source_target_pairs={{0,2},{1,3},{2,0},{3,1},{4,6},{5,7},{6,4},{7,5},{8,10},{9,11},{10,... | collective-permute-start | bytes 884744 | tf_op jit(solution)/shard_map/ppermute | solution.py:115
  9.9 12.9 %collective-permute-start.3 = (bf16[128,1024]{1,0:T(8,128)(2,1)S(1)}, bf16[128,1024]{1,0:T(8,128)(2,1)S(1)}, u32[]{:S(2)}, u32[]{:S(2)}) collective-permute-start(bf16[128,1024]{1,0:T(8,128)(2,1)S(1)} %pad_maximum_fusion.refs_0_.refs_8_), channel_id=1, source_target_pairs={{0,2},{1,3},{2,0},{3,1},{4,6},{5,7},{6,4},{7,5},{8,10},{9,11},{10,... | collective-permute-start | bytes 786440 | tf_op jit(solution)/shard_map/ppermute | solution.py:115
  22.9 17.1 %collective-permute-start.9 = (bf16[1024,512]{1,0:T(8,128)(2,1)}, bf16[1024,512]{1,0:T(8,128)(2,1)S(1)}, u32[]{:S(2)}, u32[]{:S(2)}) collective-permute-start(bf16[1024,512]{1,0:T(8,128)(2,1)} %bitcast.23), channel_id=1, source_target_pairs={{0,1},{1,0},{2,3},{3,2},{4,5},{5,4},{6,7},{7,6},{8,9},{9,8},{10,11... | collective-permute-start | bytes 3145736 | tf_op jit(solution)/shard_map/ppermute | solution.py:115
  23.0 16.9 %collective-permute-start.5 = (bf16[144,1024]{1,0:T(8,128)(2,1)S(1)}, bf16[144,1024]{1,0:T(8,128)(2,1)S(1)}, u32[]{:S(2)}, u32[]{:S(2)}) collective-permute-start(bf16[144,1024]{1,0:T(8,128)(2,1)S(1)} %collective-permute-done.1.refs_2_), channel_id=1, source_target_pairs={{0,4},{1,5},{2,6},{3,7},{4,0},{5,1},{6,2},{7,3},{8,12},{9,13},{10,... | collective-permute-start | bytes 884744 | tf_op jit(solution)/shard_map/ppermute | solution.py:115
  23.5 16.4 %collective-permute-start.7 = (bf16[144,1024]{1,0:T(8,128)(2,1)S(1)}, bf16[144,1024]{1,0:T(8,128)(2,1)S(1)}, u32[]{:S(2)}, u32[]{:S(2)}) collective-permute-start(bf16[144,1024]{1,0:T(8,128)(2,1)S(1)} %collective-permute-done.1.refs_2_), channel_id=1, source_target_pairs={{0,2},{1,3},{2,0},{3,1},{4,6},{5,7},{6,4},{7,5},{8,10},{9,11},{10,... | collective-permute-start | bytes 884744 | tf_op jit(solution)/shard_map/ppermute | solution.py:115
  25.0 15.0 %collective-permute-start.6 = (bf16[144,1024]{1,0:T(8,128)(2,1)S(1)}, bf16[144,1024]{1,0:T(8,128)(2,1)S(1)}, u32[]{:S(2)}, u32[]{:S(2)}) collective-permute-start(bf16[144,1024]{1,0:T(8,128)(2,1)S(1)} %collective-permute-done.refs_1_), channel_id=1, source_target_pairs={{0,2},{1,3},{2,0},{3,1},{4,6},{5,7},{6,4},{7,5},{8,10},{9,11},{10,... | collective-permute-start | bytes 884744 | tf_op jit(solution)/shard_map/ppermute | solution.py:115
  25.5 14.4 %collective-permute-start.8 = (bf16[128,1024]{1,0:T(8,128)(2,1)S(1)}, bf16[128,1024]{1,0:T(8,128)(2,1)S(1)}, u32[]{:S(2)}, u32[]{:S(2)}) collective-permute-start(bf16[128,1024]{1,0:T(8,128)(2,1)S(1)} %pad_maximum_fusion.refs_0_.refs_8_), channel_id=1, source_target_pairs={{0,8},{1,9},{2,10},{3,11},{4,12},{5,13},{6,14},{7,15},{8,0},{9,1},... | collective-permute-start | bytes 786440 | tf_op jit(solution)/shard_map/ppermute | solution.py:115
  40.0 15.7 %collective-permute-start.14 = (bf16[512,1024]{1,0:T(8,128)(2,1)}, bf16[512,1024]{1,0:T(8,128)(2,1)}, u32[]{:S(2)}, u32[]{:S(2)}) collective-permute-start(bf16[512,1024]{1,0:T(8,128)(2,1)} %bitcast.26), channel_id=1, source_target_pairs={{0,1},{1,0},{2,3},{3,2},{4,5},{5,4},{6,7},{7,6},{8,9},{9,8},{10,11... | collective-permute-start | bytes 3145736 | tf_op jit(solution)/shard_map/ppermute | solution.py:115
  40.1 15.6 %collective-permute-start.10 = (bf16[144,1024]{1,0:T(8,128)(2,1)S(1)}, bf16[144,1024]{1,0:T(8,128)(2,1)S(1)}, u32[]{:S(2)}, u32[]{:S(2)}) collective-permute-start(bf16[144,1024]{1,0:T(8,128)(2,1)S(1)} %collective-permute-done.5.refs_3_), channel_id=1, source_target_pairs={{0,2},{1,3},{2,0},{3,1},{4,6},{5,7},{6,4},{7,5},{8,10},{9,11},{10,... | collective-permute-start | bytes 884744 | tf_op jit(solution)/shard_map/ppermute | solution.py:115
  41.6 9.2 %collective-permute-start.11 = (bf16[128,1024]{1,0:T(8,128)(2,1)S(1)}, bf16[128,1024]{1,0:T(8,128)(2,1)S(1)}, u32[]{:S(2)}, u32[]{:S(2)}) collective-permute-start(bf16[128,1024]{1,0:T(8,128)(2,1)S(1)} %pad_maximum_fusion.refs_0_.refs_8_), channel_id=1, source_target_pairs={{0,4},{1,5},{2,6},{3,7},{4,0},{5,1},{6,2},{7,3},{8,12},{9,13},{10,... | collective-permute-start | bytes 786440 | tf_op jit(solution)/shard_map/ppermute | solution.py:115
  42.1 13.6 %collective-permute-start.12 = (bf16[128,1024]{1,0:T(8,128)(2,1)S(1)}, bf16[128,1024]{1,0:T(8,128)(2,1)}, u32[]{:S(2)}, u32[]{:S(2)}) collective-permute-start(bf16[128,1024]{1,0:T(8,128)(2,1)S(1)} %collective-permute-done.8.refs_2_.refs_10_), channel_id=1, source_target_pairs={{0,4},{1,5},{2,6},{3,7},{4,0},{5,1},{6,2},{7,3},{8,12},{9,13},{10,... | collective-permute-start | bytes 786440 | tf_op jit(solution)/shard_map/ppermute | solution.py:115
  43.7 12.0 %collective-permute-start.13 = (bf16[128,1024]{1,0:T(8,128)(2,1)S(1)}, bf16[128,1024]{1,0:T(8,128)(2,1)}, u32[]{:S(2)}, u32[]{:S(2)}) collective-permute-start(bf16[128,1024]{1,0:T(8,128)(2,1)S(1)} %collective-permute-done.8.refs_2_.refs_10_), channel_id=1, source_target_pairs={{0,2},{1,3},{2,0},{3,1},{4,6},{5,7},{6,4},{7,5},{8,10},{9,11},{10,... | collective-permute-start | bytes 786440 | tf_op jit(solution)/shard_map/ppermute | solution.py:115
  55.7 15.0 %collective-permute-start.15 = (bf16[128,1024]{1,0:T(8,128)(2,1)S(1)}, bf16[128,1024]{1,0:T(8,128)(2,1)S(1)}, u32[]{:S(2)}, u32[]{:S(2)}) collective-permute-start(bf16[128,1024]{1,0:T(8,128)(2,1)S(1)} %collective-permute-done.11.refs_1_.refs_9_), channel_id=1, source_target_pairs={{0,2},{1,3},{2,0},{3,1},{4,6},{5,7},{6,4},{7,5},{8,10},{9,11},{10,... | collective-permute-start | bytes 786440 | tf_op jit(solution)/shard_map/ppermute | solution.py:115
  56.8 14.0 %collective-permute-start.16 = (bf16[128,1024]{1,0:T(8,128)(2,1)}, bf16[128,1024]{1,0:T(8,128)(2,1)S(1)}, u32[]{:S(2)}, u32[]{:S(2)}) collective-permute-start(bf16[128,1024]{1,0:T(8,128)(2,1)} %collective-permute-done.12.refs_3_.refs_11_), channel_id=1, source_target_pairs={{0,2},{1,3},{2,0},{3,1},{4,6},{5,7},{6,4},{7,5},{8,10},{9,11},{10,... | collective-permute-start | bytes 786440 | tf_op jit(solution)/shard_map/ppermute | solution.py:115
  70.8 15.0 %collective-permute-start.17 = (bf16[128,1024]{1,0:T(8,128)(2,1)}, bf16[128,1024]{1,0:T(8,128)(2,1)S(1)}, u32[]{:S(2)}, u32[]{:S(2)}) collective-permute-start(bf16[128,1024]{1,0:T(8,128)(2,1)} %get-tuple-element.225), channel_id=1, source_target_pairs={{0,2},{1,3},{2,0},{3,1},{4,6},{5,7},{6,4},{7,5},{8,10},{9,11},{10,... | collective-permute-start | bytes 786440 | tf_op jit(solution)/shard_map/ppermute | solution.py:115
  71.8 13.9 %collective-permute-start.18 = (bf16[128,1024]{1,0:T(8,128)(2,1)}, bf16[128,1024]{1,0:T(8,128)(2,1)S(1)}, u32[]{:S(2)}, u32[]{:S(2)}) collective-permute-start(bf16[128,1024]{1,0:T(8,128)(2,1)} %get-tuple-element.223), channel_id=1, source_target_pairs={{0,2},{1,3},{2,0},{3,1},{4,6},{5,7},{6,4},{7,5},{8,10},{9,11},{10,... | collective-permute-start | bytes 786440 | tf_op jit(solution)/shard_map/ppermute | solution.py:115
  85.9 13.5 %collective-permute-start.20 = (bf16[144,1024]{1,0:T(8,128)(2,1)}, bf16[144,1024]{1,0:T(8,128)(2,1)S(1)}, u32[]{:S(2)}, u32[]{:S(2)}) collective-permute-start(bf16[144,1024]{1,0:T(8,128)(2,1)} %get-tuple-element.251), channel_id=1, source_target_pairs={{0,2},{1,3},{2,0},{3,1},{4,6},{5,7},{6,4},{7,5},{8,10},{9,11},{10,... | collective-permute-start | bytes 884744 | tf_op jit(solution)/shard_map/ppermute | solution.py:115
  87.0 11.9 %collective-permute-start.19 = (bf16[128,1024]{1,0:T(8,128)(2,1)S(1)}, bf16[128,1024]{1,0:T(8,128)(2,1)S(1)}, u32[]{:S(2)}, u32[]{:S(2)}) collective-permute-start(bf16[128,1024]{1,0:T(8,128)(2,1)S(1)} %copy-done.30), channel_id=1, source_target_pairs={{0,2},{1,3},{2,0},{3,1},{4,6},{5,7},{6,4},{7,5},{8,10},{9,11},{10,... | collective-permute-start | bytes 786440 | tf_op jit(solution)/shard_map/ppermute | solution.py:115
  88.0 10.9 %collective-permute-start.21 = (bf16[128,1024]{1,0:T(8,128)(2,1)S(1)}, bf16[128,1024]{1,0:T(8,128)(2,1)S(1)}, u32[]{:S(2)}, u32[]{:S(2)}) collective-permute-start(bf16[128,1024]{1,0:T(8,128)(2,1)S(1)} %add_convert_fusion.6), channel_id=1, source_target_pairs={{0,4},{1,5},{2,6},{3,7},{4,0},{5,1},{6,2},{7,3},{8,12},{9,13},{10,... | collective-permute-start | bytes 786440 | tf_op jit(solution)/shard_map/ppermute | solution.py:115
  88.5 10.9 %collective-permute-start.22 = (bf16[128,1024]{1,0:T(8,128)(2,1)S(1)}, bf16[128,1024]{1,0:T(8,128)(2,1)S(1)}, u32[]{:S(2)}, u32[]{:S(2)}) collective-permute-start(bf16[128,1024]{1,0:T(8,128)(2,1)S(1)} %add_convert_fusion.5), channel_id=1, source_target_pairs={{0,4},{1,5},{2,6},{3,7},{4,0},{5,1},{6,2},{7,3},{8,12},{9,13},{10,... | collective-permute-start | bytes 786440 | tf_op jit(solution)/shard_map/ppermute | solution.py:115
  99.7 17.1 %collective-permute-start.27 = (bf16[1536,1024]{1,0:T(8,128)(2,1)}, bf16[1536,1024]{1,0:T(8,128)(2,1)S(1)}, u32[]{:S(2)}, u32[]{:S(2)}) collective-permute-start(bf16[1536,1024]{1,0:T(8,128)(2,1)} %shard_map.120), channel_id=1, source_target_pairs={{0,1},{1,0},{2,3},{3,2},{4,5},{5,4},{6,7},{7,6},{8,9},{9,8},{10,11... | collective-permute-start | bytes 9437192 | tf_op jit(solution)/shard_map/ppermute | solution.py:115
  99.8 17.0 %collective-permute-start.23 = (bf16[144,1024]{1,0:T(8,128)(2,1)S(1)}, bf16[144,1024]{1,0:T(8,128)(2,1)S(1)}, u32[]{:S(2)}, u32[]{:S(2)}) collective-permute-start(bf16[144,1024]{1,0:T(8,128)(2,1)S(1)} %copy-done.28), channel_id=1, source_target_pairs={{0,2},{1,3},{2,0},{3,1},{4,6},{5,7},{6,4},{7,5},{8,10},{9,11},{10,... | collective-permute-start | bytes 884744 | tf_op jit(solution)/shard_map/ppermute | solution.py:115
  101.2 15.6 %collective-permute-start.24 = (bf16[144,1024]{1,0:T(8,128)(2,1)S(1)}, bf16[144,1024]{1,0:T(8,128)(2,1)S(1)}, u32[]{:S(2)}, u32[]{:S(2)}) collective-permute-start(bf16[144,1024]{1,0:T(8,128)(2,1)S(1)} %copy-done.27), channel_id=1, source_target_pairs={{0,2},{1,3},{2,0},{3,1},{4,6},{5,7},{6,4},{7,5},{8,10},{9,11},{10,... | collective-permute-start | bytes 884744 | tf_op jit(solution)/shard_map/ppermute | solution.py:115
  101.9 14.9 %collective-permute-start.26 = (bf16[144,1024]{1,0:T(8,128)(2,1)S(1)}, bf16[144,1024]{1,0:T(8,128)(2,1)S(1)}, u32[]{:S(2)}, u32[]{:S(2)}) collective-permute-start(bf16[144,1024]{1,0:T(8,128)(2,1)S(1)} %add_convert_fusion.2), channel_id=1, source_target_pairs={{0,4},{1,5},{2,6},{3,7},{4,0},{5,1},{6,2},{7,3},{8,12},{9,13},{10,... | collective-permute-start | bytes 884744 | tf_op jit(solution)/shard_map/ppermute | solution.py:115
  102.4 14.4 %collective-permute-start.25 = (bf16[128,1024]{1,0:T(8,128)(2,1)S(1)}, bf16[128,1024]{1,0:T(8,128)(2,1)S(1)}, u32[]{:S(2)}, u32[]{:S(2)}) collective-permute-start(bf16[128,1024]{1,0:T(8,128)(2,1)S(1)} %add_convert_fusion.4), channel_id=1, source_target_pairs={{0,8},{1,9},{2,10},{3,11},{4,12},{5,13},{6,14},{7,15},{8,0},{9,1},... | collective-permute-start | bytes 786440 | tf_op jit(solution)/shard_map/ppermute | solution.py:115
  117.1 13.0 %collective-permute-start.28 = (bf16[144,1024]{1,0:T(8,128)(2,1)S(1)}, bf16[144,1024]{1,0:T(8,128)(2,1)S(1)}, u32[]{:S(2)}, u32[]{:S(2)}) collective-permute-start(bf16[144,1024]{1,0:T(8,128)(2,1)S(1)} %copy-done.26), channel_id=1, source_target_pairs={{0,2},{1,3},{2,0},{3,1},{4,6},{5,7},{6,4},{7,5},{8,10},{9,11},{10,... | collective-permute-start | bytes 884744 | tf_op jit(solution)/shard_map/ppermute | solution.py:115
  118.5 14.2 %collective-permute-start.30 = (bf16[144,1024]{1,0:T(8,128)(2,1)S(1)}, bf16[144,1024]{1,0:T(8,128)(2,1)S(1)}, u32[]{:S(2)}, u32[]{:S(2)}) collective-permute-start(bf16[144,1024]{1,0:T(8,128)(2,1)S(1)} %add_convert_fusion.1), channel_id=1, source_target_pairs={{0,8},{1,9},{2,10},{3,11},{4,12},{5,13},{6,14},{7,15},{8,0},{9,1},... | collective-permute-start | bytes 884744 | tf_op jit(solution)/shard_map/ppermute | solution.py:115
  119.4 13.3 %collective-permute-start.31 = (bf16[144,1024]{1,0:T(8,128)(2,1)S(1)}, bf16[144,1024]{1,0:T(8,128)(2,1)S(1)}, u32[]{:S(2)}, u32[]{:S(2)}) collective-permute-start(bf16[144,1024]{1,0:T(8,128)(2,1)S(1)} %add_convert_fusion), channel_id=1, source_target_pairs={{0,4},{1,5},{2,6},{3,7},{4,0},{5,1},{6,2},{7,3},{8,12},{9,13},{10,... | collective-permute-start | bytes 884744 | tf_op jit(solution)/shard_map/ppermute | solution.py:115
  120.1 9.9 %collective-permute-start.29 = (bf16[128,1024]{1,0:T(8,128)(2,1)S(1)}, bf16[128,1024]{1,0:T(8,128)(2,1)S(1)}, u32[]{:S(2)}, u32[]{:S(2)}) collective-permute-start(bf16[128,1024]{1,0:T(8,128)(2,1)S(1)} %copy-done.29), channel_id=1, source_target_pairs={{0,2},{1,3},{2,0},{3,1},{4,6},{5,7},{6,4},{7,5},{8,10},{9,11},{10,... | collective-permute-start | bytes 786440 | tf_op jit(solution)/shard_map/ppermute | solution.py:115
  (31 other events, 631.3 us)

commit v7 on v6

--- a/solution.py
+++ b/solution.py
@@ -418,13 +418,13 @@
 
     a4, a2, a1, b4 = swap(a0, SIDE), swap(a0, FAR), swap(a0, NEAR), swap(b0, SIDE)
     gate_w = swap(own[0], CORE)
-    a0, b0, a1, a2, a4, b4, gate_w, own = fence(a0, b0, a1, a2, a4, b4, gate_w, own)
+    a2, a4, b4, a1, gate_w, a0, b0, own = fence(a2, a4, b4, a1, gate_w, a0, b0, own)
     a6, a5, b2, a3 = swap(a2, SIDE), swap(a1, SIDE), swap(b0, FAR), swap(a2, NEAR)
     up_w = swap(own[1], CORE)
-    a0, b0, a3, a5, a6, b2, up_w, own = fence(a0, b0, a3, a5, a6, b2, up_w, own)
+    b2, a5, a6, a3, up_w, a0, b0, own = fence(b2, a5, a6, a3, up_w, a0, b0, own)
     a7, b6, b1, b3 = swap(a3, SIDE), swap(b2, SIDE), swap(b0, NEAR), swap(b2, NEAR)
     down_w = swap(own[2], CORE)
-    a0, b0, a7, b1, b3, b6, down_w, own = fence(a0, b0, a7, b1, b3, b6, down_w, own)
+    a7, b6, b3, b1, down_w, a0, b0, own = fence(a7, b6, b3, b1, down_w, a0, b0, own)
     b5, b7 = swap(b1, SIDE), swap(b3, SIDE)
     weights, me = (own, (gate_w, up_w, down_w)), me.astype(jnp.int32).reshape(1)
     a = [a0, a1, a2, a3, a4, a5, a6, a7]
@@ -439,17 +439,17 @@
     q3, q1, p, q = fence(q3, q1, p, q)
     q6, p7, q3, q1 = swap(q[6], SIDE), swap(p[7], SIDE), swap(q3, NEAR), swap(q1, NEAR)
     away = weight_grads(1, (a, b), factors)
-    p, q, q6, p7, q3, q1, away = fence(p, q, q6, p7, q3, q1, away)
+    q6, p7, q3, q1, away, p, q = fence(q6, p7, q3, q1, away, p, q)
     q2, p3 = narrow(added(q[2], q6) + q3.astype(f32)), narrow(added(p[3], p7))
     q2, p3, p, q, away = fence(q2, p3, p, q, away)
     p6, p5, q2, p3 = swap(p[6], SIDE), swap(p[5], SIDE), swap(q2, FAR), swap(p3, NEAR)
     away = swap(away, CORE)
-    p, q, p6, p5, q2, p3, away = fence(p, q, p6, p5, q2, p3, away)
+    q2, p6, p5, p3, away, p, q = fence(q2, p6, p5, p3, away, p, q)
     p2, p1 = narrow(added(p[2], p6) + p3.astype(f32)), narrow(added(p[1], p5))
     p2, p1, p, q, away = fence(p2, p1, p, q, away)
     p4, q4, p2, p1 = swap(p[4], SIDE), swap(q[4], SIDE), swap(p2, FAR), swap(p1, NEAR)
     grad_w = weight_grads(0, (a, b), factors, away)
-    p4, q4, p2, p1, grad_w = fence(p4, q4, p2, p1, grad_w)
+    p2, p4, q4, p1, grad_w = fence(p2, p4, q4, p1, grad_w)
 
     q = added(q[0], q4) + added(q1, q2)
     p = added(p[0], p4) + added(p1, p2)

time: 135 us -> 135 us (level)
  transfers between devices with their start and end apart: 32 -> 32, of which waited for: 9 -> 11; matrix products, arithmetic and copies ran while one was open for 0% -> 0% of each run, Pallas kernels for 31% -> 31%
where the time goes in v7:
time: 135 us
  waiting for transfers between devices  53.4 us (40%)
  Pallas kernels  41.4 us (31%)
  starting transfers between devices  34 us (25%)
  other arithmetic  3.77 us (3%)
  local copies, waits for them, and re-layouts  1.36 us (1%)
    ppermute x32, waiting for transfers between devices, swap(): return lax.ppermute(value, 'ep', pairs)  53.4 us
    pallas_call x4, Pallas kernels, kernel(): pl.pallas_call(body, out_shape=outs, in_specs=in_specs, out_specs=[pl.Blo...  41.4 us
    ppermute x32, starting transfers between devices, swap(): return lax.ppermute(value, 'ep', pairs)  34 us
  transfers between devices with their start and end apart: 32, of which 11 were waited for; matrix products, arithmetic and copies ran while one was open for 0% of the time, Pallas kernels for 31%

profile of v7, /device:TPU:0, one launch (start us, length us, event | category | flops | bytes accessed | tf_op | source)
XLA Modules:
  0.0 135.2 jit_solution(11694121849522280809)
XLA Ops:
  0.6 0.7 select_reduce_fusion.1
  1.4 1.1 fusion.6
  3.2 3.7 %collective-permute-start = (bf16[144,1024]{1,0:T(8,128)(2,1)S(1)}, bf16[144,1024]{1,0:T(8,128)(2,1)S(1)}, u32[]{:S(2)}, u32[]{:S(2)}) collective-permute-start(bf16[144,1024]{1,0:T(8,128)(2,1)S(1)} %fusion.1.refs_0_), channel_id=1, source_target_pairs={{0,8},{1,9},{2,10},{3,11},{4,12},{5,13},{6,14},{7,15},{8,0},{9,1},... | collective-permute-start | bytes 884744 | tf_op jit(solution)/shard_map/ppermute | solution.py:115
  6.8 1.5 %collective-permute-start.1 = (bf16[144,1024]{1,0:T(8,128)(2,1)S(1)}, bf16[144,1024]{1,0:T(8,128)(2,1)S(1)}, u32[]{:S(2)}, u32[]{:S(2)}) collective-permute-start(bf16[144,1024]{1,0:T(8,128)(2,1)S(1)} %fusion.1.refs_0_), channel_id=1, source_target_pairs={{0,2},{1,3},{2,0},{3,1},{4,6},{5,7},{6,4},{7,5},{8,10},{9,11},{10,... | collective-permute-start | bytes 884744 | tf_op jit(solution)/shard_map/ppermute | solution.py:115
  8.3 1.6 %collective-permute-start.3 = (bf16[144,1024]{1,0:T(8,128)(2,1)S(1)}, bf16[144,1024]{1,0:T(8,128)(2,1)S(1)}, u32[]{:S(2)}, u32[]{:S(2)}) collective-permute-start(bf16[144,1024]{1,0:T(8,128)(2,1)S(1)} %fusion.1.refs_0_), channel_id=1, source_target_pairs={{0,4},{1,5},{2,6},{3,7},{4,0},{5,1},{6,2},{7,3},{8,12},{9,13},{10,... | collective-permute-start | bytes 884744 | tf_op jit(solution)/shard_map/ppermute | solution.py:115
  10.4 11.1 %collective-permute-done.2.refs_4_.refs_12_ = bf16[128,1024]{1,0:T(8,128)(2,1)S(1)} collective-permute-done((bf16[128,1024]{1,0:T(8,128)(2,1)S(1)}, bf16[128,1024]{1,0:T(8,128)(2,1)S(1)}, u32[]{:S(2)}, u32[]{:S(2)}) %collective-permute-start.2) | collective-permute-done | bytes 262176 | tf_op jit(solution)/shard_map/ppermute | solution.py:115
  22.4 0.9 collective-permute-start.7
  23.2 1.6 %collective-permute-start.8 = (bf16[144,1024]{1,0:T(8,128)(2,1)S(1)}, bf16[144,1024]{1,0:T(8,128)(2,1)S(1)}, u32[]{:S(2)}, u32[]{:S(2)}) collective-permute-start(bf16[144,1024]{1,0:T(8,128)(2,1)S(1)} %collective-permute-done.refs_2_), channel_id=1, source_target_pairs={{0,4},{1,5},{2,6},{3,7},{4,0},{5,1},{6,2},{7,3},{8,12},{9,13},{10,... | collective-permute-start | bytes 884744 | tf_op jit(solution)/shard_map/ppermute | solution.py:115
  25.4 2.2 %collective-permute-start.5 = (bf16[128,1024]{1,0:T(8,128)(2,1)S(1)}, bf16[128,1024]{1,0:T(8,128)(2,1)S(1)}, u32[]{:S(2)}, u32[]{:S(2)}) collective-permute-start(bf16[128,1024]{1,0:T(8,128)(2,1)S(1)} %pad_maximum_fusion.refs_0_.refs_8_), channel_id=1, source_target_pairs={{0,8},{1,9},{2,10},{3,11},{4,12},{5,13},{6,14},{7,15},{8,0},{9,1},... | collective-permute-start | bytes 786440 | tf_op jit(solution)/shard_map/ppermute | solution.py:115
  27.5 12.2 %collective-permute-done.5.refs_2_.refs_10_ = bf16[128,1024]{1,0:T(8,128)(2,1)S(1)} collective-permute-done((bf16[128,1024]{1,0:T(8,128)(2,1)S(1)}, bf16[128,1024]{1,0:T(8,128)(2,1)S(1)}, u32[]{:S(2)}, u32[]{:S(2)}) %collective-permute-start.5) | collective-permute-done | bytes 262176 | tf_op jit(solution)/shard_map/ppermute | solution.py:115
  39.9 1.6 %collective-permute-start.10 = (bf16[144,1024]{1,0:T(8,128)(2,1)S(1)}, bf16[144,1024]{1,0:T(8,128)(2,1)S(1)}, u32[]{:S(2)}, u32[]{:S(2)}) collective-permute-start(bf16[144,1024]{1,0:T(8,128)(2,1)S(1)} %collective-permute-done.8.refs_3_), channel_id=1, source_target_pairs={{0,2},{1,3},{2,0},{3,1},{4,6},{5,7},{6,4},{7,5},{8,10},{9,11},{10,... | collective-permute-start | bytes 884744 | tf_op jit(solution)/shard_map/ppermute | solution.py:115
  42.0 2.0 %collective-permute-start.13 = (bf16[128,1024]{1,0:T(8,128)(2,1)S(1)}, bf16[128,1024]{1,0:T(8,128)(2,1)}, u32[]{:S(2)}, u32[]{:S(2)}) collective-permute-start(bf16[128,1024]{1,0:T(8,128)(2,1)S(1)} %pad_maximum_fusion.refs_0_.refs_8_), channel_id=1, source_target_pairs={{0,4},{1,5},{2,6},{3,7},{4,0},{5,1},{6,2},{7,3},{8,12},{9,13},{10,... | collective-permute-start | bytes 786440 | tf_op jit(solution)/shard_map/ppermute | solution.py:115
  44.0 10.9 %collective-permute-done.11.refs_6_.refs_14_ = bf16[128,1024]{1,0:T(8,128)(2,1)S(1)} collective-permute-done((bf16[128,1024]{1,0:T(8,128)(2,1)S(1)}, bf16[128,1024]{1,0:T(8,128)(2,1)S(1)}, u32[]{:S(2)}, u32[]{:S(2)}) %collective-permute-start.11) | collective-permute-done | bytes 262176 | tf_op jit(solution)/shard_map/ppermute | solution.py:115
  54.9 0.9 collective-permute-done.13.refs_1_.refs_9_
  55.8 1.6 %collective-permute-start.15 = (bf16[128,1024]{1,0:T(8,128)(2,1)}, bf16[128,1024]{1,0:T(8,128)(2,1)S(1)}, u32[]{:S(2)}, u32[]{:S(2)}) collective-permute-start(bf16[128,1024]{1,0:T(8,128)(2,1)} %collective-permute-done.13.refs_1_.refs_9_), channel_id=1, source_target_pairs={{0,2},{1,3},{2,0},{3,1},{4,6},{5,7},{6,4},{7,5},{8,10},{9,11},{10,... | collective-permute-start | bytes 786440 | tf_op jit(solution)/shard_map/ppermute | solution.py:115
  58.0 12.8 %shard_map.118 = (bf16[128,1024]{1,0:T(8,128)(2,1)}, bf16[128,1024]{1,0:T(8,128)(2,1)}, bf16[128,1024]{1,0:T(8,128)(2,1)}, bf16[128,1024]{1,0:T(8,128)(2,1)}, bf...) custom-call(s32[1]{0:T(128)} %bitcast.me_ref, ...), custom_call_target="tpu_custom_call" | custom-call | flops 6442450944 | bytes 14024704 | tf_op jit(solution)/shard_map/pallas_call | solution.py:162
  70.9 1.6 %collective-permute-start.17 = (bf16[128,1024]{1,0:T(8,128)(2,1)}, bf16[128,1024]{1,0:T(8,128)(2,1)S(1)}, u32[]{:S(2)}, u32[]{:S(2)}) collective-permute-start(bf16[128,1024]{1,0:T(8,128)(2,1)} %get-tuple-element.225), channel_id=1, source_target_pairs={{0,2},{1,3},{2,0},{3,1},{4,6},{5,7},{6,4},{7,5},{8,10},{9,11},{10,... | collective-permute-start | bytes 786440 | tf_op jit(solution)/shard_map/ppermute | solution.py:115
  73.0 12.9 %shard_map.119 = (bf16[144,1024]{1,0:T(8,128)(2,1)}, bf16[144,1024]{1,0:T(8,128)(2,1)}, bf16[144,1024]{1,0:T(8,128)(2,1)}, bf16[144,1024]{1,0:T(8,128)(2,1)}, bf...) custom-call(s32[1]{0:T(128)} %bitcast.me_ref, ...), custom_call_target="tpu_custom_call" | custom-call | flops 6442450944 | bytes 14024704 | tf_op jit(solution)/shard_map/pallas_call | solution.py:162
  86.0 1.6 %collective-permute-start.20 = (bf16[144,1024]{1,0:T(8,128)(2,1)}, bf16[144,1024]{1,0:T(8,128)(2,1)S(1)}, u32[]{:S(2)}, u32[]{:S(2)}) collective-permute-start(bf16[144,1024]{1,0:T(8,128)(2,1)} %get-tuple-element.245), channel_id=1, source_target_pairs={{0,2},{1,3},{2,0},{3,1},{4,6},{5,7},{6,4},{7,5},{8,10},{9,11},{10,... | collective-permute-start | bytes 884744 | tf_op jit(solution)/shard_map/ppermute | solution.py:115
  88.4 1.7 %collective-permute-start.22 = (bf16[128,1024]{1,0:T(8,128)(2,1)S(1)}, bf16[128,1024]{1,0:T(8,128)(2,1)S(1)}, u32[]{:S(2)}, u32[]{:S(2)}) collective-permute-start(bf16[128,1024]{1,0:T(8,128)(2,1)S(1)} %add_convert_fusion.5), channel_id=1, source_target_pairs={{0,4},{1,5},{2,6},{3,7},{4,0},{5,1},{6,2},{7,3},{8,12},{9,13},{10,... | collective-permute-start | bytes 786440 | tf_op jit(solution)/shard_map/ppermute | solution.py:115
  90.2 7.4 %shard_map.120 = bf16[1536,1024]{1,0:T(8,128)(2,1)} custom-call(bf16[144,1024]{1,0:T(8,128)(2,1)} %copy-done.1, bf16[144,1024]{1,0:T(8,128)(2,1)} %copy-done.5, bf16[144,1024]{1,0:T(8,128)(2,1)} %copy-done.3, bf16[144,1024]{1,0:T(8,128)(2,1)} %copy-done.7, bf16[144,1024]{1,0:T(8,128)(2,1)} %copy-done.4, bf16[144,1024]{1,0:T(8,128)(2,1)} %copy-done.8, ...), custom_call_target="tpu_custom_call" | custom-call | flops 3221225472 | bytes 13893632 | tf_op jit(solution)/shard_map/pallas_call | solution.py:162
  97.6 1.1 collective-permute-done.19
  99.6 1.6 %collective-permute-start.24 = (bf16[144,1024]{1,0:T(8,128)(2,1)S(1)}, bf16[144,1024]{1,0:T(8,128)(2,1)S(1)}, u32[]{:S(2)}, u32[]{:S(2)}) collective-permute-start(bf16[144,1024]{1,0:T(8,128)(2,1)S(1)} %copy-done.28), channel_id=1, source_target_pairs={{0,2},{1,3},{2,0},{3,1},{4,6},{5,7},{6,4},{7,5},{8,10},{9,11},{10,... | collective-permute-start | bytes 884744 | tf_op jit(solution)/shard_map/ppermute | solution.py:115
  102.3 1.8 %collective-permute-start.23 = (bf16[128,1024]{1,0:T(8,128)(2,1)S(1)}, bf16[128,1024]{1,0:T(8,128)(2,1)S(1)}, u32[]{:S(2)}, u32[]{:S(2)}) collective-permute-start(bf16[128,1024]{1,0:T(8,128)(2,1)S(1)} %add_convert_fusion.4), channel_id=1, source_target_pairs={{0,8},{1,9},{2,10},{3,11},{4,12},{5,13},{6,14},{7,15},{8,0},{9,1},... | collective-permute-start | bytes 786440 | tf_op jit(solution)/shard_map/ppermute | solution.py:115
  104.1 12.5 %collective-permute-done.23 = bf16[128,1024]{1,0:T(8,128)(2,1)S(1)} collective-permute-done((bf16[128,1024]{1,0:T(8,128)(2,1)S(1)}, bf16[128,1024]{1,0:T(8,128)(2,1)S(1)}, u32[]{:S(2)}, u32[]{:S(2)}) %collective-permute-start.23) | collective-permute-done | bytes 262176 | tf_op jit(solution)/shard_map/ppermute | solution.py:115
  117.0 1.0 collective-permute-start.28
  118.0 1.5 %collective-permute-start.29 = (bf16[144,1024]{1,0:T(8,128)(2,1)S(1)}, bf16[144,1024]{1,0:T(8,128)(2,1)S(1)}, u32[]{:S(2)}, u32[]{:S(2)}) collective-permute-start(bf16[144,1024]{1,0:T(8,128)(2,1)S(1)} %copy-done.26), channel_id=1, source_target_pairs={{0,2},{1,3},{2,0},{3,1},{4,6},{5,7},{6,4},{7,5},{8,10},{9,11},{10,... | collective-permute-start | bytes 884744 | tf_op jit(solution)/shard_map/ppermute | solution.py:115
  120.0 0.9 collective-permute-start.30
  120.9 8.3 %shard_map.121 = (bf16[1024,512]{1,0:T(8,128)(2,1)}, bf16[1024,512]{1,0:T(8,128)(2,1)}, bf16[512,1024]{1,0:T(8,128)(2,1)}) custom-call(bf16[144,1024]{1,0:T(8,128)(2,1)} %copy-done.1, bf16[144,1024]{1,0:T(8,128)(2,1)} %copy-done.5, bf16[144,1024]{1,0:T(8,128)(2,1)} %copy-done.3, bf16[144,1024]{1,0:T(8,128)(2,1)} %copy-done.7, bf16[144,1024]{1,0:T(8,128)(2,1)} %copy-done.4, ...), custom_call_target="tpu_custom_call" | custom-call | flops 3221225472 | bytes 17039360 | tf_op jit(solution)/shard_map/pallas_call | solution.py:162
  129.2 2.0 %collective-permute-done.30 = bf16[128,1024]{1,0:T(8,128)(2,1)S(1)} collective-permute-done((bf16[128,1024]{1,0:T(8,128)(2,1)S(1)}, bf16[128,1024]{1,0:T(8,128)(2,1)S(1)}, u32[]{:S(2)}, u32[]{:S(2)}) %collective-permute-start.30) | collective-permute-done | bytes 262176 | tf_op jit(solution)/shard_map/ppermute | solution.py:115
  131.6 1.1 collective-permute-done.31
  133.7 0.7 pad_maximum_fusion.2
  (122 shorter events, 10.1 us)
Async XLA Ops:
  2.7 19.6 %collective-permute-start.4 = (bf16[1024,512]{1,0:T(8,128)(2,1)}, bf16[1024,512]{1,0:T(8,128)(2,1)S(1)}, u32[]{:S(2)}, u32[]{:S(2)}) collective-permute-start(bf16[1024,512]{1,0:T(8,128)(2,1)} %bitcast.20), channel_id=1, source_target_pairs={{0,1},{1,0},{2,3},{3,2},{4,5},{5,4},{6,7},{7,6},{8,9},{9,8},{10,11... | collective-permute-start | bytes 3145736 | tf_op jit(solution)/shard_map/ppermute | solution.py:115
  3.2 18.4 %collective-permute-start = (bf16[144,1024]{1,0:T(8,128)(2,1)S(1)}, bf16[144,1024]{1,0:T(8,128)(2,1)S(1)}, u32[]{:S(2)}, u32[]{:S(2)}) collective-permute-start(bf16[144,1024]{1,0:T(8,128)(2,1)S(1)} %fusion.1.refs_0_), channel_id=1, source_target_pairs={{0,8},{1,9},{2,10},{3,11},{4,12},{5,13},{6,14},{7,15},{8,0},{9,1},... | collective-permute-start | bytes 884744 | tf_op jit(solution)/shard_map/ppermute | solution.py:115
  6.8 14.7 %collective-permute-start.1 = (bf16[144,1024]{1,0:T(8,128)(2,1)S(1)}, bf16[144,1024]{1,0:T(8,128)(2,1)S(1)}, u32[]{:S(2)}, u32[]{:S(2)}) collective-permute-start(bf16[144,1024]{1,0:T(8,128)(2,1)S(1)} %fusion.1.refs_0_), channel_id=1, source_target_pairs={{0,2},{1,3},{2,0},{3,1},{4,6},{5,7},{6,4},{7,5},{8,10},{9,11},{10,... | collective-permute-start | bytes 884744 | tf_op jit(solution)/shard_map/ppermute | solution.py:115
  8.3 13.9 %collective-permute-start.3 = (bf16[144,1024]{1,0:T(8,128)(2,1)S(1)}, bf16[144,1024]{1,0:T(8,128)(2,1)S(1)}, u32[]{:S(2)}, u32[]{:S(2)}) collective-permute-start(bf16[144,1024]{1,0:T(8,128)(2,1)S(1)} %fusion.1.refs_0_), channel_id=1, source_target_pairs={{0,4},{1,5},{2,6},{3,7},{4,0},{5,1},{6,2},{7,3},{8,12},{9,13},{10,... | collective-permute-start | bytes 884744 | tf_op jit(solution)/shard_map/ppermute | solution.py:115
  9.9 11.6 %collective-permute-start.2 = (bf16[128,1024]{1,0:T(8,128)(2,1)S(1)}, bf16[128,1024]{1,0:T(8,128)(2,1)S(1)}, u32[]{:S(2)}, u32[]{:S(2)}) collective-permute-start(bf16[128,1024]{1,0:T(8,128)(2,1)S(1)} %pad_maximum_fusion.refs_0_.refs_8_), channel_id=1, source_target_pairs={{0,2},{1,3},{2,0},{3,1},{4,6},{5,7},{6,4},{7,5},{8,10},{9,11},{10,... | collective-permute-start | bytes 786440 | tf_op jit(solution)/shard_map/ppermute | solution.py:115
  22.3 17.5 %collective-permute-start.9 = (bf16[1024,512]{1,0:T(8,128)(2,1)}, bf16[1024,512]{1,0:T(8,128)(2,1)S(1)}, u32[]{:S(2)}, u32[]{:S(2)}) collective-permute-start(bf16[1024,512]{1,0:T(8,128)(2,1)} %bitcast.23), channel_id=1, source_target_pairs={{0,1},{1,0},{2,3},{3,2},{4,5},{5,4},{6,7},{7,6},{8,9},{9,8},{10,11... | collective-permute-start | bytes 3145736 | tf_op jit(solution)/shard_map/ppermute | solution.py:115
  22.4 17.4 %collective-permute-start.7 = (bf16[144,1024]{1,0:T(8,128)(2,1)S(1)}, bf16[144,1024]{1,0:T(8,128)(2,1)S(1)}, u32[]{:S(2)}, u32[]{:S(2)}) collective-permute-start(bf16[144,1024]{1,0:T(8,128)(2,1)S(1)} %collective-permute-done.refs_2_), channel_id=1, source_target_pairs={{0,2},{1,3},{2,0},{3,1},{4,6},{5,7},{6,4},{7,5},{8,10},{9,11},{10,... | collective-permute-start | bytes 884744 | tf_op jit(solution)/shard_map/ppermute | solution.py:115
  23.2 16.5 %collective-permute-start.8 = (bf16[144,1024]{1,0:T(8,128)(2,1)S(1)}, bf16[144,1024]{1,0:T(8,128)(2,1)S(1)}, u32[]{:S(2)}, u32[]{:S(2)}) collective-permute-start(bf16[144,1024]{1,0:T(8,128)(2,1)S(1)} %collective-permute-done.refs_2_), channel_id=1, source_target_pairs={{0,4},{1,5},{2,6},{3,7},{4,0},{5,1},{6,2},{7,3},{8,12},{9,13},{10,... | collective-permute-start | bytes 884744 | tf_op jit(solution)/shard_map/ppermute | solution.py:115
  24.8 14.9 %collective-permute-start.6 = (bf16[144,1024]{1,0:T(8,128)(2,1)S(1)}, bf16[144,1024]{1,0:T(8,128)(2,1)S(1)}, u32[]{:S(2)}, u32[]{:S(2)}) collective-permute-start(bf16[144,1024]{1,0:T(8,128)(2,1)S(1)} %collective-permute-done.3.refs_1_), channel_id=1, source_target_pairs={{0,2},{1,3},{2,0},{3,1},{4,6},{5,7},{6,4},{7,5},{8,10},{9,11},{10,... | collective-permute-start | bytes 884744 | tf_op jit(solution)/shard_map/ppermute | solution.py:115
  25.4 14.4 %collective-permute-start.5 = (bf16[128,1024]{1,0:T(8,128)(2,1)S(1)}, bf16[128,1024]{1,0:T(8,128)(2,1)S(1)}, u32[]{:S(2)}, u32[]{:S(2)}) collective-permute-start(bf16[128,1024]{1,0:T(8,128)(2,1)S(1)} %pad_maximum_fusion.refs_0_.refs_8_), channel_id=1, source_target_pairs={{0,8},{1,9},{2,10},{3,11},{4,12},{5,13},{6,14},{7,15},{8,0},{9,1},... | collective-permute-start | bytes 786440 | tf_op jit(solution)/shard_map/ppermute | solution.py:115
  39.8 16.0 %collective-permute-start.14 = (bf16[512,1024]{1,0:T(8,128)(2,1)}, bf16[512,1024]{1,0:T(8,128)(2,1)}, u32[]{:S(2)}, u32[]{:S(2)}) collective-permute-start(bf16[512,1024]{1,0:T(8,128)(2,1)} %bitcast.26), channel_id=1, source_target_pairs={{0,1},{1,0},{2,3},{3,2},{4,5},{5,4},{6,7},{7,6},{8,9},{9,8},{10,11... | collective-permute-start | bytes 3145736 | tf_op jit(solution)/shard_map/ppermute | solution.py:115
  39.9 15.9 %collective-permute-start.10 = (bf16[144,1024]{1,0:T(8,128)(2,1)S(1)}, bf16[144,1024]{1,0:T(8,128)(2,1)S(1)}, u32[]{:S(2)}, u32[]{:S(2)}) collective-permute-start(bf16[144,1024]{1,0:T(8,128)(2,1)S(1)} %collective-permute-done.8.refs_3_), channel_id=1, source_target_pairs={{0,2},{1,3},{2,0},{3,1},{4,6},{5,7},{6,4},{7,5},{8,10},{9,11},{10,... | collective-permute-start | bytes 884744 | tf_op jit(solution)/shard_map/ppermute | solution.py:115
  41.4 13.5 %collective-permute-start.11 = (bf16[128,1024]{1,0:T(8,128)(2,1)S(1)}, bf16[128,1024]{1,0:T(8,128)(2,1)S(1)}, u32[]{:S(2)}, u32[]{:S(2)}) collective-permute-start(bf16[128,1024]{1,0:T(8,128)(2,1)S(1)} %collective-permute-done.5.refs_2_.refs_10_), channel_id=1, source_target_pairs={{0,2},{1,3},{2,0},{3,1},{4,6},{5,7},{6,4},{7,5},{8,10},{9,11},{10,... | collective-permute-start | bytes 786440 | tf_op jit(solution)/shard_map/ppermute | solution.py:115
  42.0 12.9 %collective-permute-start.12 = (bf16[128,1024]{1,0:T(8,128)(2,1)S(1)}, bf16[128,1024]{1,0:T(8,128)(2,1)}, u32[]{:S(2)}, u32[]{:S(2)}) collective-permute-start(bf16[128,1024]{1,0:T(8,128)(2,1)S(1)} %collective-permute-done.5.refs_2_.refs_10_), channel_id=1, source_target_pairs={{0,4},{1,5},{2,6},{3,7},{4,0},{5,1},{6,2},{7,3},{8,12},{9,13},{10,... | collective-permute-start | bytes 786440 | tf_op jit(solution)/shard_map/ppermute | solution.py:115
  42.0 13.8 %collective-permute-start.13 = (bf16[128,1024]{1,0:T(8,128)(2,1)S(1)}, bf16[128,1024]{1,0:T(8,128)(2,1)}, u32[]{:S(2)}, u32[]{:S(2)}) collective-permute-start(bf16[128,1024]{1,0:T(8,128)(2,1)S(1)} %pad_maximum_fusion.refs_0_.refs_8_), channel_id=1, source_target_pairs={{0,4},{1,5},{2,6},{3,7},{4,0},{5,1},{6,2},{7,3},{8,12},{9,13},{10,... | collective-permute-start | bytes 786440 | tf_op jit(solution)/shard_map/ppermute | solution.py:115
  55.8 15.0 %collective-permute-start.15 = (bf16[128,1024]{1,0:T(8,128)(2,1)}, bf16[128,1024]{1,0:T(8,128)(2,1)S(1)}, u32[]{:S(2)}, u32[]{:S(2)}) collective-permute-start(bf16[128,1024]{1,0:T(8,128)(2,1)} %collective-permute-done.13.refs_1_.refs_9_), channel_id=1, source_target_pairs={{0,2},{1,3},{2,0},{3,1},{4,6},{5,7},{6,4},{7,5},{8,10},{9,11},{10,... | collective-permute-start | bytes 786440 | tf_op jit(solution)/shard_map/ppermute | solution.py:115
  57.4 13.4 %collective-permute-start.16 = (bf16[128,1024]{1,0:T(8,128)(2,1)}, bf16[128,1024]{1,0:T(8,128)(2,1)S(1)}, u32[]{:S(2)}, u32[]{:S(2)}) collective-permute-start(bf16[128,1024]{1,0:T(8,128)(2,1)} %collective-permute-done.12.refs_3_.refs_11_), channel_id=1, source_target_pairs={{0,2},{1,3},{2,0},{3,1},{4,6},{5,7},{6,4},{7,5},{8,10},{9,11},{10,... | collective-permute-start | bytes 786440 | tf_op jit(solution)/shard_map/ppermute | solution.py:115
  70.9 15.0 %collective-permute-start.17 = (bf16[128,1024]{1,0:T(8,128)(2,1)}, bf16[128,1024]{1,0:T(8,128)(2,1)S(1)}, u32[]{:S(2)}, u32[]{:S(2)}) collective-permute-start(bf16[128,1024]{1,0:T(8,128)(2,1)} %get-tuple-element.225), channel_id=1, source_target_pairs={{0,2},{1,3},{2,0},{3,1},{4,6},{5,7},{6,4},{7,5},{8,10},{9,11},{10,... | collective-permute-start | bytes 786440 | tf_op jit(solution)/shard_map/ppermute | solution.py:115
  72.4 13.4 %collective-permute-start.18 = (bf16[128,1024]{1,0:T(8,128)(2,1)}, bf16[128,1024]{1,0:T(8,128)(2,1)S(1)}, u32[]{:S(2)}, u32[]{:S(2)}) collective-permute-start(bf16[128,1024]{1,0:T(8,128)(2,1)} %get-tuple-element.223), channel_id=1, source_target_pairs={{0,2},{1,3},{2,0},{3,1},{4,6},{5,7},{6,4},{7,5},{8,10},{9,11},{10,... | collective-permute-start | bytes 786440 | tf_op jit(solution)/shard_map/ppermute | solution.py:115
  86.0 13.3 %collective-permute-start.20 = (bf16[144,1024]{1,0:T(8,128)(2,1)}, bf16[144,1024]{1,0:T(8,128)(2,1)S(1)}, u32[]{:S(2)}, u32[]{:S(2)}) collective-permute-start(bf16[144,1024]{1,0:T(8,128)(2,1)} %get-tuple-element.245), channel_id=1, source_target_pairs={{0,2},{1,3},{2,0},{3,1},{4,6},{5,7},{6,4},{7,5},{8,10},{9,11},{10,... | collective-permute-start | bytes 884744 | tf_op jit(solution)/shard_map/ppermute | solution.py:115
  87.6 11.1 %collective-permute-start.19 = (bf16[128,1024]{1,0:T(8,128)(2,1)S(1)}, bf16[128,1024]{1,0:T(8,128)(2,1)S(1)}, u32[]{:S(2)}, u32[]{:S(2)}) collective-permute-start(bf16[128,1024]{1,0:T(8,128)(2,1)S(1)} %copy-done.30), channel_id=1, source_target_pairs={{0,2},{1,3},{2,0},{3,1},{4,6},{5,7},{6,4},{7,5},{8,10},{9,11},{10,... | collective-permute-start | bytes 786440 | tf_op jit(solution)/shard_map/ppermute | solution.py:115
  88.1 10.6 %collective-permute-start.21 = (bf16[128,1024]{1,0:T(8,128)(2,1)S(1)}, bf16[128,1024]{1,0:T(8,128)(2,1)S(1)}, u32[]{:S(2)}, u32[]{:S(2)}) collective-permute-start(bf16[128,1024]{1,0:T(8,128)(2,1)S(1)} %add_convert_fusion.6), channel_id=1, source_target_pairs={{0,4},{1,5},{2,6},{3,7},{4,0},{5,1},{6,2},{7,3},{8,12},{9,13},{10,... | collective-permute-start | bytes 786440 | tf_op jit(solution)/shard_map/ppermute | solution.py:115
  88.4 10.9 %collective-permute-start.22 = (bf16[128,1024]{1,0:T(8,128)(2,1)S(1)}, bf16[128,1024]{1,0:T(8,128)(2,1)S(1)}, u32[]{:S(2)}, u32[]{:S(2)}) collective-permute-start(bf16[128,1024]{1,0:T(8,128)(2,1)S(1)} %add_convert_fusion.5), channel_id=1, source_target_pairs={{0,4},{1,5},{2,6},{3,7},{4,0},{5,1},{6,2},{7,3},{8,12},{9,13},{10,... | collective-permute-start | bytes 786440 | tf_op jit(solution)/shard_map/ppermute | solution.py:115
  99.5 17.2 %collective-permute-start.27 = (bf16[1536,1024]{1,0:T(8,128)(2,1)}, bf16[1536,1024]{1,0:T(8,128)(2,1)S(1)}, u32[]{:S(2)}, u32[]{:S(2)}) collective-permute-start(bf16[1536,1024]{1,0:T(8,128)(2,1)} %shard_map.120), channel_id=1, source_target_pairs={{0,1},{1,0},{2,3},{3,2},{4,5},{5,4},{6,7},{7,6},{8,9},{9,8},{10,11... | collective-permute-start | bytes 9437192 | tf_op jit(solution)/shard_map/ppermute | solution.py:115
  99.6 17.1 %collective-permute-start.24 = (bf16[144,1024]{1,0:T(8,128)(2,1)S(1)}, bf16[144,1024]{1,0:T(8,128)(2,1)S(1)}, u32[]{:S(2)}, u32[]{:S(2)}) collective-permute-start(bf16[144,1024]{1,0:T(8,128)(2,1)S(1)} %copy-done.28), channel_id=1, source_target_pairs={{0,2},{1,3},{2,0},{3,1},{4,6},{5,7},{6,4},{7,5},{8,10},{9,11},{10,... | collective-permute-start | bytes 884744 | tf_op jit(solution)/shard_map/ppermute | solution.py:115
  101.1 15.5 %collective-permute-start.25 = (bf16[144,1024]{1,0:T(8,128)(2,1)S(1)}, bf16[144,1024]{1,0:T(8,128)(2,1)S(1)}, u32[]{:S(2)}, u32[]{:S(2)}) collective-permute-start(bf16[144,1024]{1,0:T(8,128)(2,1)S(1)} %copy-done.27), channel_id=1, source_target_pairs={{0,2},{1,3},{2,0},{3,1},{4,6},{5,7},{6,4},{7,5},{8,10},{9,11},{10,... | collective-permute-start | bytes 884744 | tf_op jit(solution)/shard_map/ppermute | solution.py:115
  101.7 15.0 %collective-permute-start.26 = (bf16[144,1024]{1,0:T(8,128)(2,1)S(1)}, bf16[144,1024]{1,0:T(8,128)(2,1)S(1)}, u32[]{:S(2)}, u32[]{:S(2)}) collective-permute-start(bf16[144,1024]{1,0:T(8,128)(2,1)S(1)} %add_convert_fusion.2), channel_id=1, source_target_pairs={{0,4},{1,5},{2,6},{3,7},{4,0},{5,1},{6,2},{7,3},{8,12},{9,13},{10,... | collective-permute-start | bytes 884744 | tf_op jit(solution)/shard_map/ppermute | solution.py:115
  102.3 14.4 %collective-permute-start.23 = (bf16[128,1024]{1,0:T(8,128)(2,1)S(1)}, bf16[128,1024]{1,0:T(8,128)(2,1)S(1)}, u32[]{:S(2)}, u32[]{:S(2)}) collective-permute-start(bf16[128,1024]{1,0:T(8,128)(2,1)S(1)} %add_convert_fusion.4), channel_id=1, source_target_pairs={{0,8},{1,9},{2,10},{3,11},{4,12},{5,13},{6,14},{7,15},{8,0},{9,1},... | collective-permute-start | bytes 786440 | tf_op jit(solution)/shard_map/ppermute | solution.py:115
  117.0 14.6 %collective-permute-start.28 = (bf16[144,1024]{1,0:T(8,128)(2,1)S(1)}, bf16[144,1024]{1,0:T(8,128)(2,1)S(1)}, u32[]{:S(2)}, u32[]{:S(2)}) collective-permute-start(bf16[144,1024]{1,0:T(8,128)(2,1)S(1)} %add_convert_fusion.1), channel_id=1, source_target_pairs={{0,8},{1,9},{2,10},{3,11},{4,12},{5,13},{6,14},{7,15},{8,0},{9,1},... | collective-permute-start | bytes 884744 | tf_op jit(solution)/shard_map/ppermute | solution.py:115
  118.0 13.6 %collective-permute-start.29 = (bf16[144,1024]{1,0:T(8,128)(2,1)S(1)}, bf16[144,1024]{1,0:T(8,128)(2,1)S(1)}, u32[]{:S(2)}, u32[]{:S(2)}) collective-permute-start(bf16[144,1024]{1,0:T(8,128)(2,1)S(1)} %copy-done.26), channel_id=1, source_target_pairs={{0,2},{1,3},{2,0},{3,1},{4,6},{5,7},{6,4},{7,5},{8,10},{9,11},{10,... | collective-permute-start | bytes 884744 | tf_op jit(solution)/shard_map/ppermute | solution.py:115
  119.5 13.2 %collective-permute-start.31 = (bf16[144,1024]{1,0:T(8,128)(2,1)S(1)}, bf16[144,1024]{1,0:T(8,128)(2,1)S(1)}, u32[]{:S(2)}, u32[]{:S(2)}) collective-permute-start(bf16[144,1024]{1,0:T(8,128)(2,1)S(1)} %add_convert_fusion), channel_id=1, source_target_pairs={{0,4},{1,5},{2,6},{3,7},{4,0},{5,1},{6,2},{7,3},{8,12},{9,13},{10,... | collective-permute-start | bytes 884744 | tf_op jit(solution)/shard_map/ppermute | solution.py:115
  120.0 11.3 %collective-permute-start.30 = (bf16[128,1024]{1,0:T(8,128)(2,1)S(1)}, bf16[128,1024]{1,0:T(8,128)(2,1)S(1)}, u32[]{:S(2)}, u32[]{:S(2)}) collective-permute-start(bf16[128,1024]{1,0:T(8,128)(2,1)S(1)} %copy-done.29), channel_id=1, source_target_pairs={{0,2},{1,3},{2,0},{3,1},{4,6},{5,7},{6,4},{7,5},{8,10},{9,11},{10,... | collective-permute-start | bytes 786440 | tf_op jit(solution)/shard_map/ppermute | solution.py:115
  (31 other events, 631.9 us)

commit v8 on v7

--- a/solution.py
+++ b/solution.py
@@ -199,10 +199,15 @@
         q_refs, refs = refs[:count], refs[count:]
         weighted_ref, factor_ref, refs = refs[0], refs[1], refs[2:]
         after_refs, refs = ((), refs) if last else (refs[:2], refs[2:])
-        w_bufs, refs = refs[:6], refs[6:]
+        wide_w, down_w, refs = refs[0], refs[1], refs[2:]
         x_buf, c_buf, y_buf, g_buf, weighted_buf, factor_buf, refs = *refs[:6], refs[6:]
         share_buf, inner_buf, wide_buf, extra_buf, sems = refs
         fetch = Fetch(sems)
+        w_bufs = []
+        for e in range(2):
+            for i in (2 * e, 2 * e + 1):
+                w_bufs.append(wide_w.at[:, pl.ds(i * units, units)])
+            w_bufs.append(down_w.at[pl.ds(e * units, units)])
         me = me_ref[0]
         low = lax.rem(me, 8)
         for b in range(count):
@@ -247,26 +252,23 @@
 
         half = slice(number * tok_count, (number + 1) * tok_count)
         fetch.wait(*[("x", b) for b in range(count)])
-        x, y, g = x_buf[...], 0.0, 0.0
+        x = x_buf[...]
         for e in range(2):
-            gate_w, up_w, down_w = w_bufs[3 * e : 3 * e + 3]
             columns = slice(e * units, (e + 1) * units)
             fetch.wait(("w", 3 * e))
-            gate = dot(x, gate_w[...], ((1,), (0,)))
+            gate = dot(x, wide_w[:, 2 * e * units : (2 * e + 1) * units], ((1,), (0,)))
             fetch.wait(("w", 3 * e + 1))
-            up = dot(x, up_w[...], ((1,), (0,)))
+            up = dot(x, wide_w[:, (2 * e + 1) * units : (2 * e + 2) * units], ((1,), (0,)))
+            fetch.wait(("w", 3 * e + 2))
+            if e == 0:
+                fetch.wait(*[("c", b) for b in range(count)])
+            plain = dot(c_buf[...], down_w[columns, :], ((1,), (1,)))
             sigma = jax.nn.sigmoid(gate)
             silu_val = gate * sigma
             hidden = silu_val * up
             part = [share_buf[half, e * count + b : e * count + b + 1] for b in range(count)]
             part = jnp.concatenate(part, axis=0)
-            weighted = (part * hidden).astype(bf16)
-            weighted_buf[:, columns] = weighted
-            fetch.wait(("w", 3 * e + 2))
-            if e == 0:
-                fetch.wait(*[("c", b) for b in range(count)])
-            plain = dot(c_buf[...], down_w[...], ((1,), (1,)))
-            y = y + dot(weighted, down_w[...], ((1,), (0,)))
+            weighted_buf[:, columns] = (part * hidden).astype(bf16)
             inner = jnp.sum(hidden * plain, axis=1, keepdims=True)
             for b in range(count):
                 value = inner[b * tok_count : (b + 1) * tok_count]
@@ -276,16 +278,16 @@
             grad_up = (grad_hidden * silu_val).astype(bf16)
             factor_buf[:, 2 * e * units : (2 * e + 1) * units] = grad_gate
             factor_buf[:, (2 * e + 1) * units : (2 * e + 2) * units] = grad_up
-            g = g + dot(grad_gate, gate_w[...], ((1,), (1,)))
-            g = g + dot(grad_up, up_w[...], ((1,), (1,)))
-        y_buf[...] = y.astype(bf16)
-        g_buf[...] = g.astype(bf16)
+        fetch.start("weighted", weighted_buf, weighted_ref)
+        fetch.start("factor", factor_buf, factor_ref)
+        y_buf[...] = dot(weighted_buf[...], down_w[...], ((1,), (0,))).astype(bf16)
         for b in range(count):
             at = pl.ds(b * tok_count, tok_count)
             fetch.start(("y", b), y_buf.at[at], q_refs[b].at[pl.ds(0, tok_count)])
+        g_buf[...] = dot(factor_buf[...], wide_w[...], ((1,), (1,))).astype(bf16)
+        for b in range(count):
+            at = pl.ds(b * tok_count, tok_count)
             fetch.start(("g", b), g_buf.at[at], q_refs[b].at[pl.ds(tok_count, tok_count)])
-        fetch.start("weighted", weighted_buf, weighted_ref)
-        fetch.start("factor", factor_buf, factor_ref)
         if last:
             wide_buf[...] = jnp.zeros((count, EXTRA, width), f32)
             inner_buf[...] = inner_buf[...].T
@@ -315,7 +317,7 @@
         operands += before
     else:
         outs += [small, small]
-    scratch = [pltpu.VMEM(w.shape, bf16) for w in (*weights[0], *weights[1])]
+    scratch = [pltpu.VMEM((width, 4 * units), bf16), pltpu.VMEM((2 * units, width), bf16)]
     scratch += [pltpu.VMEM((every, width), bf16)] * 4
     scratch += [pltpu.VMEM((every, 2 * units), bf16), pltpu.VMEM((every, 4 * units), bf16)]
     scratch += [pltpu.VMEM(small.shape, f32)] * 2
@@ -425,22 +427,22 @@
     a7, b6, b1, b3 = swap(a3, SIDE), swap(b2, SIDE), swap(b0, NEAR), swap(b2, NEAR)
     down_w = swap(own[2], CORE)
     a7, b6, b3, b1, down_w, a0, b0, own = fence(a7, b6, b3, b1, down_w, a0, b0, own)
-    b5, b7 = swap(b1, SIDE), swap(b3, SIDE)
+    b5, b7 = swap(b1, SIDE), swap(b6, NEAR)
     weights, me = (own, (gate_w, up_w, down_w)), me.astype(jnp.int32).reshape(1)
     a = [a0, a1, a2, a3, a4, a5, a6, a7]
     q, (*a_factors, shares, inners) = both_ways(0, a, weights, me)
     q, shares, inners, b5, b7 = fence(q, shares, inners, b5, b7)
-    q7, q5 = swap(q[7], SIDE), swap(q[5], SIDE)
+    q5, q7, q3 = swap(q[5], SIDE), swap(q[7], NEAR), swap(q[3], NEAR)
     b = [b0, b1, b2, b3, b4, b5, b6, b7]
     p, b_factors = both_ways(1, b, weights, me, (shares, inners))
-    p, q, q7, q5, b_factors = fence(p, q, q7, q5, b_factors)
+    q5, q7, q3, p, q, b_factors = fence(q5, q7, q3, p, q, b_factors)
     factors = (a_factors, b_factors)
-    q3, q1 = narrow(added(q[3], q7)), narrow(added(q[1], q5))
-    q3, q1, p, q = fence(q3, q1, p, q)
-    q6, p7, q3, q1 = swap(q[6], SIDE), swap(p[7], SIDE), swap(q3, NEAR), swap(q1, NEAR)
+    q6, q2, q1 = narrow(added(q[6], q7)), added(q[2], q3), narrow(added(q[1], q5))
+    q6, q2, q1, p, q = fence(q6, q2, q1, p, q)
+    q6, p7, q1 = swap(q6, SIDE), swap(p[7], SIDE), swap(q1, NEAR)
     away = weight_grads(1, (a, b), factors)
-    q6, p7, q3, q1, away, p, q = fence(q6, p7, q3, q1, away, p, q)
-    q2, p3 = narrow(added(q[2], q6) + q3.astype(f32)), narrow(added(p[3], p7))
+    q6, p7, q1, q2, away, p, q = fence(q6, p7, q1, q2, away, p, q)
+    q2, p3 = narrow(q2 + q6.astype(f32)), narrow(added(p[3], p7))
     q2, p3, p, q, away = fence(q2, p3, p, q, away)
     p6, p5, q2, p3 = swap(p[6], SIDE), swap(p[5], SIDE), swap(q2, FAR), swap(p3, NEAR)
     away = swap(away, CORE)

time: 135 us -> 133 us (0.985)
  Pallas kernels: 41.4 us -> 39.3 us
    pallas_call x4, Pallas kernels: 41.4 us -> 39.3 us  [kernel(): pl.pallas_call(body, out_shape=outs, in_specs=in_specs, out_specs=[pl.Blo...]
  transfers between devices with their start and end apart: 32 -> 32, of which waited for: 11 -> 11; matrix products, arithmetic and copies ran while one was open for 0% -> 0% of each run, Pallas kernels for 31% -> 30%
where the time goes in v8:
time: 133 us
  waiting for transfers between devices  52.8 us (40%)
  Pallas kernels  39.3 us (30%)
  starting transfers between devices  34.4 us (26%)
  other arithmetic  3.76 us (3%)
  local copies, waits for them, and re-layouts  1.35 us (1%)
    ppermute x32, waiting for transfers between devices, swap(): return lax.ppermute(value, 'ep', pairs)  52.8 us
    pallas_call x4, Pallas kernels, kernel(): pl.pallas_call(body, out_shape=outs, in_specs=in_specs, out_specs=[pl.Blo...  39.3 us
    ppermute x32, starting transfers between devices, swap(): return lax.ppermute(value, 'ep', pairs)  34.4 us
  transfers between devices with their start and end apart: 32, of which 11 were waited for; matrix products, arithmetic and copies ran while one was open for 0% of the time, Pallas kernels for 30%

profile of v8, /device:TPU:0, one launch (start us, length us, event | category | flops | bytes accessed | tf_op | source)
XLA Modules:
  0.0 132.8 jit_solution(16506814201645551423)
XLA Ops:
  0.6 0.7 select_reduce_fusion.1
  1.4 1.1 fusion.6
  3.2 3.7 %collective-permute-start = (bf16[144,1024]{1,0:T(8,128)(2,1)S(1)}, bf16[144,1024]{1,0:T(8,128)(2,1)S(1)}, u32[]{:S(2)}, u32[]{:S(2)}) collective-permute-start(bf16[144,1024]{1,0:T(8,128)(2,1)S(1)} %fusion.1.refs_0_), channel_id=1, source_target_pairs={{0,8},{1,9},{2,10},{3,11},{4,12},{5,13},{6,14},{7,15},{8,0},{9,1},... | collective-permute-start | bytes 884744 | tf_op jit(solution)/shard_map/ppermute | solution.py:115
  6.8 1.5 %collective-permute-start.1 = (bf16[144,1024]{1,0:T(8,128)(2,1)S(1)}, bf16[144,1024]{1,0:T(8,128)(2,1)S(1)}, u32[]{:S(2)}, u32[]{:S(2)}) collective-permute-start(bf16[144,1024]{1,0:T(8,128)(2,1)S(1)} %fusion.1.refs_0_), channel_id=1, source_target_pairs={{0,2},{1,3},{2,0},{3,1},{4,6},{5,7},{6,4},{7,5},{8,10},{9,11},{10,... | collective-permute-start | bytes 884744 | tf_op jit(solution)/shard_map/ppermute | solution.py:115
  8.3 1.6 %collective-permute-start.3 = (bf16[144,1024]{1,0:T(8,128)(2,1)S(1)}, bf16[144,1024]{1,0:T(8,128)(2,1)S(1)}, u32[]{:S(2)}, u32[]{:S(2)}) collective-permute-start(bf16[144,1024]{1,0:T(8,128)(2,1)S(1)} %fusion.1.refs_0_), channel_id=1, source_target_pairs={{0,4},{1,5},{2,6},{3,7},{4,0},{5,1},{6,2},{7,3},{8,12},{9,13},{10,... | collective-permute-start | bytes 884744 | tf_op jit(solution)/shard_map/ppermute | solution.py:115
  10.4 11.1 %collective-permute-done.2.refs_4_.refs_12_ = bf16[128,1024]{1,0:T(8,128)(2,1)S(1)} collective-permute-done((bf16[128,1024]{1,0:T(8,128)(2,1)S(1)}, bf16[128,1024]{1,0:T(8,128)(2,1)S(1)}, u32[]{:S(2)}, u32[]{:S(2)}) %collective-permute-start.2) | collective-permute-done | bytes 262176 | tf_op jit(solution)/shard_map/ppermute | solution.py:115
  22.4 0.9 collective-permute-start.7
  23.2 1.6 %collective-permute-start.8 = (bf16[144,1024]{1,0:T(8,128)(2,1)S(1)}, bf16[144,1024]{1,0:T(8,128)(2,1)S(1)}, u32[]{:S(2)}, u32[]{:S(2)}) collective-permute-start(bf16[144,1024]{1,0:T(8,128)(2,1)S(1)} %collective-permute-done.refs_2_), channel_id=1, source_target_pairs={{0,4},{1,5},{2,6},{3,7},{4,0},{5,1},{6,2},{7,3},{8,12},{9,13},{10,... | collective-permute-start | bytes 884744 | tf_op jit(solution)/shard_map/ppermute | solution.py:115
  25.4 2.2 %collective-permute-start.5 = (bf16[128,1024]{1,0:T(8,128)(2,1)S(1)}, bf16[128,1024]{1,0:T(8,128)(2,1)S(1)}, u32[]{:S(2)}, u32[]{:S(2)}) collective-permute-start(bf16[128,1024]{1,0:T(8,128)(2,1)S(1)} %pad_maximum_fusion.refs_0_.refs_8_), channel_id=1, source_target_pairs={{0,8},{1,9},{2,10},{3,11},{4,12},{5,13},{6,14},{7,15},{8,0},{9,1},... | collective-permute-start | bytes 786440 | tf_op jit(solution)/shard_map/ppermute | solution.py:115
  27.5 12.2 %collective-permute-done.5.refs_2_.refs_10_ = bf16[128,1024]{1,0:T(8,128)(2,1)S(1)} collective-permute-done((bf16[128,1024]{1,0:T(8,128)(2,1)S(1)}, bf16[128,1024]{1,0:T(8,128)(2,1)S(1)}, u32[]{:S(2)}, u32[]{:S(2)}) %collective-permute-start.5) | collective-permute-done | bytes 262176 | tf_op jit(solution)/shard_map/ppermute | solution.py:115
  39.9 1.6 %collective-permute-start.10 = (bf16[144,1024]{1,0:T(8,128)(2,1)S(1)}, bf16[144,1024]{1,0:T(8,128)(2,1)S(1)}, u32[]{:S(2)}, u32[]{:S(2)}) collective-permute-start(bf16[144,1024]{1,0:T(8,128)(2,1)S(1)} %collective-permute-done.8.refs_3_), channel_id=1, source_target_pairs={{0,2},{1,3},{2,0},{3,1},{4,6},{5,7},{6,4},{7,5},{8,10},{9,11},{10,... | collective-permute-start | bytes 884744 | tf_op jit(solution)/shard_map/ppermute | solution.py:115
  42.0 2.0 %collective-permute-start.13 = (bf16[128,1024]{1,0:T(8,128)(2,1)S(1)}, bf16[128,1024]{1,0:T(8,128)(2,1)}, u32[]{:S(2)}, u32[]{:S(2)}) collective-permute-start(bf16[128,1024]{1,0:T(8,128)(2,1)S(1)} %pad_maximum_fusion.refs_0_.refs_8_), channel_id=1, source_target_pairs={{0,4},{1,5},{2,6},{3,7},{4,0},{5,1},{6,2},{7,3},{8,12},{9,13},{10,... | collective-permute-start | bytes 786440 | tf_op jit(solution)/shard_map/ppermute | solution.py:115
  44.0 10.9 %collective-permute-done.11.refs_6_.refs_14_ = bf16[128,1024]{1,0:T(8,128)(2,1)S(1)} collective-permute-done((bf16[128,1024]{1,0:T(8,128)(2,1)S(1)}, bf16[128,1024]{1,0:T(8,128)(2,1)S(1)}, u32[]{:S(2)}, u32[]{:S(2)}) %collective-permute-start.11) | collective-permute-done | bytes 262176 | tf_op jit(solution)/shard_map/ppermute | solution.py:115
  54.9 0.9 collective-permute-done.13.refs_1_.refs_9_
  55.8 1.6 %collective-permute-start.15 = (bf16[128,1024]{1,0:T(8,128)(2,1)}, bf16[128,1024]{1,0:T(8,128)(2,1)S(1)}, u32[]{:S(2)}, u32[]{:S(2)}) collective-permute-start(bf16[128,1024]{1,0:T(8,128)(2,1)} %collective-permute-done.13.refs_1_.refs_9_), channel_id=1, source_target_pairs={{0,2},{1,3},{2,0},{3,1},{4,6},{5,7},{6,4},{7,5},{8,10},{9,11},{10,... | collective-permute-start | bytes 786440 | tf_op jit(solution)/shard_map/ppermute | solution.py:115
  57.7 11.7 %shard_map.118 = (bf16[128,1024]{1,0:T(8,128)(2,1)}, bf16[128,1024]{1,0:T(8,128)(2,1)}, bf16[128,1024]{1,0:T(8,128)(2,1)}, bf16[128,1024]{1,0:T(8,128)(2,1)}, bf...) custom-call(s32[1]{0:T(128)} %bitcast.me_ref, ...), custom_call_target="tpu_custom_call" | custom-call | flops 6442450944 | bytes 14024704 | tf_op jit(solution)/shard_map/pallas_call | solution.py:162
  70.1 1.7 %collective-permute-start.18 = (bf16[128,1024]{1,0:T(8,128)(2,1)}, bf16[128,1024]{1,0:T(8,128)(2,1)S(1)}, u32[]{:S(2)}, u32[]{:S(2)}) collective-permute-start(bf16[128,1024]{1,0:T(8,128)(2,1)} %get-tuple-element.202), channel_id=1, source_target_pairs={{0,4},{1,5},{2,6},{3,7},{4,0},{5,1},{6,2},{7,3},{8,12},{9,13},{10,... | collective-permute-start | bytes 786440 | tf_op jit(solution)/shard_map/ppermute | solution.py:115
  72.2 11.9 %shard_map.119 = (bf16[144,1024]{1,0:T(8,128)(2,1)}, bf16[144,1024]{1,0:T(8,128)(2,1)}, bf16[144,1024]{1,0:T(8,128)(2,1)}, bf16[144,1024]{1,0:T(8,128)(2,1)}, bf...) custom-call(s32[1]{0:T(128)} %bitcast.me_ref, ...), custom_call_target="tpu_custom_call" | custom-call | flops 6442450944 | bytes 14024704 | tf_op jit(solution)/shard_map/pallas_call | solution.py:162
  84.3 1.6 %collective-permute-start.21 = (bf16[144,1024]{1,0:T(8,128)(2,1)}, bf16[144,1024]{1,0:T(8,128)(2,1)S(1)}, u32[]{:S(2)}, u32[]{:S(2)}) collective-permute-start(bf16[144,1024]{1,0:T(8,128)(2,1)} %get-tuple-element.243), channel_id=1, source_target_pairs={{0,2},{1,3},{2,0},{3,1},{4,6},{5,7},{6,4},{7,5},{8,10},{9,11},{10,... | collective-permute-start | bytes 884744 | tf_op jit(solution)/shard_map/ppermute | solution.py:115
  86.4 1.7 %collective-permute-start.22 = (bf16[128,1024]{1,0:T(8,128)(2,1)S(1)}, bf16[128,1024]{1,0:T(8,128)(2,1)S(1)}, u32[]{:S(2)}, u32[]{:S(2)}) collective-permute-start(bf16[128,1024]{1,0:T(8,128)(2,1)S(1)} %add_convert_fusion.5), channel_id=1, source_target_pairs={{0,4},{1,5},{2,6},{3,7},{4,0},{5,1},{6,2},{7,3},{8,12},{9,13},{10,... | collective-permute-start | bytes 786440 | tf_op jit(solution)/shard_map/ppermute | solution.py:115
  88.2 7.4 %shard_map.120 = bf16[1536,1024]{1,0:T(8,128)(2,1)} custom-call(bf16[144,1024]{1,0:T(8,128)(2,1)} %copy-done.1, bf16[144,1024]{1,0:T(8,128)(2,1)} %copy-done.5, bf16[144,1024]{1,0:T(8,128)(2,1)} %copy-done.3, bf16[144,1024]{1,0:T(8,128)(2,1)} %copy-done.7, bf16[144,1024]{1,0:T(8,128)(2,1)} %copy-done.4, bf16[144,1024]{1,0:T(8,128)(2,1)} %copy-done.8, ...), custom_call_target="tpu_custom_call" | custom-call | flops 3221225472 | bytes 13893632 | tf_op jit(solution)/shard_map/pallas_call | solution.py:162
  95.6 1.4 %collective-permute-done.20 = bf16[128,1024]{1,0:T(8,128)(2,1)S(1)} collective-permute-done((bf16[128,1024]{1,0:T(8,128)(2,1)S(1)}, bf16[128,1024]{1,0:T(8,128)(2,1)S(1)}, u32[]{:S(2)}, u32[]{:S(2)}) %collective-permute-start.20) | collective-permute-done | bytes 262176 | tf_op jit(solution)/shard_map/ppermute | solution.py:115
  97.3 1.6 %collective-permute-start.24 = (bf16[144,1024]{1,0:T(8,128)(2,1)S(1)}, bf16[144,1024]{1,0:T(8,128)(2,1)S(1)}, u32[]{:S(2)}, u32[]{:S(2)}) collective-permute-start(bf16[144,1024]{1,0:T(8,128)(2,1)S(1)} %copy-done.28), channel_id=1, source_target_pairs={{0,2},{1,3},{2,0},{3,1},{4,6},{5,7},{6,4},{7,5},{8,10},{9,11},{10,... | collective-permute-start | bytes 884744 | tf_op jit(solution)/shard_map/ppermute | solution.py:115
  99.4 1.4 %collective-permute-start.26 = (bf16[144,1024]{1,0:T(8,128)(2,1)S(1)}, bf16[144,1024]{1,0:T(8,128)(2,1)S(1)}, u32[]{:S(2)}, u32[]{:S(2)}) collective-permute-start(bf16[144,1024]{1,0:T(8,128)(2,1)S(1)} %add_convert_fusion.2), channel_id=1, source_target_pairs={{0,4},{1,5},{2,6},{3,7},{4,0},{5,1},{6,2},{7,3},{8,12},{9,13},{10,... | collective-permute-start | bytes 884744 | tf_op jit(solution)/shard_map/ppermute | solution.py:115
  100.8 0.8 collective-permute-start.23
  101.6 11.1 %collective-permute-done.23 = bf16[128,1024]{1,0:T(8,128)(2,1)S(1)} collective-permute-done((bf16[128,1024]{1,0:T(8,128)(2,1)S(1)}, bf16[128,1024]{1,0:T(8,128)(2,1)S(1)}, u32[]{:S(2)}, u32[]{:S(2)}) %collective-permute-start.23) | collective-permute-done | bytes 262176 | tf_op jit(solution)/shard_map/ppermute | solution.py:115
  113.0 0.8 collective-permute-done.26
  114.1 2.5 %collective-permute-start.28 = (bf16[144,1024]{1,0:T(8,128)(2,1)S(1)}, bf16[144,1024]{1,0:T(8,128)(2,1)S(1)}, u32[]{:S(2)}, u32[]{:S(2)}) collective-permute-start(bf16[144,1024]{1,0:T(8,128)(2,1)S(1)} %add_convert_fusion.1), channel_id=1, source_target_pairs={{0,8},{1,9},{2,10},{3,11},{4,12},{5,13},{6,14},{7,15},{8,0},{9,1},... | collective-permute-start | bytes 884744 | tf_op jit(solution)/shard_map/ppermute | solution.py:115
  116.6 1.4 %collective-permute-start.29 = (bf16[144,1024]{1,0:T(8,128)(2,1)S(1)}, bf16[144,1024]{1,0:T(8,128)(2,1)S(1)}, u32[]{:S(2)}, u32[]{:S(2)}) collective-permute-start(bf16[144,1024]{1,0:T(8,128)(2,1)S(1)} %copy-done.26), channel_id=1, source_target_pairs={{0,2},{1,3},{2,0},{3,1},{4,6},{5,7},{6,4},{7,5},{8,10},{9,11},{10,... | collective-permute-start | bytes 884744 | tf_op jit(solution)/shard_map/ppermute | solution.py:115
  118.6 8.3 %shard_map.121 = (bf16[1024,512]{1,0:T(8,128)(2,1)}, bf16[1024,512]{1,0:T(8,128)(2,1)}, bf16[512,1024]{1,0:T(8,128)(2,1)}) custom-call(bf16[144,1024]{1,0:T(8,128)(2,1)} %copy-done.1, bf16[144,1024]{1,0:T(8,128)(2,1)} %copy-done.5, bf16[144,1024]{1,0:T(8,128)(2,1)} %copy-done.3, bf16[144,1024]{1,0:T(8,128)(2,1)} %copy-done.7, bf16[144,1024]{1,0:T(8,128)(2,1)} %copy-done.4, ...), custom_call_target="tpu_custom_call" | custom-call | flops 3221225472 | bytes 17039360 | tf_op jit(solution)/shard_map/pallas_call | solution.py:162
  126.9 2.9 %collective-permute-done.30 = bf16[128,1024]{1,0:T(8,128)(2,1)S(1)} collective-permute-done((bf16[128,1024]{1,0:T(8,128)(2,1)S(1)}, bf16[128,1024]{1,0:T(8,128)(2,1)S(1)}, u32[]{:S(2)}, u32[]{:S(2)}) %collective-permute-start.30) | collective-permute-done | bytes 262176 | tf_op jit(solution)/shard_map/ppermute | solution.py:115
  131.3 0.7 pad_maximum_fusion.2
  (121 shorter events, 9.2 us)
Async XLA Ops:
  2.7 19.6 %collective-permute-start.4 = (bf16[1024,512]{1,0:T(8,128)(2,1)}, bf16[1024,512]{1,0:T(8,128)(2,1)S(1)}, u32[]{:S(2)}, u32[]{:S(2)}) collective-permute-start(bf16[1024,512]{1,0:T(8,128)(2,1)} %bitcast.20), channel_id=1, source_target_pairs={{0,1},{1,0},{2,3},{3,2},{4,5},{5,4},{6,7},{7,6},{8,9},{9,8},{10,11... | collective-permute-start | bytes 3145736 | tf_op jit(solution)/shard_map/ppermute | solution.py:115
  3.2 18.4 %collective-permute-start = (bf16[144,1024]{1,0:T(8,128)(2,1)S(1)}, bf16[144,1024]{1,0:T(8,128)(2,1)S(1)}, u32[]{:S(2)}, u32[]{:S(2)}) collective-permute-start(bf16[144,1024]{1,0:T(8,128)(2,1)S(1)} %fusion.1.refs_0_), channel_id=1, source_target_pairs={{0,8},{1,9},{2,10},{3,11},{4,12},{5,13},{6,14},{7,15},{8,0},{9,1},... | collective-permute-start | bytes 884744 | tf_op jit(solution)/shard_map/ppermute | solution.py:115
  6.8 14.7 %collective-permute-start.1 = (bf16[144,1024]{1,0:T(8,128)(2,1)S(1)}, bf16[144,1024]{1,0:T(8,128)(2,1)S(1)}, u32[]{:S(2)}, u32[]{:S(2)}) collective-permute-start(bf16[144,1024]{1,0:T(8,128)(2,1)S(1)} %fusion.1.refs_0_), channel_id=1, source_target_pairs={{0,2},{1,3},{2,0},{3,1},{4,6},{5,7},{6,4},{7,5},{8,10},{9,11},{10,... | collective-permute-start | bytes 884744 | tf_op jit(solution)/shard_map/ppermute | solution.py:115
  8.3 13.9 %collective-permute-start.3 = (bf16[144,1024]{1,0:T(8,128)(2,1)S(1)}, bf16[144,1024]{1,0:T(8,128)(2,1)S(1)}, u32[]{:S(2)}, u32[]{:S(2)}) collective-permute-start(bf16[144,1024]{1,0:T(8,128)(2,1)S(1)} %fusion.1.refs_0_), channel_id=1, source_target_pairs={{0,4},{1,5},{2,6},{3,7},{4,0},{5,1},{6,2},{7,3},{8,12},{9,13},{10,... | collective-permute-start | bytes 884744 | tf_op jit(solution)/shard_map/ppermute | solution.py:115
  9.9 11.6 %collective-permute-start.2 = (bf16[128,1024]{1,0:T(8,128)(2,1)S(1)}, bf16[128,1024]{1,0:T(8,128)(2,1)S(1)}, u32[]{:S(2)}, u32[]{:S(2)}) collective-permute-start(bf16[128,1024]{1,0:T(8,128)(2,1)S(1)} %pad_maximum_fusion.refs_0_.refs_8_), channel_id=1, source_target_pairs={{0,2},{1,3},{2,0},{3,1},{4,6},{5,7},{6,4},{7,5},{8,10},{9,11},{10,... | collective-permute-start | bytes 786440 | tf_op jit(solution)/shard_map/ppermute | solution.py:115
  22.3 17.5 %collective-permute-start.9 = (bf16[1024,512]{1,0:T(8,128)(2,1)}, bf16[1024,512]{1,0:T(8,128)(2,1)S(1)}, u32[]{:S(2)}, u32[]{:S(2)}) collective-permute-start(bf16[1024,512]{1,0:T(8,128)(2,1)} %bitcast.23), channel_id=1, source_target_pairs={{0,1},{1,0},{2,3},{3,2},{4,5},{5,4},{6,7},{7,6},{8,9},{9,8},{10,11... | collective-permute-start | bytes 3145736 | tf_op jit(solution)/shard_map/ppermute | solution.py:115
  22.4 17.4 %collective-permute-start.7 = (bf16[144,1024]{1,0:T(8,128)(2,1)S(1)}, bf16[144,1024]{1,0:T(8,128)(2,1)S(1)}, u32[]{:S(2)}, u32[]{:S(2)}) collective-permute-start(bf16[144,1024]{1,0:T(8,128)(2,1)S(1)} %collective-permute-done.refs_2_), channel_id=1, source_target_pairs={{0,2},{1,3},{2,0},{3,1},{4,6},{5,7},{6,4},{7,5},{8,10},{9,11},{10,... | collective-permute-start | bytes 884744 | tf_op jit(solution)/shard_map/ppermute | solution.py:115
  23.2 16.5 %collective-permute-start.8 = (bf16[144,1024]{1,0:T(8,128)(2,1)S(1)}, bf16[144,1024]{1,0:T(8,128)(2,1)S(1)}, u32[]{:S(2)}, u32[]{:S(2)}) collective-permute-start(bf16[144,1024]{1,0:T(8,128)(2,1)S(1)} %collective-permute-done.refs_2_), channel_id=1, source_target_pairs={{0,4},{1,5},{2,6},{3,7},{4,0},{5,1},{6,2},{7,3},{8,12},{9,13},{10,... | collective-permute-start | bytes 884744 | tf_op jit(solution)/shard_map/ppermute | solution.py:115
  24.8 14.9 %collective-permute-start.6 = (bf16[144,1024]{1,0:T(8,128)(2,1)S(1)}, bf16[144,1024]{1,0:T(8,128)(2,1)S(1)}, u32[]{:S(2)}, u32[]{:S(2)}) collective-permute-start(bf16[144,1024]{1,0:T(8,128)(2,1)S(1)} %collective-permute-done.3.refs_1_), channel_id=1, source_target_pairs={{0,2},{1,3},{2,0},{3,1},{4,6},{5,7},{6,4},{7,5},{8,10},{9,11},{10,... | collective-permute-start | bytes 884744 | tf_op jit(solution)/shard_map/ppermute | solution.py:115
  25.4 14.4 %collective-permute-start.5 = (bf16[128,1024]{1,0:T(8,128)(2,1)S(1)}, bf16[128,1024]{1,0:T(8,128)(2,1)S(1)}, u32[]{:S(2)}, u32[]{:S(2)}) collective-permute-start(bf16[128,1024]{1,0:T(8,128)(2,1)S(1)} %pad_maximum_fusion.refs_0_.refs_8_), channel_id=1, source_target_pairs={{0,8},{1,9},{2,10},{3,11},{4,12},{5,13},{6,14},{7,15},{8,0},{9,1},... | collective-permute-start | bytes 786440 | tf_op jit(solution)/shard_map/ppermute | solution.py:115
  39.8 16.0 %collective-permute-start.14 = (bf16[512,1024]{1,0:T(8,128)(2,1)}, bf16[512,1024]{1,0:T(8,128)(2,1)}, u32[]{:S(2)}, u32[]{:S(2)}) collective-permute-start(bf16[512,1024]{1,0:T(8,128)(2,1)} %bitcast.26), channel_id=1, source_target_pairs={{0,1},{1,0},{2,3},{3,2},{4,5},{5,4},{6,7},{7,6},{8,9},{9,8},{10,11... | collective-permute-start | bytes 3145736 | tf_op jit(solution)/shard_map/ppermute | solution.py:115
  39.9 15.9 %collective-permute-start.10 = (bf16[144,1024]{1,0:T(8,128)(2,1)S(1)}, bf16[144,1024]{1,0:T(8,128)(2,1)S(1)}, u32[]{:S(2)}, u32[]{:S(2)}) collective-permute-start(bf16[144,1024]{1,0:T(8,128)(2,1)S(1)} %collective-permute-done.8.refs_3_), channel_id=1, source_target_pairs={{0,2},{1,3},{2,0},{3,1},{4,6},{5,7},{6,4},{7,5},{8,10},{9,11},{10,... | collective-permute-start | bytes 884744 | tf_op jit(solution)/shard_map/ppermute | solution.py:115
  41.4 13.5 %collective-permute-start.11 = (bf16[128,1024]{1,0:T(8,128)(2,1)S(1)}, bf16[128,1024]{1,0:T(8,128)(2,1)S(1)}, u32[]{:S(2)}, u32[]{:S(2)}) collective-permute-start(bf16[128,1024]{1,0:T(8,128)(2,1)S(1)} %collective-permute-done.5.refs_2_.refs_10_), channel_id=1, source_target_pairs={{0,2},{1,3},{2,0},{3,1},{4,6},{5,7},{6,4},{7,5},{8,10},{9,11},{10,... | collective-permute-start | bytes 786440 | tf_op jit(solution)/shard_map/ppermute | solution.py:115
  42.0 12.9 %collective-permute-start.12 = (bf16[128,1024]{1,0:T(8,128)(2,1)S(1)}, bf16[128,1024]{1,0:T(8,128)(2,1)}, u32[]{:S(2)}, u32[]{:S(2)}) collective-permute-start(bf16[128,1024]{1,0:T(8,128)(2,1)S(1)} %collective-permute-done.5.refs_2_.refs_10_), channel_id=1, source_target_pairs={{0,4},{1,5},{2,6},{3,7},{4,0},{5,1},{6,2},{7,3},{8,12},{9,13},{10,... | collective-permute-start | bytes 786440 | tf_op jit(solution)/shard_map/ppermute | solution.py:115
  42.0 13.8 %collective-permute-start.13 = (bf16[128,1024]{1,0:T(8,128)(2,1)S(1)}, bf16[128,1024]{1,0:T(8,128)(2,1)}, u32[]{:S(2)}, u32[]{:S(2)}) collective-permute-start(bf16[128,1024]{1,0:T(8,128)(2,1)S(1)} %pad_maximum_fusion.refs_0_.refs_8_), channel_id=1, source_target_pairs={{0,4},{1,5},{2,6},{3,7},{4,0},{5,1},{6,2},{7,3},{8,12},{9,13},{10,... | collective-permute-start | bytes 786440 | tf_op jit(solution)/shard_map/ppermute | solution.py:115
  55.8 13.7 %collective-permute-start.15 = (bf16[128,1024]{1,0:T(8,128)(2,1)}, bf16[128,1024]{1,0:T(8,128)(2,1)S(1)}, u32[]{:S(2)}, u32[]{:S(2)}) collective-permute-start(bf16[128,1024]{1,0:T(8,128)(2,1)} %collective-permute-done.13.refs_1_.refs_9_), channel_id=1, source_target_pairs={{0,2},{1,3},{2,0},{3,1},{4,6},{5,7},{6,4},{7,5},{8,10},{9,11},{10,... | collective-permute-start | bytes 786440 | tf_op jit(solution)/shard_map/ppermute | solution.py:115
  57.4 12.1 %collective-permute-start.16 = (bf16[128,1024]{1,0:T(8,128)(2,1)S(1)}, bf16[128,1024]{1,0:T(8,128)(2,1)S(1)}, u32[]{:S(2)}, u32[]{:S(2)}) collective-permute-start(bf16[128,1024]{1,0:T(8,128)(2,1)S(1)} %collective-permute-done.11.refs_6_.refs_14_), channel_id=1, source_target_pairs={{0,4},{1,5},{2,6},{3,7},{4,0},{5,1},{6,2},{7,3},{8,12},{9,13},{10,... | collective-permute-start | bytes 786440 | tf_op jit(solution)/shard_map/ppermute | solution.py:115
  69.5 14.5 %collective-permute-start.17 = (bf16[128,1024]{1,0:T(8,128)(2,1)}, bf16[128,1024]{1,0:T(8,128)(2,1)S(1)}, u32[]{:S(2)}, u32[]{:S(2)}) collective-permute-start(bf16[128,1024]{1,0:T(8,128)(2,1)} %get-tuple-element.201), channel_id=1, source_target_pairs={{0,2},{1,3},{2,0},{3,1},{4,6},{5,7},{6,4},{7,5},{8,10},{9,11},{10,... | collective-permute-start | bytes 786440 | tf_op jit(solution)/shard_map/ppermute | solution.py:115
  70.1 13.9 %collective-permute-start.18 = (bf16[128,1024]{1,0:T(8,128)(2,1)}, bf16[128,1024]{1,0:T(8,128)(2,1)S(1)}, u32[]{:S(2)}, u32[]{:S(2)}) collective-permute-start(bf16[128,1024]{1,0:T(8,128)(2,1)} %get-tuple-element.202), channel_id=1, source_target_pairs={{0,4},{1,5},{2,6},{3,7},{4,0},{5,1},{6,2},{7,3},{8,12},{9,13},{10,... | collective-permute-start | bytes 786440 | tf_op jit(solution)/shard_map/ppermute | solution.py:115
  71.9 12.2 %collective-permute-start.19 = (bf16[128,1024]{1,0:T(8,128)(2,1)}, bf16[128,1024]{1,0:T(8,128)(2,1)S(1)}, u32[]{:S(2)}, u32[]{:S(2)}) collective-permute-start(bf16[128,1024]{1,0:T(8,128)(2,1)} %get-tuple-element.203), channel_id=1, source_target_pairs={{0,4},{1,5},{2,6},{3,7},{4,0},{5,1},{6,2},{7,3},{8,12},{9,13},{10,... | collective-permute-start | bytes 786440 | tf_op jit(solution)/shard_map/ppermute | solution.py:115
  84.3 12.7 %collective-permute-start.21 = (bf16[144,1024]{1,0:T(8,128)(2,1)}, bf16[144,1024]{1,0:T(8,128)(2,1)S(1)}, u32[]{:S(2)}, u32[]{:S(2)}) collective-permute-start(bf16[144,1024]{1,0:T(8,128)(2,1)} %get-tuple-element.243), channel_id=1, source_target_pairs={{0,2},{1,3},{2,0},{3,1},{4,6},{5,7},{6,4},{7,5},{8,10},{9,11},{10,... | collective-permute-start | bytes 884744 | tf_op jit(solution)/shard_map/ppermute | solution.py:115
  85.9 11.2 %collective-permute-start.20 = (bf16[128,1024]{1,0:T(8,128)(2,1)S(1)}, bf16[128,1024]{1,0:T(8,128)(2,1)S(1)}, u32[]{:S(2)}, u32[]{:S(2)}) collective-permute-start(bf16[128,1024]{1,0:T(8,128)(2,1)S(1)} %add_convert_fusion.6), channel_id=1, source_target_pairs={{0,2},{1,3},{2,0},{3,1},{4,6},{5,7},{6,4},{7,5},{8,10},{9,11},{10,... | collective-permute-start | bytes 786440 | tf_op jit(solution)/shard_map/ppermute | solution.py:115
  86.4 10.6 %collective-permute-start.22 = (bf16[128,1024]{1,0:T(8,128)(2,1)S(1)}, bf16[128,1024]{1,0:T(8,128)(2,1)S(1)}, u32[]{:S(2)}, u32[]{:S(2)}) collective-permute-start(bf16[128,1024]{1,0:T(8,128)(2,1)S(1)} %add_convert_fusion.5), channel_id=1, source_target_pairs={{0,4},{1,5},{2,6},{3,7},{4,0},{5,1},{6,2},{7,3},{8,12},{9,13},{10,... | collective-permute-start | bytes 786440 | tf_op jit(solution)/shard_map/ppermute | solution.py:115
  97.2 16.6 %collective-permute-start.27 = (bf16[1536,1024]{1,0:T(8,128)(2,1)}, bf16[1536,1024]{1,0:T(8,128)(2,1)S(1)}, u32[]{:S(2)}, u32[]{:S(2)}) collective-permute-start(bf16[1536,1024]{1,0:T(8,128)(2,1)} %shard_map.120), channel_id=1, source_target_pairs={{0,1},{1,0},{2,3},{3,2},{4,5},{5,4},{6,7},{7,6},{8,9},{9,8},{10,11... | collective-permute-start | bytes 9437192 | tf_op jit(solution)/shard_map/ppermute | solution.py:115
  97.3 15.5 %collective-permute-start.24 = (bf16[144,1024]{1,0:T(8,128)(2,1)S(1)}, bf16[144,1024]{1,0:T(8,128)(2,1)S(1)}, u32[]{:S(2)}, u32[]{:S(2)}) collective-permute-start(bf16[144,1024]{1,0:T(8,128)(2,1)S(1)} %copy-done.28), channel_id=1, source_target_pairs={{0,2},{1,3},{2,0},{3,1},{4,6},{5,7},{6,4},{7,5},{8,10},{9,11},{10,... | collective-permute-start | bytes 884744 | tf_op jit(solution)/shard_map/ppermute | solution.py:115
  98.9 14.2 %collective-permute-start.25 = (bf16[144,1024]{1,0:T(8,128)(2,1)S(1)}, bf16[144,1024]{1,0:T(8,128)(2,1)S(1)}, u32[]{:S(2)}, u32[]{:S(2)}) collective-permute-start(bf16[144,1024]{1,0:T(8,128)(2,1)S(1)} %copy-done.27), channel_id=1, source_target_pairs={{0,2},{1,3},{2,0},{3,1},{4,6},{5,7},{6,4},{7,5},{8,10},{9,11},{10,... | collective-permute-start | bytes 884744 | tf_op jit(solution)/shard_map/ppermute | solution.py:115
  99.4 14.4 %collective-permute-start.26 = (bf16[144,1024]{1,0:T(8,128)(2,1)S(1)}, bf16[144,1024]{1,0:T(8,128)(2,1)S(1)}, u32[]{:S(2)}, u32[]{:S(2)}) collective-permute-start(bf16[144,1024]{1,0:T(8,128)(2,1)S(1)} %add_convert_fusion.2), channel_id=1, source_target_pairs={{0,4},{1,5},{2,6},{3,7},{4,0},{5,1},{6,2},{7,3},{8,12},{9,13},{10,... | collective-permute-start | bytes 884744 | tf_op jit(solution)/shard_map/ppermute | solution.py:115
  100.8 11.9 %collective-permute-start.23 = (bf16[128,1024]{1,0:T(8,128)(2,1)S(1)}, bf16[128,1024]{1,0:T(8,128)(2,1)S(1)}, u32[]{:S(2)}, u32[]{:S(2)}) collective-permute-start(bf16[128,1024]{1,0:T(8,128)(2,1)S(1)} %add_convert_fusion.4), channel_id=1, source_target_pairs={{0,8},{1,9},{2,10},{3,11},{4,12},{5,13},{6,14},{7,15},{8,0},{9,1},... | collective-permute-start | bytes 786440 | tf_op jit(solution)/shard_map/ppermute | solution.py:115
  114.1 15.7 %collective-permute-start.28 = (bf16[144,1024]{1,0:T(8,128)(2,1)S(1)}, bf16[144,1024]{1,0:T(8,128)(2,1)S(1)}, u32[]{:S(2)}, u32[]{:S(2)}) collective-permute-start(bf16[144,1024]{1,0:T(8,128)(2,1)S(1)} %add_convert_fusion.1), channel_id=1, source_target_pairs={{0,8},{1,9},{2,10},{3,11},{4,12},{5,13},{6,14},{7,15},{8,0},{9,1},... | collective-permute-start | bytes 884744 | tf_op jit(solution)/shard_map/ppermute | solution.py:115
  116.6 13.2 %collective-permute-start.29 = (bf16[144,1024]{1,0:T(8,128)(2,1)S(1)}, bf16[144,1024]{1,0:T(8,128)(2,1)S(1)}, u32[]{:S(2)}, u32[]{:S(2)}) collective-permute-start(bf16[144,1024]{1,0:T(8,128)(2,1)S(1)} %copy-done.26), channel_id=1, source_target_pairs={{0,2},{1,3},{2,0},{3,1},{4,6},{5,7},{6,4},{7,5},{8,10},{9,11},{10,... | collective-permute-start | bytes 884744 | tf_op jit(solution)/shard_map/ppermute | solution.py:115
  118.0 12.2 %collective-permute-start.31 = (bf16[144,1024]{1,0:T(8,128)(2,1)S(1)}, bf16[144,1024]{1,0:T(8,128)(2,1)S(1)}, u32[]{:S(2)}, u32[]{:S(2)}) collective-permute-start(bf16[144,1024]{1,0:T(8,128)(2,1)S(1)} %add_convert_fusion), channel_id=1, source_target_pairs={{0,4},{1,5},{2,6},{3,7},{4,0},{5,1},{6,2},{7,3},{8,12},{9,13},{10,... | collective-permute-start | bytes 884744 | tf_op jit(solution)/shard_map/ppermute | solution.py:115
  118.0 11.8 %collective-permute-start.30 = (bf16[128,1024]{1,0:T(8,128)(2,1)S(1)}, bf16[128,1024]{1,0:T(8,128)(2,1)S(1)}, u32[]{:S(2)}, u32[]{:S(2)}) collective-permute-start(bf16[128,1024]{1,0:T(8,128)(2,1)S(1)} %copy-done.29), channel_id=1, source_target_pairs={{0,2},{1,3},{2,0},{3,1},{4,6},{5,7},{6,4},{7,5},{8,10},{9,11},{10,... | collective-permute-start | bytes 786440 | tf_op jit(solution)/shard_map/ppermute | solution.py:115
  (30 other events, 613.0 us)

commit v9 on v8

--- a/solution.py
+++ b/solution.py
@@ -416,26 +416,26 @@
     lines = jnp.pad(lines, ((0, EXTRA - lines.shape[0]), (0, 0)))
     a0 = jnp.concatenate([latent_in[:mid], cotangent[:mid], lines], axis=0)
     b0 = jnp.concatenate([latent_in[mid:], cotangent[mid:]], axis=0)
-    a0, b0, own = fence(a0, b0, own)
-
-    a4, a2, a1, b4 = swap(a0, SIDE), swap(a0, FAR), swap(a0, NEAR), swap(b0, SIDE)
-    gate_w = swap(own[0], CORE)
-    a2, a4, b4, a1, gate_w, a0, b0, own = fence(a2, a4, b4, a1, gate_w, a0, b0, own)
-    a6, a5, b2, a3 = swap(a2, SIDE), swap(a1, SIDE), swap(b0, FAR), swap(a2, NEAR)
-    up_w = swap(own[1], CORE)
-    b2, a5, a6, a3, up_w, a0, b0, own = fence(b2, a5, a6, a3, up_w, a0, b0, own)
-    a7, b6, b1, b3 = swap(a3, SIDE), swap(b2, SIDE), swap(b0, NEAR), swap(b2, NEAR)
-    down_w = swap(own[2], CORE)
-    a7, b6, b3, b1, down_w, a0, b0, own = fence(a7, b6, b3, b1, down_w, a0, b0, own)
+    gate_w, up_w, down_w = [swap(w, CORE) for w in own]
+    a0, b0, gate_w, up_w, down_w, own = fence(a0, b0, gate_w, up_w, down_w, own)
+
+    a2, a4, b4, a1 = swap(a0, FAR), swap(a0, SIDE), swap(b0, SIDE), swap(a0, NEAR)
+    a2, a1, a4, b4, b0 = fence(a2, a1, a4, b4, b0)
+    a5, a6, a3, b2 = swap(a1, SIDE), swap(a2, SIDE), swap(a2, NEAR), swap(b0, FAR)
+    (a3,) = fence(a3)
+    a7 = swap(a3, SIDE)
+    b2, a5, a6 = fence(b2, a5, a6)
+    b6, b1, b3 = swap(b2, SIDE), swap(b0, NEAR), swap(b2, NEAR)
+    a7, b1, b6 = fence(a7, b1, b6)
     b5, b7 = swap(b1, SIDE), swap(b6, NEAR)
     weights, me = (own, (gate_w, up_w, down_w)), me.astype(jnp.int32).reshape(1)
     a = [a0, a1, a2, a3, a4, a5, a6, a7]
     q, (*a_factors, shares, inners) = both_ways(0, a, weights, me)
     q, shares, inners, b5, b7 = fence(q, shares, inners, b5, b7)
-    q5, q7, q3 = swap(q[5], SIDE), swap(q[7], NEAR), swap(q[3], NEAR)
+    q5, q7, q3, q4 = swap(q[5], SIDE), swap(q[7], NEAR), swap(q[3], NEAR), swap(q[4], SIDE)
     b = [b0, b1, b2, b3, b4, b5, b6, b7]
     p, b_factors = both_ways(1, b, weights, me, (shares, inners))
-    q5, q7, q3, p, q, b_factors = fence(q5, q7, q3, p, q, b_factors)
+    q5, q7, q3, q4, p, q, b_factors = fence(q5, q7, q3, q4, p, q, b_factors)
     factors = (a_factors, b_factors)
     q6, q2, q1 = narrow(added(q[6], q7)), added(q[2], q3), narrow(added(q[1], q5))
     q6, q2, q1, p, q = fence(q6, q2, q1, p, q)
@@ -449,9 +449,9 @@
     q2, p6, p5, p3, away, p, q = fence(q2, p6, p5, p3, away, p, q)
     p2, p1 = narrow(added(p[2], p6) + p3.astype(f32)), narrow(added(p[1], p5))
     p2, p1, p, q, away = fence(p2, p1, p, q, away)
-    p4, q4, p2, p1 = swap(p[4], SIDE), swap(q[4], SIDE), swap(p2, FAR), swap(p1, NEAR)
+    p4, p2, p1 = swap(p[4], SIDE), swap(p2, FAR), swap(p1, NEAR)
     grad_w = weight_grads(0, (a, b), factors, away)
-    p2, p4, q4, p1, grad_w = fence(p2, p4, q4, p1, grad_w)
+    p2, p4, p1, grad_w = fence(p2, p4, p1, grad_w)
 
     q = added(q[0], q4) + added(q1, q2)
     p = added(p[0], p4) + added(p1, p2)

time: 133 us -> 131 us (0.985)
  waiting for transfers between devices: 52.8 us -> 42.9 us
  starting transfers between devices: 34.4 us -> 41.2 us
    ppermute x32, waiting for transfers between devices: 52.8 us -> 42.9 us  [swap(): return lax.ppermute(value, 'ep', pairs)]
    ppermute x32, starting transfers between devices: 34.4 us -> 41.2 us  [swap(): return lax.ppermute(value, 'ep', pairs)]
  transfers between devices with their start and end apart: 32 -> 32, of which waited for: 11 -> 12; matrix products, arithmetic and copies ran while one was open for 0% -> 2% of each run, Pallas kernels for 30% -> 30%
where the time goes in v9:
time: 131 us; the launch traced here: 130 us
  waiting for transfers between devices  42.9 us (33%)
  starting transfers between devices  41.2 us (31%)
  Pallas kernels  39.2 us (30%)
  other arithmetic  3.76 us (3%)
  local copies, waits for them, and re-layouts  2.04 us (2%)
    ppermute x32, waiting for transfers between devices, swap(): return lax.ppermute(value, 'ep', pairs)  42.9 us
    ppermute x32, starting transfers between devices, swap(): return lax.ppermute(value, 'ep', pairs)  41.2 us
    pallas_call x4, Pallas kernels, kernel(): pl.pallas_call(body, out_shape=outs, in_specs=in_specs, out_specs=[pl.Blo...  39.2 us
  transfers between devices with their start and end apart: 32, of which 12 were waited for; matrix products, arithmetic and copies ran while one was open for 2% of the time, Pallas kernels for 30%

profile of v9, /device:TPU:0, one launch (start us, length us, event | category | flops | bytes accessed | tf_op | source)
XLA Modules:
  0.0 130.3 jit_solution(15905643595530589716)
XLA Ops:
  2.5 1.1 fusion.6
  3.7 2.9 %collective-permute-done.1.refs_12_ = bf16[1024,512]{1,0:T(8,128)(2,1)S(1)} collective-permute-done((bf16[1024,512]{1,0:T(8,128)(2,1)}, bf16[1024,512]{1,0:T(8,128)(2,1)S(1)}, u32[]{:S(2)}, u32[]{:S(2)}) %collective-permute-start.1) | collective-permute-done | bytes 1048608 | tf_op jit(solution)/shard_map/ppermute | solution.py:115
  6.8 4.0 %collective-permute-start.3 = (bf16[144,1024]{1,0:T(8,128)(2,1)S(1)}, bf16[144,1024]{1,0:T(8,128)(2,1)S(1)}, u32[]{:S(2)}, u32[]{:S(2)}) collective-permute-start(bf16[144,1024]{1,0:T(8,128)(2,1)S(1)} %fusion.1.refs_0_), channel_id=1, source_target_pairs={{0,8},{1,9},{2,10},{3,11},{4,12},{5,13},{6,14},{7,15},{8,0},{9,1},... | collective-permute-start | bytes 884744 | tf_op jit(solution)/shard_map/ppermute | solution.py:115
  10.7 1.6 %collective-permute-start.4 = (bf16[144,1024]{1,0:T(8,128)(2,1)S(1)}, bf16[144,1024]{1,0:T(8,128)(2,1)S(1)}, u32[]{:S(2)}, u32[]{:S(2)}) collective-permute-start(bf16[144,1024]{1,0:T(8,128)(2,1)S(1)} %fusion.1.refs_0_), channel_id=1, source_target_pairs={{0,4},{1,5},{2,6},{3,7},{4,0},{5,1},{6,2},{7,3},{8,12},{9,13},{10,... | collective-permute-start | bytes 884744 | tf_op jit(solution)/shard_map/ppermute | solution.py:115
  12.3 1.5 %collective-permute-start.5 = (bf16[144,1024]{1,0:T(8,128)(2,1)S(1)}, bf16[144,1024]{1,0:T(8,128)(2,1)S(1)}, u32[]{:S(2)}, u32[]{:S(2)}) collective-permute-start(bf16[144,1024]{1,0:T(8,128)(2,1)S(1)} %fusion.1.refs_0_), channel_id=1, source_target_pairs={{0,2},{1,3},{2,0},{3,1},{4,6},{5,7},{6,4},{7,5},{8,10},{9,11},{10,... | collective-permute-start | bytes 884744 | tf_op jit(solution)/shard_map/ppermute | solution.py:115
  14.3 12.1 %collective-permute-done.6.refs_4_.refs_12_ = bf16[128,1024]{1,0:T(8,128)(2,1)S(1)} collective-permute-done((bf16[128,1024]{1,0:T(8,128)(2,1)S(1)}, bf16[128,1024]{1,0:T(8,128)(2,1)S(1)}, u32[]{:S(2)}, u32[]{:S(2)}) %collective-permute-start.6) | collective-permute-done | bytes 262176 | tf_op jit(solution)/shard_map/ppermute | solution.py:115
  27.0 1.5 %collective-permute-start.10 = (bf16[144,1024]{1,0:T(8,128)(2,1)S(1)}, bf16[144,1024]{1,0:T(8,128)(2,1)S(1)}, u32[]{:S(2)}, u32[]{:S(2)}) collective-permute-start(bf16[144,1024]{1,0:T(8,128)(2,1)S(1)} %collective-permute-done.3.refs_2_), channel_id=1, source_target_pairs={{0,2},{1,3},{2,0},{3,1},{4,6},{5,7},{6,4},{7,5},{8,10},{9,11},{10,... | collective-permute-start | bytes 884744 | tf_op jit(solution)/shard_map/ppermute | solution.py:115
  29.0 1.6 %collective-permute-start.8 = (bf16[128,1024]{1,0:T(8,128)(2,1)S(1)}, bf16[128,1024]{1,0:T(8,128)(2,1)S(1)}, u32[]{:S(2)}, u32[]{:S(2)}) collective-permute-start(bf16[128,1024]{1,0:T(8,128)(2,1)S(1)} %pad_maximum_fusion.refs_0_.refs_8_), channel_id=1, source_target_pairs={{0,8},{1,9},{2,10},{3,11},{4,12},{5,13},{6,14},{7,15},{8,0},{9,1},... | collective-permute-start | bytes 786440 | tf_op jit(solution)/shard_map/ppermute | solution.py:115
  30.6 8.2 %collective-permute-done.7.refs_3_ = bf16[144,1024]{1,0:T(8,128)(2,1)S(1)} collective-permute-done((bf16[144,1024]{1,0:T(8,128)(2,1)S(1)}, bf16[144,1024]{1,0:T(8,128)(2,1)S(1)}, u32[]{:S(2)}, u32[]{:S(2)}) %collective-permute-start.7) | collective-permute-done | bytes 294944 | tf_op jit(solution)/shard_map/ppermute | solution.py:115
  38.7 1.5 %collective-permute-start.11 = (bf16[144,1024]{1,0:T(8,128)(2,1)S(1)}, bf16[144,1024]{1,0:T(8,128)(2,1)S(1)}, u32[]{:S(2)}, u32[]{:S(2)}) collective-permute-start(bf16[144,1024]{1,0:T(8,128)(2,1)S(1)} %collective-permute-done.7.refs_3_), channel_id=1, source_target_pairs={{0,2},{1,3},{2,0},{3,1},{4,6},{5,7},{6,4},{7,5},{8,10},{9,11},{10,... | collective-permute-start | bytes 884744 | tf_op jit(solution)/shard_map/ppermute | solution.py:115
  40.2 1.8 %collective-permute-done.8.refs_2_.refs_10_ = bf16[128,1024]{1,0:T(8,128)(2,1)S(1)} collective-permute-done((bf16[128,1024]{1,0:T(8,128)(2,1)S(1)}, bf16[128,1024]{1,0:T(8,128)(2,1)S(1)}, u32[]{:S(2)}, u32[]{:S(2)}) %collective-permute-start.8) | collective-permute-done | bytes 262176 | tf_op jit(solution)/shard_map/ppermute | solution.py:115
  42.1 1.5 %collective-permute-start.13 = (bf16[128,1024]{1,0:T(8,128)(2,1)S(1)}, bf16[128,1024]{1,0:T(8,128)(2,1)}, u32[]{:S(2)}, u32[]{:S(2)}) collective-permute-start(bf16[128,1024]{1,0:T(8,128)(2,1)S(1)} %collective-permute-done.8.refs_2_.refs_10_), channel_id=1, source_target_pairs={{0,2},{1,3},{2,0},{3,1},{4,6},{5,7},{6,4},{7,5},{8,10},{9,11},{10,... | collective-permute-start | bytes 786440 | tf_op jit(solution)/shard_map/ppermute | solution.py:115
  43.6 2.7 %collective-permute-start.20 = (bf16[128,1024]{1,0:T(8,128)(2,1)S(1)}, bf16[128,1024]{1,0:T(8,128)(2,1)S(1)}, u32[]{:S(2)}, u32[]{:S(2)}) collective-permute-start(bf16[128,1024]{1,0:T(8,128)(2,1)S(1)} %collective-permute-done.8.refs_2_.refs_10_), channel_id=1, source_target_pairs={{0,4},{1,5},{2,6},{3,7},{4,0},{5,1},{6,2},{7,3},{8,12},{9,13},{10,... | collective-permute-start | bytes 786440 | tf_op jit(solution)/shard_map/ppermute | solution.py:115
  46.3 3.2 %collective-permute-done.12.refs_1_.refs_9_ = bf16[128,1024]{1,0:T(8,128)(2,1)S(1)} collective-permute-done((bf16[128,1024]{1,0:T(8,128)(2,1)S(1)}, bf16[128,1024]{1,0:T(8,128)(2,1)S(1)}, u32[]{:S(2)}, u32[]{:S(2)}) %collective-permute-start.12) | collective-permute-done | bytes 262176 | tf_op jit(solution)/shard_map/ppermute | solution.py:115
  49.5 3.2 %collective-permute-done.13.refs_6_.refs_14_ = bf16[128,1024]{1,0:T(8,128)(2,1)} collective-permute-done((bf16[128,1024]{1,0:T(8,128)(2,1)S(1)}, bf16[128,1024]{1,0:T(8,128)(2,1)}, u32[]{:S(2)}, u32[]{:S(2)}) %collective-permute-start.13) | collective-permute-done | bytes 262176 | tf_op jit(solution)/shard_map/ppermute | solution.py:115
  52.7 1.5 %collective-permute-start.14 = (bf16[128,1024]{1,0:T(8,128)(2,1)S(1)}, bf16[128,1024]{1,0:T(8,128)(2,1)S(1)}, u32[]{:S(2)}, u32[]{:S(2)}) collective-permute-start(bf16[128,1024]{1,0:T(8,128)(2,1)S(1)} %collective-permute-done.12.refs_1_.refs_9_), channel_id=1, source_target_pairs={{0,2},{1,3},{2,0},{3,1},{4,6},{5,7},{6,4},{7,5},{8,10},{9,11},{10,... | collective-permute-start | bytes 786440 | tf_op jit(solution)/shard_map/ppermute | solution.py:115
  54.1 1.6 %collective-permute-start.15 = (bf16[128,1024]{1,0:T(8,128)(2,1)}, bf16[128,1024]{1,0:T(8,128)(2,1)S(1)}, u32[]{:S(2)}, u32[]{:S(2)}) collective-permute-start(bf16[128,1024]{1,0:T(8,128)(2,1)} %collective-permute-done.13.refs_6_.refs_14_), channel_id=1, source_target_pairs={{0,4},{1,5},{2,6},{3,7},{4,0},{5,1},{6,2},{7,3},{8,12},{9,13},{10,... | collective-permute-start | bytes 786440 | tf_op jit(solution)/shard_map/ppermute | solution.py:115
  55.8 11.7 %shard_map.118 = (bf16[128,1024]{1,0:T(8,128)(2,1)}, bf16[128,1024]{1,0:T(8,128)(2,1)}, bf16[128,1024]{1,0:T(8,128)(2,1)}, bf16[128,1024]{1,0:T(8,128)(2,1)}, bf...) custom-call(s32[1]{0:T(128)} %bitcast.me_ref, ...), custom_call_target="tpu_custom_call" | custom-call | flops 6442450944 | bytes 14024704 | tf_op jit(solution)/shard_map/pallas_call | solution.py:162
  68.6 1.6 %collective-permute-start.18 = (bf16[128,1024]{1,0:T(8,128)(2,1)}, bf16[128,1024]{1,0:T(8,128)(2,1)S(1)}, u32[]{:S(2)}, u32[]{:S(2)}) collective-permute-start(bf16[128,1024]{1,0:T(8,128)(2,1)} %get-tuple-element.167), channel_id=1, source_target_pairs={{0,4},{1,5},{2,6},{3,7},{4,0},{5,1},{6,2},{7,3},{8,12},{9,13},{10,... | collective-permute-start | bytes 786440 | tf_op jit(solution)/shard_map/ppermute | solution.py:115
  70.2 1.5 %collective-permute-start.19 = (bf16[128,1024]{1,0:T(8,128)(2,1)}, bf16[128,1024]{1,0:T(8,128)(2,1)S(1)}, u32[]{:S(2)}, u32[]{:S(2)}) collective-permute-start(bf16[128,1024]{1,0:T(8,128)(2,1)} %get-tuple-element.168), channel_id=1, source_target_pairs={{0,2},{1,3},{2,0},{3,1},{4,6},{5,7},{6,4},{7,5},{8,10},{9,11},{10,... | collective-permute-start | bytes 786440 | tf_op jit(solution)/shard_map/ppermute | solution.py:115
  72.4 11.9 %shard_map.119 = (bf16[144,1024]{1,0:T(8,128)(2,1)}, bf16[144,1024]{1,0:T(8,128)(2,1)}, bf16[144,1024]{1,0:T(8,128)(2,1)}, bf16[144,1024]{1,0:T(8,128)(2,1)}, bf...) custom-call(s32[1]{0:T(128)} %bitcast.me_ref, ...), custom_call_target="tpu_custom_call" | custom-call | flops 6442450944 | bytes 14024704 | tf_op jit(solution)/shard_map/pallas_call | solution.py:162
  85.1 1.5 %collective-permute-start.21 = (bf16[128,1024]{1,0:T(8,128)(2,1)S(1)}, bf16[128,1024]{1,0:T(8,128)(2,1)S(1)}, u32[]{:S(2)}, u32[]{:S(2)}) collective-permute-start(bf16[128,1024]{1,0:T(8,128)(2,1)S(1)} %add_convert_fusion.6), channel_id=1, source_target_pairs={{0,2},{1,3},{2,0},{3,1},{4,6},{5,7},{6,4},{7,5},{8,10},{9,11},{10,... | collective-permute-start | bytes 786440 | tf_op jit(solution)/shard_map/ppermute | solution.py:115
  87.1 7.4 %shard_map.120 = bf16[1536,1024]{1,0:T(8,128)(2,1)} custom-call(bf16[144,1024]{1,0:T(8,128)(2,1)} %copy-done.1, bf16[144,1024]{1,0:T(8,128)(2,1)} %copy-done.4, bf16[144,1024]{1,0:T(8,128)(2,1)} %copy-done.3, bf16[144,1024]{1,0:T(8,128)(2,1)} %copy-done.6, bf16[144,1024]{1,0:T(8,128)(2,1)} %copy-done.5, bf16[144,1024]{1,0:T(8,128)(2,1)} %copy-done.8, ...), custom_call_target="tpu_custom_call" | custom-call | flops 3221225472 | bytes 13893632 | tf_op jit(solution)/shard_map/pallas_call | solution.py:162
  96.0 1.5 %collective-permute-start.26 = (bf16[144,1024]{1,0:T(8,128)(2,1)S(1)}, bf16[144,1024]{1,0:T(8,128)(2,1)S(1)}, u32[]{:S(2)}, u32[]{:S(2)}) collective-permute-start(bf16[144,1024]{1,0:T(8,128)(2,1)S(1)} %copy-done.28), channel_id=1, source_target_pairs={{0,2},{1,3},{2,0},{3,1},{4,6},{5,7},{6,4},{7,5},{8,10},{9,11},{10,... | collective-permute-start | bytes 884744 | tf_op jit(solution)/shard_map/ppermute | solution.py:115
  97.5 1.3 %collective-permute-start.27 = (bf16[144,1024]{1,0:T(8,128)(2,1)S(1)}, bf16[144,1024]{1,0:T(8,128)(2,1)S(1)}, u32[]{:S(2)}, u32[]{:S(2)}) collective-permute-start(bf16[144,1024]{1,0:T(8,128)(2,1)S(1)} %add_convert_fusion.2), channel_id=1, source_target_pairs={{0,4},{1,5},{2,6},{3,7},{4,0},{5,1},{6,2},{7,3},{8,12},{9,13},{10,... | collective-permute-start | bytes 884744 | tf_op jit(solution)/shard_map/ppermute | solution.py:115
  98.8 3.5 %collective-permute-start.24 = (bf16[128,1024]{1,0:T(8,128)(2,1)S(1)}, bf16[128,1024]{1,0:T(8,128)(2,1)S(1)}, u32[]{:S(2)}, u32[]{:S(2)}) collective-permute-start(bf16[128,1024]{1,0:T(8,128)(2,1)S(1)} %add_convert_fusion.4), channel_id=1, source_target_pairs={{0,8},{1,9},{2,10},{3,11},{4,12},{5,13},{6,14},{7,15},{8,0},{9,1},... | collective-permute-start | bytes 786440 | tf_op jit(solution)/shard_map/ppermute | solution.py:115
  102.3 8.5 %collective-permute-done.24 = bf16[128,1024]{1,0:T(8,128)(2,1)S(1)} collective-permute-done((bf16[128,1024]{1,0:T(8,128)(2,1)S(1)}, bf16[128,1024]{1,0:T(8,128)(2,1)S(1)}, u32[]{:S(2)}, u32[]{:S(2)}) %collective-permute-start.24) | collective-permute-done | bytes 262176 | tf_op jit(solution)/shard_map/ppermute | solution.py:115
  112.4 2.5 %collective-permute-start.29 = (bf16[144,1024]{1,0:T(8,128)(2,1)S(1)}, bf16[144,1024]{1,0:T(8,128)(2,1)S(1)}, u32[]{:S(2)}, u32[]{:S(2)}) collective-permute-start(bf16[144,1024]{1,0:T(8,128)(2,1)S(1)} %add_convert_fusion.1), channel_id=1, source_target_pairs={{0,8},{1,9},{2,10},{3,11},{4,12},{5,13},{6,14},{7,15},{8,0},{9,1},... | collective-permute-start | bytes 884744 | tf_op jit(solution)/shard_map/ppermute | solution.py:115
  114.8 0.8 collective-permute-start.30
  115.7 2.8 %collective-permute-start.31 = (bf16[144,1024]{1,0:T(8,128)(2,1)S(1)}, bf16[144,1024]{1,0:T(8,128)(2,1)S(1)}, u32[]{:S(2)}, u32[]{:S(2)}) collective-permute-start(bf16[144,1024]{1,0:T(8,128)(2,1)S(1)} %add_convert_fusion), channel_id=1, source_target_pairs={{0,4},{1,5},{2,6},{3,7},{4,0},{5,1},{6,2},{7,3},{8,12},{9,13},{10,... | collective-permute-start | bytes 884744 | tf_op jit(solution)/shard_map/ppermute | solution.py:115
  118.4 8.3 %shard_map.121 = (bf16[1024,512]{1,0:T(8,128)(2,1)}, bf16[1024,512]{1,0:T(8,128)(2,1)}, bf16[512,1024]{1,0:T(8,128)(2,1)}) custom-call(bf16[144,1024]{1,0:T(8,128)(2,1)} %copy-done.1, bf16[144,1024]{1,0:T(8,128)(2,1)} %copy-done.4, bf16[144,1024]{1,0:T(8,128)(2,1)} %copy-done.3, bf16[144,1024]{1,0:T(8,128)(2,1)} %copy-done.6, bf16[144,1024]{1,0:T(8,128)(2,1)} %copy-done.5, ...), custom_call_target="tpu_custom_call" | custom-call | flops 3221225472 | bytes 17039360 | tf_op jit(solution)/shard_map/pallas_call | solution.py:162
  126.7 1.2 collective-permute-done.29
  (121 shorter events, 11.9 us)
Async XLA Ops:
  0.6 3.1 %collective-permute-start = (bf16[1024,512]{1,0:T(8,128)(2,1)}, bf16[1024,512]{1,0:T(8,128)(2,1)S(1)}, u32[]{:S(2)}, u32[]{:S(2)}) collective-permute-start(bf16[1024,512]{1,0:T(8,128)(2,1)} %bitcast.20), channel_id=1, source_target_pairs={{0,1},{1,0},{2,3},{3,2},{4,5},{5,4},{6,7},{7,6},{8,9},{9,8},{10,11... | collective-permute-start | bytes 3145736 | tf_op jit(solution)/shard_map/ppermute | solution.py:115
  1.1 5.5 %collective-permute-start.1 = (bf16[1024,512]{1,0:T(8,128)(2,1)}, bf16[1024,512]{1,0:T(8,128)(2,1)S(1)}, u32[]{:S(2)}, u32[]{:S(2)}) collective-permute-start(bf16[1024,512]{1,0:T(8,128)(2,1)} %bitcast.23), channel_id=1, source_target_pairs={{0,1},{1,0},{2,3},{3,2},{4,5},{5,4},{6,7},{7,6},{8,9},{9,8},{10,11... | collective-permute-start | bytes 3145736 | tf_op jit(solution)/shard_map/ppermute | solution.py:115
  1.2 5.5 %collective-permute-start.2 = (bf16[512,1024]{1,0:T(8,128)(2,1)}, bf16[512,1024]{1,0:T(8,128)(2,1)}, u32[]{:S(2)}, u32[]{:S(2)}) collective-permute-start(bf16[512,1024]{1,0:T(8,128)(2,1)} %bitcast.26), channel_id=1, source_target_pairs={{0,1},{1,0},{2,3},{3,2},{4,5},{5,4},{6,7},{7,6},{8,9},{9,8},{10,11... | collective-permute-start | bytes 3145736 | tf_op jit(solution)/shard_map/ppermute | solution.py:115
  6.8 19.6 %collective-permute-start.3 = (bf16[144,1024]{1,0:T(8,128)(2,1)S(1)}, bf16[144,1024]{1,0:T(8,128)(2,1)S(1)}, u32[]{:S(2)}, u32[]{:S(2)}) collective-permute-start(bf16[144,1024]{1,0:T(8,128)(2,1)S(1)} %fusion.1.refs_0_), channel_id=1, source_target_pairs={{0,8},{1,9},{2,10},{3,11},{4,12},{5,13},{6,14},{7,15},{8,0},{9,1},... | collective-permute-start | bytes 884744 | tf_op jit(solution)/shard_map/ppermute | solution.py:115
  10.7 15.7 %collective-permute-start.4 = (bf16[144,1024]{1,0:T(8,128)(2,1)S(1)}, bf16[144,1024]{1,0:T(8,128)(2,1)S(1)}, u32[]{:S(2)}, u32[]{:S(2)}) collective-permute-start(bf16[144,1024]{1,0:T(8,128)(2,1)S(1)} %fusion.1.refs_0_), channel_id=1, source_target_pairs={{0,4},{1,5},{2,6},{3,7},{4,0},{5,1},{6,2},{7,3},{8,12},{9,13},{10,... | collective-permute-start | bytes 884744 | tf_op jit(solution)/shard_map/ppermute | solution.py:115
  12.3 14.1 %collective-permute-start.5 = (bf16[144,1024]{1,0:T(8,128)(2,1)S(1)}, bf16[144,1024]{1,0:T(8,128)(2,1)S(1)}, u32[]{:S(2)}, u32[]{:S(2)}) collective-permute-start(bf16[144,1024]{1,0:T(8,128)(2,1)S(1)} %fusion.1.refs_0_), channel_id=1, source_target_pairs={{0,2},{1,3},{2,0},{3,1},{4,6},{5,7},{6,4},{7,5},{8,10},{9,11},{10,... | collective-permute-start | bytes 884744 | tf_op jit(solution)/shard_map/ppermute | solution.py:115
  13.8 12.6 %collective-permute-start.6 = (bf16[128,1024]{1,0:T(8,128)(2,1)S(1)}, bf16[128,1024]{1,0:T(8,128)(2,1)S(1)}, u32[]{:S(2)}, u32[]{:S(2)}) collective-permute-start(bf16[128,1024]{1,0:T(8,128)(2,1)S(1)} %pad_maximum_fusion.refs_0_.refs_8_), channel_id=1, source_target_pairs={{0,2},{1,3},{2,0},{3,1},{4,6},{5,7},{6,4},{7,5},{8,10},{9,11},{10,... | collective-permute-start | bytes 786440 | tf_op jit(solution)/shard_map/ppermute | solution.py:115
  26.5 12.3 %collective-permute-start.7 = (bf16[144,1024]{1,0:T(8,128)(2,1)S(1)}, bf16[144,1024]{1,0:T(8,128)(2,1)S(1)}, u32[]{:S(2)}, u32[]{:S(2)}) collective-permute-start(bf16[144,1024]{1,0:T(8,128)(2,1)S(1)} %collective-permute-done.3.refs_2_), channel_id=1, source_target_pairs={{0,4},{1,5},{2,6},{3,7},{4,0},{5,1},{6,2},{7,3},{8,12},{9,13},{10,... | collective-permute-start | bytes 884744 | tf_op jit(solution)/shard_map/ppermute | solution.py:115
  27.0 15.0 %collective-permute-start.10 = (bf16[144,1024]{1,0:T(8,128)(2,1)S(1)}, bf16[144,1024]{1,0:T(8,128)(2,1)S(1)}, u32[]{:S(2)}, u32[]{:S(2)}) collective-permute-start(bf16[144,1024]{1,0:T(8,128)(2,1)S(1)} %collective-permute-done.3.refs_2_), channel_id=1, source_target_pairs={{0,2},{1,3},{2,0},{3,1},{4,6},{5,7},{6,4},{7,5},{8,10},{9,11},{10,... | collective-permute-start | bytes 884744 | tf_op jit(solution)/shard_map/ppermute | solution.py:115
  28.5 13.6 %collective-permute-start.9 = (bf16[144,1024]{1,0:T(8,128)(2,1)S(1)}, bf16[144,1024]{1,0:T(8,128)(2,1)S(1)}, u32[]{:S(2)}, u32[]{:S(2)}) collective-permute-start(bf16[144,1024]{1,0:T(8,128)(2,1)S(1)} %collective-permute-done.4.refs_1_), channel_id=1, source_target_pairs={{0,2},{1,3},{2,0},{3,1},{4,6},{5,7},{6,4},{7,5},{8,10},{9,11},{10,... | collective-permute-start | bytes 884744 | tf_op jit(solution)/shard_map/ppermute | solution.py:115
  29.0 13.0 %collective-permute-start.8 = (bf16[128,1024]{1,0:T(8,128)(2,1)S(1)}, bf16[128,1024]{1,0:T(8,128)(2,1)S(1)}, u32[]{:S(2)}, u32[]{:S(2)}) collective-permute-start(bf16[128,1024]{1,0:T(8,128)(2,1)S(1)} %pad_maximum_fusion.refs_0_.refs_8_), channel_id=1, source_target_pairs={{0,8},{1,9},{2,10},{3,11},{4,12},{5,13},{6,14},{7,15},{8,0},{9,1},... | collective-permute-start | bytes 786440 | tf_op jit(solution)/shard_map/ppermute | solution.py:115
  38.7 13.9 %collective-permute-start.11 = (bf16[144,1024]{1,0:T(8,128)(2,1)S(1)}, bf16[144,1024]{1,0:T(8,128)(2,1)S(1)}, u32[]{:S(2)}, u32[]{:S(2)}) collective-permute-start(bf16[144,1024]{1,0:T(8,128)(2,1)S(1)} %collective-permute-done.7.refs_3_), channel_id=1, source_target_pairs={{0,2},{1,3},{2,0},{3,1},{4,6},{5,7},{6,4},{7,5},{8,10},{9,11},{10,... | collective-permute-start | bytes 884744 | tf_op jit(solution)/shard_map/ppermute | solution.py:115
  40.2 9.2 %collective-permute-start.12 = (bf16[128,1024]{1,0:T(8,128)(2,1)S(1)}, bf16[128,1024]{1,0:T(8,128)(2,1)S(1)}, u32[]{:S(2)}, u32[]{:S(2)}) collective-permute-start(bf16[128,1024]{1,0:T(8,128)(2,1)S(1)} %pad_maximum_fusion.refs_0_.refs_8_), channel_id=1, source_target_pairs={{0,4},{1,5},{2,6},{3,7},{4,0},{5,1},{6,2},{7,3},{8,12},{9,13},{10,... | collective-permute-start | bytes 786440 | tf_op jit(solution)/shard_map/ppermute | solution.py:115
  42.1 10.6 %collective-permute-start.13 = (bf16[128,1024]{1,0:T(8,128)(2,1)S(1)}, bf16[128,1024]{1,0:T(8,128)(2,1)}, u32[]{:S(2)}, u32[]{:S(2)}) collective-permute-start(bf16[128,1024]{1,0:T(8,128)(2,1)S(1)} %collective-permute-done.8.refs_2_.refs_10_), channel_id=1, source_target_pairs={{0,2},{1,3},{2,0},{3,1},{4,6},{5,7},{6,4},{7,5},{8,10},{9,11},{10,... | collective-permute-start | bytes 786440 | tf_op jit(solution)/shard_map/ppermute | solution.py:115
  43.6 28.1 %collective-permute-start.20 = (bf16[128,1024]{1,0:T(8,128)(2,1)S(1)}, bf16[128,1024]{1,0:T(8,128)(2,1)S(1)}, u32[]{:S(2)}, u32[]{:S(2)}) collective-permute-start(bf16[128,1024]{1,0:T(8,128)(2,1)S(1)} %collective-permute-done.8.refs_2_.refs_10_), channel_id=1, source_target_pairs={{0,4},{1,5},{2,6},{3,7},{4,0},{5,1},{6,2},{7,3},{8,12},{9,13},{10,... | collective-permute-start | bytes 786440 | tf_op jit(solution)/shard_map/ppermute | solution.py:115
  52.7 14.8 %collective-permute-start.14 = (bf16[128,1024]{1,0:T(8,128)(2,1)S(1)}, bf16[128,1024]{1,0:T(8,128)(2,1)S(1)}, u32[]{:S(2)}, u32[]{:S(2)}) collective-permute-start(bf16[128,1024]{1,0:T(8,128)(2,1)S(1)} %collective-permute-done.12.refs_1_.refs_9_), channel_id=1, source_target_pairs={{0,2},{1,3},{2,0},{3,1},{4,6},{5,7},{6,4},{7,5},{8,10},{9,11},{10,... | collective-permute-start | bytes 786440 | tf_op jit(solution)/shard_map/ppermute | solution.py:115
  54.1 13.4 %collective-permute-start.15 = (bf16[128,1024]{1,0:T(8,128)(2,1)}, bf16[128,1024]{1,0:T(8,128)(2,1)S(1)}, u32[]{:S(2)}, u32[]{:S(2)}) collective-permute-start(bf16[128,1024]{1,0:T(8,128)(2,1)} %collective-permute-done.13.refs_6_.refs_14_), channel_id=1, source_target_pairs={{0,4},{1,5},{2,6},{3,7},{4,0},{5,1},{6,2},{7,3},{8,12},{9,13},{10,... | collective-permute-start | bytes 786440 | tf_op jit(solution)/shard_map/ppermute | solution.py:115
  67.6 16.7 %collective-permute-start.16 = (bf16[128,1024]{1,0:T(8,128)(2,1)}, bf16[128,1024]{1,0:T(8,128)(2,1)S(1)}, u32[]{:S(2)}, u32[]{:S(2)}) collective-permute-start(bf16[128,1024]{1,0:T(8,128)(2,1)} %get-tuple-element.165), channel_id=1, source_target_pairs={{0,2},{1,3},{2,0},{3,1},{4,6},{5,7},{6,4},{7,5},{8,10},{9,11},{10,... | collective-permute-start | bytes 786440 | tf_op jit(solution)/shard_map/ppermute | solution.py:115
  68.2 16.1 %collective-permute-start.17 = (bf16[128,1024]{1,0:T(8,128)(2,1)}, bf16[128,1024]{1,0:T(8,128)(2,1)S(1)}, u32[]{:S(2)}, u32[]{:S(2)}) collective-permute-start(bf16[128,1024]{1,0:T(8,128)(2,1)} %get-tuple-element.166), channel_id=1, source_target_pairs={{0,4},{1,5},{2,6},{3,7},{4,0},{5,1},{6,2},{7,3},{8,12},{9,13},{10,... | collective-permute-start | bytes 786440 | tf_op jit(solution)/shard_map/ppermute | solution.py:115
  68.6 15.7 %collective-permute-start.18 = (bf16[128,1024]{1,0:T(8,128)(2,1)}, bf16[128,1024]{1,0:T(8,128)(2,1)S(1)}, u32[]{:S(2)}, u32[]{:S(2)}) collective-permute-start(bf16[128,1024]{1,0:T(8,128)(2,1)} %get-tuple-element.167), channel_id=1, source_target_pairs={{0,4},{1,5},{2,6},{3,7},{4,0},{5,1},{6,2},{7,3},{8,12},{9,13},{10,... | collective-permute-start | bytes 786440 | tf_op jit(solution)/shard_map/ppermute | solution.py:115
  70.2 14.1 %collective-permute-start.19 = (bf16[128,1024]{1,0:T(8,128)(2,1)}, bf16[128,1024]{1,0:T(8,128)(2,1)S(1)}, u32[]{:S(2)}, u32[]{:S(2)}) collective-permute-start(bf16[128,1024]{1,0:T(8,128)(2,1)} %get-tuple-element.168), channel_id=1, source_target_pairs={{0,2},{1,3},{2,0},{3,1},{4,6},{5,7},{6,4},{7,5},{8,10},{9,11},{10,... | collective-permute-start | bytes 786440 | tf_op jit(solution)/shard_map/ppermute | solution.py:115
  84.5 10.6 %collective-permute-start.22 = (bf16[144,1024]{1,0:T(8,128)(2,1)}, bf16[144,1024]{1,0:T(8,128)(2,1)S(1)}, u32[]{:S(2)}, u32[]{:S(2)}) collective-permute-start(bf16[144,1024]{1,0:T(8,128)(2,1)} %get-tuple-element.204), channel_id=1, source_target_pairs={{0,2},{1,3},{2,0},{3,1},{4,6},{5,7},{6,4},{7,5},{8,10},{9,11},{10,... | collective-permute-start | bytes 884744 | tf_op jit(solution)/shard_map/ppermute | solution.py:115
  85.1 10.0 %collective-permute-start.21 = (bf16[128,1024]{1,0:T(8,128)(2,1)S(1)}, bf16[128,1024]{1,0:T(8,128)(2,1)S(1)}, u32[]{:S(2)}, u32[]{:S(2)}) collective-permute-start(bf16[128,1024]{1,0:T(8,128)(2,1)S(1)} %add_convert_fusion.6), channel_id=1, source_target_pairs={{0,2},{1,3},{2,0},{3,1},{4,6},{5,7},{6,4},{7,5},{8,10},{9,11},{10,... | collective-permute-start | bytes 786440 | tf_op jit(solution)/shard_map/ppermute | solution.py:115
  86.6 8.5 %collective-permute-start.23 = (bf16[128,1024]{1,0:T(8,128)(2,1)S(1)}, bf16[128,1024]{1,0:T(8,128)(2,1)S(1)}, u32[]{:S(2)}, u32[]{:S(2)}) collective-permute-start(bf16[128,1024]{1,0:T(8,128)(2,1)S(1)} %add_convert_fusion.5), channel_id=1, source_target_pairs={{0,4},{1,5},{2,6},{3,7},{4,0},{5,1},{6,2},{7,3},{8,12},{9,13},{10,... | collective-permute-start | bytes 786440 | tf_op jit(solution)/shard_map/ppermute | solution.py:115
  95.3 16.6 %collective-permute-start.28 = (bf16[1536,1024]{1,0:T(8,128)(2,1)}, bf16[1536,1024]{1,0:T(8,128)(2,1)S(1)}, u32[]{:S(2)}, u32[]{:S(2)}) collective-permute-start(bf16[1536,1024]{1,0:T(8,128)(2,1)} %shard_map.120), channel_id=1, source_target_pairs={{0,1},{1,0},{2,3},{3,2},{4,5},{5,4},{6,7},{7,6},{8,9},{9,8},{10,11... | collective-permute-start | bytes 9437192 | tf_op jit(solution)/shard_map/ppermute | solution.py:115
  95.4 15.4 %collective-permute-start.25 = (bf16[144,1024]{1,0:T(8,128)(2,1)S(1)}, bf16[144,1024]{1,0:T(8,128)(2,1)S(1)}, u32[]{:S(2)}, u32[]{:S(2)}) collective-permute-start(bf16[144,1024]{1,0:T(8,128)(2,1)S(1)} %copy-done.29), channel_id=1, source_target_pairs={{0,2},{1,3},{2,0},{3,1},{4,6},{5,7},{6,4},{7,5},{8,10},{9,11},{10,... | collective-permute-start | bytes 884744 | tf_op jit(solution)/shard_map/ppermute | solution.py:115
  96.0 15.1 %collective-permute-start.26 = (bf16[144,1024]{1,0:T(8,128)(2,1)S(1)}, bf16[144,1024]{1,0:T(8,128)(2,1)S(1)}, u32[]{:S(2)}, u32[]{:S(2)}) collective-permute-start(bf16[144,1024]{1,0:T(8,128)(2,1)S(1)} %copy-done.28), channel_id=1, source_target_pairs={{0,2},{1,3},{2,0},{3,1},{4,6},{5,7},{6,4},{7,5},{8,10},{9,11},{10,... | collective-permute-start | bytes 884744 | tf_op jit(solution)/shard_map/ppermute | solution.py:115
  97.5 14.4 %collective-permute-start.27 = (bf16[144,1024]{1,0:T(8,128)(2,1)S(1)}, bf16[144,1024]{1,0:T(8,128)(2,1)S(1)}, u32[]{:S(2)}, u32[]{:S(2)}) collective-permute-start(bf16[144,1024]{1,0:T(8,128)(2,1)S(1)} %add_convert_fusion.2), channel_id=1, source_target_pairs={{0,4},{1,5},{2,6},{3,7},{4,0},{5,1},{6,2},{7,3},{8,12},{9,13},{10,... | collective-permute-start | bytes 884744 | tf_op jit(solution)/shard_map/ppermute | solution.py:115
  98.8 12.0 %collective-permute-start.24 = (bf16[128,1024]{1,0:T(8,128)(2,1)S(1)}, bf16[128,1024]{1,0:T(8,128)(2,1)S(1)}, u32[]{:S(2)}, u32[]{:S(2)}) collective-permute-start(bf16[128,1024]{1,0:T(8,128)(2,1)S(1)} %add_convert_fusion.4), channel_id=1, source_target_pairs={{0,8},{1,9},{2,10},{3,11},{4,12},{5,13},{6,14},{7,15},{8,0},{9,1},... | collective-permute-start | bytes 786440 | tf_op jit(solution)/shard_map/ppermute | solution.py:115
  112.4 15.6 %collective-permute-start.29 = (bf16[144,1024]{1,0:T(8,128)(2,1)S(1)}, bf16[144,1024]{1,0:T(8,128)(2,1)S(1)}, u32[]{:S(2)}, u32[]{:S(2)}) collective-permute-start(bf16[144,1024]{1,0:T(8,128)(2,1)S(1)} %add_convert_fusion.1), channel_id=1, source_target_pairs={{0,8},{1,9},{2,10},{3,11},{4,12},{5,13},{6,14},{7,15},{8,0},{9,1},... | collective-permute-start | bytes 884744 | tf_op jit(solution)/shard_map/ppermute | solution.py:115
  114.8 13.1 %collective-permute-start.30 = (bf16[144,1024]{1,0:T(8,128)(2,1)S(1)}, bf16[144,1024]{1,0:T(8,128)(2,1)S(1)}, u32[]{:S(2)}, u32[]{:S(2)}) collective-permute-start(bf16[144,1024]{1,0:T(8,128)(2,1)S(1)} %copy-done.27), channel_id=1, source_target_pairs={{0,2},{1,3},{2,0},{3,1},{4,6},{5,7},{6,4},{7,5},{8,10},{9,11},{10,... | collective-permute-start | bytes 884744 | tf_op jit(solution)/shard_map/ppermute | solution.py:115
  115.7 12.3 %collective-permute-start.31 = (bf16[144,1024]{1,0:T(8,128)(2,1)S(1)}, bf16[144,1024]{1,0:T(8,128)(2,1)S(1)}, u32[]{:S(2)}, u32[]{:S(2)}) collective-permute-start(bf16[144,1024]{1,0:T(8,128)(2,1)S(1)} %add_convert_fusion), channel_id=1, source_target_pairs={{0,4},{1,5},{2,6},{3,7},{4,0},{5,1},{6,2},{7,3},{8,12},{9,13},{10,... | collective-permute-start | bytes 884744 | tf_op jit(solution)/shard_map/ppermute | solution.py:115
  (30 other events, 554.9 us)

commit v10 on v9

--- a/solution.py
+++ b/solution.py
@@ -192,11 +192,13 @@
     every, size = count * tok_count, 2 * tok_count
     lanes = 128
     back = size + (EXTRA if last else 0)
+    layout = [[b] for b in range(count)] if last else [[0], [1], [2], [4], [5], [6], [7, 3]]
+    place_of = {b: (i, j * back) for i, held in enumerate(layout) for j, b in enumerate(held)}
 
     def body(me_ref, *refs):
         b_refs, w_refs, refs = refs[:count], refs[count : count + 6], refs[count + 6 :]
         before_refs, refs = (refs[:2], refs[2:]) if last else ((), refs)
-        q_refs, refs = refs[:count], refs[count:]
+        q_refs, refs = refs[: len(layout)], refs[len(layout) :]
         weighted_ref, factor_ref, refs = refs[0], refs[1], refs[2:]
         after_refs, refs = ((), refs) if last else (refs[:2], refs[2:])
         wide_w, down_w, refs = refs[0], refs[1], refs[2:]
@@ -228,6 +230,10 @@
             fetch.start(("c", b), b_refs[b].at[pl.ds(tok_count, tok_count)], c_buf.at[at])
         for i in (3, 4, 5):
             fetch.start(("w", i), w_refs[i], w_bufs[i])
+
+        def returned(b, first, rows):
+            ref, offset = place_of[b]
+            return q_refs[ref].at[pl.ds(offset + first, rows)]
 
         def place(e):
             number = lax.rem(low + e, 2) + low - lax.rem(low, 2)
@@ -283,11 +289,11 @@
         y_buf[...] = dot(weighted_buf[...], down_w[...], ((1,), (0,))).astype(bf16)
         for b in range(count):
             at = pl.ds(b * tok_count, tok_count)
-            fetch.start(("y", b), y_buf.at[at], q_refs[b].at[pl.ds(0, tok_count)])
+            fetch.start(("y", b), y_buf.at[at], returned(b, 0, tok_count))
         g_buf[...] = dot(factor_buf[...], wide_w[...], ((1,), (1,))).astype(bf16)
         for b in range(count):
             at = pl.ds(b * tok_count, tok_count)
-            fetch.start(("g", b), g_buf.at[at], q_refs[b].at[pl.ds(tok_count, tok_count)])
+            fetch.start(("g", b), g_buf.at[at], returned(b, tok_count, tok_count))
         if last:
             wide_buf[...] = jnp.zeros((count, EXTRA, width), f32)
             inner_buf[...] = inner_buf[...].T
@@ -303,13 +309,13 @@
                     wide_buf[b, 0:8, place(e)] = jnp.concatenate(lines, axis=0)
             for b in range(count):
                 extra_buf[b] = wide_buf[b].astype(bf16)
-                fetch.start(("i", b), extra_buf.at[b], q_refs[b].at[pl.ds(size, EXTRA)])
+                fetch.start(("i", b), extra_buf.at[b], returned(b, size, EXTRA))
         else:
             fetch.start("share", share_buf, after_refs[0])
             fetch.start("inner", inner_buf, after_refs[1])
         fetch.wait_all()
 
-    outs = [shape(back, width, bf16)] * count
+    outs = [shape(len(held) * back, width, bf16) for held in layout]
     outs += [shape(every, 2 * units, bf16), shape(every, 4 * units, bf16)]
     small = shape(lanes, lanes, f32)
     operands = (*blocks, *weights[0], *weights[1])
@@ -325,7 +331,7 @@
     flops = 24 * every * width * units
     copies = 5 * count + 6 + 2 + 2
     outs = kernel(body, outs, scratch, copies, flops, *operands, scalar=me)
-    return outs[:count], outs[count:]
+    return outs[: len(layout)], outs[len(layout) :]
 
 
 def weight_grads(expert, blocks, factors, away=None):
@@ -416,12 +422,14 @@
     lines = jnp.pad(lines, ((0, EXTRA - lines.shape[0]), (0, 0)))
     a0 = jnp.concatenate([latent_in[:mid], cotangent[:mid], lines], axis=0)
     b0 = jnp.concatenate([latent_in[mid:], cotangent[mid:]], axis=0)
-    gate_w, up_w, down_w = [swap(w, CORE) for w in own]
-    a0, b0, gate_w, up_w, down_w, own = fence(a0, b0, gate_w, up_w, down_w, own)
+    gate_w = swap(own[0], CORE)
+    a0, b0, gate_w, own = fence(a0, b0, gate_w, own)
 
     a2, a4, b4, a1 = swap(a0, FAR), swap(a0, SIDE), swap(b0, SIDE), swap(a0, NEAR)
-    a2, a1, a4, b4, b0 = fence(a2, a1, a4, b4, b0)
+    up_w = swap(own[1], CORE)
+    a1, a4, a2, b4, up_w, b0, own = fence(a1, a4, a2, b4, up_w, b0, own)
     a5, a6, a3, b2 = swap(a1, SIDE), swap(a2, SIDE), swap(a2, NEAR), swap(b0, FAR)
+    down_w = swap(own[2], CORE)
     (a3,) = fence(a3)
     a7 = swap(a3, SIDE)
     b2, a5, a6 = fence(b2, a5, a6)
@@ -431,30 +439,33 @@
     weights, me = (own, (gate_w, up_w, down_w)), me.astype(jnp.int32).reshape(1)
     a = [a0, a1, a2, a3, a4, a5, a6, a7]
     q, (*a_factors, shares, inners) = both_ways(0, a, weights, me)
-    q, shares, inners, b5, b7 = fence(q, shares, inners, b5, b7)
-    q5, q7, q3, q4 = swap(q[5], SIDE), swap(q[7], NEAR), swap(q[3], NEAR), swap(q[4], SIDE)
+    q0, q1, q2, q4, q5, q6, q73 = q
+    q73, q5, shares, inners, b5, b7 = fence(q73, q5, shares, inners, b5, b7)
+    r73, r5 = swap(q73, NEAR), swap(q5, SIDE)
     b = [b0, b1, b2, b3, b4, b5, b6, b7]
     p, b_factors = both_ways(1, b, weights, me, (shares, inners))
-    q5, q7, q3, q4, p, q, b_factors = fence(q5, q7, q3, q4, p, q, b_factors)
-    factors = (a_factors, b_factors)
-    q6, q2, q1 = narrow(added(q[6], q7)), added(q[2], q3), narrow(added(q[1], q5))
-    q6, q2, q1, p, q = fence(q6, q2, q1, p, q)
-    q6, p7, q1 = swap(q6, SIDE), swap(p[7], SIDE), swap(q1, NEAR)
+    p0, p1, p2, p3, p4, p5, p6, p7 = p
+    r73, r5, q6, q4, p7, p6, p5, p4, b_factors = fence(r73, r5, q6, q4, p7, p6, p5, p4, b_factors)
+    factors, size = (a_factors, b_factors), q6.shape[0]
+    q6, q2, q1 = narrow(added(q6, r73[:size])), added(q2, r73[size:]), narrow(added(q1, r5))
+    q6, p7, q1 = fence(q6, p7, q1)
+    r6, r7, q1 = swap(q6, SIDE), swap(p7, SIDE), swap(q1, NEAR)
     away = weight_grads(1, (a, b), factors)
-    q6, p7, q1, q2, away, p, q = fence(q6, p7, q1, q2, away, p, q)
-    q2, p3 = narrow(q2 + q6.astype(f32)), narrow(added(p[3], p7))
-    q2, p3, p, q, away = fence(q2, p3, p, q, away)
-    p6, p5, q2, p3 = swap(p[6], SIDE), swap(p[5], SIDE), swap(q2, FAR), swap(p3, NEAR)
-    away = swap(away, CORE)
-    q2, p6, p5, p3, away, p, q = fence(q2, p6, p5, p3, away, p, q)
-    p2, p1 = narrow(added(p[2], p6) + p3.astype(f32)), narrow(added(p[1], p5))
-    p2, p1, p, q, away = fence(p2, p1, p, q, away)
-    p4, p2, p1 = swap(p[4], SIDE), swap(p2, FAR), swap(p1, NEAR)
+    r6, r7, q1, away, p6, p5 = fence(r6, r7, q1, away, p6, p5)
+    q2, p3 = narrow(q2 + r6.astype(f32)), narrow(added(p3, r7))
+    q2, p3, p6, p5, away = fence(q2, p3, p6, p5, away)
+    q2, r6, r5, p3, away = (
+        swap(q2, FAR), swap(p6, SIDE), swap(p5, SIDE), swap(p3, NEAR), swap(away, CORE),
+    )
+    q2, r6, r5, p3, away, q4, p4 = fence(q2, r6, r5, p3, away, q4, p4)
+    p2, p1 = narrow(added(p2, r6) + p3.astype(f32)), narrow(added(p1, r5))
+    p2, p1, p4, q4, away = fence(p2, p1, p4, q4, away)
+    p2, p4, q4, p1 = swap(p2, FAR), swap(p4, SIDE), swap(q4, SIDE), swap(p1, NEAR)
     grad_w = weight_grads(0, (a, b), factors, away)
-    p2, p4, p1, grad_w = fence(p2, p4, p1, grad_w)
-
-    q = added(q[0], q4) + added(q1, q2)
-    p = added(p[0], p4) + added(p1, p2)
+    p2, p4, q4, p1, grad_w = fence(p2, p4, q4, p1, grad_w)
+
+    q = added(q0, q4) + added(q1, q2)
+    p = added(p0, p4) + added(p1, p2)
     combined = narrow(jnp.concatenate([q[:mid], p[:mid]], axis=0))
     grad_latent = narrow(jnp.concatenate([q[mid : 2 * mid], p[mid : 2 * mid]], axis=0))
     inner = p[2 * mid :].reshape(-1, devices_ep, tok_count)[:3].sum(axis=0)

time: 131 us -> 130 us (level)
  starting transfers between devices: 41.2 us -> 35.6 us
  waiting for transfers between devices: 42.9 us -> 47.4 us
    ppermute x32 -> x31, starting transfers between devices: 41.2 us -> 35.6 us  [swap(): return lax.ppermute(value, 'ep', pairs)]
    ppermute x32 -> x31, waiting for transfers between devices: 42.9 us -> 47.4 us  [swap(): return lax.ppermute(value, 'ep', pairs)]
  transfers between devices with their start and end apart: 32 -> 31, of which waited for: 12 -> 12; matrix products, arithmetic and copies ran while one was open for 2% -> 2% of each run, Pallas kernels for 30% -> 30%
where the time goes in v10:
time: 130 us
  waiting for transfers between devices  47.4 us (36%)
  Pallas kernels  39.3 us (30%)
  starting transfers between devices  35.6 us (27%)
  other arithmetic  3.77 us (3%)
  local copies, waits for them, and re-layouts  3.02 us (2%)
    ppermute x31, waiting for transfers between devices, swap(): return lax.ppermute(value, 'ep', pairs)  47.4 us
    pallas_call x4, Pallas kernels, kernel(): pl.pallas_call(body, out_shape=outs, in_specs=in_specs, out_specs=[pl.Blo...  39.3 us
    ppermute x31, starting transfers between devices, swap(): return lax.ppermute(value, 'ep', pairs)  35.6 us
  transfers between devices with their start and end apart: 31, of which 12 were waited for; matrix products, arithmetic and copies ran while one was open for 2% of the time, Pallas kernels for 30%

profile of v10, /device:TPU:0, one launch (start us, length us, event | category | flops | bytes accessed | tf_op | source)
XLA Modules:
  0.0 130.3 jit_solution(18185983309811497125)
XLA Ops:
  2.0 1.1 fusion.6
  3.6 1.0 copy-done.25
  5.0 3.7 %collective-permute-start.3 = (bf16[144,1024]{1,0:T(8,128)(2,1)S(1)}, bf16[144,1024]{1,0:T(8,128)(2,1)S(1)}, u32[]{:S(2)}, u32[]{:S(2)}) collective-permute-start(bf16[144,1024]{1,0:T(8,128)(2,1)S(1)} %fusion.1.refs_0_), channel_id=1, source_target_pairs={{0,8},{1,9},{2,10},{3,11},{4,12},{5,13},{6,14},{7,15},{8,0},{9,1},... | collective-permute-start | bytes 884744 | tf_op jit(solution)/shard_map/ppermute | solution.py:115
  8.7 1.5 %collective-permute-start.2 = (bf16[144,1024]{1,0:T(8,128)(2,1)S(1)}, bf16[144,1024]{1,0:T(8,128)(2,1)S(1)}, u32[]{:S(2)}, u32[]{:S(2)}) collective-permute-start(bf16[144,1024]{1,0:T(8,128)(2,1)S(1)} %fusion.1.refs_0_), channel_id=1, source_target_pairs={{0,2},{1,3},{2,0},{3,1},{4,6},{5,7},{6,4},{7,5},{8,10},{9,11},{10,... | collective-permute-start | bytes 884744 | tf_op jit(solution)/shard_map/ppermute | solution.py:115
  10.2 1.6 %collective-permute-start.1 = (bf16[144,1024]{1,0:T(8,128)(2,1)S(1)}, bf16[144,1024]{1,0:T(8,128)(2,1)S(1)}, u32[]{:S(2)}, u32[]{:S(2)}) collective-permute-start(bf16[144,1024]{1,0:T(8,128)(2,1)S(1)} %fusion.1.refs_0_), channel_id=1, source_target_pairs={{0,4},{1,5},{2,6},{3,7},{4,0},{5,1},{6,2},{7,3},{8,12},{9,13},{10,... | collective-permute-start | bytes 884744 | tf_op jit(solution)/shard_map/ppermute | solution.py:115
  12.3 11.0 %collective-permute-done.4.refs_4_.refs_12_ = bf16[128,1024]{1,0:T(8,128)(2,1)S(1)} collective-permute-done((bf16[128,1024]{1,0:T(8,128)(2,1)S(1)}, bf16[128,1024]{1,0:T(8,128)(2,1)S(1)}, u32[]{:S(2)}, u32[]{:S(2)}) %collective-permute-start.4) | collective-permute-done | bytes 262176 | tf_op jit(solution)/shard_map/ppermute | solution.py:115
  25.1 1.5 %collective-permute-start.8 = (bf16[144,1024]{1,0:T(8,128)(2,1)S(1)}, bf16[144,1024]{1,0:T(8,128)(2,1)S(1)}, u32[]{:S(2)}, u32[]{:S(2)}) collective-permute-start(bf16[144,1024]{1,0:T(8,128)(2,1)S(1)} %collective-permute-done.1.refs_1_), channel_id=1, source_target_pairs={{0,2},{1,3},{2,0},{3,1},{4,6},{5,7},{6,4},{7,5},{8,10},{9,11},{10,... | collective-permute-start | bytes 884744 | tf_op jit(solution)/shard_map/ppermute | solution.py:115
  27.2 2.2 %collective-permute-start.7 = (bf16[128,1024]{1,0:T(8,128)(2,1)S(1)}, bf16[128,1024]{1,0:T(8,128)(2,1)S(1)}, u32[]{:S(2)}, u32[]{:S(2)}) collective-permute-start(bf16[128,1024]{1,0:T(8,128)(2,1)S(1)} %pad_maximum_fusion.refs_0_.refs_8_), channel_id=1, source_target_pairs={{0,8},{1,9},{2,10},{3,11},{4,12},{5,13},{6,14},{7,15},{8,0},{9,1},... | collective-permute-start | bytes 786440 | tf_op jit(solution)/shard_map/ppermute | solution.py:115
  29.3 8.4 %collective-permute-done.6.refs_3_ = bf16[144,1024]{1,0:T(8,128)(2,1)S(1)} collective-permute-done((bf16[144,1024]{1,0:T(8,128)(2,1)S(1)}, bf16[144,1024]{1,0:T(8,128)(2,1)S(1)}, u32[]{:S(2)}, u32[]{:S(2)}) %collective-permute-start.6) | collective-permute-done | bytes 294944 | tf_op jit(solution)/shard_map/ppermute | solution.py:115
  38.1 3.4 %collective-permute-done.7.refs_2_.refs_10_ = bf16[128,1024]{1,0:T(8,128)(2,1)S(1)} collective-permute-done((bf16[128,1024]{1,0:T(8,128)(2,1)S(1)}, bf16[128,1024]{1,0:T(8,128)(2,1)S(1)}, u32[]{:S(2)}, u32[]{:S(2)}) %collective-permute-start.7) | collective-permute-done | bytes 262176 | tf_op jit(solution)/shard_map/ppermute | solution.py:115
  41.6 1.5 %collective-permute-start.12 = (bf16[128,1024]{1,0:T(8,128)(2,1)S(1)}, bf16[128,1024]{1,0:T(8,128)(2,1)}, u32[]{:S(2)}, u32[]{:S(2)}) collective-permute-start(bf16[128,1024]{1,0:T(8,128)(2,1)S(1)} %collective-permute-done.7.refs_2_.refs_10_), channel_id=1, source_target_pairs={{0,2},{1,3},{2,0},{3,1},{4,6},{5,7},{6,4},{7,5},{8,10},{9,11},{10,... | collective-permute-start | bytes 786440 | tf_op jit(solution)/shard_map/ppermute | solution.py:115
  43.1 2.0 %collective-permute-start.14 = (bf16[128,1024]{1,0:T(8,128)(2,1)S(1)}, bf16[128,1024]{1,0:T(8,128)(2,1)S(1)}, u32[]{:S(2)}, u32[]{:S(2)}) collective-permute-start(bf16[128,1024]{1,0:T(8,128)(2,1)S(1)} %collective-permute-done.7.refs_2_.refs_10_), channel_id=1, source_target_pairs={{0,4},{1,5},{2,6},{3,7},{4,0},{5,1},{6,2},{7,3},{8,12},{9,13},{10,... | collective-permute-start | bytes 786440 | tf_op jit(solution)/shard_map/ppermute | solution.py:115
  45.1 5.6 %collective-permute-done.11.refs_1_.refs_9_ = bf16[128,1024]{1,0:T(8,128)(2,1)S(1)} collective-permute-done((bf16[128,1024]{1,0:T(8,128)(2,1)S(1)}, bf16[128,1024]{1,0:T(8,128)(2,1)S(1)}, u32[]{:S(2)}, u32[]{:S(2)}) %collective-permute-start.11) | collective-permute-done | bytes 262176 | tf_op jit(solution)/shard_map/ppermute | solution.py:115
  50.8 1.8 %collective-permute-done.12.refs_6_.refs_14_ = bf16[128,1024]{1,0:T(8,128)(2,1)} collective-permute-done((bf16[128,1024]{1,0:T(8,128)(2,1)S(1)}, bf16[128,1024]{1,0:T(8,128)(2,1)}, u32[]{:S(2)}, u32[]{:S(2)}) %collective-permute-start.12) | collective-permute-done | bytes 262176 | tf_op jit(solution)/shard_map/ppermute | solution.py:115
  52.6 1.5 %collective-permute-start.15 = (bf16[128,1024]{1,0:T(8,128)(2,1)S(1)}, bf16[128,1024]{1,0:T(8,128)(2,1)S(1)}, u32[]{:S(2)}, u32[]{:S(2)}) collective-permute-start(bf16[128,1024]{1,0:T(8,128)(2,1)S(1)} %collective-permute-done.11.refs_1_.refs_9_), channel_id=1, source_target_pairs={{0,2},{1,3},{2,0},{3,1},{4,6},{5,7},{6,4},{7,5},{8,10},{9,11},{10,... | collective-permute-start | bytes 786440 | tf_op jit(solution)/shard_map/ppermute | solution.py:115
  54.6 11.6 %shard_map.118 = (bf16[128,1024]{1,0:T(8,128)(2,1)}, bf16[128,1024]{1,0:T(8,128)(2,1)}, bf16[128,1024]{1,0:T(8,128)(2,1)}, bf16[128,1024]{1,0:T(8,128)(2,1)}, bf...) custom-call(s32[1]{0:T(128)} %bitcast.me_ref, ...), custom_call_target="tpu_custom_call" | custom-call | flops 6442450944 | bytes 14024704 | tf_op jit(solution)/shard_map/pallas_call | solution.py:162
  66.3 1.3 collective-permute-start.18
  69.2 11.9 %shard_map.119 = (bf16[144,1024]{1,0:T(8,128)(2,1)}, bf16[144,1024]{1,0:T(8,128)(2,1)}, bf16[144,1024]{1,0:T(8,128)(2,1)}, bf16[144,1024]{1,0:T(8,128)(2,1)}, bf...) custom-call(s32[1]{0:T(128)} %bitcast.me_ref, ...), custom_call_target="tpu_custom_call" | custom-call | flops 6442450944 | bytes 14024704 | tf_op jit(solution)/shard_map/pallas_call | solution.py:162
  81.3 1.6 %collective-permute-start.19 = (bf16[128,1024]{1,0:T(8,128)(2,1)S(1)}, bf16[128,1024]{1,0:T(8,128)(2,1)S(1)}, u32[]{:S(2)}, u32[]{:S(2)}) collective-permute-start(bf16[128,1024]{1,0:T(8,128)(2,1)S(1)} %add_convert_fusion.6), channel_id=1, source_target_pairs={{0,2},{1,3},{2,0},{3,1},{4,6},{5,7},{6,4},{7,5},{8,10},{9,11},{10,... | collective-permute-start | bytes 786440 | tf_op jit(solution)/shard_map/ppermute | solution.py:115
  83.3 1.2 collective-permute-start.20
  84.6 7.4 %shard_map.120 = bf16[1536,1024]{1,0:T(8,128)(2,1)} custom-call(bf16[144,1024]{1,0:T(8,128)(2,1)} %copy-done.1, bf16[144,1024]{1,0:T(8,128)(2,1)} %copy-done.5, bf16[144,1024]{1,0:T(8,128)(2,1)} %copy-done.3, bf16[144,1024]{1,0:T(8,128)(2,1)} %copy-done.6, bf16[144,1024]{1,0:T(8,128)(2,1)} %copy-done.4, bf16[144,1024]{1,0:T(8,128)(2,1)} %copy-done.7, ...), custom_call_target="tpu_custom_call" | custom-call | flops 3221225472 | bytes 13893632 | tf_op jit(solution)/shard_map/pallas_call | solution.py:162
  92.1 2.1 %collective-permute-done.20 = bf16[144,1024]{1,0:T(8,128)(2,1)S(1)} collective-permute-done((bf16[144,1024]{1,0:T(8,128)(2,1)}, bf16[144,1024]{1,0:T(8,128)(2,1)S(1)}, u32[]{:S(2)}, u32[]{:S(2)}) %collective-permute-start.20) | collective-permute-done | bytes 294944 | tf_op jit(solution)/shard_map/ppermute | solution.py:115
  94.5 1.6 %collective-permute-start.23 = (bf16[144,1024]{1,0:T(8,128)(2,1)S(1)}, bf16[144,1024]{1,0:T(8,128)(2,1)S(1)}, u32[]{:S(2)}, u32[]{:S(2)}) collective-permute-start(bf16[144,1024]{1,0:T(8,128)(2,1)S(1)} %copy-done.29), channel_id=1, source_target_pairs={{0,2},{1,3},{2,0},{3,1},{4,6},{5,7},{6,4},{7,5},{8,10},{9,11},{10,... | collective-permute-start | bytes 884744 | tf_op jit(solution)/shard_map/ppermute | solution.py:115
  96.6 1.1 collective-permute-start.25
  97.7 1.3 %collective-permute-start.22 = (bf16[128,1024]{1,0:T(8,128)(2,1)S(1)}, bf16[128,1024]{1,0:T(8,128)(2,1)S(1)}, u32[]{:S(2)}, u32[]{:S(2)}) collective-permute-start(bf16[128,1024]{1,0:T(8,128)(2,1)S(1)} %add_convert_fusion.4), channel_id=1, source_target_pairs={{0,8},{1,9},{2,10},{3,11},{4,12},{5,13},{6,14},{7,15},{8,0},{9,1},... | collective-permute-start | bytes 786440 | tf_op jit(solution)/shard_map/ppermute | solution.py:115
  99.0 10.6 %collective-permute-done.22 = bf16[128,1024]{1,0:T(8,128)(2,1)S(1)} collective-permute-done((bf16[128,1024]{1,0:T(8,128)(2,1)S(1)}, bf16[128,1024]{1,0:T(8,128)(2,1)S(1)}, u32[]{:S(2)}, u32[]{:S(2)}) %collective-permute-start.22) | collective-permute-done | bytes 262176 | tf_op jit(solution)/shard_map/ppermute | solution.py:115
  111.3 1.6 %collective-permute-start.29 = (bf16[128,1024]{1,0:T(8,128)(2,1)S(1)}, bf16[128,1024]{1,0:T(8,128)(2,1)S(1)}, u32[]{:S(2)}, u32[]{:S(2)}) collective-permute-start(bf16[128,1024]{1,0:T(8,128)(2,1)S(1)} %copy-done.30), channel_id=1, source_target_pairs={{0,2},{1,3},{2,0},{3,1},{4,6},{5,7},{6,4},{7,5},{8,10},{9,11},{10,... | collective-permute-start | bytes 786440 | tf_op jit(solution)/shard_map/ppermute | solution.py:115
  112.8 1.5 %collective-permute-start.27 = (bf16[144,1024]{1,0:T(8,128)(2,1)S(1)}, bf16[144,1024]{1,0:T(8,128)(2,1)S(1)}, u32[]{:S(2)}, u32[]{:S(2)}) collective-permute-start(bf16[144,1024]{1,0:T(8,128)(2,1)S(1)} %add_convert_fusion.1), channel_id=1, source_target_pairs={{0,8},{1,9},{2,10},{3,11},{4,12},{5,13},{6,14},{7,15},{8,0},{9,1},... | collective-permute-start | bytes 884744 | tf_op jit(solution)/shard_map/ppermute | solution.py:115
  114.3 1.2 collective-permute-start.28
  115.5 2.0 %collective-permute-start.30 = (bf16[144,1024]{1,0:T(8,128)(2,1)S(1)}, bf16[144,1024]{1,0:T(8,128)(2,1)S(1)}, u32[]{:S(2)}, u32[]{:S(2)}) collective-permute-start(bf16[144,1024]{1,0:T(8,128)(2,1)S(1)} %add_convert_fusion), channel_id=1, source_target_pairs={{0,4},{1,5},{2,6},{3,7},{4,0},{5,1},{6,2},{7,3},{8,12},{9,13},{10,... | collective-permute-start | bytes 884744 | tf_op jit(solution)/shard_map/ppermute | solution.py:115
  117.5 8.3 %shard_map.121 = (bf16[1024,512]{1,0:T(8,128)(2,1)}, bf16[1024,512]{1,0:T(8,128)(2,1)}, bf16[512,1024]{1,0:T(8,128)(2,1)}) custom-call(bf16[144,1024]{1,0:T(8,128)(2,1)} %copy-done.1, bf16[144,1024]{1,0:T(8,128)(2,1)} %copy-done.5, bf16[144,1024]{1,0:T(8,128)(2,1)} %copy-done.3, bf16[144,1024]{1,0:T(8,128)(2,1)} %copy-done.6, bf16[144,1024]{1,0:T(8,128)(2,1)} %copy-done.4, ...), custom_call_target="tpu_custom_call" | custom-call | flops 3221225472 | bytes 17039360 | tf_op jit(solution)/shard_map/pallas_call | solution.py:162
  125.9 1.8 %collective-permute-done.27 = bf16[144,1024]{1,0:T(8,128)(2,1)S(1)} collective-permute-done((bf16[144,1024]{1,0:T(8,128)(2,1)S(1)}, bf16[144,1024]{1,0:T(8,128)(2,1)S(1)}, u32[]{:S(2)}, u32[]{:S(2)}) %collective-permute-start.27) | collective-permute-done | bytes 294944 | tf_op jit(solution)/shard_map/ppermute | solution.py:115
  (120 shorter events, 13.0 us)
Async XLA Ops:
  0.6 3.0 %collective-permute-start = (bf16[1024,512]{1,0:T(8,128)(2,1)}, bf16[1024,512]{1,0:T(8,128)(2,1)S(1)}, u32[]{:S(2)}, u32[]{:S(2)}) collective-permute-start(bf16[1024,512]{1,0:T(8,128)(2,1)} %bitcast.20), channel_id=1, source_target_pairs={{0,1},{1,0},{2,3},{3,2},{4,5},{5,4},{6,7},{7,6},{8,9},{9,8},{10,11... | collective-permute-start | bytes 3145736 | tf_op jit(solution)/shard_map/ppermute | solution.py:115
  3.1 63.1 %copy-start.2 = (bf16[128,1024]{1,0:T(8,128)(2,1)}, bf16[128,1024]{1,0:T(8,128)(2,1)S(1)}, u32[]{:S(2)}) copy-start(bf16[128,1024]{1,0:T(8,128)(2,1)S(1)} %pad_maximum_fusion.refs_0_.refs_8_) | copy-start | bytes 786436
  4.6 19.5 %collective-permute-start.5 = (bf16[1024,512]{1,0:T(8,128)(2,1)}, bf16[1024,512]{1,0:T(8,128)(2,1)S(1)}, u32[]{:S(2)}, u32[]{:S(2)}) collective-permute-start(bf16[1024,512]{1,0:T(8,128)(2,1)} %bitcast.23), channel_id=1, source_target_pairs={{0,1},{1,0},{2,3},{3,2},{4,5},{5,4},{6,7},{7,6},{8,9},{9,8},{10,11... | collective-permute-start | bytes 3145736 | tf_op jit(solution)/shard_map/ppermute | solution.py:115
  5.0 18.4 %collective-permute-start.3 = (bf16[144,1024]{1,0:T(8,128)(2,1)S(1)}, bf16[144,1024]{1,0:T(8,128)(2,1)S(1)}, u32[]{:S(2)}, u32[]{:S(2)}) collective-permute-start(bf16[144,1024]{1,0:T(8,128)(2,1)S(1)} %fusion.1.refs_0_), channel_id=1, source_target_pairs={{0,8},{1,9},{2,10},{3,11},{4,12},{5,13},{6,14},{7,15},{8,0},{9,1},... | collective-permute-start | bytes 884744 | tf_op jit(solution)/shard_map/ppermute | solution.py:115
  8.7 14.6 %collective-permute-start.2 = (bf16[144,1024]{1,0:T(8,128)(2,1)S(1)}, bf16[144,1024]{1,0:T(8,128)(2,1)S(1)}, u32[]{:S(2)}, u32[]{:S(2)}) collective-permute-start(bf16[144,1024]{1,0:T(8,128)(2,1)S(1)} %fusion.1.refs_0_), channel_id=1, source_target_pairs={{0,2},{1,3},{2,0},{3,1},{4,6},{5,7},{6,4},{7,5},{8,10},{9,11},{10,... | collective-permute-start | bytes 884744 | tf_op jit(solution)/shard_map/ppermute | solution.py:115
  10.2 13.9 %collective-permute-start.1 = (bf16[144,1024]{1,0:T(8,128)(2,1)S(1)}, bf16[144,1024]{1,0:T(8,128)(2,1)S(1)}, u32[]{:S(2)}, u32[]{:S(2)}) collective-permute-start(bf16[144,1024]{1,0:T(8,128)(2,1)S(1)} %fusion.1.refs_0_), channel_id=1, source_target_pairs={{0,4},{1,5},{2,6},{3,7},{4,0},{5,1},{6,2},{7,3},{8,12},{9,13},{10,... | collective-permute-start | bytes 884744 | tf_op jit(solution)/shard_map/ppermute | solution.py:115
  11.8 11.5 %collective-permute-start.4 = (bf16[128,1024]{1,0:T(8,128)(2,1)S(1)}, bf16[128,1024]{1,0:T(8,128)(2,1)S(1)}, u32[]{:S(2)}, u32[]{:S(2)}) collective-permute-start(bf16[128,1024]{1,0:T(8,128)(2,1)S(1)} %pad_maximum_fusion.refs_0_.refs_8_), channel_id=1, source_target_pairs={{0,2},{1,3},{2,0},{3,1},{4,6},{5,7},{6,4},{7,5},{8,10},{9,11},{10,... | collective-permute-start | bytes 786440 | tf_op jit(solution)/shard_map/ppermute | solution.py:115
  24.1 30.4 %collective-permute-start.13 = (bf16[512,1024]{1,0:T(8,128)(2,1)}, bf16[512,1024]{1,0:T(8,128)(2,1)}, u32[]{:S(2)}, u32[]{:S(2)}) collective-permute-start(bf16[512,1024]{1,0:T(8,128)(2,1)} %bitcast.26), channel_id=1, source_target_pairs={{0,1},{1,0},{2,3},{3,2},{4,5},{5,4},{6,7},{7,6},{8,9},{9,8},{10,11... | collective-permute-start | bytes 3145736 | tf_op jit(solution)/shard_map/ppermute | solution.py:115
  24.2 13.5 %collective-permute-start.6 = (bf16[144,1024]{1,0:T(8,128)(2,1)S(1)}, bf16[144,1024]{1,0:T(8,128)(2,1)S(1)}, u32[]{:S(2)}, u32[]{:S(2)}) collective-permute-start(bf16[144,1024]{1,0:T(8,128)(2,1)S(1)} %collective-permute-done.3.refs_2_), channel_id=1, source_target_pairs={{0,4},{1,5},{2,6},{3,7},{4,0},{5,1},{6,2},{7,3},{8,12},{9,13},{10,... | collective-permute-start | bytes 884744 | tf_op jit(solution)/shard_map/ppermute | solution.py:115
  25.1 16.4 %collective-permute-start.8 = (bf16[144,1024]{1,0:T(8,128)(2,1)S(1)}, bf16[144,1024]{1,0:T(8,128)(2,1)S(1)}, u32[]{:S(2)}, u32[]{:S(2)}) collective-permute-start(bf16[144,1024]{1,0:T(8,128)(2,1)S(1)} %collective-permute-done.1.refs_1_), channel_id=1, source_target_pairs={{0,2},{1,3},{2,0},{3,1},{4,6},{5,7},{6,4},{7,5},{8,10},{9,11},{10,... | collective-permute-start | bytes 884744 | tf_op jit(solution)/shard_map/ppermute | solution.py:115
  26.6 15.0 %collective-permute-start.9 = (bf16[144,1024]{1,0:T(8,128)(2,1)S(1)}, bf16[144,1024]{1,0:T(8,128)(2,1)S(1)}, u32[]{:S(2)}, u32[]{:S(2)}) collective-permute-start(bf16[144,1024]{1,0:T(8,128)(2,1)S(1)} %collective-permute-done.3.refs_2_), channel_id=1, source_target_pairs={{0,2},{1,3},{2,0},{3,1},{4,6},{5,7},{6,4},{7,5},{8,10},{9,11},{10,... | collective-permute-start | bytes 884744 | tf_op jit(solution)/shard_map/ppermute | solution.py:115
  27.2 14.4 %collective-permute-start.7 = (bf16[128,1024]{1,0:T(8,128)(2,1)S(1)}, bf16[128,1024]{1,0:T(8,128)(2,1)S(1)}, u32[]{:S(2)}, u32[]{:S(2)}) collective-permute-start(bf16[128,1024]{1,0:T(8,128)(2,1)S(1)} %pad_maximum_fusion.refs_0_.refs_8_), channel_id=1, source_target_pairs={{0,8},{1,9},{2,10},{3,11},{4,12},{5,13},{6,14},{7,15},{8,0},{9,1},... | collective-permute-start | bytes 786440 | tf_op jit(solution)/shard_map/ppermute | solution.py:115
  37.7 14.9 %collective-permute-start.10 = (bf16[144,1024]{1,0:T(8,128)(2,1)S(1)}, bf16[144,1024]{1,0:T(8,128)(2,1)S(1)}, u32[]{:S(2)}, u32[]{:S(2)}) collective-permute-start(bf16[144,1024]{1,0:T(8,128)(2,1)S(1)} %collective-permute-done.6.refs_3_), channel_id=1, source_target_pairs={{0,2},{1,3},{2,0},{3,1},{4,6},{5,7},{6,4},{7,5},{8,10},{9,11},{10,... | collective-permute-start | bytes 884744 | tf_op jit(solution)/shard_map/ppermute | solution.py:115
  41.6 9.2 %collective-permute-start.11 = (bf16[128,1024]{1,0:T(8,128)(2,1)S(1)}, bf16[128,1024]{1,0:T(8,128)(2,1)S(1)}, u32[]{:S(2)}, u32[]{:S(2)}) collective-permute-start(bf16[128,1024]{1,0:T(8,128)(2,1)S(1)} %pad_maximum_fusion.refs_0_.refs_8_), channel_id=1, source_target_pairs={{0,4},{1,5},{2,6},{3,7},{4,0},{5,1},{6,2},{7,3},{8,12},{9,13},{10,... | collective-permute-start | bytes 786440 | tf_op jit(solution)/shard_map/ppermute | solution.py:115
  41.6 11.0 %collective-permute-start.12 = (bf16[128,1024]{1,0:T(8,128)(2,1)S(1)}, bf16[128,1024]{1,0:T(8,128)(2,1)}, u32[]{:S(2)}, u32[]{:S(2)}) collective-permute-start(bf16[128,1024]{1,0:T(8,128)(2,1)S(1)} %collective-permute-done.7.refs_2_.refs_10_), channel_id=1, source_target_pairs={{0,2},{1,3},{2,0},{3,1},{4,6},{5,7},{6,4},{7,5},{8,10},{9,11},{10,... | collective-permute-start | bytes 786440 | tf_op jit(solution)/shard_map/ppermute | solution.py:115
  43.1 25.4 %collective-permute-start.14 = (bf16[128,1024]{1,0:T(8,128)(2,1)S(1)}, bf16[128,1024]{1,0:T(8,128)(2,1)S(1)}, u32[]{:S(2)}, u32[]{:S(2)}) collective-permute-start(bf16[128,1024]{1,0:T(8,128)(2,1)S(1)} %collective-permute-done.7.refs_2_.refs_10_), channel_id=1, source_target_pairs={{0,4},{1,5},{2,6},{3,7},{4,0},{5,1},{6,2},{7,3},{8,12},{9,13},{10,... | collective-permute-start | bytes 786440 | tf_op jit(solution)/shard_map/ppermute | solution.py:115
  52.6 13.7 %collective-permute-start.15 = (bf16[128,1024]{1,0:T(8,128)(2,1)S(1)}, bf16[128,1024]{1,0:T(8,128)(2,1)S(1)}, u32[]{:S(2)}, u32[]{:S(2)}) collective-permute-start(bf16[128,1024]{1,0:T(8,128)(2,1)S(1)} %collective-permute-done.11.refs_1_.refs_9_), channel_id=1, source_target_pairs={{0,2},{1,3},{2,0},{3,1},{4,6},{5,7},{6,4},{7,5},{8,10},{9,11},{10,... | collective-permute-start | bytes 786440 | tf_op jit(solution)/shard_map/ppermute | solution.py:115
  54.1 12.2 %collective-permute-start.16 = (bf16[128,1024]{1,0:T(8,128)(2,1)}, bf16[128,1024]{1,0:T(8,128)(2,1)S(1)}, u32[]{:S(2)}, u32[]{:S(2)}) collective-permute-start(bf16[128,1024]{1,0:T(8,128)(2,1)} %collective-permute-done.12.refs_6_.refs_14_), channel_id=1, source_target_pairs={{0,4},{1,5},{2,6},{3,7},{4,0},{5,1},{6,2},{7,3},{8,12},{9,13},{10,... | collective-permute-start | bytes 786440 | tf_op jit(solution)/shard_map/ppermute | solution.py:115
  66.3 14.8 %collective-permute-start.18 = (bf16[128,1024]{1,0:T(8,128)(2,1)}, bf16[128,1024]{1,0:T(8,128)(2,1)S(1)}, u32[]{:S(2)}, u32[]{:S(2)}) collective-permute-start(bf16[128,1024]{1,0:T(8,128)(2,1)} %get-tuple-element.133), channel_id=1, source_target_pairs={{0,2},{1,3},{2,0},{3,1},{4,6},{5,7},{6,4},{7,5},{8,10},{9,11},{10,... | collective-permute-start | bytes 786440 | tf_op jit(solution)/shard_map/ppermute | solution.py:115
  67.6 13.5 %collective-permute-start.17 = (bf16[256,1024]{1,0:T(8,128)(2,1)}, bf16[256,1024]{1,0:T(8,128)(2,1)S(1)}, u32[]{:S(2)}, u32[]{:S(2)}) collective-permute-start(bf16[256,1024]{1,0:T(8,128)(2,1)} %get-tuple-element.132), channel_id=1, source_target_pairs={{0,4},{1,5},{2,6},{3,7},{4,0},{5,1},{6,2},{7,3},{8,12},{9,13},{10,... | collective-permute-start | bytes 1572872 | tf_op jit(solution)/shard_map/ppermute | solution.py:115
  81.3 10.7 %collective-permute-start.19 = (bf16[128,1024]{1,0:T(8,128)(2,1)S(1)}, bf16[128,1024]{1,0:T(8,128)(2,1)S(1)}, u32[]{:S(2)}, u32[]{:S(2)}) collective-permute-start(bf16[128,1024]{1,0:T(8,128)(2,1)S(1)} %add_convert_fusion.6), channel_id=1, source_target_pairs={{0,2},{1,3},{2,0},{3,1},{4,6},{5,7},{6,4},{7,5},{8,10},{9,11},{10,... | collective-permute-start | bytes 786440 | tf_op jit(solution)/shard_map/ppermute | solution.py:115
  82.9 9.2 %collective-permute-start.21 = (bf16[128,1024]{1,0:T(8,128)(2,1)S(1)}, bf16[128,1024]{1,0:T(8,128)(2,1)S(1)}, u32[]{:S(2)}, u32[]{:S(2)}) collective-permute-start(bf16[128,1024]{1,0:T(8,128)(2,1)S(1)} %add_convert_fusion.5), channel_id=1, source_target_pairs={{0,4},{1,5},{2,6},{3,7},{4,0},{5,1},{6,2},{7,3},{8,12},{9,13},{10,... | collective-permute-start | bytes 786440 | tf_op jit(solution)/shard_map/ppermute | solution.py:115
  83.3 10.8 %collective-permute-start.20 = (bf16[144,1024]{1,0:T(8,128)(2,1)}, bf16[144,1024]{1,0:T(8,128)(2,1)S(1)}, u32[]{:S(2)}, u32[]{:S(2)}) collective-permute-start(bf16[144,1024]{1,0:T(8,128)(2,1)} %get-tuple-element.148), channel_id=1, source_target_pairs={{0,2},{1,3},{2,0},{3,1},{4,6},{5,7},{6,4},{7,5},{8,10},{9,11},{10,... | collective-permute-start | bytes 884744 | tf_op jit(solution)/shard_map/ppermute | solution.py:115
  94.4 16.6 %collective-permute-start.26 = (bf16[1536,1024]{1,0:T(8,128)(2,1)}, bf16[1536,1024]{1,0:T(8,128)(2,1)S(1)}, u32[]{:S(2)}, u32[]{:S(2)}) collective-permute-start(bf16[1536,1024]{1,0:T(8,128)(2,1)} %shard_map.120), channel_id=1, source_target_pairs={{0,1},{1,0},{2,3},{3,2},{4,5},{5,4},{6,7},{7,6},{8,9},{9,8},{10,11... | collective-permute-start | bytes 9437192 | tf_op jit(solution)/shard_map/ppermute | solution.py:115
  94.5 15.2 %collective-permute-start.23 = (bf16[144,1024]{1,0:T(8,128)(2,1)S(1)}, bf16[144,1024]{1,0:T(8,128)(2,1)S(1)}, u32[]{:S(2)}, u32[]{:S(2)}) collective-permute-start(bf16[144,1024]{1,0:T(8,128)(2,1)S(1)} %copy-done.29), channel_id=1, source_target_pairs={{0,2},{1,3},{2,0},{3,1},{4,6},{5,7},{6,4},{7,5},{8,10},{9,11},{10,... | collective-permute-start | bytes 884744 | tf_op jit(solution)/shard_map/ppermute | solution.py:115
  96.0 14.2 %collective-permute-start.24 = (bf16[144,1024]{1,0:T(8,128)(2,1)S(1)}, bf16[144,1024]{1,0:T(8,128)(2,1)S(1)}, u32[]{:S(2)}, u32[]{:S(2)}) collective-permute-start(bf16[144,1024]{1,0:T(8,128)(2,1)S(1)} %copy-done.28), channel_id=1, source_target_pairs={{0,2},{1,3},{2,0},{3,1},{4,6},{5,7},{6,4},{7,5},{8,10},{9,11},{10,... | collective-permute-start | bytes 884744 | tf_op jit(solution)/shard_map/ppermute | solution.py:115
  96.6 14.4 %collective-permute-start.25 = (bf16[144,1024]{1,0:T(8,128)(2,1)S(1)}, bf16[144,1024]{1,0:T(8,128)(2,1)S(1)}, u32[]{:S(2)}, u32[]{:S(2)}) collective-permute-start(bf16[144,1024]{1,0:T(8,128)(2,1)S(1)} %add_convert_fusion.2), channel_id=1, source_target_pairs={{0,4},{1,5},{2,6},{3,7},{4,0},{5,1},{6,2},{7,3},{8,12},{9,13},{10,... | collective-permute-start | bytes 884744 | tf_op jit(solution)/shard_map/ppermute | solution.py:115
  97.7 12.0 %collective-permute-start.22 = (bf16[128,1024]{1,0:T(8,128)(2,1)S(1)}, bf16[128,1024]{1,0:T(8,128)(2,1)S(1)}, u32[]{:S(2)}, u32[]{:S(2)}) collective-permute-start(bf16[128,1024]{1,0:T(8,128)(2,1)S(1)} %add_convert_fusion.4), channel_id=1, source_target_pairs={{0,8},{1,9},{2,10},{3,11},{4,12},{5,13},{6,14},{7,15},{8,0},{9,1},... | collective-permute-start | bytes 786440 | tf_op jit(solution)/shard_map/ppermute | solution.py:115
  111.3 14.6 %collective-permute-start.29 = (bf16[128,1024]{1,0:T(8,128)(2,1)S(1)}, bf16[128,1024]{1,0:T(8,128)(2,1)S(1)}, u32[]{:S(2)}, u32[]{:S(2)}) collective-permute-start(bf16[128,1024]{1,0:T(8,128)(2,1)S(1)} %copy-done.30), channel_id=1, source_target_pairs={{0,2},{1,3},{2,0},{3,1},{4,6},{5,7},{6,4},{7,5},{8,10},{9,11},{10,... | collective-permute-start | bytes 786440 | tf_op jit(solution)/shard_map/ppermute | solution.py:115
  112.8 14.9 %collective-permute-start.27 = (bf16[144,1024]{1,0:T(8,128)(2,1)S(1)}, bf16[144,1024]{1,0:T(8,128)(2,1)S(1)}, u32[]{:S(2)}, u32[]{:S(2)}) collective-permute-start(bf16[144,1024]{1,0:T(8,128)(2,1)S(1)} %add_convert_fusion.1), channel_id=1, source_target_pairs={{0,8},{1,9},{2,10},{3,11},{4,12},{5,13},{6,14},{7,15},{8,0},{9,1},... | collective-permute-start | bytes 884744 | tf_op jit(solution)/shard_map/ppermute | solution.py:115
  114.3 13.4 %collective-permute-start.28 = (bf16[144,1024]{1,0:T(8,128)(2,1)S(1)}, bf16[144,1024]{1,0:T(8,128)(2,1)S(1)}, u32[]{:S(2)}, u32[]{:S(2)}) collective-permute-start(bf16[144,1024]{1,0:T(8,128)(2,1)S(1)} %copy-done.27), channel_id=1, source_target_pairs={{0,2},{1,3},{2,0},{3,1},{4,6},{5,7},{6,4},{7,5},{8,10},{9,11},{10,... | collective-permute-start | bytes 884744 | tf_op jit(solution)/shard_map/ppermute | solution.py:115
  115.5 12.2 %collective-permute-start.30 = (bf16[144,1024]{1,0:T(8,128)(2,1)S(1)}, bf16[144,1024]{1,0:T(8,128)(2,1)S(1)}, u32[]{:S(2)}, u32[]{:S(2)}) collective-permute-start(bf16[144,1024]{1,0:T(8,128)(2,1)S(1)} %add_convert_fusion), channel_id=1, source_target_pairs={{0,4},{1,5},{2,6},{3,7},{4,0},{5,1},{6,2},{7,3},{8,12},{9,13},{10,... | collective-permute-start | bytes 884744 | tf_op jit(solution)/shard_map/ppermute | solution.py:115
  (30 other events, 502.6 us)

commit v11 on v10

--- a/solution.py
+++ b/solution.py
@@ -451,16 +451,18 @@
     q6, p7, q1 = fence(q6, p7, q1)
     r6, r7, q1 = swap(q6, SIDE), swap(p7, SIDE), swap(q1, NEAR)
     away = weight_grads(1, (a, b), factors)
-    r6, r7, q1, away, p6, p5 = fence(r6, r7, q1, away, p6, p5)
-    q2, p3 = narrow(q2 + r6.astype(f32)), narrow(added(p3, r7))
-    q2, p3, p6, p5, away = fence(q2, p3, p6, p5, away)
-    q2, r6, r5, p3, away = (
-        swap(q2, FAR), swap(p6, SIDE), swap(p5, SIDE), swap(p3, NEAR), swap(away, CORE),
-    )
-    q2, r6, r5, p3, away, q4, p4 = fence(q2, r6, r5, p3, away, q4, p4)
-    p2, p1 = narrow(added(p2, r6) + p3.astype(f32)), narrow(added(p1, r5))
-    p2, p1, p4, q4, away = fence(p2, p1, p4, q4, away)
-    p2, p4, q4, p1 = swap(p2, FAR), swap(p4, SIDE), swap(q4, SIDE), swap(p1, NEAR)
+    r6, away, p6, p5 = fence(r6, away, p6, p5)
+    q2 = swap(narrow(q2 + r6.astype(f32)), FAR)
+    r7, p6, p5, away = fence(r7, p6, p5, away)
+    p3 = narrow(added(p3, r7))
+    p3, p6, p5, away = fence(p3, p6, p5, away)
+    r6, p3, r5, away = swap(p6, SIDE), swap(p3, NEAR), swap(p5, SIDE), swap(away, CORE)
+    r6, p3, q4, p4 = fence(r6, p3, q4, p4)
+    p2 = swap(narrow(added(p2, r6) + p3.astype(f32)), FAR)
+    r5, away, p4, q4, q2 = fence(r5, away, p4, q4, q2)
+    p1 = narrow(added(p1, r5))
+    p1, p4, q4, away = fence(p1, p4, q4, away)
+    p4, q4, p1 = swap(p4, SIDE), swap(q4, SIDE), swap(p1, NEAR)
     grad_w = weight_grads(0, (a, b), factors, away)
     p2, p4, q4, p1, grad_w = fence(p2, p4, q4, p1, grad_w)
 

time: 130 us -> 132 us (1.015)
  waiting for transfers between devices: 47.4 us -> 51.1 us
  starting transfers between devices: 35.6 us -> 33.1 us
    ppermute x31, waiting for transfers between devices: 47.4 us -> 51.1 us  [swap(): return lax.ppermute(value, 'ep', pairs)]
    ppermute x31, starting transfers between devices: 35.6 us -> 33.1 us  [swap(): return lax.ppermute(value, 'ep', pairs)]
  transfers between devices with their start and end apart: 31 -> 31, of which waited for: 12 -> 13; matrix products, arithmetic and copies ran while one was open for 2% -> 2% of each run, Pallas kernels for 30% -> 30%
where the time goes in v11:
time: 132 us; the launch traced here: 131 us
  waiting for transfers between devices  51.1 us (39%)
  Pallas kernels  39.2 us (30%)
  starting transfers between devices  33.1 us (25%)
  other arithmetic  3.76 us (3%)
  local copies, waits for them, and re-layouts  3.02 us (2%)
    ppermute x31, waiting for transfers between devices, swap(): return lax.ppermute(value, 'ep', pairs)  51.1 us
    pallas_call x4, Pallas kernels, kernel(): pl.pallas_call(body, out_shape=outs, in_specs=in_specs, out_specs=[pl.Blo...  39.2 us
    ppermute x31, starting transfers between devices, swap(): return lax.ppermute(value, 'ep', pairs)  33.1 us
  transfers between devices with their start and end apart: 31, of which 13 were waited for; matrix products, arithmetic and copies ran while one was open for 2% of the time, Pallas kernels for 30%

profile of v11, /device:TPU:0, one launch (start us, length us, event | category | flops | bytes accessed | tf_op | source)
XLA Modules:
  0.0 131.4 jit_solution(12571437751174374433)
XLA Ops:
  2.0 1.1 fusion.6
  3.6 1.0 copy-done.25
  5.0 3.7 %collective-permute-start.3 = (bf16[144,1024]{1,0:T(8,128)(2,1)S(1)}, bf16[144,1024]{1,0:T(8,128)(2,1)S(1)}, u32[]{:S(2)}, u32[]{:S(2)}) collective-permute-start(bf16[144,1024]{1,0:T(8,128)(2,1)S(1)} %fusion.1.refs_0_), channel_id=1, source_target_pairs={{0,8},{1,9},{2,10},{3,11},{4,12},{5,13},{6,14},{7,15},{8,0},{9,1},... | collective-permute-start | bytes 884744 | tf_op jit(solution)/shard_map/ppermute | solution.py:115
  8.7 1.5 %collective-permute-start.2 = (bf16[144,1024]{1,0:T(8,128)(2,1)S(1)}, bf16[144,1024]{1,0:T(8,128)(2,1)S(1)}, u32[]{:S(2)}, u32[]{:S(2)}) collective-permute-start(bf16[144,1024]{1,0:T(8,128)(2,1)S(1)} %fusion.1.refs_0_), channel_id=1, source_target_pairs={{0,2},{1,3},{2,0},{3,1},{4,6},{5,7},{6,4},{7,5},{8,10},{9,11},{10,... | collective-permute-start | bytes 884744 | tf_op jit(solution)/shard_map/ppermute | solution.py:115
  10.2 1.6 %collective-permute-start.1 = (bf16[144,1024]{1,0:T(8,128)(2,1)S(1)}, bf16[144,1024]{1,0:T(8,128)(2,1)S(1)}, u32[]{:S(2)}, u32[]{:S(2)}) collective-permute-start(bf16[144,1024]{1,0:T(8,128)(2,1)S(1)} %fusion.1.refs_0_), channel_id=1, source_target_pairs={{0,4},{1,5},{2,6},{3,7},{4,0},{5,1},{6,2},{7,3},{8,12},{9,13},{10,... | collective-permute-start | bytes 884744 | tf_op jit(solution)/shard_map/ppermute | solution.py:115
  12.3 11.0 %collective-permute-done.4.refs_4_.refs_12_ = bf16[128,1024]{1,0:T(8,128)(2,1)S(1)} collective-permute-done((bf16[128,1024]{1,0:T(8,128)(2,1)S(1)}, bf16[128,1024]{1,0:T(8,128)(2,1)S(1)}, u32[]{:S(2)}, u32[]{:S(2)}) %collective-permute-start.4) | collective-permute-done | bytes 262176 | tf_op jit(solution)/shard_map/ppermute | solution.py:115
  25.1 1.5 %collective-permute-start.8 = (bf16[144,1024]{1,0:T(8,128)(2,1)S(1)}, bf16[144,1024]{1,0:T(8,128)(2,1)S(1)}, u32[]{:S(2)}, u32[]{:S(2)}) collective-permute-start(bf16[144,1024]{1,0:T(8,128)(2,1)S(1)} %collective-permute-done.1.refs_1_), channel_id=1, source_target_pairs={{0,2},{1,3},{2,0},{3,1},{4,6},{5,7},{6,4},{7,5},{8,10},{9,11},{10,... | collective-permute-start | bytes 884744 | tf_op jit(solution)/shard_map/ppermute | solution.py:115
  27.2 2.2 %collective-permute-start.7 = (bf16[128,1024]{1,0:T(8,128)(2,1)S(1)}, bf16[128,1024]{1,0:T(8,128)(2,1)S(1)}, u32[]{:S(2)}, u32[]{:S(2)}) collective-permute-start(bf16[128,1024]{1,0:T(8,128)(2,1)S(1)} %pad_maximum_fusion.refs_0_.refs_8_), channel_id=1, source_target_pairs={{0,8},{1,9},{2,10},{3,11},{4,12},{5,13},{6,14},{7,15},{8,0},{9,1},... | collective-permute-start | bytes 786440 | tf_op jit(solution)/shard_map/ppermute | solution.py:115
  29.3 8.4 %collective-permute-done.6.refs_3_ = bf16[144,1024]{1,0:T(8,128)(2,1)S(1)} collective-permute-done((bf16[144,1024]{1,0:T(8,128)(2,1)S(1)}, bf16[144,1024]{1,0:T(8,128)(2,1)S(1)}, u32[]{:S(2)}, u32[]{:S(2)}) %collective-permute-start.6) | collective-permute-done | bytes 294944 | tf_op jit(solution)/shard_map/ppermute | solution.py:115
  38.1 3.4 %collective-permute-done.7.refs_2_.refs_10_ = bf16[128,1024]{1,0:T(8,128)(2,1)S(1)} collective-permute-done((bf16[128,1024]{1,0:T(8,128)(2,1)S(1)}, bf16[128,1024]{1,0:T(8,128)(2,1)S(1)}, u32[]{:S(2)}, u32[]{:S(2)}) %collective-permute-start.7) | collective-permute-done | bytes 262176 | tf_op jit(solution)/shard_map/ppermute | solution.py:115
  41.6 1.5 %collective-permute-start.12 = (bf16[128,1024]{1,0:T(8,128)(2,1)S(1)}, bf16[128,1024]{1,0:T(8,128)(2,1)}, u32[]{:S(2)}, u32[]{:S(2)}) collective-permute-start(bf16[128,1024]{1,0:T(8,128)(2,1)S(1)} %collective-permute-done.7.refs_2_.refs_10_), channel_id=1, source_target_pairs={{0,2},{1,3},{2,0},{3,1},{4,6},{5,7},{6,4},{7,5},{8,10},{9,11},{10,... | collective-permute-start | bytes 786440 | tf_op jit(solution)/shard_map/ppermute | solution.py:115
  43.1 2.0 %collective-permute-start.14 = (bf16[128,1024]{1,0:T(8,128)(2,1)S(1)}, bf16[128,1024]{1,0:T(8,128)(2,1)S(1)}, u32[]{:S(2)}, u32[]{:S(2)}) collective-permute-start(bf16[128,1024]{1,0:T(8,128)(2,1)S(1)} %collective-permute-done.7.refs_2_.refs_10_), channel_id=1, source_target_pairs={{0,4},{1,5},{2,6},{3,7},{4,0},{5,1},{6,2},{7,3},{8,12},{9,13},{10,... | collective-permute-start | bytes 786440 | tf_op jit(solution)/shard_map/ppermute | solution.py:115
  45.1 5.6 %collective-permute-done.11.refs_1_.refs_9_ = bf16[128,1024]{1,0:T(8,128)(2,1)S(1)} collective-permute-done((bf16[128,1024]{1,0:T(8,128)(2,1)S(1)}, bf16[128,1024]{1,0:T(8,128)(2,1)S(1)}, u32[]{:S(2)}, u32[]{:S(2)}) %collective-permute-start.11) | collective-permute-done | bytes 262176 | tf_op jit(solution)/shard_map/ppermute | solution.py:115
  50.8 1.8 %collective-permute-done.12.refs_6_.refs_14_ = bf16[128,1024]{1,0:T(8,128)(2,1)} collective-permute-done((bf16[128,1024]{1,0:T(8,128)(2,1)S(1)}, bf16[128,1024]{1,0:T(8,128)(2,1)}, u32[]{:S(2)}, u32[]{:S(2)}) %collective-permute-start.12) | collective-permute-done | bytes 262176 | tf_op jit(solution)/shard_map/ppermute | solution.py:115
  52.6 1.5 %collective-permute-start.15 = (bf16[128,1024]{1,0:T(8,128)(2,1)S(1)}, bf16[128,1024]{1,0:T(8,128)(2,1)S(1)}, u32[]{:S(2)}, u32[]{:S(2)}) collective-permute-start(bf16[128,1024]{1,0:T(8,128)(2,1)S(1)} %collective-permute-done.11.refs_1_.refs_9_), channel_id=1, source_target_pairs={{0,2},{1,3},{2,0},{3,1},{4,6},{5,7},{6,4},{7,5},{8,10},{9,11},{10,... | collective-permute-start | bytes 786440 | tf_op jit(solution)/shard_map/ppermute | solution.py:115
  54.6 11.6 %shard_map.118 = (bf16[128,1024]{1,0:T(8,128)(2,1)}, bf16[128,1024]{1,0:T(8,128)(2,1)}, bf16[128,1024]{1,0:T(8,128)(2,1)}, bf16[128,1024]{1,0:T(8,128)(2,1)}, bf...) custom-call(s32[1]{0:T(128)} %bitcast.me_ref, ...), custom_call_target="tpu_custom_call" | custom-call | flops 6442450944 | bytes 14024704 | tf_op jit(solution)/shard_map/pallas_call | solution.py:162
  66.3 1.3 collective-permute-start.18
  69.2 11.9 %shard_map.119 = (bf16[144,1024]{1,0:T(8,128)(2,1)}, bf16[144,1024]{1,0:T(8,128)(2,1)}, bf16[144,1024]{1,0:T(8,128)(2,1)}, bf16[144,1024]{1,0:T(8,128)(2,1)}, bf...) custom-call(s32[1]{0:T(128)} %bitcast.me_ref, ...), custom_call_target="tpu_custom_call" | custom-call | flops 6442450944 | bytes 14024704 | tf_op jit(solution)/shard_map/pallas_call | solution.py:162
  81.3 1.6 %collective-permute-start.20 = (bf16[128,1024]{1,0:T(8,128)(2,1)S(1)}, bf16[128,1024]{1,0:T(8,128)(2,1)S(1)}, u32[]{:S(2)}, u32[]{:S(2)}) collective-permute-start(bf16[128,1024]{1,0:T(8,128)(2,1)S(1)} %add_convert_fusion.6), channel_id=1, source_target_pairs={{0,2},{1,3},{2,0},{3,1},{4,6},{5,7},{6,4},{7,5},{8,10},{9,11},{10,... | collective-permute-start | bytes 786440 | tf_op jit(solution)/shard_map/ppermute | solution.py:115
  83.5 7.4 %shard_map.120 = bf16[1536,1024]{1,0:T(8,128)(2,1)} custom-call(bf16[144,1024]{1,0:T(8,128)(2,1)} %copy-done.1, bf16[144,1024]{1,0:T(8,128)(2,1)} %copy-done.5, bf16[144,1024]{1,0:T(8,128)(2,1)} %copy-done.3, bf16[144,1024]{1,0:T(8,128)(2,1)} %copy-done.6, bf16[144,1024]{1,0:T(8,128)(2,1)} %copy-done.4, bf16[144,1024]{1,0:T(8,128)(2,1)} %copy-done.7, ...), custom_call_target="tpu_custom_call" | custom-call | flops 3221225472 | bytes 13893632 | tf_op jit(solution)/shard_map/pallas_call | solution.py:162
  90.9 3.2 %collective-permute-done.19 = bf16[144,1024]{1,0:T(8,128)(2,1)S(1)} collective-permute-done((bf16[144,1024]{1,0:T(8,128)(2,1)}, bf16[144,1024]{1,0:T(8,128)(2,1)S(1)}, u32[]{:S(2)}, u32[]{:S(2)}) %collective-permute-start.19) | collective-permute-done | bytes 294944 | tf_op jit(solution)/shard_map/ppermute | solution.py:115
  94.3 1.6 %collective-permute-start.21 = (bf16[144,1024]{1,0:T(8,128)(2,1)S(1)}, bf16[144,1024]{1,0:T(8,128)(2,1)S(1)}, u32[]{:S(2)}, u32[]{:S(2)}) collective-permute-start(bf16[144,1024]{1,0:T(8,128)(2,1)S(1)} %copy-done.29), channel_id=1, source_target_pairs={{0,2},{1,3},{2,0},{3,1},{4,6},{5,7},{6,4},{7,5},{8,10},{9,11},{10,... | collective-permute-start | bytes 884744 | tf_op jit(solution)/shard_map/ppermute | solution.py:115
  96.3 1.2 collective-permute-start.24
  97.7 1.4 %collective-permute-start.26 = (bf16[128,1024]{1,0:T(8,128)(2,1)S(1)}, bf16[128,1024]{1,0:T(8,128)(2,1)S(1)}, u32[]{:S(2)}, u32[]{:S(2)}) collective-permute-start(bf16[128,1024]{1,0:T(8,128)(2,1)S(1)} %add_convert_fusion.4), channel_id=1, source_target_pairs={{0,8},{1,9},{2,10},{3,11},{4,12},{5,13},{6,14},{7,15},{8,0},{9,1},... | collective-permute-start | bytes 786440 | tf_op jit(solution)/shard_map/ppermute | solution.py:115
  99.1 5.1 %collective-permute-done.21 = bf16[144,1024]{1,0:T(8,128)(2,1)S(1)} collective-permute-done((bf16[144,1024]{1,0:T(8,128)(2,1)S(1)}, bf16[144,1024]{1,0:T(8,128)(2,1)S(1)}, u32[]{:S(2)}, u32[]{:S(2)}) %collective-permute-start.21) | collective-permute-done | bytes 294944 | tf_op jit(solution)/shard_map/ppermute | solution.py:115
  104.2 1.1 collective-permute-start.30
  105.3 5.8 %collective-permute-done.22 = bf16[144,1024]{1,0:T(8,128)(2,1)S(1)} collective-permute-done((bf16[144,1024]{1,0:T(8,128)(2,1)S(1)}, bf16[144,1024]{1,0:T(8,128)(2,1)S(1)}, u32[]{:S(2)}, u32[]{:S(2)}) %collective-permute-start.22) | collective-permute-done | bytes 294944 | tf_op jit(solution)/shard_map/ppermute | solution.py:115
  112.6 1.3 %collective-permute-start.27 = (bf16[144,1024]{1,0:T(8,128)(2,1)S(1)}, bf16[144,1024]{1,0:T(8,128)(2,1)S(1)}, u32[]{:S(2)}, u32[]{:S(2)}) collective-permute-start(bf16[144,1024]{1,0:T(8,128)(2,1)S(1)} %copy-done.27), channel_id=1, source_target_pairs={{0,2},{1,3},{2,0},{3,1},{4,6},{5,7},{6,4},{7,5},{8,10},{9,11},{10,... | collective-permute-start | bytes 884744 | tf_op jit(solution)/shard_map/ppermute | solution.py:115
  113.9 1.5 %collective-permute-start.29 = (bf16[144,1024]{1,0:T(8,128)(2,1)S(1)}, bf16[144,1024]{1,0:T(8,128)(2,1)S(1)}, u32[]{:S(2)}, u32[]{:S(2)}) collective-permute-start(bf16[144,1024]{1,0:T(8,128)(2,1)S(1)} %add_convert_fusion), channel_id=1, source_target_pairs={{0,4},{1,5},{2,6},{3,7},{4,0},{5,1},{6,2},{7,3},{8,12},{9,13},{10,... | collective-permute-start | bytes 884744 | tf_op jit(solution)/shard_map/ppermute | solution.py:115
  115.4 8.3 %shard_map.121 = (bf16[1024,512]{1,0:T(8,128)(2,1)}, bf16[1024,512]{1,0:T(8,128)(2,1)}, bf16[512,1024]{1,0:T(8,128)(2,1)}) custom-call(bf16[144,1024]{1,0:T(8,128)(2,1)} %copy-done.1, bf16[144,1024]{1,0:T(8,128)(2,1)} %copy-done.5, bf16[144,1024]{1,0:T(8,128)(2,1)} %copy-done.3, bf16[144,1024]{1,0:T(8,128)(2,1)} %copy-done.6, bf16[144,1024]{1,0:T(8,128)(2,1)} %copy-done.4, ...), custom_call_target="tpu_custom_call" | custom-call | flops 3221225472 | bytes 17039360 | tf_op jit(solution)/shard_map/pallas_call | solution.py:162
  123.7 2.4 %collective-permute-done.23 = bf16[144,1024]{1,0:T(8,128)(2,1)S(1)} collective-permute-done((bf16[144,1024]{1,0:T(8,128)(2,1)S(1)}, bf16[144,1024]{1,0:T(8,128)(2,1)S(1)}, u32[]{:S(2)}, u32[]{:S(2)}) %collective-permute-start.23) | collective-permute-done | bytes 294944 | tf_op jit(solution)/shard_map/ppermute | solution.py:115
  126.2 2.7 %collective-permute-done.29 = bf16[144,1024]{1,0:T(8,128)(2,1)S(1)} collective-permute-done((bf16[144,1024]{1,0:T(8,128)(2,1)S(1)}, bf16[144,1024]{1,0:T(8,128)(2,1)S(1)}, u32[]{:S(2)}, u32[]{:S(2)}) %collective-permute-start.29) | collective-permute-done | bytes 294944 | tf_op jit(solution)/shard_map/ppermute | solution.py:115
  (120 shorter events, 12.9 us)
Async XLA Ops:
  0.6 3.0 %collective-permute-start = (bf16[1024,512]{1,0:T(8,128)(2,1)}, bf16[1024,512]{1,0:T(8,128)(2,1)S(1)}, u32[]{:S(2)}, u32[]{:S(2)}) collective-permute-start(bf16[1024,512]{1,0:T(8,128)(2,1)} %bitcast.20), channel_id=1, source_target_pairs={{0,1},{1,0},{2,3},{3,2},{4,5},{5,4},{6,7},{7,6},{8,9},{9,8},{10,11... | collective-permute-start | bytes 3145736 | tf_op jit(solution)/shard_map/ppermute | solution.py:115
  3.1 63.1 %copy-start.2 = (bf16[128,1024]{1,0:T(8,128)(2,1)}, bf16[128,1024]{1,0:T(8,128)(2,1)S(1)}, u32[]{:S(2)}) copy-start(bf16[128,1024]{1,0:T(8,128)(2,1)S(1)} %pad_maximum_fusion.refs_0_.refs_8_) | copy-start | bytes 786436
  4.6 19.5 %collective-permute-start.5 = (bf16[1024,512]{1,0:T(8,128)(2,1)}, bf16[1024,512]{1,0:T(8,128)(2,1)S(1)}, u32[]{:S(2)}, u32[]{:S(2)}) collective-permute-start(bf16[1024,512]{1,0:T(8,128)(2,1)} %bitcast.23), channel_id=1, source_target_pairs={{0,1},{1,0},{2,3},{3,2},{4,5},{5,4},{6,7},{7,6},{8,9},{9,8},{10,11... | collective-permute-start | bytes 3145736 | tf_op jit(solution)/shard_map/ppermute | solution.py:115
  5.0 18.4 %collective-permute-start.3 = (bf16[144,1024]{1,0:T(8,128)(2,1)S(1)}, bf16[144,1024]{1,0:T(8,128)(2,1)S(1)}, u32[]{:S(2)}, u32[]{:S(2)}) collective-permute-start(bf16[144,1024]{1,0:T(8,128)(2,1)S(1)} %fusion.1.refs_0_), channel_id=1, source_target_pairs={{0,8},{1,9},{2,10},{3,11},{4,12},{5,13},{6,14},{7,15},{8,0},{9,1},... | collective-permute-start | bytes 884744 | tf_op jit(solution)/shard_map/ppermute | solution.py:115
  8.7 14.6 %collective-permute-start.2 = (bf16[144,1024]{1,0:T(8,128)(2,1)S(1)}, bf16[144,1024]{1,0:T(8,128)(2,1)S(1)}, u32[]{:S(2)}, u32[]{:S(2)}) collective-permute-start(bf16[144,1024]{1,0:T(8,128)(2,1)S(1)} %fusion.1.refs_0_), channel_id=1, source_target_pairs={{0,2},{1,3},{2,0},{3,1},{4,6},{5,7},{6,4},{7,5},{8,10},{9,11},{10,... | collective-permute-start | bytes 884744 | tf_op jit(solution)/shard_map/ppermute | solution.py:115
  10.2 13.9 %collective-permute-start.1 = (bf16[144,1024]{1,0:T(8,128)(2,1)S(1)}, bf16[144,1024]{1,0:T(8,128)(2,1)S(1)}, u32[]{:S(2)}, u32[]{:S(2)}) collective-permute-start(bf16[144,1024]{1,0:T(8,128)(2,1)S(1)} %fusion.1.refs_0_), channel_id=1, source_target_pairs={{0,4},{1,5},{2,6},{3,7},{4,0},{5,1},{6,2},{7,3},{8,12},{9,13},{10,... | collective-permute-start | bytes 884744 | tf_op jit(solution)/shard_map/ppermute | solution.py:115
  11.8 11.5 %collective-permute-start.4 = (bf16[128,1024]{1,0:T(8,128)(2,1)S(1)}, bf16[128,1024]{1,0:T(8,128)(2,1)S(1)}, u32[]{:S(2)}, u32[]{:S(2)}) collective-permute-start(bf16[128,1024]{1,0:T(8,128)(2,1)S(1)} %pad_maximum_fusion.refs_0_.refs_8_), channel_id=1, source_target_pairs={{0,2},{1,3},{2,0},{3,1},{4,6},{5,7},{6,4},{7,5},{8,10},{9,11},{10,... | collective-permute-start | bytes 786440 | tf_op jit(solution)/shard_map/ppermute | solution.py:115
  24.1 30.4 %collective-permute-start.13 = (bf16[512,1024]{1,0:T(8,128)(2,1)}, bf16[512,1024]{1,0:T(8,128)(2,1)}, u32[]{:S(2)}, u32[]{:S(2)}) collective-permute-start(bf16[512,1024]{1,0:T(8,128)(2,1)} %bitcast.26), channel_id=1, source_target_pairs={{0,1},{1,0},{2,3},{3,2},{4,5},{5,4},{6,7},{7,6},{8,9},{9,8},{10,11... | collective-permute-start | bytes 3145736 | tf_op jit(solution)/shard_map/ppermute | solution.py:115
  24.2 13.5 %collective-permute-start.6 = (bf16[144,1024]{1,0:T(8,128)(2,1)S(1)}, bf16[144,1024]{1,0:T(8,128)(2,1)S(1)}, u32[]{:S(2)}, u32[]{:S(2)}) collective-permute-start(bf16[144,1024]{1,0:T(8,128)(2,1)S(1)} %collective-permute-done.3.refs_2_), channel_id=1, source_target_pairs={{0,4},{1,5},{2,6},{3,7},{4,0},{5,1},{6,2},{7,3},{8,12},{9,13},{10,... | collective-permute-start | bytes 884744 | tf_op jit(solution)/shard_map/ppermute | solution.py:115
  25.1 16.4 %collective-permute-start.8 = (bf16[144,1024]{1,0:T(8,128)(2,1)S(1)}, bf16[144,1024]{1,0:T(8,128)(2,1)S(1)}, u32[]{:S(2)}, u32[]{:S(2)}) collective-permute-start(bf16[144,1024]{1,0:T(8,128)(2,1)S(1)} %collective-permute-done.1.refs_1_), channel_id=1, source_target_pairs={{0,2},{1,3},{2,0},{3,1},{4,6},{5,7},{6,4},{7,5},{8,10},{9,11},{10,... | collective-permute-start | bytes 884744 | tf_op jit(solution)/shard_map/ppermute | solution.py:115
  26.6 15.0 %collective-permute-start.9 = (bf16[144,1024]{1,0:T(8,128)(2,1)S(1)}, bf16[144,1024]{1,0:T(8,128)(2,1)S(1)}, u32[]{:S(2)}, u32[]{:S(2)}) collective-permute-start(bf16[144,1024]{1,0:T(8,128)(2,1)S(1)} %collective-permute-done.3.refs_2_), channel_id=1, source_target_pairs={{0,2},{1,3},{2,0},{3,1},{4,6},{5,7},{6,4},{7,5},{8,10},{9,11},{10,... | collective-permute-start | bytes 884744 | tf_op jit(solution)/shard_map/ppermute | solution.py:115
  27.2 14.4 %collective-permute-start.7 = (bf16[128,1024]{1,0:T(8,128)(2,1)S(1)}, bf16[128,1024]{1,0:T(8,128)(2,1)S(1)}, u32[]{:S(2)}, u32[]{:S(2)}) collective-permute-start(bf16[128,1024]{1,0:T(8,128)(2,1)S(1)} %pad_maximum_fusion.refs_0_.refs_8_), channel_id=1, source_target_pairs={{0,8},{1,9},{2,10},{3,11},{4,12},{5,13},{6,14},{7,15},{8,0},{9,1},... | collective-permute-start | bytes 786440 | tf_op jit(solution)/shard_map/ppermute | solution.py:115
  37.7 14.9 %collective-permute-start.10 = (bf16[144,1024]{1,0:T(8,128)(2,1)S(1)}, bf16[144,1024]{1,0:T(8,128)(2,1)S(1)}, u32[]{:S(2)}, u32[]{:S(2)}) collective-permute-start(bf16[144,1024]{1,0:T(8,128)(2,1)S(1)} %collective-permute-done.6.refs_3_), channel_id=1, source_target_pairs={{0,2},{1,3},{2,0},{3,1},{4,6},{5,7},{6,4},{7,5},{8,10},{9,11},{10,... | collective-permute-start | bytes 884744 | tf_op jit(solution)/shard_map/ppermute | solution.py:115
  41.6 9.2 %collective-permute-start.11 = (bf16[128,1024]{1,0:T(8,128)(2,1)S(1)}, bf16[128,1024]{1,0:T(8,128)(2,1)S(1)}, u32[]{:S(2)}, u32[]{:S(2)}) collective-permute-start(bf16[128,1024]{1,0:T(8,128)(2,1)S(1)} %pad_maximum_fusion.refs_0_.refs_8_), channel_id=1, source_target_pairs={{0,4},{1,5},{2,6},{3,7},{4,0},{5,1},{6,2},{7,3},{8,12},{9,13},{10,... | collective-permute-start | bytes 786440 | tf_op jit(solution)/shard_map/ppermute | solution.py:115
  41.6 11.0 %collective-permute-start.12 = (bf16[128,1024]{1,0:T(8,128)(2,1)S(1)}, bf16[128,1024]{1,0:T(8,128)(2,1)}, u32[]{:S(2)}, u32[]{:S(2)}) collective-permute-start(bf16[128,1024]{1,0:T(8,128)(2,1)S(1)} %collective-permute-done.7.refs_2_.refs_10_), channel_id=1, source_target_pairs={{0,2},{1,3},{2,0},{3,1},{4,6},{5,7},{6,4},{7,5},{8,10},{9,11},{10,... | collective-permute-start | bytes 786440 | tf_op jit(solution)/shard_map/ppermute | solution.py:115
  43.1 25.4 %collective-permute-start.14 = (bf16[128,1024]{1,0:T(8,128)(2,1)S(1)}, bf16[128,1024]{1,0:T(8,128)(2,1)S(1)}, u32[]{:S(2)}, u32[]{:S(2)}) collective-permute-start(bf16[128,1024]{1,0:T(8,128)(2,1)S(1)} %collective-permute-done.7.refs_2_.refs_10_), channel_id=1, source_target_pairs={{0,4},{1,5},{2,6},{3,7},{4,0},{5,1},{6,2},{7,3},{8,12},{9,13},{10,... | collective-permute-start | bytes 786440 | tf_op jit(solution)/shard_map/ppermute | solution.py:115
  52.6 13.7 %collective-permute-start.15 = (bf16[128,1024]{1,0:T(8,128)(2,1)S(1)}, bf16[128,1024]{1,0:T(8,128)(2,1)S(1)}, u32[]{:S(2)}, u32[]{:S(2)}) collective-permute-start(bf16[128,1024]{1,0:T(8,128)(2,1)S(1)} %collective-permute-done.11.refs_1_.refs_9_), channel_id=1, source_target_pairs={{0,2},{1,3},{2,0},{3,1},{4,6},{5,7},{6,4},{7,5},{8,10},{9,11},{10,... | collective-permute-start | bytes 786440 | tf_op jit(solution)/shard_map/ppermute | solution.py:115
  54.1 12.2 %collective-permute-start.16 = (bf16[128,1024]{1,0:T(8,128)(2,1)}, bf16[128,1024]{1,0:T(8,128)(2,1)S(1)}, u32[]{:S(2)}, u32[]{:S(2)}) collective-permute-start(bf16[128,1024]{1,0:T(8,128)(2,1)} %collective-permute-done.12.refs_6_.refs_14_), channel_id=1, source_target_pairs={{0,4},{1,5},{2,6},{3,7},{4,0},{5,1},{6,2},{7,3},{8,12},{9,13},{10,... | collective-permute-start | bytes 786440 | tf_op jit(solution)/shard_map/ppermute | solution.py:115
  66.3 14.8 %collective-permute-start.18 = (bf16[128,1024]{1,0:T(8,128)(2,1)}, bf16[128,1024]{1,0:T(8,128)(2,1)S(1)}, u32[]{:S(2)}, u32[]{:S(2)}) collective-permute-start(bf16[128,1024]{1,0:T(8,128)(2,1)} %get-tuple-element.135), channel_id=1, source_target_pairs={{0,2},{1,3},{2,0},{3,1},{4,6},{5,7},{6,4},{7,5},{8,10},{9,11},{10,... | collective-permute-start | bytes 786440 | tf_op jit(solution)/shard_map/ppermute | solution.py:115
  67.6 13.5 %collective-permute-start.17 = (bf16[256,1024]{1,0:T(8,128)(2,1)}, bf16[256,1024]{1,0:T(8,128)(2,1)S(1)}, u32[]{:S(2)}, u32[]{:S(2)}) collective-permute-start(bf16[256,1024]{1,0:T(8,128)(2,1)} %get-tuple-element.134), channel_id=1, source_target_pairs={{0,4},{1,5},{2,6},{3,7},{4,0},{5,1},{6,2},{7,3},{8,12},{9,13},{10,... | collective-permute-start | bytes 1572872 | tf_op jit(solution)/shard_map/ppermute | solution.py:115
  81.3 9.6 %collective-permute-start.20 = (bf16[128,1024]{1,0:T(8,128)(2,1)S(1)}, bf16[128,1024]{1,0:T(8,128)(2,1)S(1)}, u32[]{:S(2)}, u32[]{:S(2)}) collective-permute-start(bf16[128,1024]{1,0:T(8,128)(2,1)S(1)} %add_convert_fusion.6), channel_id=1, source_target_pairs={{0,2},{1,3},{2,0},{3,1},{4,6},{5,7},{6,4},{7,5},{8,10},{9,11},{10,... | collective-permute-start | bytes 786440 | tf_op jit(solution)/shard_map/ppermute | solution.py:115
  82.9 11.3 %collective-permute-start.19 = (bf16[144,1024]{1,0:T(8,128)(2,1)}, bf16[144,1024]{1,0:T(8,128)(2,1)S(1)}, u32[]{:S(2)}, u32[]{:S(2)}) collective-permute-start(bf16[144,1024]{1,0:T(8,128)(2,1)} %get-tuple-element.149), channel_id=1, source_target_pairs={{0,2},{1,3},{2,0},{3,1},{4,6},{5,7},{6,4},{7,5},{8,10},{9,11},{10,... | collective-permute-start | bytes 884744 | tf_op jit(solution)/shard_map/ppermute | solution.py:115
  94.2 17.4 %collective-permute-start.25 = (bf16[1536,1024]{1,0:T(8,128)(2,1)}, bf16[1536,1024]{1,0:T(8,128)(2,1)S(1)}, u32[]{:S(2)}, u32[]{:S(2)}) collective-permute-start(bf16[1536,1024]{1,0:T(8,128)(2,1)} %shard_map.120), channel_id=1, source_target_pairs={{0,1},{1,0},{2,3},{3,2},{4,5},{5,4},{6,7},{7,6},{8,9},{9,8},{10,11... | collective-permute-start | bytes 9437192 | tf_op jit(solution)/shard_map/ppermute | solution.py:115
  94.3 9.9 %collective-permute-start.21 = (bf16[144,1024]{1,0:T(8,128)(2,1)S(1)}, bf16[144,1024]{1,0:T(8,128)(2,1)S(1)}, u32[]{:S(2)}, u32[]{:S(2)}) collective-permute-start(bf16[144,1024]{1,0:T(8,128)(2,1)S(1)} %copy-done.29), channel_id=1, source_target_pairs={{0,2},{1,3},{2,0},{3,1},{4,6},{5,7},{6,4},{7,5},{8,10},{9,11},{10,... | collective-permute-start | bytes 884744 | tf_op jit(solution)/shard_map/ppermute | solution.py:115
  95.9 15.2 %collective-permute-start.22 = (bf16[144,1024]{1,0:T(8,128)(2,1)S(1)}, bf16[144,1024]{1,0:T(8,128)(2,1)S(1)}, u32[]{:S(2)}, u32[]{:S(2)}) collective-permute-start(bf16[144,1024]{1,0:T(8,128)(2,1)S(1)} %add_convert_fusion.2), channel_id=1, source_target_pairs={{0,4},{1,5},{2,6},{3,7},{4,0},{5,1},{6,2},{7,3},{8,12},{9,13},{10,... | collective-permute-start | bytes 884744 | tf_op jit(solution)/shard_map/ppermute | solution.py:115
  96.3 15.3 %collective-permute-start.24 = (bf16[144,1024]{1,0:T(8,128)(2,1)S(1)}, bf16[144,1024]{1,0:T(8,128)(2,1)S(1)}, u32[]{:S(2)}, u32[]{:S(2)}) collective-permute-start(bf16[144,1024]{1,0:T(8,128)(2,1)S(1)} %copy-done.28), channel_id=1, source_target_pairs={{0,2},{1,3},{2,0},{3,1},{4,6},{5,7},{6,4},{7,5},{8,10},{9,11},{10,... | collective-permute-start | bytes 884744 | tf_op jit(solution)/shard_map/ppermute | solution.py:115
  97.7 14.0 %collective-permute-start.26 = (bf16[128,1024]{1,0:T(8,128)(2,1)S(1)}, bf16[128,1024]{1,0:T(8,128)(2,1)S(1)}, u32[]{:S(2)}, u32[]{:S(2)}) collective-permute-start(bf16[128,1024]{1,0:T(8,128)(2,1)S(1)} %add_convert_fusion.4), channel_id=1, source_target_pairs={{0,8},{1,9},{2,10},{3,11},{4,12},{5,13},{6,14},{7,15},{8,0},{9,1},... | collective-permute-start | bytes 786440 | tf_op jit(solution)/shard_map/ppermute | solution.py:115
  104.2 24.6 %collective-permute-start.30 = (bf16[128,1024]{1,0:T(8,128)(2,1)S(1)}, bf16[128,1024]{1,0:T(8,128)(2,1)S(1)}, u32[]{:S(2)}, u32[]{:S(2)}) collective-permute-start(bf16[128,1024]{1,0:T(8,128)(2,1)S(1)} %add_convert_fusion.5), channel_id=1, source_target_pairs={{0,4},{1,5},{2,6},{3,7},{4,0},{5,1},{6,2},{7,3},{8,12},{9,13},{10,... | collective-permute-start | bytes 786440 | tf_op jit(solution)/shard_map/ppermute | solution.py:115
  111.2 14.9 %collective-permute-start.23 = (bf16[144,1024]{1,0:T(8,128)(2,1)S(1)}, bf16[144,1024]{1,0:T(8,128)(2,1)S(1)}, u32[]{:S(2)}, u32[]{:S(2)}) collective-permute-start(bf16[144,1024]{1,0:T(8,128)(2,1)S(1)} %add_convert_fusion.1), channel_id=1, source_target_pairs={{0,8},{1,9},{2,10},{3,11},{4,12},{5,13},{6,14},{7,15},{8,0},{9,1},... | collective-permute-start | bytes 884744 | tf_op jit(solution)/shard_map/ppermute | solution.py:115
  111.8 14.3 %collective-permute-start.28 = (bf16[128,1024]{1,0:T(8,128)(2,1)S(1)}, bf16[128,1024]{1,0:T(8,128)(2,1)S(1)}, u32[]{:S(2)}, u32[]{:S(2)}) collective-permute-start(bf16[128,1024]{1,0:T(8,128)(2,1)S(1)} %copy-done.30), channel_id=1, source_target_pairs={{0,2},{1,3},{2,0},{3,1},{4,6},{5,7},{6,4},{7,5},{8,10},{9,11},{10,... | collective-permute-start | bytes 786440 | tf_op jit(solution)/shard_map/ppermute | solution.py:115
  112.6 13.6 %collective-permute-start.27 = (bf16[144,1024]{1,0:T(8,128)(2,1)S(1)}, bf16[144,1024]{1,0:T(8,128)(2,1)S(1)}, u32[]{:S(2)}, u32[]{:S(2)}) collective-permute-start(bf16[144,1024]{1,0:T(8,128)(2,1)S(1)} %copy-done.27), channel_id=1, source_target_pairs={{0,2},{1,3},{2,0},{3,1},{4,6},{5,7},{6,4},{7,5},{8,10},{9,11},{10,... | collective-permute-start | bytes 884744 | tf_op jit(solution)/shard_map/ppermute | solution.py:115
  113.9 14.9 %collective-permute-start.29 = (bf16[144,1024]{1,0:T(8,128)(2,1)S(1)}, bf16[144,1024]{1,0:T(8,128)(2,1)S(1)}, u32[]{:S(2)}, u32[]{:S(2)}) collective-permute-start(bf16[144,1024]{1,0:T(8,128)(2,1)S(1)} %add_convert_fusion), channel_id=1, source_target_pairs={{0,4},{1,5},{2,6},{3,7},{4,0},{5,1},{6,2},{7,3},{8,12},{9,13},{10,... | collective-permute-start | bytes 884744 | tf_op jit(solution)/shard_map/ppermute | solution.py:115
  (30 other events, 508.9 us)

commit v12 on v11

--- a/solution.py
+++ b/solution.py
@@ -440,8 +440,8 @@
     a = [a0, a1, a2, a3, a4, a5, a6, a7]
     q, (*a_factors, shares, inners) = both_ways(0, a, weights, me)
     q0, q1, q2, q4, q5, q6, q73 = q
-    q73, q5, shares, inners, b5, b7 = fence(q73, q5, shares, inners, b5, b7)
-    r73, r5 = swap(q73, NEAR), swap(q5, SIDE)
+    q73, q5, q4, shares, inners, b5, b7 = fence(q73, q5, q4, shares, inners, b5, b7)
+    r73, r5, q4 = swap(q73, NEAR), swap(q5, SIDE), swap(q4, SIDE)
     b = [b0, b1, b2, b3, b4, b5, b6, b7]
     p, b_factors = both_ways(1, b, weights, me, (shares, inners))
     p0, p1, p2, p3, p4, p5, p6, p7 = p
@@ -451,20 +451,20 @@
     q6, p7, q1 = fence(q6, p7, q1)
     r6, r7, q1 = swap(q6, SIDE), swap(p7, SIDE), swap(q1, NEAR)
     away = weight_grads(1, (a, b), factors)
-    r6, away, p6, p5 = fence(r6, away, p6, p5)
+    r6, q1, away, p6, p5 = fence(r6, q1, away, p6, p5)
     q2 = swap(narrow(q2 + r6.astype(f32)), FAR)
     r7, p6, p5, away = fence(r7, p6, p5, away)
     p3 = narrow(added(p3, r7))
     p3, p6, p5, away = fence(p3, p6, p5, away)
     r6, p3, r5, away = swap(p6, SIDE), swap(p3, NEAR), swap(p5, SIDE), swap(away, CORE)
-    r6, p3, q4, p4 = fence(r6, p3, q4, p4)
+    r6, p3, p4 = fence(r6, p3, p4)
     p2 = swap(narrow(added(p2, r6) + p3.astype(f32)), FAR)
-    r5, away, p4, q4, q2 = fence(r5, away, p4, q4, q2)
+    r5, away, p4, q2 = fence(r5, away, p4, q2)
     p1 = narrow(added(p1, r5))
-    p1, p4, q4, away = fence(p1, p4, q4, away)
-    p4, q4, p1 = swap(p4, SIDE), swap(q4, SIDE), swap(p1, NEAR)
+    p1, p4, away = fence(p1, p4, away)
+    p4, p1 = swap(p4, SIDE), swap(p1, NEAR)
     grad_w = weight_grads(0, (a, b), factors, away)
-    p2, p4, q4, p1, grad_w = fence(p2, p4, q4, p1, grad_w)
+    p2, p4, p1, grad_w = fence(p2, p4, p1, grad_w)
 
     q = added(q0, q4) + added(q1, q2)
     p = added(p0, p4) + added(p1, p2)

time: 132 us -> 132 us (level)
  waiting for transfers between devices: 51.1 us -> 46.5 us
  starting transfers between devices: 33.1 us -> 37.6 us
    ppermute x31, starting transfers between devices: 33.1 us -> 37.6 us  [swap(): return lax.ppermute(value, 'ep', pairs)]
    ppermute x31, waiting for transfers between devices: 51.1 us -> 46.5 us  [swap(): return lax.ppermute(value, 'ep', pairs)]
  transfers between devices with their start and end apart: 31 -> 31, of which waited for: 13 -> 11; matrix products, arithmetic and copies ran while one was open for 2% -> 2% of each run, Pallas kernels for 30% -> 30%
where the time goes in v12:
time: 132 us; the launch traced here: 131 us
  waiting for transfers between devices  46.5 us (35%)
  Pallas kernels  39.3 us (30%)
  starting transfers between devices  37.6 us (28%)
  other arithmetic  3.76 us (3%)
  local copies, waits for them, and re-layouts  3.01 us (2%)
    ppermute x31, waiting for transfers between devices, swap(): return lax.ppermute(value, 'ep', pairs)  46.5 us
    pallas_call x4, Pallas kernels, kernel(): pl.pallas_call(body, out_shape=outs, in_specs=in_specs, out_specs=[pl.Blo...  39.3 us
    ppermute x31, starting transfers between devices, swap(): return lax.ppermute(value, 'ep', pairs)  37.6 us
  transfers between devices with their start and end apart: 31, of which 11 were waited for; matrix products, arithmetic and copies ran while one was open for 2% of the time, Pallas kernels for 30%

profile of v12, /device:TPU:0, one launch (start us, length us, event | category | flops | bytes accessed | tf_op | source)
XLA Modules:
  0.0 131.4 jit_solution(15153576519952804313)
XLA Ops:
  2.0 1.1 fusion.6
  3.6 1.0 copy-done.25
  5.0 3.7 %collective-permute-start.3 = (bf16[144,1024]{1,0:T(8,128)(2,1)S(1)}, bf16[144,1024]{1,0:T(8,128)(2,1)S(1)}, u32[]{:S(2)}, u32[]{:S(2)}) collective-permute-start(bf16[144,1024]{1,0:T(8,128)(2,1)S(1)} %fusion.1.refs_0_), channel_id=1, source_target_pairs={{0,8},{1,9},{2,10},{3,11},{4,12},{5,13},{6,14},{7,15},{8,0},{9,1},... | collective-permute-start | bytes 884744 | tf_op jit(solution)/shard_map/ppermute | solution.py:115
  8.7 1.5 %collective-permute-start.2 = (bf16[144,1024]{1,0:T(8,128)(2,1)S(1)}, bf16[144,1024]{1,0:T(8,128)(2,1)S(1)}, u32[]{:S(2)}, u32[]{:S(2)}) collective-permute-start(bf16[144,1024]{1,0:T(8,128)(2,1)S(1)} %fusion.1.refs_0_), channel_id=1, source_target_pairs={{0,2},{1,3},{2,0},{3,1},{4,6},{5,7},{6,4},{7,5},{8,10},{9,11},{10,... | collective-permute-start | bytes 884744 | tf_op jit(solution)/shard_map/ppermute | solution.py:115
  10.2 1.6 %collective-permute-start.1 = (bf16[144,1024]{1,0:T(8,128)(2,1)S(1)}, bf16[144,1024]{1,0:T(8,128)(2,1)S(1)}, u32[]{:S(2)}, u32[]{:S(2)}) collective-permute-start(bf16[144,1024]{1,0:T(8,128)(2,1)S(1)} %fusion.1.refs_0_), channel_id=1, source_target_pairs={{0,4},{1,5},{2,6},{3,7},{4,0},{5,1},{6,2},{7,3},{8,12},{9,13},{10,... | collective-permute-start | bytes 884744 | tf_op jit(solution)/shard_map/ppermute | solution.py:115
  12.3 11.0 %collective-permute-done.4.refs_4_.refs_12_ = bf16[128,1024]{1,0:T(8,128)(2,1)S(1)} collective-permute-done((bf16[128,1024]{1,0:T(8,128)(2,1)S(1)}, bf16[128,1024]{1,0:T(8,128)(2,1)S(1)}, u32[]{:S(2)}, u32[]{:S(2)}) %collective-permute-start.4) | collective-permute-done | bytes 262176 | tf_op jit(solution)/shard_map/ppermute | solution.py:115
  24.2 1.0 collective-permute-start.6
  25.1 1.5 %collective-permute-start.8 = (bf16[144,1024]{1,0:T(8,128)(2,1)S(1)}, bf16[144,1024]{1,0:T(8,128)(2,1)S(1)}, u32[]{:S(2)}, u32[]{:S(2)}) collective-permute-start(bf16[144,1024]{1,0:T(8,128)(2,1)S(1)} %collective-permute-done.1.refs_1_), channel_id=1, source_target_pairs={{0,2},{1,3},{2,0},{3,1},{4,6},{5,7},{6,4},{7,5},{8,10},{9,11},{10,... | collective-permute-start | bytes 884744 | tf_op jit(solution)/shard_map/ppermute | solution.py:115
  27.2 2.2 %collective-permute-start.7 = (bf16[128,1024]{1,0:T(8,128)(2,1)S(1)}, bf16[128,1024]{1,0:T(8,128)(2,1)S(1)}, u32[]{:S(2)}, u32[]{:S(2)}) collective-permute-start(bf16[128,1024]{1,0:T(8,128)(2,1)S(1)} %pad_maximum_fusion.refs_0_.refs_8_), channel_id=1, source_target_pairs={{0,8},{1,9},{2,10},{3,11},{4,12},{5,13},{6,14},{7,15},{8,0},{9,1},... | collective-permute-start | bytes 786440 | tf_op jit(solution)/shard_map/ppermute | solution.py:115
  29.3 8.4 %collective-permute-done.6.refs_3_ = bf16[144,1024]{1,0:T(8,128)(2,1)S(1)} collective-permute-done((bf16[144,1024]{1,0:T(8,128)(2,1)S(1)}, bf16[144,1024]{1,0:T(8,128)(2,1)S(1)}, u32[]{:S(2)}, u32[]{:S(2)}) %collective-permute-start.6) | collective-permute-done | bytes 294944 | tf_op jit(solution)/shard_map/ppermute | solution.py:115
  38.1 3.4 %collective-permute-done.7.refs_2_.refs_10_ = bf16[128,1024]{1,0:T(8,128)(2,1)S(1)} collective-permute-done((bf16[128,1024]{1,0:T(8,128)(2,1)S(1)}, bf16[128,1024]{1,0:T(8,128)(2,1)S(1)}, u32[]{:S(2)}, u32[]{:S(2)}) %collective-permute-start.7) | collective-permute-done | bytes 262176 | tf_op jit(solution)/shard_map/ppermute | solution.py:115
  41.6 1.5 %collective-permute-start.12 = (bf16[128,1024]{1,0:T(8,128)(2,1)S(1)}, bf16[128,1024]{1,0:T(8,128)(2,1)}, u32[]{:S(2)}, u32[]{:S(2)}) collective-permute-start(bf16[128,1024]{1,0:T(8,128)(2,1)S(1)} %collective-permute-done.7.refs_2_.refs_10_), channel_id=1, source_target_pairs={{0,2},{1,3},{2,0},{3,1},{4,6},{5,7},{6,4},{7,5},{8,10},{9,11},{10,... | collective-permute-start | bytes 786440 | tf_op jit(solution)/shard_map/ppermute | solution.py:115
  43.1 2.0 %collective-permute-start.19 = (bf16[128,1024]{1,0:T(8,128)(2,1)S(1)}, bf16[128,1024]{1,0:T(8,128)(2,1)S(1)}, u32[]{:S(2)}, u32[]{:S(2)}) collective-permute-start(bf16[128,1024]{1,0:T(8,128)(2,1)S(1)} %collective-permute-done.7.refs_2_.refs_10_), channel_id=1, source_target_pairs={{0,4},{1,5},{2,6},{3,7},{4,0},{5,1},{6,2},{7,3},{8,12},{9,13},{10,... | collective-permute-start | bytes 786440 | tf_op jit(solution)/shard_map/ppermute | solution.py:115
  45.1 5.6 %collective-permute-done.11.refs_1_.refs_9_ = bf16[128,1024]{1,0:T(8,128)(2,1)S(1)} collective-permute-done((bf16[128,1024]{1,0:T(8,128)(2,1)S(1)}, bf16[128,1024]{1,0:T(8,128)(2,1)S(1)}, u32[]{:S(2)}, u32[]{:S(2)}) %collective-permute-start.11) | collective-permute-done | bytes 262176 | tf_op jit(solution)/shard_map/ppermute | solution.py:115
  50.8 1.8 %collective-permute-done.12.refs_6_.refs_14_ = bf16[128,1024]{1,0:T(8,128)(2,1)} collective-permute-done((bf16[128,1024]{1,0:T(8,128)(2,1)S(1)}, bf16[128,1024]{1,0:T(8,128)(2,1)}, u32[]{:S(2)}, u32[]{:S(2)}) %collective-permute-start.12) | collective-permute-done | bytes 262176 | tf_op jit(solution)/shard_map/ppermute | solution.py:115
  52.6 1.5 %collective-permute-start.14 = (bf16[128,1024]{1,0:T(8,128)(2,1)S(1)}, bf16[128,1024]{1,0:T(8,128)(2,1)S(1)}, u32[]{:S(2)}, u32[]{:S(2)}) collective-permute-start(bf16[128,1024]{1,0:T(8,128)(2,1)S(1)} %collective-permute-done.11.refs_1_.refs_9_), channel_id=1, source_target_pairs={{0,2},{1,3},{2,0},{3,1},{4,6},{5,7},{6,4},{7,5},{8,10},{9,11},{10,... | collective-permute-start | bytes 786440 | tf_op jit(solution)/shard_map/ppermute | solution.py:115
  54.6 11.7 %shard_map.118 = (bf16[128,1024]{1,0:T(8,128)(2,1)}, bf16[128,1024]{1,0:T(8,128)(2,1)}, bf16[128,1024]{1,0:T(8,128)(2,1)}, bf16[128,1024]{1,0:T(8,128)(2,1)}, bf...) custom-call(s32[1]{0:T(128)} %bitcast.me_ref, ...), custom_call_target="tpu_custom_call" | custom-call | flops 6442450944 | bytes 14024704 | tf_op jit(solution)/shard_map/pallas_call | solution.py:162
  66.3 1.3 collective-permute-start.17
  67.6 0.8 collective-permute-start.18
  68.4 1.6 %collective-permute-start.16 = (bf16[256,1024]{1,0:T(8,128)(2,1)}, bf16[256,1024]{1,0:T(8,128)(2,1)S(1)}, u32[]{:S(2)}, u32[]{:S(2)}) collective-permute-start(bf16[256,1024]{1,0:T(8,128)(2,1)} %get-tuple-element.126), channel_id=1, source_target_pairs={{0,4},{1,5},{2,6},{3,7},{4,0},{5,1},{6,2},{7,3},{8,12},{9,13},{10,... | collective-permute-start | bytes 1572872 | tf_op jit(solution)/shard_map/ppermute | solution.py:115
  70.7 11.9 %shard_map.119 = (bf16[144,1024]{1,0:T(8,128)(2,1)}, bf16[144,1024]{1,0:T(8,128)(2,1)}, bf16[144,1024]{1,0:T(8,128)(2,1)}, bf16[144,1024]{1,0:T(8,128)(2,1)}, bf...) custom-call(s32[1]{0:T(128)} %bitcast.me_ref, ...), custom_call_target="tpu_custom_call" | custom-call | flops 6442450944 | bytes 14024704 | tf_op jit(solution)/shard_map/pallas_call | solution.py:162
  83.5 1.1 collective-permute-start.21
  85.4 7.4 %shard_map.120 = bf16[1536,1024]{1,0:T(8,128)(2,1)} custom-call(bf16[144,1024]{1,0:T(8,128)(2,1)} %copy-done.1, bf16[144,1024]{1,0:T(8,128)(2,1)} %copy-done.5, bf16[144,1024]{1,0:T(8,128)(2,1)} %copy-done.3, bf16[144,1024]{1,0:T(8,128)(2,1)} %copy-done.6, bf16[144,1024]{1,0:T(8,128)(2,1)} %copy-done.4, bf16[144,1024]{1,0:T(8,128)(2,1)} %copy-done.7, ...), custom_call_target="tpu_custom_call" | custom-call | flops 3221225472 | bytes 13893632 | tf_op jit(solution)/shard_map/pallas_call | solution.py:162
  92.9 2.5 %collective-permute-done.22 = bf16[144,1024]{1,0:T(8,128)(2,1)S(1)} collective-permute-done((bf16[144,1024]{1,0:T(8,128)(2,1)}, bf16[144,1024]{1,0:T(8,128)(2,1)S(1)}, u32[]{:S(2)}, u32[]{:S(2)}) %collective-permute-start.22) | collective-permute-done | bytes 294944 | tf_op jit(solution)/shard_map/ppermute | solution.py:115
  96.2 1.1 collective-permute-start.26
  98.2 1.7 %collective-permute-start.27 = (bf16[128,1024]{1,0:T(8,128)(2,1)S(1)}, bf16[128,1024]{1,0:T(8,128)(2,1)S(1)}, u32[]{:S(2)}, u32[]{:S(2)}) collective-permute-start(bf16[128,1024]{1,0:T(8,128)(2,1)S(1)} %add_convert_fusion.4), channel_id=1, source_target_pairs={{0,8},{1,9},{2,10},{3,11},{4,12},{5,13},{6,14},{7,15},{8,0},{9,1},... | collective-permute-start | bytes 786440 | tf_op jit(solution)/shard_map/ppermute | solution.py:115
  99.9 5.5 %collective-permute-done.25 = bf16[144,1024]{1,0:T(8,128)(2,1)S(1)} collective-permute-done((bf16[144,1024]{1,0:T(8,128)(2,1)S(1)}, bf16[144,1024]{1,0:T(8,128)(2,1)S(1)}, u32[]{:S(2)}, u32[]{:S(2)}) %collective-permute-start.25) | collective-permute-done | bytes 294944 | tf_op jit(solution)/shard_map/ppermute | solution.py:115
  105.4 5.3 %collective-permute-done.26 = bf16[144,1024]{1,0:T(8,128)(2,1)S(1)} collective-permute-done((bf16[144,1024]{1,0:T(8,128)(2,1)S(1)}, bf16[144,1024]{1,0:T(8,128)(2,1)S(1)}, u32[]{:S(2)}, u32[]{:S(2)}) %collective-permute-start.26) | collective-permute-done | bytes 294944 | tf_op jit(solution)/shard_map/ppermute | solution.py:115
  110.9 1.7 %collective-permute-done.27 = bf16[128,1024]{1,0:T(8,128)(2,1)S(1)} collective-permute-done((bf16[128,1024]{1,0:T(8,128)(2,1)S(1)}, bf16[128,1024]{1,0:T(8,128)(2,1)S(1)}, u32[]{:S(2)}, u32[]{:S(2)}) %collective-permute-start.27) | collective-permute-done | bytes 262176 | tf_op jit(solution)/shard_map/ppermute | solution.py:115
  113.0 1.3 collective-permute-start.29
  114.3 6.5 %collective-permute-start.30 = (bf16[144,1024]{1,0:T(8,128)(2,1)S(1)}, bf16[144,1024]{1,0:T(8,128)(2,1)S(1)}, u32[]{:S(2)}, u32[]{:S(2)}) collective-permute-start(bf16[144,1024]{1,0:T(8,128)(2,1)S(1)} %add_convert_fusion), channel_id=1, source_target_pairs={{0,4},{1,5},{2,6},{3,7},{4,0},{5,1},{6,2},{7,3},{8,12},{9,13},{10,... | collective-permute-start | bytes 884744 | tf_op jit(solution)/shard_map/ppermute | solution.py:115
  120.8 8.3 %shard_map.121 = (bf16[1024,512]{1,0:T(8,128)(2,1)}, bf16[1024,512]{1,0:T(8,128)(2,1)}, bf16[512,1024]{1,0:T(8,128)(2,1)}) custom-call(bf16[144,1024]{1,0:T(8,128)(2,1)} %copy-done.1, bf16[144,1024]{1,0:T(8,128)(2,1)} %copy-done.5, bf16[144,1024]{1,0:T(8,128)(2,1)} %copy-done.3, bf16[144,1024]{1,0:T(8,128)(2,1)} %copy-done.6, bf16[144,1024]{1,0:T(8,128)(2,1)} %copy-done.4, ...), custom_call_target="tpu_custom_call" | custom-call | flops 3221225472 | bytes 17039360 | tf_op jit(solution)/shard_map/pallas_call | solution.py:162
  (118 shorter events, 11.8 us)
Async XLA Ops:
  0.6 3.0 %collective-permute-start = (bf16[1024,512]{1,0:T(8,128)(2,1)}, bf16[1024,512]{1,0:T(8,128)(2,1)S(1)}, u32[]{:S(2)}, u32[]{:S(2)}) collective-permute-start(bf16[1024,512]{1,0:T(8,128)(2,1)} %bitcast.20), channel_id=1, source_target_pairs={{0,1},{1,0},{2,3},{3,2},{4,5},{5,4},{6,7},{7,6},{8,9},{9,8},{10,11... | collective-permute-start | bytes 3145736 | tf_op jit(solution)/shard_map/ppermute | solution.py:115
  3.1 63.1 %copy-start.2 = (bf16[128,1024]{1,0:T(8,128)(2,1)}, bf16[128,1024]{1,0:T(8,128)(2,1)S(1)}, u32[]{:S(2)}) copy-start(bf16[128,1024]{1,0:T(8,128)(2,1)S(1)} %pad_maximum_fusion.refs_0_.refs_8_) | copy-start | bytes 786436
  4.6 19.5 %collective-permute-start.5 = (bf16[1024,512]{1,0:T(8,128)(2,1)}, bf16[1024,512]{1,0:T(8,128)(2,1)S(1)}, u32[]{:S(2)}, u32[]{:S(2)}) collective-permute-start(bf16[1024,512]{1,0:T(8,128)(2,1)} %bitcast.23), channel_id=1, source_target_pairs={{0,1},{1,0},{2,3},{3,2},{4,5},{5,4},{6,7},{7,6},{8,9},{9,8},{10,11... | collective-permute-start | bytes 3145736 | tf_op jit(solution)/shard_map/ppermute | solution.py:115
  5.0 18.4 %collective-permute-start.3 = (bf16[144,1024]{1,0:T(8,128)(2,1)S(1)}, bf16[144,1024]{1,0:T(8,128)(2,1)S(1)}, u32[]{:S(2)}, u32[]{:S(2)}) collective-permute-start(bf16[144,1024]{1,0:T(8,128)(2,1)S(1)} %fusion.1.refs_0_), channel_id=1, source_target_pairs={{0,8},{1,9},{2,10},{3,11},{4,12},{5,13},{6,14},{7,15},{8,0},{9,1},... | collective-permute-start | bytes 884744 | tf_op jit(solution)/shard_map/ppermute | solution.py:115
  8.7 14.6 %collective-permute-start.2 = (bf16[144,1024]{1,0:T(8,128)(2,1)S(1)}, bf16[144,1024]{1,0:T(8,128)(2,1)S(1)}, u32[]{:S(2)}, u32[]{:S(2)}) collective-permute-start(bf16[144,1024]{1,0:T(8,128)(2,1)S(1)} %fusion.1.refs_0_), channel_id=1, source_target_pairs={{0,2},{1,3},{2,0},{3,1},{4,6},{5,7},{6,4},{7,5},{8,10},{9,11},{10,... | collective-permute-start | bytes 884744 | tf_op jit(solution)/shard_map/ppermute | solution.py:115
  10.2 13.9 %collective-permute-start.1 = (bf16[144,1024]{1,0:T(8,128)(2,1)S(1)}, bf16[144,1024]{1,0:T(8,128)(2,1)S(1)}, u32[]{:S(2)}, u32[]{:S(2)}) collective-permute-start(bf16[144,1024]{1,0:T(8,128)(2,1)S(1)} %fusion.1.refs_0_), channel_id=1, source_target_pairs={{0,4},{1,5},{2,6},{3,7},{4,0},{5,1},{6,2},{7,3},{8,12},{9,13},{10,... | collective-permute-start | bytes 884744 | tf_op jit(solution)/shard_map/ppermute | solution.py:115
  11.8 11.5 %collective-permute-start.4 = (bf16[128,1024]{1,0:T(8,128)(2,1)S(1)}, bf16[128,1024]{1,0:T(8,128)(2,1)S(1)}, u32[]{:S(2)}, u32[]{:S(2)}) collective-permute-start(bf16[128,1024]{1,0:T(8,128)(2,1)S(1)} %pad_maximum_fusion.refs_0_.refs_8_), channel_id=1, source_target_pairs={{0,2},{1,3},{2,0},{3,1},{4,6},{5,7},{6,4},{7,5},{8,10},{9,11},{10,... | collective-permute-start | bytes 786440 | tf_op jit(solution)/shard_map/ppermute | solution.py:115
  24.1 30.4 %collective-permute-start.13 = (bf16[512,1024]{1,0:T(8,128)(2,1)}, bf16[512,1024]{1,0:T(8,128)(2,1)}, u32[]{:S(2)}, u32[]{:S(2)}) collective-permute-start(bf16[512,1024]{1,0:T(8,128)(2,1)} %bitcast.26), channel_id=1, source_target_pairs={{0,1},{1,0},{2,3},{3,2},{4,5},{5,4},{6,7},{7,6},{8,9},{9,8},{10,11... | collective-permute-start | bytes 3145736 | tf_op jit(solution)/shard_map/ppermute | solution.py:115
  24.2 13.5 %collective-permute-start.6 = (bf16[144,1024]{1,0:T(8,128)(2,1)S(1)}, bf16[144,1024]{1,0:T(8,128)(2,1)S(1)}, u32[]{:S(2)}, u32[]{:S(2)}) collective-permute-start(bf16[144,1024]{1,0:T(8,128)(2,1)S(1)} %collective-permute-done.3.refs_2_), channel_id=1, source_target_pairs={{0,4},{1,5},{2,6},{3,7},{4,0},{5,1},{6,2},{7,3},{8,12},{9,13},{10,... | collective-permute-start | bytes 884744 | tf_op jit(solution)/shard_map/ppermute | solution.py:115
  25.1 16.4 %collective-permute-start.8 = (bf16[144,1024]{1,0:T(8,128)(2,1)S(1)}, bf16[144,1024]{1,0:T(8,128)(2,1)S(1)}, u32[]{:S(2)}, u32[]{:S(2)}) collective-permute-start(bf16[144,1024]{1,0:T(8,128)(2,1)S(1)} %collective-permute-done.1.refs_1_), channel_id=1, source_target_pairs={{0,2},{1,3},{2,0},{3,1},{4,6},{5,7},{6,4},{7,5},{8,10},{9,11},{10,... | collective-permute-start | bytes 884744 | tf_op jit(solution)/shard_map/ppermute | solution.py:115
  26.6 15.0 %collective-permute-start.9 = (bf16[144,1024]{1,0:T(8,128)(2,1)S(1)}, bf16[144,1024]{1,0:T(8,128)(2,1)S(1)}, u32[]{:S(2)}, u32[]{:S(2)}) collective-permute-start(bf16[144,1024]{1,0:T(8,128)(2,1)S(1)} %collective-permute-done.3.refs_2_), channel_id=1, source_target_pairs={{0,2},{1,3},{2,0},{3,1},{4,6},{5,7},{6,4},{7,5},{8,10},{9,11},{10,... | collective-permute-start | bytes 884744 | tf_op jit(solution)/shard_map/ppermute | solution.py:115
  27.2 14.4 %collective-permute-start.7 = (bf16[128,1024]{1,0:T(8,128)(2,1)S(1)}, bf16[128,1024]{1,0:T(8,128)(2,1)S(1)}, u32[]{:S(2)}, u32[]{:S(2)}) collective-permute-start(bf16[128,1024]{1,0:T(8,128)(2,1)S(1)} %pad_maximum_fusion.refs_0_.refs_8_), channel_id=1, source_target_pairs={{0,8},{1,9},{2,10},{3,11},{4,12},{5,13},{6,14},{7,15},{8,0},{9,1},... | collective-permute-start | bytes 786440 | tf_op jit(solution)/shard_map/ppermute | solution.py:115
  37.7 14.9 %collective-permute-start.10 = (bf16[144,1024]{1,0:T(8,128)(2,1)S(1)}, bf16[144,1024]{1,0:T(8,128)(2,1)S(1)}, u32[]{:S(2)}, u32[]{:S(2)}) collective-permute-start(bf16[144,1024]{1,0:T(8,128)(2,1)S(1)} %collective-permute-done.6.refs_3_), channel_id=1, source_target_pairs={{0,2},{1,3},{2,0},{3,1},{4,6},{5,7},{6,4},{7,5},{8,10},{9,11},{10,... | collective-permute-start | bytes 884744 | tf_op jit(solution)/shard_map/ppermute | solution.py:115
  41.6 9.2 %collective-permute-start.11 = (bf16[128,1024]{1,0:T(8,128)(2,1)S(1)}, bf16[128,1024]{1,0:T(8,128)(2,1)S(1)}, u32[]{:S(2)}, u32[]{:S(2)}) collective-permute-start(bf16[128,1024]{1,0:T(8,128)(2,1)S(1)} %pad_maximum_fusion.refs_0_.refs_8_), channel_id=1, source_target_pairs={{0,4},{1,5},{2,6},{3,7},{4,0},{5,1},{6,2},{7,3},{8,12},{9,13},{10,... | collective-permute-start | bytes 786440 | tf_op jit(solution)/shard_map/ppermute | solution.py:115
  41.6 11.0 %collective-permute-start.12 = (bf16[128,1024]{1,0:T(8,128)(2,1)S(1)}, bf16[128,1024]{1,0:T(8,128)(2,1)}, u32[]{:S(2)}, u32[]{:S(2)}) collective-permute-start(bf16[128,1024]{1,0:T(8,128)(2,1)S(1)} %collective-permute-done.7.refs_2_.refs_10_), channel_id=1, source_target_pairs={{0,2},{1,3},{2,0},{3,1},{4,6},{5,7},{6,4},{7,5},{8,10},{9,11},{10,... | collective-permute-start | bytes 786440 | tf_op jit(solution)/shard_map/ppermute | solution.py:115
  43.1 26.9 %collective-permute-start.19 = (bf16[128,1024]{1,0:T(8,128)(2,1)S(1)}, bf16[128,1024]{1,0:T(8,128)(2,1)S(1)}, u32[]{:S(2)}, u32[]{:S(2)}) collective-permute-start(bf16[128,1024]{1,0:T(8,128)(2,1)S(1)} %collective-permute-done.7.refs_2_.refs_10_), channel_id=1, source_target_pairs={{0,4},{1,5},{2,6},{3,7},{4,0},{5,1},{6,2},{7,3},{8,12},{9,13},{10,... | collective-permute-start | bytes 786440 | tf_op jit(solution)/shard_map/ppermute | solution.py:115
  52.6 13.7 %collective-permute-start.14 = (bf16[128,1024]{1,0:T(8,128)(2,1)S(1)}, bf16[128,1024]{1,0:T(8,128)(2,1)S(1)}, u32[]{:S(2)}, u32[]{:S(2)}) collective-permute-start(bf16[128,1024]{1,0:T(8,128)(2,1)S(1)} %collective-permute-done.11.refs_1_.refs_9_), channel_id=1, source_target_pairs={{0,2},{1,3},{2,0},{3,1},{4,6},{5,7},{6,4},{7,5},{8,10},{9,11},{10,... | collective-permute-start | bytes 786440 | tf_op jit(solution)/shard_map/ppermute | solution.py:115
  54.1 12.2 %collective-permute-start.15 = (bf16[128,1024]{1,0:T(8,128)(2,1)}, bf16[128,1024]{1,0:T(8,128)(2,1)S(1)}, u32[]{:S(2)}, u32[]{:S(2)}) collective-permute-start(bf16[128,1024]{1,0:T(8,128)(2,1)} %collective-permute-done.12.refs_6_.refs_14_), channel_id=1, source_target_pairs={{0,4},{1,5},{2,6},{3,7},{4,0},{5,1},{6,2},{7,3},{8,12},{9,13},{10,... | collective-permute-start | bytes 786440 | tf_op jit(solution)/shard_map/ppermute | solution.py:115
  66.3 16.3 %collective-permute-start.17 = (bf16[128,1024]{1,0:T(8,128)(2,1)}, bf16[128,1024]{1,0:T(8,128)(2,1)S(1)}, u32[]{:S(2)}, u32[]{:S(2)}) collective-permute-start(bf16[128,1024]{1,0:T(8,128)(2,1)} %get-tuple-element.127), channel_id=1, source_target_pairs={{0,2},{1,3},{2,0},{3,1},{4,6},{5,7},{6,4},{7,5},{8,10},{9,11},{10,... | collective-permute-start | bytes 786440 | tf_op jit(solution)/shard_map/ppermute | solution.py:115
  67.6 15.0 %collective-permute-start.18 = (bf16[128,1024]{1,0:T(8,128)(2,1)}, bf16[128,1024]{1,0:T(8,128)(2,1)S(1)}, u32[]{:S(2)}, u32[]{:S(2)}) collective-permute-start(bf16[128,1024]{1,0:T(8,128)(2,1)} %get-tuple-element.129), channel_id=1, source_target_pairs={{0,2},{1,3},{2,0},{3,1},{4,6},{5,7},{6,4},{7,5},{8,10},{9,11},{10,... | collective-permute-start | bytes 786440 | tf_op jit(solution)/shard_map/ppermute | solution.py:115
  68.4 14.2 %collective-permute-start.16 = (bf16[256,1024]{1,0:T(8,128)(2,1)}, bf16[256,1024]{1,0:T(8,128)(2,1)S(1)}, u32[]{:S(2)}, u32[]{:S(2)}) collective-permute-start(bf16[256,1024]{1,0:T(8,128)(2,1)} %get-tuple-element.126), channel_id=1, source_target_pairs={{0,4},{1,5},{2,6},{3,7},{4,0},{5,1},{6,2},{7,3},{8,12},{9,13},{10,... | collective-permute-start | bytes 1572872 | tf_op jit(solution)/shard_map/ppermute | solution.py:115
  82.9 10.0 %collective-permute-start.20 = (bf16[128,1024]{1,0:T(8,128)(2,1)S(1)}, bf16[128,1024]{1,0:T(8,128)(2,1)S(1)}, u32[]{:S(2)}, u32[]{:S(2)}) collective-permute-start(bf16[128,1024]{1,0:T(8,128)(2,1)S(1)} %add_convert_fusion.6), channel_id=1, source_target_pairs={{0,2},{1,3},{2,0},{3,1},{4,6},{5,7},{6,4},{7,5},{8,10},{9,11},{10,... | collective-permute-start | bytes 786440 | tf_op jit(solution)/shard_map/ppermute | solution.py:115
  83.5 9.4 %collective-permute-start.21 = (bf16[128,1024]{1,0:T(8,128)(2,1)S(1)}, bf16[128,1024]{1,0:T(8,128)(2,1)S(1)}, u32[]{:S(2)}, u32[]{:S(2)}) collective-permute-start(bf16[128,1024]{1,0:T(8,128)(2,1)S(1)} %add_convert_fusion.5), channel_id=1, source_target_pairs={{0,4},{1,5},{2,6},{3,7},{4,0},{5,1},{6,2},{7,3},{8,12},{9,13},{10,... | collective-permute-start | bytes 786440 | tf_op jit(solution)/shard_map/ppermute | solution.py:115
  84.6 10.8 %collective-permute-start.22 = (bf16[144,1024]{1,0:T(8,128)(2,1)}, bf16[144,1024]{1,0:T(8,128)(2,1)S(1)}, u32[]{:S(2)}, u32[]{:S(2)}) collective-permute-start(bf16[144,1024]{1,0:T(8,128)(2,1)} %get-tuple-element.157), channel_id=1, source_target_pairs={{0,2},{1,3},{2,0},{3,1},{4,6},{5,7},{6,4},{7,5},{8,10},{9,11},{10,... | collective-permute-start | bytes 884744 | tf_op jit(solution)/shard_map/ppermute | solution.py:115
  95.5 17.2 %collective-permute-start.24 = (bf16[1536,1024]{1,0:T(8,128)(2,1)}, bf16[1536,1024]{1,0:T(8,128)(2,1)S(1)}, u32[]{:S(2)}, u32[]{:S(2)}) collective-permute-start(bf16[1536,1024]{1,0:T(8,128)(2,1)} %shard_map.120), channel_id=1, source_target_pairs={{0,1},{1,0},{2,3},{3,2},{4,5},{5,4},{6,7},{7,6},{8,9},{9,8},{10,11... | collective-permute-start | bytes 9437192 | tf_op jit(solution)/shard_map/ppermute | solution.py:115
  95.6 9.9 %collective-permute-start.25 = (bf16[144,1024]{1,0:T(8,128)(2,1)S(1)}, bf16[144,1024]{1,0:T(8,128)(2,1)S(1)}, u32[]{:S(2)}, u32[]{:S(2)}) collective-permute-start(bf16[144,1024]{1,0:T(8,128)(2,1)S(1)} %copy-done.29), channel_id=1, source_target_pairs={{0,2},{1,3},{2,0},{3,1},{4,6},{5,7},{6,4},{7,5},{8,10},{9,11},{10,... | collective-permute-start | bytes 884744 | tf_op jit(solution)/shard_map/ppermute | solution.py:115
  96.2 14.6 %collective-permute-start.26 = (bf16[144,1024]{1,0:T(8,128)(2,1)S(1)}, bf16[144,1024]{1,0:T(8,128)(2,1)S(1)}, u32[]{:S(2)}, u32[]{:S(2)}) collective-permute-start(bf16[144,1024]{1,0:T(8,128)(2,1)S(1)} %add_convert_fusion.2), channel_id=1, source_target_pairs={{0,4},{1,5},{2,6},{3,7},{4,0},{5,1},{6,2},{7,3},{8,12},{9,13},{10,... | collective-permute-start | bytes 884744 | tf_op jit(solution)/shard_map/ppermute | solution.py:115
  97.3 15.4 %collective-permute-start.23 = (bf16[144,1024]{1,0:T(8,128)(2,1)S(1)}, bf16[144,1024]{1,0:T(8,128)(2,1)S(1)}, u32[]{:S(2)}, u32[]{:S(2)}) collective-permute-start(bf16[144,1024]{1,0:T(8,128)(2,1)S(1)} %copy-done.28), channel_id=1, source_target_pairs={{0,2},{1,3},{2,0},{3,1},{4,6},{5,7},{6,4},{7,5},{8,10},{9,11},{10,... | collective-permute-start | bytes 884744 | tf_op jit(solution)/shard_map/ppermute | solution.py:115
  98.2 14.4 %collective-permute-start.27 = (bf16[128,1024]{1,0:T(8,128)(2,1)S(1)}, bf16[128,1024]{1,0:T(8,128)(2,1)S(1)}, u32[]{:S(2)}, u32[]{:S(2)}) collective-permute-start(bf16[128,1024]{1,0:T(8,128)(2,1)S(1)} %add_convert_fusion.4), channel_id=1, source_target_pairs={{0,8},{1,9},{2,10},{3,11},{4,12},{5,13},{6,14},{7,15},{8,0},{9,1},... | collective-permute-start | bytes 786440 | tf_op jit(solution)/shard_map/ppermute | solution.py:115
  110.9 18.2 %collective-permute-start.28 = (bf16[144,1024]{1,0:T(8,128)(2,1)S(1)}, bf16[144,1024]{1,0:T(8,128)(2,1)S(1)}, u32[]{:S(2)}, u32[]{:S(2)}) collective-permute-start(bf16[144,1024]{1,0:T(8,128)(2,1)S(1)} %add_convert_fusion.1), channel_id=1, source_target_pairs={{0,8},{1,9},{2,10},{3,11},{4,12},{5,13},{6,14},{7,15},{8,0},{9,1},... | collective-permute-start | bytes 884744 | tf_op jit(solution)/shard_map/ppermute | solution.py:115
  113.0 16.1 %collective-permute-start.29 = (bf16[144,1024]{1,0:T(8,128)(2,1)S(1)}, bf16[144,1024]{1,0:T(8,128)(2,1)S(1)}, u32[]{:S(2)}, u32[]{:S(2)}) collective-permute-start(bf16[144,1024]{1,0:T(8,128)(2,1)S(1)} %copy-done.27), channel_id=1, source_target_pairs={{0,2},{1,3},{2,0},{3,1},{4,6},{5,7},{6,4},{7,5},{8,10},{9,11},{10,... | collective-permute-start | bytes 884744 | tf_op jit(solution)/shard_map/ppermute | solution.py:115
  114.3 14.8 %collective-permute-start.30 = (bf16[144,1024]{1,0:T(8,128)(2,1)S(1)}, bf16[144,1024]{1,0:T(8,128)(2,1)S(1)}, u32[]{:S(2)}, u32[]{:S(2)}) collective-permute-start(bf16[144,1024]{1,0:T(8,128)(2,1)S(1)} %add_convert_fusion), channel_id=1, source_target_pairs={{0,4},{1,5},{2,6},{3,7},{4,0},{5,1},{6,2},{7,3},{8,12},{9,13},{10,... | collective-permute-start | bytes 884744 | tf_op jit(solution)/shard_map/ppermute | solution.py:115
  (29 other events, 502.2 us)

commit v13 on v11

--- a/solution.py
+++ b/solution.py
@@ -192,7 +192,7 @@
     every, size = count * tok_count, 2 * tok_count
     lanes = 128
     back = size + (EXTRA if last else 0)
-    layout = [[b] for b in range(count)] if last else [[0], [1], [2], [4], [5], [6], [7, 3]]
+    layout = [[0], [1], [2], [4], [5], [6], [7, 3]]
     place_of = {b: (i, j * back) for i, held in enumerate(layout) for j, b in enumerate(held)}
 
     def body(me_ref, *refs):
@@ -444,27 +444,27 @@
     r73, r5 = swap(q73, NEAR), swap(q5, SIDE)
     b = [b0, b1, b2, b3, b4, b5, b6, b7]
     p, b_factors = both_ways(1, b, weights, me, (shares, inners))
-    p0, p1, p2, p3, p4, p5, p6, p7 = p
-    r73, r5, q6, q4, p7, p6, p5, p4, b_factors = fence(r73, r5, q6, q4, p7, p6, p5, p4, b_factors)
+    p0, p1, p2, p4, p5, p6, p73 = p
+    r73, r5, q6, q4, p73, p6, p5, p4, b_factors = fence(r73, r5, q6, q4, p73, p6, p5, p4, b_factors)
     factors, size = (a_factors, b_factors), q6.shape[0]
     q6, q2, q1 = narrow(added(q6, r73[:size])), added(q2, r73[size:]), narrow(added(q1, r5))
-    q6, p7, q1 = fence(q6, p7, q1)
-    r6, r7, q1 = swap(q6, SIDE), swap(p7, SIDE), swap(q1, NEAR)
+    q6, p73, p5, q1 = fence(q6, p73, p5, q1)
+    r6, r73, r5 = swap(q6, SIDE), swap(p73, NEAR), swap(p5, SIDE)
     away = weight_grads(1, (a, b), factors)
-    r6, away, p6, p5 = fence(r6, away, p6, p5)
+    r6, r5, away = fence(r6, r5, away)
     q2 = swap(narrow(q2 + r6.astype(f32)), FAR)
-    r7, p6, p5, away = fence(r7, p6, p5, away)
-    p3 = narrow(added(p3, r7))
-    p3, p6, p5, away = fence(p3, p6, p5, away)
-    r6, p3, r5, away = swap(p6, SIDE), swap(p3, NEAR), swap(p5, SIDE), swap(away, CORE)
-    r6, p3, q4, p4 = fence(r6, p3, q4, p4)
-    p2 = swap(narrow(added(p2, r6) + p3.astype(f32)), FAR)
-    r5, away, p4, q4, q2 = fence(r5, away, p4, q4, q2)
+    size = p6.shape[0]
     p1 = narrow(added(p1, r5))
-    p1, p4, q4, away = fence(p1, p4, q4, away)
-    p4, q4, p1 = swap(p4, SIDE), swap(q4, SIDE), swap(p1, NEAR)
+    p6, r73, away, q1, p1 = fence(p6, r73, away, q1, p1)
+    p6 = narrow(added(p6, r73[:size]))
+    p6, away, q1, q4 = fence(p6, away, q1, q4)
+    r6, q1, q4, away = swap(p6, SIDE), swap(q1, NEAR), swap(q4, SIDE), swap(away, CORE)
+    r6, p1, p4 = fence(r6, p1, p4)
+    p2 = narrow(added(p2, r73[size:]) + r6.astype(f32))
+    p2, p1, p4, away = fence(p2, p1, p4, away)
+    p2, p1, p4 = swap(p2, FAR), swap(p1, NEAR), swap(p4, SIDE)
     grad_w = weight_grads(0, (a, b), factors, away)
-    p2, p4, q4, p1, grad_w = fence(p2, p4, q4, p1, grad_w)
+    p2, p1, p4, q4, q2, q1, grad_w = fence(p2, p1, p4, q4, q2, q1, grad_w)
 
     q = added(q0, q4) + added(q1, q2)
     p = added(p0, p4) + added(p1, p2)

time: 132 us -> 128 us (0.970)
  waiting for transfers between devices: 51.1 us -> 46.7 us
    ppermute x31 -> x30, waiting for transfers between devices: 51.1 us -> 46.7 us  [swap(): return lax.ppermute(value, 'ep', pairs)]
    ppermute x31 -> x30, starting transfers between devices: 33.1 us -> 33.9 us  [swap(): return lax.ppermute(value, 'ep', pairs)]
  transfers between devices with their start and end apart: 31 -> 30, of which waited for: 13 -> 12; matrix products, arithmetic and copies ran while one was open for 2% -> 2% of each run, Pallas kernels for 30% -> 31%
where the time goes in v13:
time: 128 us
  waiting for transfers between devices  46.7 us (36%)
  Pallas kernels  39.4 us (31%)
  starting transfers between devices  33.9 us (26%)
  other arithmetic  3.76 us (3%)
  local copies, waits for them, and re-layouts  3.01 us (2%)
    ppermute x30, waiting for transfers between devices, swap(): return lax.ppermute(value, 'ep', pairs)  46.7 us
    pallas_call x4, Pallas kernels, kernel(): pl.pallas_call(body, out_shape=outs, in_specs=in_specs, out_specs=[pl.Blo...  39.4 us
    ppermute x30, starting transfers between devices, swap(): return lax.ppermute(value, 'ep', pairs)  33.9 us
  transfers between devices with their start and end apart: 30, of which 12 were waited for; matrix products, arithmetic and copies ran while one was open for 2% of the time, Pallas kernels for 31%

profile of v13, /device:TPU:0, one launch (start us, length us, event | category | flops | bytes accessed | tf_op | source)
XLA Modules:
  0.0 128.0 jit_solution(11752053078017438344)
XLA Ops:
  2.0 1.1 fusion.6
  3.7 1.0 copy-done.25
  5.0 3.7 %collective-permute-start.3 = (bf16[144,1024]{1,0:T(8,128)(2,1)S(1)}, bf16[144,1024]{1,0:T(8,128)(2,1)S(1)}, u32[]{:S(2)}, u32[]{:S(2)}) collective-permute-start(bf16[144,1024]{1,0:T(8,128)(2,1)S(1)} %fusion.1.refs_0_), channel_id=1, source_target_pairs={{0,8},{1,9},{2,10},{3,11},{4,12},{5,13},{6,14},{7,15},{8,0},{9,1},... | collective-permute-start | bytes 884744 | tf_op jit(solution)/shard_map/ppermute | solution.py:115
  8.7 1.5 %collective-permute-start.2 = (bf16[144,1024]{1,0:T(8,128)(2,1)S(1)}, bf16[144,1024]{1,0:T(8,128)(2,1)S(1)}, u32[]{:S(2)}, u32[]{:S(2)}) collective-permute-start(bf16[144,1024]{1,0:T(8,128)(2,1)S(1)} %fusion.1.refs_0_), channel_id=1, source_target_pairs={{0,2},{1,3},{2,0},{3,1},{4,6},{5,7},{6,4},{7,5},{8,10},{9,11},{10,... | collective-permute-start | bytes 884744 | tf_op jit(solution)/shard_map/ppermute | solution.py:115
  10.2 1.6 %collective-permute-start.1 = (bf16[144,1024]{1,0:T(8,128)(2,1)S(1)}, bf16[144,1024]{1,0:T(8,128)(2,1)S(1)}, u32[]{:S(2)}, u32[]{:S(2)}) collective-permute-start(bf16[144,1024]{1,0:T(8,128)(2,1)S(1)} %fusion.1.refs_0_), channel_id=1, source_target_pairs={{0,4},{1,5},{2,6},{3,7},{4,0},{5,1},{6,2},{7,3},{8,12},{9,13},{10,... | collective-permute-start | bytes 884744 | tf_op jit(solution)/shard_map/ppermute | solution.py:115
  12.3 11.0 %collective-permute-done.4.refs_4_.refs_12_ = bf16[128,1024]{1,0:T(8,128)(2,1)S(1)} collective-permute-done((bf16[128,1024]{1,0:T(8,128)(2,1)S(1)}, bf16[128,1024]{1,0:T(8,128)(2,1)S(1)}, u32[]{:S(2)}, u32[]{:S(2)}) %collective-permute-start.4) | collective-permute-done | bytes 262176 | tf_op jit(solution)/shard_map/ppermute | solution.py:115
  24.2 1.0 collective-permute-start.6
  25.1 1.5 %collective-permute-start.8 = (bf16[144,1024]{1,0:T(8,128)(2,1)S(1)}, bf16[144,1024]{1,0:T(8,128)(2,1)S(1)}, u32[]{:S(2)}, u32[]{:S(2)}) collective-permute-start(bf16[144,1024]{1,0:T(8,128)(2,1)S(1)} %collective-permute-done.1.refs_1_), channel_id=1, source_target_pairs={{0,2},{1,3},{2,0},{3,1},{4,6},{5,7},{6,4},{7,5},{8,10},{9,11},{10,... | collective-permute-start | bytes 884744 | tf_op jit(solution)/shard_map/ppermute | solution.py:115
  27.2 2.2 %collective-permute-start.7 = (bf16[128,1024]{1,0:T(8,128)(2,1)S(1)}, bf16[128,1024]{1,0:T(8,128)(2,1)S(1)}, u32[]{:S(2)}, u32[]{:S(2)}) collective-permute-start(bf16[128,1024]{1,0:T(8,128)(2,1)S(1)} %pad_maximum_fusion.refs_0_.refs_8_), channel_id=1, source_target_pairs={{0,8},{1,9},{2,10},{3,11},{4,12},{5,13},{6,14},{7,15},{8,0},{9,1},... | collective-permute-start | bytes 786440 | tf_op jit(solution)/shard_map/ppermute | solution.py:115
  29.3 8.4 %collective-permute-done.6.refs_3_ = bf16[144,1024]{1,0:T(8,128)(2,1)S(1)} collective-permute-done((bf16[144,1024]{1,0:T(8,128)(2,1)S(1)}, bf16[144,1024]{1,0:T(8,128)(2,1)S(1)}, u32[]{:S(2)}, u32[]{:S(2)}) %collective-permute-start.6) | collective-permute-done | bytes 294944 | tf_op jit(solution)/shard_map/ppermute | solution.py:115
  38.1 3.4 %collective-permute-done.7.refs_2_.refs_10_ = bf16[128,1024]{1,0:T(8,128)(2,1)S(1)} collective-permute-done((bf16[128,1024]{1,0:T(8,128)(2,1)S(1)}, bf16[128,1024]{1,0:T(8,128)(2,1)S(1)}, u32[]{:S(2)}, u32[]{:S(2)}) %collective-permute-start.7) | collective-permute-done | bytes 262176 | tf_op jit(solution)/shard_map/ppermute | solution.py:115
  41.6 1.5 %collective-permute-start.12 = (bf16[128,1024]{1,0:T(8,128)(2,1)S(1)}, bf16[128,1024]{1,0:T(8,128)(2,1)}, u32[]{:S(2)}, u32[]{:S(2)}) collective-permute-start(bf16[128,1024]{1,0:T(8,128)(2,1)S(1)} %collective-permute-done.7.refs_2_.refs_10_), channel_id=1, source_target_pairs={{0,2},{1,3},{2,0},{3,1},{4,6},{5,7},{6,4},{7,5},{8,10},{9,11},{10,... | collective-permute-start | bytes 786440 | tf_op jit(solution)/shard_map/ppermute | solution.py:115
  43.1 2.0 %collective-permute-start.14 = (bf16[128,1024]{1,0:T(8,128)(2,1)S(1)}, bf16[128,1024]{1,0:T(8,128)(2,1)S(1)}, u32[]{:S(2)}, u32[]{:S(2)}) collective-permute-start(bf16[128,1024]{1,0:T(8,128)(2,1)S(1)} %collective-permute-done.7.refs_2_.refs_10_), channel_id=1, source_target_pairs={{0,4},{1,5},{2,6},{3,7},{4,0},{5,1},{6,2},{7,3},{8,12},{9,13},{10,... | collective-permute-start | bytes 786440 | tf_op jit(solution)/shard_map/ppermute | solution.py:115
  45.1 5.6 %collective-permute-done.11.refs_1_.refs_9_ = bf16[128,1024]{1,0:T(8,128)(2,1)S(1)} collective-permute-done((bf16[128,1024]{1,0:T(8,128)(2,1)S(1)}, bf16[128,1024]{1,0:T(8,128)(2,1)S(1)}, u32[]{:S(2)}, u32[]{:S(2)}) %collective-permute-start.11) | collective-permute-done | bytes 262176 | tf_op jit(solution)/shard_map/ppermute | solution.py:115
  50.8 1.8 %collective-permute-done.12.refs_6_.refs_14_ = bf16[128,1024]{1,0:T(8,128)(2,1)} collective-permute-done((bf16[128,1024]{1,0:T(8,128)(2,1)S(1)}, bf16[128,1024]{1,0:T(8,128)(2,1)}, u32[]{:S(2)}, u32[]{:S(2)}) %collective-permute-start.12) | collective-permute-done | bytes 262176 | tf_op jit(solution)/shard_map/ppermute | solution.py:115
  52.6 1.5 %collective-permute-start.15 = (bf16[128,1024]{1,0:T(8,128)(2,1)S(1)}, bf16[128,1024]{1,0:T(8,128)(2,1)S(1)}, u32[]{:S(2)}, u32[]{:S(2)}) collective-permute-start(bf16[128,1024]{1,0:T(8,128)(2,1)S(1)} %collective-permute-done.11.refs_1_.refs_9_), channel_id=1, source_target_pairs={{0,2},{1,3},{2,0},{3,1},{4,6},{5,7},{6,4},{7,5},{8,10},{9,11},{10,... | collective-permute-start | bytes 786440 | tf_op jit(solution)/shard_map/ppermute | solution.py:115
  54.6 11.7 %shard_map.118 = (bf16[128,1024]{1,0:T(8,128)(2,1)}, bf16[128,1024]{1,0:T(8,128)(2,1)}, bf16[128,1024]{1,0:T(8,128)(2,1)}, bf16[128,1024]{1,0:T(8,128)(2,1)}, bf...) custom-call(s32[1]{0:T(128)} %bitcast.me_ref, ...), custom_call_target="tpu_custom_call" | custom-call | flops 6442450944 | bytes 14024704 | tf_op jit(solution)/shard_map/pallas_call | solution.py:162
  66.4 1.3 collective-permute-start.18
  69.3 12.0 %shard_map.119 = (bf16[144,1024]{1,0:T(8,128)(2,1)}, bf16[144,1024]{1,0:T(8,128)(2,1)}, bf16[144,1024]{1,0:T(8,128)(2,1)}, bf16[144,1024]{1,0:T(8,128)(2,1)}, bf...) custom-call(s32[1]{0:T(128)} %bitcast.me_ref, ...), custom_call_target="tpu_custom_call" | custom-call | flops 6442450944 | bytes 14024704 | tf_op jit(solution)/shard_map/pallas_call | solution.py:162
  81.5 1.2 collective-permute-start.19
  83.5 1.2 collective-permute-start.21
  84.7 7.4 %shard_map.120 = bf16[1536,1024]{1,0:T(8,128)(2,1)} custom-call(bf16[144,1024]{1,0:T(8,128)(2,1)} %copy-done.1, bf16[144,1024]{1,0:T(8,128)(2,1)} %copy-done.5, bf16[144,1024]{1,0:T(8,128)(2,1)} %copy-done.3, bf16[144,1024]{1,0:T(8,128)(2,1)} %copy-done.6, bf16[144,1024]{1,0:T(8,128)(2,1)} %copy-done.4, bf16[144,1024]{1,0:T(8,128)(2,1)} %copy-done.7, ...), custom_call_target="tpu_custom_call" | custom-call | flops 3221225472 | bytes 13893632 | tf_op jit(solution)/shard_map/pallas_call | solution.py:162
  92.2 3.0 %collective-permute-done.21 = bf16[144,1024]{1,0:T(8,128)(2,1)S(1)} collective-permute-done((bf16[144,1024]{1,0:T(8,128)(2,1)}, bf16[144,1024]{1,0:T(8,128)(2,1)S(1)}, u32[]{:S(2)}, u32[]{:S(2)}) %collective-permute-start.21) | collective-permute-done | bytes 294944 | tf_op jit(solution)/shard_map/ppermute | solution.py:115
  95.4 1.5 %collective-permute-start.22 = (bf16[144,1024]{1,0:T(8,128)(2,1)S(1)}, bf16[144,1024]{1,0:T(8,128)(2,1)S(1)}, u32[]{:S(2)}, u32[]{:S(2)}) collective-permute-start(bf16[144,1024]{1,0:T(8,128)(2,1)S(1)} %add_convert_fusion.1), channel_id=1, source_target_pairs={{0,2},{1,3},{2,0},{3,1},{4,6},{5,7},{6,4},{7,5},{8,10},{9,11},{10,... | collective-permute-start | bytes 884744 | tf_op jit(solution)/shard_map/ppermute | solution.py:115
  97.1 1.8 %collective-permute-start.28 = (bf16[128,1024]{1,0:T(8,128)(2,1)S(1)}, bf16[128,1024]{1,0:T(8,128)(2,1)S(1)}, u32[]{:S(2)}, u32[]{:S(2)}) collective-permute-start(bf16[128,1024]{1,0:T(8,128)(2,1)S(1)} %add_convert_fusion.4), channel_id=1, source_target_pairs={{0,8},{1,9},{2,10},{3,11},{4,12},{5,13},{6,14},{7,15},{8,0},{9,1},... | collective-permute-start | bytes 786440 | tf_op jit(solution)/shard_map/ppermute | solution.py:115
  98.9 0.9 collective-permute-start.27
  100.8 4.5 %collective-permute-done.22 = bf16[144,1024]{1,0:T(8,128)(2,1)S(1)} collective-permute-done((bf16[144,1024]{1,0:T(8,128)(2,1)S(1)}, bf16[144,1024]{1,0:T(8,128)(2,1)S(1)}, u32[]{:S(2)}, u32[]{:S(2)}) %collective-permute-start.22) | collective-permute-done | bytes 294944 | tf_op jit(solution)/shard_map/ppermute | solution.py:115
  105.5 2.2 %collective-permute-start.24 = (bf16[144,1024]{1,0:T(8,128)(2,1)S(1)}, bf16[144,1024]{1,0:T(8,128)(2,1)S(1)}, u32[]{:S(2)}, u32[]{:S(2)}) collective-permute-start(bf16[144,1024]{1,0:T(8,128)(2,1)S(1)} %add_convert_fusion), channel_id=1, source_target_pairs={{0,8},{1,9},{2,10},{3,11},{4,12},{5,13},{6,14},{7,15},{8,0},{9,1},... | collective-permute-start | bytes 884744 | tf_op jit(solution)/shard_map/ppermute | solution.py:115
  107.7 0.9 collective-permute-start.25
  108.6 4.7 %collective-permute-done.28 = bf16[128,1024]{1,0:T(8,128)(2,1)S(1)} collective-permute-done((bf16[128,1024]{1,0:T(8,128)(2,1)S(1)}, bf16[128,1024]{1,0:T(8,128)(2,1)S(1)}, u32[]{:S(2)}, u32[]{:S(2)}) %collective-permute-start.28) | collective-permute-done | bytes 262176 | tf_op jit(solution)/shard_map/ppermute | solution.py:115
  114.0 8.3 %shard_map.121 = (bf16[1024,512]{1,0:T(8,128)(2,1)}, bf16[1024,512]{1,0:T(8,128)(2,1)}, bf16[512,1024]{1,0:T(8,128)(2,1)}) custom-call(bf16[144,1024]{1,0:T(8,128)(2,1)} %copy-done.1, bf16[144,1024]{1,0:T(8,128)(2,1)} %copy-done.5, bf16[144,1024]{1,0:T(8,128)(2,1)} %copy-done.3, bf16[144,1024]{1,0:T(8,128)(2,1)} %copy-done.6, bf16[144,1024]{1,0:T(8,128)(2,1)} %copy-done.4, ...), custom_call_target="tpu_custom_call" | custom-call | flops 3221225472 | bytes 17039360 | tf_op jit(solution)/shard_map/pallas_call | solution.py:162
  122.4 2.4 %collective-permute-done.24 = bf16[144,1024]{1,0:T(8,128)(2,1)S(1)} collective-permute-done((bf16[144,1024]{1,0:T(8,128)(2,1)S(1)}, bf16[144,1024]{1,0:T(8,128)(2,1)S(1)}, u32[]{:S(2)}, u32[]{:S(2)}) %collective-permute-start.24) | collective-permute-done | bytes 294944 | tf_op jit(solution)/shard_map/ppermute | solution.py:115
  (114 shorter events, 12.9 us)
Async XLA Ops:
  0.6 3.0 %collective-permute-start = (bf16[1024,512]{1,0:T(8,128)(2,1)}, bf16[1024,512]{1,0:T(8,128)(2,1)S(1)}, u32[]{:S(2)}, u32[]{:S(2)}) collective-permute-start(bf16[1024,512]{1,0:T(8,128)(2,1)} %bitcast.20), channel_id=1, source_target_pairs={{0,1},{1,0},{2,3},{3,2},{4,5},{5,4},{6,7},{7,6},{8,9},{9,8},{10,11... | collective-permute-start | bytes 3145736 | tf_op jit(solution)/shard_map/ppermute | solution.py:115
  3.1 63.2 %copy-start.2 = (bf16[128,1024]{1,0:T(8,128)(2,1)}, bf16[128,1024]{1,0:T(8,128)(2,1)S(1)}, u32[]{:S(2)}) copy-start(bf16[128,1024]{1,0:T(8,128)(2,1)S(1)} %pad_maximum_fusion.refs_0_.refs_8_) | copy-start | bytes 786436
  3.2 51.4 %copy-start.1 = (bf16[144,1024]{1,0:T(8,128)(2,1)}, bf16[144,1024]{1,0:T(8,128)(2,1)S(1)}, u32[]{:S(2)}) copy-start(bf16[144,1024]{1,0:T(8,128)(2,1)S(1)} %fusion.1.refs_0_) | copy-start | bytes 884740
  4.6 19.5 %collective-permute-start.5 = (bf16[1024,512]{1,0:T(8,128)(2,1)}, bf16[1024,512]{1,0:T(8,128)(2,1)S(1)}, u32[]{:S(2)}, u32[]{:S(2)}) collective-permute-start(bf16[1024,512]{1,0:T(8,128)(2,1)} %bitcast.23), channel_id=1, source_target_pairs={{0,1},{1,0},{2,3},{3,2},{4,5},{5,4},{6,7},{7,6},{8,9},{9,8},{10,11... | collective-permute-start | bytes 3145736 | tf_op jit(solution)/shard_map/ppermute | solution.py:115
  5.0 18.4 %collective-permute-start.3 = (bf16[144,1024]{1,0:T(8,128)(2,1)S(1)}, bf16[144,1024]{1,0:T(8,128)(2,1)S(1)}, u32[]{:S(2)}, u32[]{:S(2)}) collective-permute-start(bf16[144,1024]{1,0:T(8,128)(2,1)S(1)} %fusion.1.refs_0_), channel_id=1, source_target_pairs={{0,8},{1,9},{2,10},{3,11},{4,12},{5,13},{6,14},{7,15},{8,0},{9,1},... | collective-permute-start | bytes 884744 | tf_op jit(solution)/shard_map/ppermute | solution.py:115
  8.7 14.6 %collective-permute-start.2 = (bf16[144,1024]{1,0:T(8,128)(2,1)S(1)}, bf16[144,1024]{1,0:T(8,128)(2,1)S(1)}, u32[]{:S(2)}, u32[]{:S(2)}) collective-permute-start(bf16[144,1024]{1,0:T(8,128)(2,1)S(1)} %fusion.1.refs_0_), channel_id=1, source_target_pairs={{0,2},{1,3},{2,0},{3,1},{4,6},{5,7},{6,4},{7,5},{8,10},{9,11},{10,... | collective-permute-start | bytes 884744 | tf_op jit(solution)/shard_map/ppermute | solution.py:115
  10.2 13.9 %collective-permute-start.1 = (bf16[144,1024]{1,0:T(8,128)(2,1)S(1)}, bf16[144,1024]{1,0:T(8,128)(2,1)S(1)}, u32[]{:S(2)}, u32[]{:S(2)}) collective-permute-start(bf16[144,1024]{1,0:T(8,128)(2,1)S(1)} %fusion.1.refs_0_), channel_id=1, source_target_pairs={{0,4},{1,5},{2,6},{3,7},{4,0},{5,1},{6,2},{7,3},{8,12},{9,13},{10,... | collective-permute-start | bytes 884744 | tf_op jit(solution)/shard_map/ppermute | solution.py:115
  11.8 11.5 %collective-permute-start.4 = (bf16[128,1024]{1,0:T(8,128)(2,1)S(1)}, bf16[128,1024]{1,0:T(8,128)(2,1)S(1)}, u32[]{:S(2)}, u32[]{:S(2)}) collective-permute-start(bf16[128,1024]{1,0:T(8,128)(2,1)S(1)} %pad_maximum_fusion.refs_0_.refs_8_), channel_id=1, source_target_pairs={{0,2},{1,3},{2,0},{3,1},{4,6},{5,7},{6,4},{7,5},{8,10},{9,11},{10,... | collective-permute-start | bytes 786440 | tf_op jit(solution)/shard_map/ppermute | solution.py:115
  24.1 30.4 %collective-permute-start.13 = (bf16[512,1024]{1,0:T(8,128)(2,1)}, bf16[512,1024]{1,0:T(8,128)(2,1)}, u32[]{:S(2)}, u32[]{:S(2)}) collective-permute-start(bf16[512,1024]{1,0:T(8,128)(2,1)} %bitcast.26), channel_id=1, source_target_pairs={{0,1},{1,0},{2,3},{3,2},{4,5},{5,4},{6,7},{7,6},{8,9},{9,8},{10,11... | collective-permute-start | bytes 3145736 | tf_op jit(solution)/shard_map/ppermute | solution.py:115
  24.2 13.5 %collective-permute-start.6 = (bf16[144,1024]{1,0:T(8,128)(2,1)S(1)}, bf16[144,1024]{1,0:T(8,128)(2,1)S(1)}, u32[]{:S(2)}, u32[]{:S(2)}) collective-permute-start(bf16[144,1024]{1,0:T(8,128)(2,1)S(1)} %collective-permute-done.3.refs_2_), channel_id=1, source_target_pairs={{0,4},{1,5},{2,6},{3,7},{4,0},{5,1},{6,2},{7,3},{8,12},{9,13},{10,... | collective-permute-start | bytes 884744 | tf_op jit(solution)/shard_map/ppermute | solution.py:115
  25.1 16.4 %collective-permute-start.8 = (bf16[144,1024]{1,0:T(8,128)(2,1)S(1)}, bf16[144,1024]{1,0:T(8,128)(2,1)S(1)}, u32[]{:S(2)}, u32[]{:S(2)}) collective-permute-start(bf16[144,1024]{1,0:T(8,128)(2,1)S(1)} %collective-permute-done.1.refs_1_), channel_id=1, source_target_pairs={{0,2},{1,3},{2,0},{3,1},{4,6},{5,7},{6,4},{7,5},{8,10},{9,11},{10,... | collective-permute-start | bytes 884744 | tf_op jit(solution)/shard_map/ppermute | solution.py:115
  26.6 15.0 %collective-permute-start.9 = (bf16[144,1024]{1,0:T(8,128)(2,1)S(1)}, bf16[144,1024]{1,0:T(8,128)(2,1)S(1)}, u32[]{:S(2)}, u32[]{:S(2)}) collective-permute-start(bf16[144,1024]{1,0:T(8,128)(2,1)S(1)} %collective-permute-done.3.refs_2_), channel_id=1, source_target_pairs={{0,2},{1,3},{2,0},{3,1},{4,6},{5,7},{6,4},{7,5},{8,10},{9,11},{10,... | collective-permute-start | bytes 884744 | tf_op jit(solution)/shard_map/ppermute | solution.py:115
  27.2 14.4 %collective-permute-start.7 = (bf16[128,1024]{1,0:T(8,128)(2,1)S(1)}, bf16[128,1024]{1,0:T(8,128)(2,1)S(1)}, u32[]{:S(2)}, u32[]{:S(2)}) collective-permute-start(bf16[128,1024]{1,0:T(8,128)(2,1)S(1)} %pad_maximum_fusion.refs_0_.refs_8_), channel_id=1, source_target_pairs={{0,8},{1,9},{2,10},{3,11},{4,12},{5,13},{6,14},{7,15},{8,0},{9,1},... | collective-permute-start | bytes 786440 | tf_op jit(solution)/shard_map/ppermute | solution.py:115
  37.7 14.9 %collective-permute-start.10 = (bf16[144,1024]{1,0:T(8,128)(2,1)S(1)}, bf16[144,1024]{1,0:T(8,128)(2,1)S(1)}, u32[]{:S(2)}, u32[]{:S(2)}) collective-permute-start(bf16[144,1024]{1,0:T(8,128)(2,1)S(1)} %collective-permute-done.6.refs_3_), channel_id=1, source_target_pairs={{0,2},{1,3},{2,0},{3,1},{4,6},{5,7},{6,4},{7,5},{8,10},{9,11},{10,... | collective-permute-start | bytes 884744 | tf_op jit(solution)/shard_map/ppermute | solution.py:115
  41.6 9.2 %collective-permute-start.11 = (bf16[128,1024]{1,0:T(8,128)(2,1)S(1)}, bf16[128,1024]{1,0:T(8,128)(2,1)S(1)}, u32[]{:S(2)}, u32[]{:S(2)}) collective-permute-start(bf16[128,1024]{1,0:T(8,128)(2,1)S(1)} %pad_maximum_fusion.refs_0_.refs_8_), channel_id=1, source_target_pairs={{0,4},{1,5},{2,6},{3,7},{4,0},{5,1},{6,2},{7,3},{8,12},{9,13},{10,... | collective-permute-start | bytes 786440 | tf_op jit(solution)/shard_map/ppermute | solution.py:115
  41.6 11.0 %collective-permute-start.12 = (bf16[128,1024]{1,0:T(8,128)(2,1)S(1)}, bf16[128,1024]{1,0:T(8,128)(2,1)}, u32[]{:S(2)}, u32[]{:S(2)}) collective-permute-start(bf16[128,1024]{1,0:T(8,128)(2,1)S(1)} %collective-permute-done.7.refs_2_.refs_10_), channel_id=1, source_target_pairs={{0,2},{1,3},{2,0},{3,1},{4,6},{5,7},{6,4},{7,5},{8,10},{9,11},{10,... | collective-permute-start | bytes 786440 | tf_op jit(solution)/shard_map/ppermute | solution.py:115
  43.1 25.5 %collective-permute-start.14 = (bf16[128,1024]{1,0:T(8,128)(2,1)S(1)}, bf16[128,1024]{1,0:T(8,128)(2,1)S(1)}, u32[]{:S(2)}, u32[]{:S(2)}) collective-permute-start(bf16[128,1024]{1,0:T(8,128)(2,1)S(1)} %collective-permute-done.7.refs_2_.refs_10_), channel_id=1, source_target_pairs={{0,4},{1,5},{2,6},{3,7},{4,0},{5,1},{6,2},{7,3},{8,12},{9,13},{10,... | collective-permute-start | bytes 786440 | tf_op jit(solution)/shard_map/ppermute | solution.py:115
  52.6 13.8 %collective-permute-start.15 = (bf16[128,1024]{1,0:T(8,128)(2,1)S(1)}, bf16[128,1024]{1,0:T(8,128)(2,1)S(1)}, u32[]{:S(2)}, u32[]{:S(2)}) collective-permute-start(bf16[128,1024]{1,0:T(8,128)(2,1)S(1)} %collective-permute-done.11.refs_1_.refs_9_), channel_id=1, source_target_pairs={{0,2},{1,3},{2,0},{3,1},{4,6},{5,7},{6,4},{7,5},{8,10},{9,11},{10,... | collective-permute-start | bytes 786440 | tf_op jit(solution)/shard_map/ppermute | solution.py:115
  54.1 12.3 %collective-permute-start.16 = (bf16[128,1024]{1,0:T(8,128)(2,1)}, bf16[128,1024]{1,0:T(8,128)(2,1)S(1)}, u32[]{:S(2)}, u32[]{:S(2)}) collective-permute-start(bf16[128,1024]{1,0:T(8,128)(2,1)} %collective-permute-done.12.refs_6_.refs_14_), channel_id=1, source_target_pairs={{0,4},{1,5},{2,6},{3,7},{4,0},{5,1},{6,2},{7,3},{8,12},{9,13},{10,... | collective-permute-start | bytes 786440 | tf_op jit(solution)/shard_map/ppermute | solution.py:115
  66.4 14.9 %collective-permute-start.18 = (bf16[128,1024]{1,0:T(8,128)(2,1)}, bf16[128,1024]{1,0:T(8,128)(2,1)S(1)}, u32[]{:S(2)}, u32[]{:S(2)}) collective-permute-start(bf16[128,1024]{1,0:T(8,128)(2,1)} %get-tuple-element.130), channel_id=1, source_target_pairs={{0,2},{1,3},{2,0},{3,1},{4,6},{5,7},{6,4},{7,5},{8,10},{9,11},{10,... | collective-permute-start | bytes 786440 | tf_op jit(solution)/shard_map/ppermute | solution.py:115
  67.7 13.6 %collective-permute-start.17 = (bf16[256,1024]{1,0:T(8,128)(2,1)}, bf16[256,1024]{1,0:T(8,128)(2,1)S(1)}, u32[]{:S(2)}, u32[]{:S(2)}) collective-permute-start(bf16[256,1024]{1,0:T(8,128)(2,1)} %get-tuple-element.129), channel_id=1, source_target_pairs={{0,4},{1,5},{2,6},{3,7},{4,0},{5,1},{6,2},{7,3},{8,12},{9,13},{10,... | collective-permute-start | bytes 1572872 | tf_op jit(solution)/shard_map/ppermute | solution.py:115
  81.5 13.8 %collective-permute-start.19 = (bf16[288,1024]{1,0:T(8,128)(2,1)}, bf16[288,1024]{1,0:T(8,128)(2,1)S(1)}, u32[]{:S(2)}, u32[]{:S(2)}) collective-permute-start(bf16[288,1024]{1,0:T(8,128)(2,1)} %get-tuple-element.146), channel_id=1, source_target_pairs={{0,4},{1,5},{2,6},{3,7},{4,0},{5,1},{6,2},{7,3},{8,12},{9,13},{10,... | collective-permute-start | bytes 1769480 | tf_op jit(solution)/shard_map/ppermute | solution.py:115
  82.7 9.5 %collective-permute-start.20 = (bf16[128,1024]{1,0:T(8,128)(2,1)S(1)}, bf16[128,1024]{1,0:T(8,128)(2,1)S(1)}, u32[]{:S(2)}, u32[]{:S(2)}) collective-permute-start(bf16[128,1024]{1,0:T(8,128)(2,1)S(1)} %add_convert_fusion.6), channel_id=1, source_target_pairs={{0,2},{1,3},{2,0},{3,1},{4,6},{5,7},{6,4},{7,5},{8,10},{9,11},{10,... | collective-permute-start | bytes 786440 | tf_op jit(solution)/shard_map/ppermute | solution.py:115
  83.5 11.7 %collective-permute-start.21 = (bf16[144,1024]{1,0:T(8,128)(2,1)}, bf16[144,1024]{1,0:T(8,128)(2,1)S(1)}, u32[]{:S(2)}, u32[]{:S(2)}) collective-permute-start(bf16[144,1024]{1,0:T(8,128)(2,1)} %get-tuple-element.148), channel_id=1, source_target_pairs={{0,2},{1,3},{2,0},{3,1},{4,6},{5,7},{6,4},{7,5},{8,10},{9,11},{10,... | collective-permute-start | bytes 884744 | tf_op jit(solution)/shard_map/ppermute | solution.py:115
  95.3 10.1 %collective-permute-start.23 = (bf16[1536,1024]{1,0:T(8,128)(2,1)}, bf16[1536,1024]{1,0:T(8,128)(2,1)S(1)}, u32[]{:S(2)}, u32[]{:S(2)}) collective-permute-start(bf16[1536,1024]{1,0:T(8,128)(2,1)} %shard_map.120), channel_id=1, source_target_pairs={{0,1},{1,0},{2,3},{3,2},{4,5},{5,4},{6,7},{7,6},{8,9},{9,8},{10,11... | collective-permute-start | bytes 9437192 | tf_op jit(solution)/shard_map/ppermute | solution.py:115
  95.4 9.9 %collective-permute-start.22 = (bf16[144,1024]{1,0:T(8,128)(2,1)S(1)}, bf16[144,1024]{1,0:T(8,128)(2,1)S(1)}, u32[]{:S(2)}, u32[]{:S(2)}) collective-permute-start(bf16[144,1024]{1,0:T(8,128)(2,1)S(1)} %add_convert_fusion.1), channel_id=1, source_target_pairs={{0,2},{1,3},{2,0},{3,1},{4,6},{5,7},{6,4},{7,5},{8,10},{9,11},{10,... | collective-permute-start | bytes 884744 | tf_op jit(solution)/shard_map/ppermute | solution.py:115
  97.1 16.2 %collective-permute-start.28 = (bf16[128,1024]{1,0:T(8,128)(2,1)S(1)}, bf16[128,1024]{1,0:T(8,128)(2,1)S(1)}, u32[]{:S(2)}, u32[]{:S(2)}) collective-permute-start(bf16[128,1024]{1,0:T(8,128)(2,1)S(1)} %add_convert_fusion.4), channel_id=1, source_target_pairs={{0,8},{1,9},{2,10},{3,11},{4,12},{5,13},{6,14},{7,15},{8,0},{9,1},... | collective-permute-start | bytes 786440 | tf_op jit(solution)/shard_map/ppermute | solution.py:115
  98.9 23.5 %collective-permute-start.27 = (bf16[128,1024]{1,0:T(8,128)(2,1)S(1)}, bf16[128,1024]{1,0:T(8,128)(2,1)S(1)}, u32[]{:S(2)}, u32[]{:S(2)}) collective-permute-start(bf16[128,1024]{1,0:T(8,128)(2,1)S(1)} %copy-done.28), channel_id=1, source_target_pairs={{0,2},{1,3},{2,0},{3,1},{4,6},{5,7},{6,4},{7,5},{8,10},{9,11},{10,... | collective-permute-start | bytes 786440 | tf_op jit(solution)/shard_map/ppermute | solution.py:115
  99.8 22.5 %collective-permute-start.29 = (bf16[128,1024]{1,0:T(8,128)(2,1)S(1)}, bf16[128,1024]{1,0:T(8,128)(2,1)S(1)}, u32[]{:S(2)}, u32[]{:S(2)}) collective-permute-start(bf16[128,1024]{1,0:T(8,128)(2,1)S(1)} %add_convert_fusion.5), channel_id=1, source_target_pairs={{0,4},{1,5},{2,6},{3,7},{4,0},{5,1},{6,2},{7,3},{8,12},{9,13},{10,... | collective-permute-start | bytes 786440 | tf_op jit(solution)/shard_map/ppermute | solution.py:115
  105.5 19.3 %collective-permute-start.24 = (bf16[144,1024]{1,0:T(8,128)(2,1)S(1)}, bf16[144,1024]{1,0:T(8,128)(2,1)S(1)}, u32[]{:S(2)}, u32[]{:S(2)}) collective-permute-start(bf16[144,1024]{1,0:T(8,128)(2,1)S(1)} %add_convert_fusion), channel_id=1, source_target_pairs={{0,8},{1,9},{2,10},{3,11},{4,12},{5,13},{6,14},{7,15},{8,0},{9,1},... | collective-permute-start | bytes 884744 | tf_op jit(solution)/shard_map/ppermute | solution.py:115
  107.7 17.8 %collective-permute-start.25 = (bf16[144,1024]{1,0:T(8,128)(2,1)S(1)}, bf16[144,1024]{1,0:T(8,128)(2,1)S(1)}, u32[]{:S(2)}, u32[]{:S(2)}) collective-permute-start(bf16[144,1024]{1,0:T(8,128)(2,1)S(1)} %add_convert_fusion.2), channel_id=1, source_target_pairs={{0,4},{1,5},{2,6},{3,7},{4,0},{5,1},{6,2},{7,3},{8,12},{9,13},{10,... | collective-permute-start | bytes 884744 | tf_op jit(solution)/shard_map/ppermute | solution.py:115
  113.3 12.1 %collective-permute-start.26 = (bf16[144,1024]{1,0:T(8,128)(2,1)S(1)}, bf16[144,1024]{1,0:T(8,128)(2,1)S(1)}, u32[]{:S(2)}, u32[]{:S(2)}) collective-permute-start(bf16[144,1024]{1,0:T(8,128)(2,1)S(1)} %copy-done.27), channel_id=1, source_target_pairs={{0,2},{1,3},{2,0},{3,1},{4,6},{5,7},{6,4},{7,5},{8,10},{9,11},{10,... | collective-permute-start | bytes 884744 | tf_op jit(solution)/shard_map/ppermute | solution.py:115
  (27 other events, 415.9 us)

commit v14 on v13

--- a/solution.py
+++ b/solution.py
@@ -334,7 +334,7 @@
     return outs[: len(layout)], outs[len(layout) :]
 
 
-def weight_grads(expert, blocks, factors, away=None):
+def weight_grads(expert, blocks, factors, away=None, sums=()):
     bf16 = jnp.bfloat16
     parts, count, width = len(blocks), len(blocks[0]), blocks[0][0].shape[1]
     each = factors[0][0].shape[0]
@@ -344,9 +344,11 @@
     def body(*refs):
         b_refs, refs = refs[: parts * count], refs[parts * count :]
         f_refs, refs = refs[: 2 * parts], refs[2 * parts :]
-        away_refs, out_refs, refs = refs[:extra], refs[extra : 3 * extra + 1], refs[3 * extra + 1 :]
+        away_refs, sum_refs, refs = refs[:extra], refs[extra : extra + len(sums)], refs[extra + len(sums) :]
+        out_refs, refs = refs[: len(outs)], refs[len(outs) :]
         x_buf, c_buf, weighted_buf, factor_buf, *bufs, sems = refs
-        away_bufs, out_bufs = bufs[:extra], bufs[extra:]
+        away_bufs, out_bufs = bufs[:extra], bufs[extra : 3 * extra + 1]
+        sum_bufs = bufs[3 * extra + 1 :]
         fetch = Fetch(sems)
         names = range(parts * count)
         for i in names:
@@ -365,6 +367,8 @@
         for i in names:
             at = pl.ds(i * tok_count, tok_count)
             fetch.start(("c", i), b_refs[i].at[pl.ds(tok_count, tok_count)], c_buf.at[at])
+        for i, ref in enumerate(sum_refs):
+            fetch.start(("sum", i), ref, sum_bufs[i])
         fetch.wait(*[("x", i) for i in names], *[("f", p) for p in range(parts)])
         for number in range(3):
             if number < 2:
@@ -389,6 +393,13 @@
             if not extra and number:
                 at = pl.ds(into.start, into.stop - into.start)
                 fetch.start(("out", number), out_bufs[0].at[at], out_refs[0].at[at])
+        if extra:
+            fetch.wait(*[("sum", i) for i in range(len(sums))])
+            total = sum(buf[...].astype(jnp.float32) for buf in sum_bufs[: len(sums)])
+            sum_bufs[-1][...] = total.astype(bf16)
+            for i, ref in enumerate(out_refs[3:]):
+                half = sum_bufs[-1].at[pl.ds(i * tok_count, tok_count)]
+                fetch.start(("half", i), half, ref.at[pl.ds(0, tok_count)])
         fetch.wait_all()
 
     flops = 6 * every * width * units
@@ -400,10 +411,11 @@
         outs = [packed]
         scratch += [pltpu.VMEM(packed.shape, bf16)]
     else:
-        operands += (away,)
+        operands += (away, *sums)
         outs = [shape(width, units, bf16)] * 2 + [shape(units, width, bf16)]
-        scratch += [pltpu.VMEM(v.shape, bf16) for v in (packed, *outs)]
-    copies = 2 * parts * count + 2 * parts + 1 + 2 * -(-width // units) + 1
+        scratch += [pltpu.VMEM(v.shape, bf16) for v in (packed, *outs, *sums, sums[0])]
+        outs += [shape(*sums[0].shape, bf16)] * 2
+    copies = 2 * parts * count + 2 * parts + 1 + 2 * -(-width // units) + 1 + len(sums) + 2
     outs = kernel(body, outs, scratch, copies, flops, *operands)
     return outs if extra else outs[0]
 
@@ -463,13 +475,12 @@
     p2 = narrow(added(p2, r73[size:]) + r6.astype(f32))
     p2, p1, p4, away = fence(p2, p1, p4, away)
     p2, p1, p4 = swap(p2, FAR), swap(p1, NEAR), swap(p4, SIDE)
-    grad_w = weight_grads(0, (a, b), factors, away)
-    p2, p1, p4, q4, q2, q1, grad_w = fence(p2, p1, p4, q4, q2, q1, grad_w)
-
-    q = added(q0, q4) + added(q1, q2)
+    *grad_w, combined, grad_latent = weight_grads(0, (a, b), factors, away, (q0, q4, q1, q2))
+    p2, p1, p4, combined, grad_latent = fence(p2, p1, p4, combined, grad_latent)
+
     p = added(p0, p4) + added(p1, p2)
-    combined = narrow(jnp.concatenate([q[:mid], p[:mid]], axis=0))
-    grad_latent = narrow(jnp.concatenate([q[mid : 2 * mid], p[mid : 2 * mid]], axis=0))
+    combined = lax.dynamic_update_slice(combined, narrow(p[:mid]), (mid, 0))
+    grad_latent = lax.dynamic_update_slice(grad_latent, narrow(p[mid : 2 * mid]), (mid, 0))
     inner = p[2 * mid :].reshape(-1, devices_ep, tok_count)[:3].sum(axis=0)
     grad_combine = jnp.sum(jnp.where(chosen, inner[:, :, None], 0.0), axis=0)
     return (combined, grad_latent, grad_combine, *[v[None] for v in grad_w])

time: 128 us -> 127 us (level)
  other arithmetic: 3.76 us -> 2.15 us
  local copies, waits for them, and re-layouts: 3.01 us -> 4.49 us
    concatenate x2 -> x0, other arithmetic: 1.44 us -> none  [the longest x1 0.72 us: paired(): jnp.concatenate([q[mid:2 * mid], p[mid:2 * mid]], axis=0)]
    unnamed x58 -> x62, local copies, waits for them, and re-layouts: 1.79 us -> 2.59 us
where the time goes in v14:
time: 127 us
  waiting for transfers between devices  45.8 us (36%)
  Pallas kernels  39.5 us (31%)
  starting transfers between devices  33.9 us (27%)
  local copies, waits for them, and re-layouts  4.49 us (4%)
  other arithmetic  2.15 us (2%)
    ppermute x30, waiting for transfers between devices, swap(): return lax.ppermute(value, 'ep', pairs)  45.8 us
    pallas_call x4, Pallas kernels, kernel(): pl.pallas_call(body, out_shape=outs, in_specs=in_specs, out_specs=[pl.Blo...  39.5 us
    ppermute x30, starting transfers between devices, swap(): return lax.ppermute(value, 'ep', pairs)  33.9 us
    unnamed x62, local copies, waits for them, and re-layouts  2.59 us
  transfers between devices with their start and end apart: 30, of which 12 were waited for; matrix products, arithmetic and copies ran while one was open for 2% of the time, Pallas kernels for 31%

profile of v14, /device:TPU:0, one launch (start us, length us, event | category | flops | bytes accessed | tf_op | source)
XLA Modules:
  0.0 126.9 jit_solution(15083112097373330190)
XLA Ops:
  2.0 1.1 fusion.4
  3.6 1.0 copy-done.27
  5.0 3.7 %collective-permute-start.3 = (bf16[144,1024]{1,0:T(8,128)(2,1)S(1)}, bf16[144,1024]{1,0:T(8,128)(2,1)S(1)}, u32[]{:S(2)}, u32[]{:S(2)}) collective-permute-start(bf16[144,1024]{1,0:T(8,128)(2,1)S(1)} %fusion.1.refs_0_), channel_id=1, source_target_pairs={{0,8},{1,9},{2,10},{3,11},{4,12},{5,13},{6,14},{7,15},{8,0},{9,1},... | collective-permute-start | bytes 884744 | tf_op jit(solution)/shard_map/ppermute | solution.py:115
  8.7 1.5 %collective-permute-start.2 = (bf16[144,1024]{1,0:T(8,128)(2,1)S(1)}, bf16[144,1024]{1,0:T(8,128)(2,1)S(1)}, u32[]{:S(2)}, u32[]{:S(2)}) collective-permute-start(bf16[144,1024]{1,0:T(8,128)(2,1)S(1)} %fusion.1.refs_0_), channel_id=1, source_target_pairs={{0,2},{1,3},{2,0},{3,1},{4,6},{5,7},{6,4},{7,5},{8,10},{9,11},{10,... | collective-permute-start | bytes 884744 | tf_op jit(solution)/shard_map/ppermute | solution.py:115
  10.2 1.6 %collective-permute-start.1 = (bf16[144,1024]{1,0:T(8,128)(2,1)S(1)}, bf16[144,1024]{1,0:T(8,128)(2,1)S(1)}, u32[]{:S(2)}, u32[]{:S(2)}) collective-permute-start(bf16[144,1024]{1,0:T(8,128)(2,1)S(1)} %fusion.1.refs_0_), channel_id=1, source_target_pairs={{0,4},{1,5},{2,6},{3,7},{4,0},{5,1},{6,2},{7,3},{8,12},{9,13},{10,... | collective-permute-start | bytes 884744 | tf_op jit(solution)/shard_map/ppermute | solution.py:115
  12.3 11.0 %collective-permute-done.4.refs_4_.refs_12_ = bf16[128,1024]{1,0:T(8,128)(2,1)S(1)} collective-permute-done((bf16[128,1024]{1,0:T(8,128)(2,1)S(1)}, bf16[128,1024]{1,0:T(8,128)(2,1)S(1)}, u32[]{:S(2)}, u32[]{:S(2)}) %collective-permute-start.4) | collective-permute-done | bytes 262176 | tf_op jit(solution)/shard_map/ppermute | solution.py:115
  24.2 1.0 collective-permute-start.6
  25.1 1.5 %collective-permute-start.10 = (bf16[144,1024]{1,0:T(8,128)(2,1)S(1)}, bf16[144,1024]{1,0:T(8,128)(2,1)S(1)}, u32[]{:S(2)}, u32[]{:S(2)}) collective-permute-start(bf16[144,1024]{1,0:T(8,128)(2,1)S(1)} %collective-permute-done.1.refs_1_), channel_id=1, source_target_pairs={{0,2},{1,3},{2,0},{3,1},{4,6},{5,7},{6,4},{7,5},{8,10},{9,11},{10,... | collective-permute-start | bytes 884744 | tf_op jit(solution)/shard_map/ppermute | solution.py:115
  27.2 2.2 %collective-permute-start.9 = (bf16[128,1024]{1,0:T(8,128)(2,1)S(1)}, bf16[128,1024]{1,0:T(8,128)(2,1)S(1)}, u32[]{:S(2)}, u32[]{:S(2)}) collective-permute-start(bf16[128,1024]{1,0:T(8,128)(2,1)S(1)} %pad_maximum_fusion.refs_0_.refs_8_), channel_id=1, source_target_pairs={{0,8},{1,9},{2,10},{3,11},{4,12},{5,13},{6,14},{7,15},{8,0},{9,1},... | collective-permute-start | bytes 786440 | tf_op jit(solution)/shard_map/ppermute | solution.py:115
  29.3 8.4 %collective-permute-done.6.refs_3_ = bf16[144,1024]{1,0:T(8,128)(2,1)S(1)} collective-permute-done((bf16[144,1024]{1,0:T(8,128)(2,1)S(1)}, bf16[144,1024]{1,0:T(8,128)(2,1)S(1)}, u32[]{:S(2)}, u32[]{:S(2)}) %collective-permute-start.6) | collective-permute-done | bytes 294944 | tf_op jit(solution)/shard_map/ppermute | solution.py:115
  38.1 3.4 %collective-permute-done.9.refs_2_.refs_10_ = bf16[128,1024]{1,0:T(8,128)(2,1)S(1)} collective-permute-done((bf16[128,1024]{1,0:T(8,128)(2,1)S(1)}, bf16[128,1024]{1,0:T(8,128)(2,1)S(1)}, u32[]{:S(2)}, u32[]{:S(2)}) %collective-permute-start.9) | collective-permute-done | bytes 262176 | tf_op jit(solution)/shard_map/ppermute | solution.py:115
  41.6 1.5 %collective-permute-start.12 = (bf16[128,1024]{1,0:T(8,128)(2,1)S(1)}, bf16[128,1024]{1,0:T(8,128)(2,1)}, u32[]{:S(2)}, u32[]{:S(2)}) collective-permute-start(bf16[128,1024]{1,0:T(8,128)(2,1)S(1)} %collective-permute-done.9.refs_2_.refs_10_), channel_id=1, source_target_pairs={{0,2},{1,3},{2,0},{3,1},{4,6},{5,7},{6,4},{7,5},{8,10},{9,11},{10,... | collective-permute-start | bytes 786440 | tf_op jit(solution)/shard_map/ppermute | solution.py:115
  43.1 2.0 %collective-permute-start.13 = (bf16[128,1024]{1,0:T(8,128)(2,1)S(1)}, bf16[128,1024]{1,0:T(8,128)(2,1)S(1)}, u32[]{:S(2)}, u32[]{:S(2)}) collective-permute-start(bf16[128,1024]{1,0:T(8,128)(2,1)S(1)} %collective-permute-done.9.refs_2_.refs_10_), channel_id=1, source_target_pairs={{0,4},{1,5},{2,6},{3,7},{4,0},{5,1},{6,2},{7,3},{8,12},{9,13},{10,... | collective-permute-start | bytes 786440 | tf_op jit(solution)/shard_map/ppermute | solution.py:115
  45.1 5.6 %collective-permute-done.8.refs_1_.refs_9_ = bf16[128,1024]{1,0:T(8,128)(2,1)S(1)} collective-permute-done((bf16[128,1024]{1,0:T(8,128)(2,1)S(1)}, bf16[128,1024]{1,0:T(8,128)(2,1)S(1)}, u32[]{:S(2)}, u32[]{:S(2)}) %collective-permute-start.8) | collective-permute-done | bytes 262176 | tf_op jit(solution)/shard_map/ppermute | solution.py:115
  50.8 1.8 %collective-permute-done.12.refs_6_.refs_14_ = bf16[128,1024]{1,0:T(8,128)(2,1)} collective-permute-done((bf16[128,1024]{1,0:T(8,128)(2,1)S(1)}, bf16[128,1024]{1,0:T(8,128)(2,1)}, u32[]{:S(2)}, u32[]{:S(2)}) %collective-permute-start.12) | collective-permute-done | bytes 262176 | tf_op jit(solution)/shard_map/ppermute | solution.py:115
  52.6 1.5 %collective-permute-start.15 = (bf16[128,1024]{1,0:T(8,128)(2,1)S(1)}, bf16[128,1024]{1,0:T(8,128)(2,1)S(1)}, u32[]{:S(2)}, u32[]{:S(2)}) collective-permute-start(bf16[128,1024]{1,0:T(8,128)(2,1)S(1)} %collective-permute-done.8.refs_1_.refs_9_), channel_id=1, source_target_pairs={{0,2},{1,3},{2,0},{3,1},{4,6},{5,7},{6,4},{7,5},{8,10},{9,11},{10,... | collective-permute-start | bytes 786440 | tf_op jit(solution)/shard_map/ppermute | solution.py:115
  54.6 11.6 %shard_map.118 = (bf16[128,1024]{1,0:T(8,128)(2,1)}, bf16[128,1024]{1,0:T(8,128)(2,1)}, bf16[128,1024]{1,0:T(8,128)(2,1)}, bf16[128,1024]{1,0:T(8,128)(2,1)}, bf...) custom-call(s32[1]{0:T(128)} %bitcast.me_ref, ...), custom_call_target="tpu_custom_call" | custom-call | flops 6442450944 | bytes 14024704 | tf_op jit(solution)/shard_map/pallas_call | solution.py:162
  66.3 1.3 %collective-permute-start.18 = (bf16[128,1024]{1,0:T(8,128)(2,1)}, bf16[128,1024]{1,0:T(8,128)(2,1)S(1)}, u32[]{:S(2)}, u32[]{:S(2)}) collective-permute-start(bf16[128,1024]{1,0:T(8,128)(2,1)} %get-tuple-element.127), channel_id=1, source_target_pairs={{0,2},{1,3},{2,0},{3,1},{4,6},{5,7},{6,4},{7,5},{8,10},{9,11},{10,... | collective-permute-start | bytes 786440 | tf_op jit(solution)/shard_map/ppermute | solution.py:115
  69.2 12.0 %shard_map.119 = (bf16[144,1024]{1,0:T(8,128)(2,1)}, bf16[144,1024]{1,0:T(8,128)(2,1)}, bf16[144,1024]{1,0:T(8,128)(2,1)}, bf16[144,1024]{1,0:T(8,128)(2,1)}, bf...) custom-call(s32[1]{0:T(128)} %bitcast.me_ref, ...), custom_call_target="tpu_custom_call" | custom-call | flops 6442450944 | bytes 14024704 | tf_op jit(solution)/shard_map/pallas_call | solution.py:162
  81.4 1.2 collective-permute-start.19
  83.4 1.2 collective-permute-start.21
  84.6 7.4 %shard_map.120 = bf16[1536,1024]{1,0:T(8,128)(2,1)} custom-call(bf16[144,1024]{1,0:T(8,128)(2,1)} %copy-done.1, bf16[144,1024]{1,0:T(8,128)(2,1)} %copy-done.5, bf16[144,1024]{1,0:T(8,128)(2,1)} %copy-done.3, bf16[144,1024]{1,0:T(8,128)(2,1)} %copy-done.6, bf16[144,1024]{1,0:T(8,128)(2,1)} %copy-done.4, bf16[144,1024]{1,0:T(8,128)(2,1)} %copy-done.7, ...), custom_call_target="tpu_custom_call" | custom-call | flops 3221225472 | bytes 13893632 | tf_op jit(solution)/shard_map/pallas_call | solution.py:162
  92.1 3.0 %collective-permute-done.21 = bf16[144,1024]{1,0:T(8,128)(2,1)S(1)} collective-permute-done((bf16[144,1024]{1,0:T(8,128)(2,1)}, bf16[144,1024]{1,0:T(8,128)(2,1)S(1)}, u32[]{:S(2)}, u32[]{:S(2)}) %collective-permute-start.21) | collective-permute-done | bytes 294944 | tf_op jit(solution)/shard_map/ppermute | solution.py:115
  95.3 1.5 %collective-permute-start.22 = (bf16[144,1024]{1,0:T(8,128)(2,1)S(1)}, bf16[144,1024]{1,0:T(8,128)(2,1)S(1)}, u32[]{:S(2)}, u32[]{:S(2)}) collective-permute-start(bf16[144,1024]{1,0:T(8,128)(2,1)S(1)} %add_convert_fusion.1), channel_id=1, source_target_pairs={{0,2},{1,3},{2,0},{3,1},{4,6},{5,7},{6,4},{7,5},{8,10},{9,11},{10,... | collective-permute-start | bytes 884744 | tf_op jit(solution)/shard_map/ppermute | solution.py:115
  97.0 1.8 %collective-permute-start.29 = (bf16[128,1024]{1,0:T(8,128)(2,1)S(1)}, bf16[128,1024]{1,0:T(8,128)(2,1)S(1)}, u32[]{:S(2)}, u32[]{:S(2)}) collective-permute-start(bf16[128,1024]{1,0:T(8,128)(2,1)S(1)} %add_convert_fusion.3), channel_id=1, source_target_pairs={{0,8},{1,9},{2,10},{3,11},{4,12},{5,13},{6,14},{7,15},{8,0},{9,1},... | collective-permute-start | bytes 786440 | tf_op jit(solution)/shard_map/ppermute | solution.py:115
  98.8 0.9 collective-permute-start.27
  99.7 0.9 collective-permute-start.28
  100.7 4.5 %collective-permute-done.22 = bf16[144,1024]{1,0:T(8,128)(2,1)S(1)} collective-permute-done((bf16[144,1024]{1,0:T(8,128)(2,1)S(1)}, bf16[144,1024]{1,0:T(8,128)(2,1)S(1)}, u32[]{:S(2)}, u32[]{:S(2)}) %collective-permute-start.22) | collective-permute-done | bytes 294944 | tf_op jit(solution)/shard_map/ppermute | solution.py:115
  105.4 2.2 %collective-permute-start.24 = (bf16[144,1024]{1,0:T(8,128)(2,1)S(1)}, bf16[144,1024]{1,0:T(8,128)(2,1)S(1)}, u32[]{:S(2)}, u32[]{:S(2)}) collective-permute-start(bf16[144,1024]{1,0:T(8,128)(2,1)S(1)} %add_convert_fusion), channel_id=1, source_target_pairs={{0,8},{1,9},{2,10},{3,11},{4,12},{5,13},{6,14},{7,15},{8,0},{9,1},... | collective-permute-start | bytes 884744 | tf_op jit(solution)/shard_map/ppermute | solution.py:115
  108.5 4.7 %collective-permute-done.29.refs_24_ = bf16[128,1024]{1,0:T(8,128)(2,1)S(1)} collective-permute-done((bf16[128,1024]{1,0:T(8,128)(2,1)S(1)}, bf16[128,1024]{1,0:T(8,128)(2,1)S(1)}, u32[]{:S(2)}, u32[]{:S(2)}) %collective-permute-start.29) | collective-permute-done | bytes 262176 | tf_op jit(solution)/shard_map/ppermute | solution.py:115
  114.8 8.5 %shard_map.121 = (bf16[1024,512]{1,0:T(8,128)(2,1)}, bf16[1024,512]{1,0:T(8,128)(2,1)}, bf16[512,1024]{1,0:T(8,128)(2,1)}, bf16[128,1024]{1,0:T(8,128)(2,1)}, bf16[128,1024]{1,0:T(8,128)(2,1)}) custom-call(bf16[144,1024]{1,0:T(8,128)(2,1)} %copy-done.1, bf16[144,1024]{1,0:T(8,128)(2,1)} %copy-done.5, bf16[144,1024]{1,0:T(8,128)(2,1)} %copy-done.3, ...), custom_call_target="tpu_custom_call" | custom-call | flops 3221225472 | bytes 18612224 | tf_op jit(solution)/shard_map/pallas_call | solution.py:162
  123.3 1.4 %collective-permute-done.24 = bf16[144,1024]{1,0:T(8,128)(2,1)S(1)} collective-permute-done((bf16[144,1024]{1,0:T(8,128)(2,1)S(1)}, bf16[144,1024]{1,0:T(8,128)(2,1)S(1)}, u32[]{:S(2)}, u32[]{:S(2)}) %collective-permute-start.24) | collective-permute-done | bytes 294944 | tf_op jit(solution)/shard_map/ppermute | solution.py:115
  (114 shorter events, 12.7 us)
Async XLA Ops:
  0.6 3.0 %collective-permute-start = (bf16[1024,512]{1,0:T(8,128)(2,1)}, bf16[1024,512]{1,0:T(8,128)(2,1)S(1)}, u32[]{:S(2)}, u32[]{:S(2)}) collective-permute-start(bf16[1024,512]{1,0:T(8,128)(2,1)} %bitcast.20), channel_id=1, source_target_pairs={{0,1},{1,0},{2,3},{3,2},{4,5},{5,4},{6,7},{7,6},{8,9},{9,8},{10,11... | collective-permute-start | bytes 3145736 | tf_op jit(solution)/shard_map/ppermute | solution.py:115
  3.1 63.1 %copy-start.2 = (bf16[128,1024]{1,0:T(8,128)(2,1)}, bf16[128,1024]{1,0:T(8,128)(2,1)S(1)}, u32[]{:S(2)}) copy-start(bf16[128,1024]{1,0:T(8,128)(2,1)S(1)} %pad_maximum_fusion.refs_0_.refs_8_) | copy-start | bytes 786436
  3.2 51.4 %copy-start.1 = (bf16[144,1024]{1,0:T(8,128)(2,1)}, bf16[144,1024]{1,0:T(8,128)(2,1)S(1)}, u32[]{:S(2)}) copy-start(bf16[144,1024]{1,0:T(8,128)(2,1)S(1)} %fusion.1.refs_0_) | copy-start | bytes 884740
  4.6 19.5 %collective-permute-start.5 = (bf16[1024,512]{1,0:T(8,128)(2,1)}, bf16[1024,512]{1,0:T(8,128)(2,1)S(1)}, u32[]{:S(2)}, u32[]{:S(2)}) collective-permute-start(bf16[1024,512]{1,0:T(8,128)(2,1)} %bitcast.23), channel_id=1, source_target_pairs={{0,1},{1,0},{2,3},{3,2},{4,5},{5,4},{6,7},{7,6},{8,9},{9,8},{10,11... | collective-permute-start | bytes 3145736 | tf_op jit(solution)/shard_map/ppermute | solution.py:115
  5.0 18.4 %collective-permute-start.3 = (bf16[144,1024]{1,0:T(8,128)(2,1)S(1)}, bf16[144,1024]{1,0:T(8,128)(2,1)S(1)}, u32[]{:S(2)}, u32[]{:S(2)}) collective-permute-start(bf16[144,1024]{1,0:T(8,128)(2,1)S(1)} %fusion.1.refs_0_), channel_id=1, source_target_pairs={{0,8},{1,9},{2,10},{3,11},{4,12},{5,13},{6,14},{7,15},{8,0},{9,1},... | collective-permute-start | bytes 884744 | tf_op jit(solution)/shard_map/ppermute | solution.py:115
  8.7 14.6 %collective-permute-start.2 = (bf16[144,1024]{1,0:T(8,128)(2,1)S(1)}, bf16[144,1024]{1,0:T(8,128)(2,1)S(1)}, u32[]{:S(2)}, u32[]{:S(2)}) collective-permute-start(bf16[144,1024]{1,0:T(8,128)(2,1)S(1)} %fusion.1.refs_0_), channel_id=1, source_target_pairs={{0,2},{1,3},{2,0},{3,1},{4,6},{5,7},{6,4},{7,5},{8,10},{9,11},{10,... | collective-permute-start | bytes 884744 | tf_op jit(solution)/shard_map/ppermute | solution.py:115
  10.2 13.9 %collective-permute-start.1 = (bf16[144,1024]{1,0:T(8,128)(2,1)S(1)}, bf16[144,1024]{1,0:T(8,128)(2,1)S(1)}, u32[]{:S(2)}, u32[]{:S(2)}) collective-permute-start(bf16[144,1024]{1,0:T(8,128)(2,1)S(1)} %fusion.1.refs_0_), channel_id=1, source_target_pairs={{0,4},{1,5},{2,6},{3,7},{4,0},{5,1},{6,2},{7,3},{8,12},{9,13},{10,... | collective-permute-start | bytes 884744 | tf_op jit(solution)/shard_map/ppermute | solution.py:115
  11.8 11.5 %collective-permute-start.4 = (bf16[128,1024]{1,0:T(8,128)(2,1)S(1)}, bf16[128,1024]{1,0:T(8,128)(2,1)S(1)}, u32[]{:S(2)}, u32[]{:S(2)}) collective-permute-start(bf16[128,1024]{1,0:T(8,128)(2,1)S(1)} %pad_maximum_fusion.refs_0_.refs_8_), channel_id=1, source_target_pairs={{0,2},{1,3},{2,0},{3,1},{4,6},{5,7},{6,4},{7,5},{8,10},{9,11},{10,... | collective-permute-start | bytes 786440 | tf_op jit(solution)/shard_map/ppermute | solution.py:115
  24.1 30.4 %collective-permute-start.14 = (bf16[512,1024]{1,0:T(8,128)(2,1)}, bf16[512,1024]{1,0:T(8,128)(2,1)}, u32[]{:S(2)}, u32[]{:S(2)}) collective-permute-start(bf16[512,1024]{1,0:T(8,128)(2,1)} %bitcast.26), channel_id=1, source_target_pairs={{0,1},{1,0},{2,3},{3,2},{4,5},{5,4},{6,7},{7,6},{8,9},{9,8},{10,11... | collective-permute-start | bytes 3145736 | tf_op jit(solution)/shard_map/ppermute | solution.py:115
  24.2 13.5 %collective-permute-start.6 = (bf16[144,1024]{1,0:T(8,128)(2,1)S(1)}, bf16[144,1024]{1,0:T(8,128)(2,1)S(1)}, u32[]{:S(2)}, u32[]{:S(2)}) collective-permute-start(bf16[144,1024]{1,0:T(8,128)(2,1)S(1)} %collective-permute-done.3.refs_2_), channel_id=1, source_target_pairs={{0,4},{1,5},{2,6},{3,7},{4,0},{5,1},{6,2},{7,3},{8,12},{9,13},{10,... | collective-permute-start | bytes 884744 | tf_op jit(solution)/shard_map/ppermute | solution.py:115
  25.1 16.4 %collective-permute-start.10 = (bf16[144,1024]{1,0:T(8,128)(2,1)S(1)}, bf16[144,1024]{1,0:T(8,128)(2,1)S(1)}, u32[]{:S(2)}, u32[]{:S(2)}) collective-permute-start(bf16[144,1024]{1,0:T(8,128)(2,1)S(1)} %collective-permute-done.1.refs_1_), channel_id=1, source_target_pairs={{0,2},{1,3},{2,0},{3,1},{4,6},{5,7},{6,4},{7,5},{8,10},{9,11},{10,... | collective-permute-start | bytes 884744 | tf_op jit(solution)/shard_map/ppermute | solution.py:115
  26.6 15.0 %collective-permute-start.11 = (bf16[144,1024]{1,0:T(8,128)(2,1)S(1)}, bf16[144,1024]{1,0:T(8,128)(2,1)S(1)}, u32[]{:S(2)}, u32[]{:S(2)}) collective-permute-start(bf16[144,1024]{1,0:T(8,128)(2,1)S(1)} %collective-permute-done.3.refs_2_), channel_id=1, source_target_pairs={{0,2},{1,3},{2,0},{3,1},{4,6},{5,7},{6,4},{7,5},{8,10},{9,11},{10,... | collective-permute-start | bytes 884744 | tf_op jit(solution)/shard_map/ppermute | solution.py:115
  27.2 14.4 %collective-permute-start.9 = (bf16[128,1024]{1,0:T(8,128)(2,1)S(1)}, bf16[128,1024]{1,0:T(8,128)(2,1)S(1)}, u32[]{:S(2)}, u32[]{:S(2)}) collective-permute-start(bf16[128,1024]{1,0:T(8,128)(2,1)S(1)} %pad_maximum_fusion.refs_0_.refs_8_), channel_id=1, source_target_pairs={{0,8},{1,9},{2,10},{3,11},{4,12},{5,13},{6,14},{7,15},{8,0},{9,1},... | collective-permute-start | bytes 786440 | tf_op jit(solution)/shard_map/ppermute | solution.py:115
  37.7 14.9 %collective-permute-start.7 = (bf16[144,1024]{1,0:T(8,128)(2,1)S(1)}, bf16[144,1024]{1,0:T(8,128)(2,1)S(1)}, u32[]{:S(2)}, u32[]{:S(2)}) collective-permute-start(bf16[144,1024]{1,0:T(8,128)(2,1)S(1)} %collective-permute-done.6.refs_3_), channel_id=1, source_target_pairs={{0,2},{1,3},{2,0},{3,1},{4,6},{5,7},{6,4},{7,5},{8,10},{9,11},{10,... | collective-permute-start | bytes 884744 | tf_op jit(solution)/shard_map/ppermute | solution.py:115
  41.6 9.2 %collective-permute-start.8 = (bf16[128,1024]{1,0:T(8,128)(2,1)S(1)}, bf16[128,1024]{1,0:T(8,128)(2,1)S(1)}, u32[]{:S(2)}, u32[]{:S(2)}) collective-permute-start(bf16[128,1024]{1,0:T(8,128)(2,1)S(1)} %pad_maximum_fusion.refs_0_.refs_8_), channel_id=1, source_target_pairs={{0,4},{1,5},{2,6},{3,7},{4,0},{5,1},{6,2},{7,3},{8,12},{9,13},{10,... | collective-permute-start | bytes 786440 | tf_op jit(solution)/shard_map/ppermute | solution.py:115
  41.6 11.0 %collective-permute-start.12 = (bf16[128,1024]{1,0:T(8,128)(2,1)S(1)}, bf16[128,1024]{1,0:T(8,128)(2,1)}, u32[]{:S(2)}, u32[]{:S(2)}) collective-permute-start(bf16[128,1024]{1,0:T(8,128)(2,1)S(1)} %collective-permute-done.9.refs_2_.refs_10_), channel_id=1, source_target_pairs={{0,2},{1,3},{2,0},{3,1},{4,6},{5,7},{6,4},{7,5},{8,10},{9,11},{10,... | collective-permute-start | bytes 786440 | tf_op jit(solution)/shard_map/ppermute | solution.py:115
  43.1 25.4 %collective-permute-start.13 = (bf16[128,1024]{1,0:T(8,128)(2,1)S(1)}, bf16[128,1024]{1,0:T(8,128)(2,1)S(1)}, u32[]{:S(2)}, u32[]{:S(2)}) collective-permute-start(bf16[128,1024]{1,0:T(8,128)(2,1)S(1)} %collective-permute-done.9.refs_2_.refs_10_), channel_id=1, source_target_pairs={{0,4},{1,5},{2,6},{3,7},{4,0},{5,1},{6,2},{7,3},{8,12},{9,13},{10,... | collective-permute-start | bytes 786440 | tf_op jit(solution)/shard_map/ppermute | solution.py:115
  52.6 13.7 %collective-permute-start.15 = (bf16[128,1024]{1,0:T(8,128)(2,1)S(1)}, bf16[128,1024]{1,0:T(8,128)(2,1)S(1)}, u32[]{:S(2)}, u32[]{:S(2)}) collective-permute-start(bf16[128,1024]{1,0:T(8,128)(2,1)S(1)} %collective-permute-done.8.refs_1_.refs_9_), channel_id=1, source_target_pairs={{0,2},{1,3},{2,0},{3,1},{4,6},{5,7},{6,4},{7,5},{8,10},{9,11},{10,... | collective-permute-start | bytes 786440 | tf_op jit(solution)/shard_map/ppermute | solution.py:115
  54.1 12.2 %collective-permute-start.16 = (bf16[128,1024]{1,0:T(8,128)(2,1)}, bf16[128,1024]{1,0:T(8,128)(2,1)S(1)}, u32[]{:S(2)}, u32[]{:S(2)}) collective-permute-start(bf16[128,1024]{1,0:T(8,128)(2,1)} %collective-permute-done.12.refs_6_.refs_14_), channel_id=1, source_target_pairs={{0,4},{1,5},{2,6},{3,7},{4,0},{5,1},{6,2},{7,3},{8,12},{9,13},{10,... | collective-permute-start | bytes 786440 | tf_op jit(solution)/shard_map/ppermute | solution.py:115
  66.3 14.9 %collective-permute-start.18 = (bf16[128,1024]{1,0:T(8,128)(2,1)}, bf16[128,1024]{1,0:T(8,128)(2,1)S(1)}, u32[]{:S(2)}, u32[]{:S(2)}) collective-permute-start(bf16[128,1024]{1,0:T(8,128)(2,1)} %get-tuple-element.127), channel_id=1, source_target_pairs={{0,2},{1,3},{2,0},{3,1},{4,6},{5,7},{6,4},{7,5},{8,10},{9,11},{10,... | collective-permute-start | bytes 786440 | tf_op jit(solution)/shard_map/ppermute | solution.py:115
  67.6 13.6 %collective-permute-start.17 = (bf16[256,1024]{1,0:T(8,128)(2,1)}, bf16[256,1024]{1,0:T(8,128)(2,1)S(1)}, u32[]{:S(2)}, u32[]{:S(2)}) collective-permute-start(bf16[256,1024]{1,0:T(8,128)(2,1)} %get-tuple-element.126), channel_id=1, source_target_pairs={{0,4},{1,5},{2,6},{3,7},{4,0},{5,1},{6,2},{7,3},{8,12},{9,13},{10,... | collective-permute-start | bytes 1572872 | tf_op jit(solution)/shard_map/ppermute | solution.py:115
  81.4 13.8 %collective-permute-start.19 = (bf16[288,1024]{1,0:T(8,128)(2,1)}, bf16[288,1024]{1,0:T(8,128)(2,1)S(1)}, u32[]{:S(2)}, u32[]{:S(2)}) collective-permute-start(bf16[288,1024]{1,0:T(8,128)(2,1)} %get-tuple-element.143), channel_id=1, source_target_pairs={{0,4},{1,5},{2,6},{3,7},{4,0},{5,1},{6,2},{7,3},{8,12},{9,13},{10,... | collective-permute-start | bytes 1769480 | tf_op jit(solution)/shard_map/ppermute | solution.py:115
  82.6 9.5 %collective-permute-start.20 = (bf16[128,1024]{1,0:T(8,128)(2,1)S(1)}, bf16[128,1024]{1,0:T(8,128)(2,1)S(1)}, u32[]{:S(2)}, u32[]{:S(2)}) collective-permute-start(bf16[128,1024]{1,0:T(8,128)(2,1)S(1)} %add_convert_fusion.5), channel_id=1, source_target_pairs={{0,2},{1,3},{2,0},{3,1},{4,6},{5,7},{6,4},{7,5},{8,10},{9,11},{10,... | collective-permute-start | bytes 786440 | tf_op jit(solution)/shard_map/ppermute | solution.py:115
  83.4 11.7 %collective-permute-start.21 = (bf16[144,1024]{1,0:T(8,128)(2,1)}, bf16[144,1024]{1,0:T(8,128)(2,1)S(1)}, u32[]{:S(2)}, u32[]{:S(2)}) collective-permute-start(bf16[144,1024]{1,0:T(8,128)(2,1)} %get-tuple-element.145), channel_id=1, source_target_pairs={{0,2},{1,3},{2,0},{3,1},{4,6},{5,7},{6,4},{7,5},{8,10},{9,11},{10,... | collective-permute-start | bytes 884744 | tf_op jit(solution)/shard_map/ppermute | solution.py:115
  95.3 10.1 %collective-permute-start.23 = (bf16[1536,1024]{1,0:T(8,128)(2,1)}, bf16[1536,1024]{1,0:T(8,128)(2,1)S(1)}, u32[]{:S(2)}, u32[]{:S(2)}) collective-permute-start(bf16[1536,1024]{1,0:T(8,128)(2,1)} %shard_map.120), channel_id=1, source_target_pairs={{0,1},{1,0},{2,3},{3,2},{4,5},{5,4},{6,7},{7,6},{8,9},{9,8},{10,11... | collective-permute-start | bytes 9437192 | tf_op jit(solution)/shard_map/ppermute | solution.py:115
  95.3 9.9 %collective-permute-start.22 = (bf16[144,1024]{1,0:T(8,128)(2,1)S(1)}, bf16[144,1024]{1,0:T(8,128)(2,1)S(1)}, u32[]{:S(2)}, u32[]{:S(2)}) collective-permute-start(bf16[144,1024]{1,0:T(8,128)(2,1)S(1)} %add_convert_fusion.1), channel_id=1, source_target_pairs={{0,2},{1,3},{2,0},{3,1},{4,6},{5,7},{6,4},{7,5},{8,10},{9,11},{10,... | collective-permute-start | bytes 884744 | tf_op jit(solution)/shard_map/ppermute | solution.py:115
  97.0 16.2 %collective-permute-start.29 = (bf16[128,1024]{1,0:T(8,128)(2,1)S(1)}, bf16[128,1024]{1,0:T(8,128)(2,1)S(1)}, u32[]{:S(2)}, u32[]{:S(2)}) collective-permute-start(bf16[128,1024]{1,0:T(8,128)(2,1)S(1)} %add_convert_fusion.3), channel_id=1, source_target_pairs={{0,8},{1,9},{2,10},{3,11},{4,12},{5,13},{6,14},{7,15},{8,0},{9,1},... | collective-permute-start | bytes 786440 | tf_op jit(solution)/shard_map/ppermute | solution.py:115
  98.8 15.2 %collective-permute-start.27 = (bf16[128,1024]{1,0:T(8,128)(2,1)S(1)}, bf16[128,1024]{1,0:T(8,128)(2,1)S(1)}, u32[]{:S(2)}, u32[]{:S(2)}) collective-permute-start(bf16[128,1024]{1,0:T(8,128)(2,1)S(1)} %copy-done.30), channel_id=1, source_target_pairs={{0,2},{1,3},{2,0},{3,1},{4,6},{5,7},{6,4},{7,5},{8,10},{9,11},{10,... | collective-permute-start | bytes 786440 | tf_op jit(solution)/shard_map/ppermute | solution.py:115
  99.7 14.2 %collective-permute-start.28 = (bf16[128,1024]{1,0:T(8,128)(2,1)S(1)}, bf16[128,1024]{1,0:T(8,128)(2,1)S(1)}, u32[]{:S(2)}, u32[]{:S(2)}) collective-permute-start(bf16[128,1024]{1,0:T(8,128)(2,1)S(1)} %add_convert_fusion.4), channel_id=1, source_target_pairs={{0,4},{1,5},{2,6},{3,7},{4,0},{5,1},{6,2},{7,3},{8,12},{9,13},{10,... | collective-permute-start | bytes 786440 | tf_op jit(solution)/shard_map/ppermute | solution.py:115
  105.4 19.3 %collective-permute-start.24 = (bf16[144,1024]{1,0:T(8,128)(2,1)S(1)}, bf16[144,1024]{1,0:T(8,128)(2,1)S(1)}, u32[]{:S(2)}, u32[]{:S(2)}) collective-permute-start(bf16[144,1024]{1,0:T(8,128)(2,1)S(1)} %add_convert_fusion), channel_id=1, source_target_pairs={{0,8},{1,9},{2,10},{3,11},{4,12},{5,13},{6,14},{7,15},{8,0},{9,1},... | collective-permute-start | bytes 884744 | tf_op jit(solution)/shard_map/ppermute | solution.py:115
  107.5 17.8 %collective-permute-start.25 = (bf16[144,1024]{1,0:T(8,128)(2,1)S(1)}, bf16[144,1024]{1,0:T(8,128)(2,1)S(1)}, u32[]{:S(2)}, u32[]{:S(2)}) collective-permute-start(bf16[144,1024]{1,0:T(8,128)(2,1)S(1)} %add_convert_fusion.2), channel_id=1, source_target_pairs={{0,4},{1,5},{2,6},{3,7},{4,0},{5,1},{6,2},{7,3},{8,12},{9,13},{10,... | collective-permute-start | bytes 884744 | tf_op jit(solution)/shard_map/ppermute | solution.py:115
  113.2 12.1 %collective-permute-start.26 = (bf16[144,1024]{1,0:T(8,128)(2,1)S(1)}, bf16[144,1024]{1,0:T(8,128)(2,1)S(1)}, u32[]{:S(2)}, u32[]{:S(2)}) collective-permute-start(bf16[144,1024]{1,0:T(8,128)(2,1)S(1)} %copy-done.29), channel_id=1, source_target_pairs={{0,2},{1,3},{2,0},{3,1},{4,6},{5,7},{6,4},{7,5},{8,10},{9,11},{10,... | collective-permute-start | bytes 884744 | tf_op jit(solution)/shard_map/ppermute | solution.py:115
  (29 other events, 395.6 us)

commit v15 on v14

--- a/solution.py
+++ b/solution.py
@@ -258,7 +258,7 @@
 
         half = slice(number * tok_count, (number + 1) * tok_count)
         fetch.wait(*[("x", b) for b in range(count)])
-        x = x_buf[...]
+        x, products = x_buf[...], []
         for e in range(2):
             columns = slice(e * units, (e + 1) * units)
             fetch.wait(("w", 3 * e))
@@ -269,6 +269,9 @@
             if e == 0:
                 fetch.wait(*[("c", b) for b in range(count)])
             plain = dot(c_buf[...], down_w[columns, :], ((1,), (1,)))
+            products.append((gate, up, plain))
+        for e, (gate, up, plain) in enumerate(products):
+            columns = slice(e * units, (e + 1) * units)
             sigma = jax.nn.sigmoid(gate)
             silu_val = gate * sigma
             hidden = silu_val * up

time: 127 us -> 127 us (level)
  no operation moved by 1% of the time
where the time goes in v15:
time: 127 us
  waiting for transfers between devices  45.8 us (36%)
  Pallas kernels  39.5 us (31%)
  starting transfers between devices  33.9 us (27%)
  local copies, waits for them, and re-layouts  4.49 us (4%)
  other arithmetic  2.15 us (2%)
    ppermute x30, waiting for transfers between devices, swap(): return lax.ppermute(value, 'ep', pairs)  45.8 us
    pallas_call x4, Pallas kernels, kernel(): pl.pallas_call(body, out_shape=outs, in_specs=in_specs, out_specs=[pl.Blo...  39.5 us
    ppermute x30, starting transfers between devices, swap(): return lax.ppermute(value, 'ep', pairs)  33.9 us
    unnamed x62, local copies, waits for them, and re-layouts  2.59 us
  transfers between devices with their start and end apart: 30, of which 12 were waited for; matrix products, arithmetic and copies ran while one was open for 2% of the time, Pallas kernels for 31%

profile of v15, /device:TPU:0, one launch (start us, length us, event | category | flops | bytes accessed | tf_op | source)
XLA Modules:
  0.0 126.9 jit_solution(13182920003625586198)
XLA Ops:
  2.0 1.1 fusion.4
  3.6 1.0 copy-done.27
  5.0 3.7 %collective-permute-start.3 = (bf16[144,1024]{1,0:T(8,128)(2,1)S(1)}, bf16[144,1024]{1,0:T(8,128)(2,1)S(1)}, u32[]{:S(2)}, u32[]{:S(2)}) collective-permute-start(bf16[144,1024]{1,0:T(8,128)(2,1)S(1)} %fusion.1.refs_0_), channel_id=1, source_target_pairs={{0,8},{1,9},{2,10},{3,11},{4,12},{5,13},{6,14},{7,15},{8,0},{9,1},... | collective-permute-start | bytes 884744 | tf_op jit(solution)/shard_map/ppermute | solution.py:115
  8.7 1.5 %collective-permute-start.2 = (bf16[144,1024]{1,0:T(8,128)(2,1)S(1)}, bf16[144,1024]{1,0:T(8,128)(2,1)S(1)}, u32[]{:S(2)}, u32[]{:S(2)}) collective-permute-start(bf16[144,1024]{1,0:T(8,128)(2,1)S(1)} %fusion.1.refs_0_), channel_id=1, source_target_pairs={{0,2},{1,3},{2,0},{3,1},{4,6},{5,7},{6,4},{7,5},{8,10},{9,11},{10,... | collective-permute-start | bytes 884744 | tf_op jit(solution)/shard_map/ppermute | solution.py:115
  10.2 1.6 %collective-permute-start.1 = (bf16[144,1024]{1,0:T(8,128)(2,1)S(1)}, bf16[144,1024]{1,0:T(8,128)(2,1)S(1)}, u32[]{:S(2)}, u32[]{:S(2)}) collective-permute-start(bf16[144,1024]{1,0:T(8,128)(2,1)S(1)} %fusion.1.refs_0_), channel_id=1, source_target_pairs={{0,4},{1,5},{2,6},{3,7},{4,0},{5,1},{6,2},{7,3},{8,12},{9,13},{10,... | collective-permute-start | bytes 884744 | tf_op jit(solution)/shard_map/ppermute | solution.py:115
  12.3 11.0 %collective-permute-done.4.refs_4_.refs_12_ = bf16[128,1024]{1,0:T(8,128)(2,1)S(1)} collective-permute-done((bf16[128,1024]{1,0:T(8,128)(2,1)S(1)}, bf16[128,1024]{1,0:T(8,128)(2,1)S(1)}, u32[]{:S(2)}, u32[]{:S(2)}) %collective-permute-start.4) | collective-permute-done | bytes 262176 | tf_op jit(solution)/shard_map/ppermute | solution.py:115
  24.2 1.0 collective-permute-start.6
  25.1 1.5 %collective-permute-start.10 = (bf16[144,1024]{1,0:T(8,128)(2,1)S(1)}, bf16[144,1024]{1,0:T(8,128)(2,1)S(1)}, u32[]{:S(2)}, u32[]{:S(2)}) collective-permute-start(bf16[144,1024]{1,0:T(8,128)(2,1)S(1)} %collective-permute-done.1.refs_1_), channel_id=1, source_target_pairs={{0,2},{1,3},{2,0},{3,1},{4,6},{5,7},{6,4},{7,5},{8,10},{9,11},{10,... | collective-permute-start | bytes 884744 | tf_op jit(solution)/shard_map/ppermute | solution.py:115
  27.2 2.2 %collective-permute-start.9 = (bf16[128,1024]{1,0:T(8,128)(2,1)S(1)}, bf16[128,1024]{1,0:T(8,128)(2,1)S(1)}, u32[]{:S(2)}, u32[]{:S(2)}) collective-permute-start(bf16[128,1024]{1,0:T(8,128)(2,1)S(1)} %pad_maximum_fusion.refs_0_.refs_8_), channel_id=1, source_target_pairs={{0,8},{1,9},{2,10},{3,11},{4,12},{5,13},{6,14},{7,15},{8,0},{9,1},... | collective-permute-start | bytes 786440 | tf_op jit(solution)/shard_map/ppermute | solution.py:115
  29.3 8.4 %collective-permute-done.6.refs_3_ = bf16[144,1024]{1,0:T(8,128)(2,1)S(1)} collective-permute-done((bf16[144,1024]{1,0:T(8,128)(2,1)S(1)}, bf16[144,1024]{1,0:T(8,128)(2,1)S(1)}, u32[]{:S(2)}, u32[]{:S(2)}) %collective-permute-start.6) | collective-permute-done | bytes 294944 | tf_op jit(solution)/shard_map/ppermute | solution.py:115
  38.1 3.4 %collective-permute-done.9.refs_2_.refs_10_ = bf16[128,1024]{1,0:T(8,128)(2,1)S(1)} collective-permute-done((bf16[128,1024]{1,0:T(8,128)(2,1)S(1)}, bf16[128,1024]{1,0:T(8,128)(2,1)S(1)}, u32[]{:S(2)}, u32[]{:S(2)}) %collective-permute-start.9) | collective-permute-done | bytes 262176 | tf_op jit(solution)/shard_map/ppermute | solution.py:115
  41.6 1.5 %collective-permute-start.12 = (bf16[128,1024]{1,0:T(8,128)(2,1)S(1)}, bf16[128,1024]{1,0:T(8,128)(2,1)}, u32[]{:S(2)}, u32[]{:S(2)}) collective-permute-start(bf16[128,1024]{1,0:T(8,128)(2,1)S(1)} %collective-permute-done.9.refs_2_.refs_10_), channel_id=1, source_target_pairs={{0,2},{1,3},{2,0},{3,1},{4,6},{5,7},{6,4},{7,5},{8,10},{9,11},{10,... | collective-permute-start | bytes 786440 | tf_op jit(solution)/shard_map/ppermute | solution.py:115
  43.1 2.0 %collective-permute-start.13 = (bf16[128,1024]{1,0:T(8,128)(2,1)S(1)}, bf16[128,1024]{1,0:T(8,128)(2,1)S(1)}, u32[]{:S(2)}, u32[]{:S(2)}) collective-permute-start(bf16[128,1024]{1,0:T(8,128)(2,1)S(1)} %collective-permute-done.9.refs_2_.refs_10_), channel_id=1, source_target_pairs={{0,4},{1,5},{2,6},{3,7},{4,0},{5,1},{6,2},{7,3},{8,12},{9,13},{10,... | collective-permute-start | bytes 786440 | tf_op jit(solution)/shard_map/ppermute | solution.py:115
  45.1 5.6 %collective-permute-done.8.refs_1_.refs_9_ = bf16[128,1024]{1,0:T(8,128)(2,1)S(1)} collective-permute-done((bf16[128,1024]{1,0:T(8,128)(2,1)S(1)}, bf16[128,1024]{1,0:T(8,128)(2,1)S(1)}, u32[]{:S(2)}, u32[]{:S(2)}) %collective-permute-start.8) | collective-permute-done | bytes 262176 | tf_op jit(solution)/shard_map/ppermute | solution.py:115
  50.8 1.8 %collective-permute-done.12.refs_6_.refs_14_ = bf16[128,1024]{1,0:T(8,128)(2,1)} collective-permute-done((bf16[128,1024]{1,0:T(8,128)(2,1)S(1)}, bf16[128,1024]{1,0:T(8,128)(2,1)}, u32[]{:S(2)}, u32[]{:S(2)}) %collective-permute-start.12) | collective-permute-done | bytes 262176 | tf_op jit(solution)/shard_map/ppermute | solution.py:115
  52.6 1.5 %collective-permute-start.15 = (bf16[128,1024]{1,0:T(8,128)(2,1)S(1)}, bf16[128,1024]{1,0:T(8,128)(2,1)S(1)}, u32[]{:S(2)}, u32[]{:S(2)}) collective-permute-start(bf16[128,1024]{1,0:T(8,128)(2,1)S(1)} %collective-permute-done.8.refs_1_.refs_9_), channel_id=1, source_target_pairs={{0,2},{1,3},{2,0},{3,1},{4,6},{5,7},{6,4},{7,5},{8,10},{9,11},{10,... | collective-permute-start | bytes 786440 | tf_op jit(solution)/shard_map/ppermute | solution.py:115
  54.6 11.7 %shard_map.118 = (bf16[128,1024]{1,0:T(8,128)(2,1)}, bf16[128,1024]{1,0:T(8,128)(2,1)}, bf16[128,1024]{1,0:T(8,128)(2,1)}, bf16[128,1024]{1,0:T(8,128)(2,1)}, bf...) custom-call(s32[1]{0:T(128)} %bitcast.me_ref, ...), custom_call_target="tpu_custom_call" | custom-call | flops 6442450944 | bytes 14024704 | tf_op jit(solution)/shard_map/pallas_call | solution.py:162
  66.4 1.3 %collective-permute-start.18 = (bf16[128,1024]{1,0:T(8,128)(2,1)}, bf16[128,1024]{1,0:T(8,128)(2,1)S(1)}, u32[]{:S(2)}, u32[]{:S(2)}) collective-permute-start(bf16[128,1024]{1,0:T(8,128)(2,1)} %get-tuple-element.127), channel_id=1, source_target_pairs={{0,2},{1,3},{2,0},{3,1},{4,6},{5,7},{6,4},{7,5},{8,10},{9,11},{10,... | collective-permute-start | bytes 786440 | tf_op jit(solution)/shard_map/ppermute | solution.py:115
  69.3 11.9 %shard_map.119 = (bf16[144,1024]{1,0:T(8,128)(2,1)}, bf16[144,1024]{1,0:T(8,128)(2,1)}, bf16[144,1024]{1,0:T(8,128)(2,1)}, bf16[144,1024]{1,0:T(8,128)(2,1)}, bf...) custom-call(s32[1]{0:T(128)} %bitcast.me_ref, ...), custom_call_target="tpu_custom_call" | custom-call | flops 6442450944 | bytes 14024704 | tf_op jit(solution)/shard_map/pallas_call | solution.py:162
  81.4 1.2 collective-permute-start.19
  83.4 1.2 collective-permute-start.21
  84.6 7.4 %shard_map.120 = bf16[1536,1024]{1,0:T(8,128)(2,1)} custom-call(bf16[144,1024]{1,0:T(8,128)(2,1)} %copy-done.1, bf16[144,1024]{1,0:T(8,128)(2,1)} %copy-done.5, bf16[144,1024]{1,0:T(8,128)(2,1)} %copy-done.3, bf16[144,1024]{1,0:T(8,128)(2,1)} %copy-done.6, bf16[144,1024]{1,0:T(8,128)(2,1)} %copy-done.4, bf16[144,1024]{1,0:T(8,128)(2,1)} %copy-done.7, ...), custom_call_target="tpu_custom_call" | custom-call | flops 3221225472 | bytes 13893632 | tf_op jit(solution)/shard_map/pallas_call | solution.py:162
  92.1 3.0 %collective-permute-done.21 = bf16[144,1024]{1,0:T(8,128)(2,1)S(1)} collective-permute-done((bf16[144,1024]{1,0:T(8,128)(2,1)}, bf16[144,1024]{1,0:T(8,128)(2,1)S(1)}, u32[]{:S(2)}, u32[]{:S(2)}) %collective-permute-start.21) | collective-permute-done | bytes 294944 | tf_op jit(solution)/shard_map/ppermute | solution.py:115
  95.3 1.5 %collective-permute-start.22 = (bf16[144,1024]{1,0:T(8,128)(2,1)S(1)}, bf16[144,1024]{1,0:T(8,128)(2,1)S(1)}, u32[]{:S(2)}, u32[]{:S(2)}) collective-permute-start(bf16[144,1024]{1,0:T(8,128)(2,1)S(1)} %add_convert_fusion.1), channel_id=1, source_target_pairs={{0,2},{1,3},{2,0},{3,1},{4,6},{5,7},{6,4},{7,5},{8,10},{9,11},{10,... | collective-permute-start | bytes 884744 | tf_op jit(solution)/shard_map/ppermute | solution.py:115
  97.0 1.8 %collective-permute-start.29 = (bf16[128,1024]{1,0:T(8,128)(2,1)S(1)}, bf16[128,1024]{1,0:T(8,128)(2,1)S(1)}, u32[]{:S(2)}, u32[]{:S(2)}) collective-permute-start(bf16[128,1024]{1,0:T(8,128)(2,1)S(1)} %add_convert_fusion.3), channel_id=1, source_target_pairs={{0,8},{1,9},{2,10},{3,11},{4,12},{5,13},{6,14},{7,15},{8,0},{9,1},... | collective-permute-start | bytes 786440 | tf_op jit(solution)/shard_map/ppermute | solution.py:115
  98.8 0.9 collective-permute-start.27
  99.7 0.9 collective-permute-start.28
  100.7 4.5 %collective-permute-done.22 = bf16[144,1024]{1,0:T(8,128)(2,1)S(1)} collective-permute-done((bf16[144,1024]{1,0:T(8,128)(2,1)S(1)}, bf16[144,1024]{1,0:T(8,128)(2,1)S(1)}, u32[]{:S(2)}, u32[]{:S(2)}) %collective-permute-start.22) | collective-permute-done | bytes 294944 | tf_op jit(solution)/shard_map/ppermute | solution.py:115
  105.4 2.2 %collective-permute-start.24 = (bf16[144,1024]{1,0:T(8,128)(2,1)S(1)}, bf16[144,1024]{1,0:T(8,128)(2,1)S(1)}, u32[]{:S(2)}, u32[]{:S(2)}) collective-permute-start(bf16[144,1024]{1,0:T(8,128)(2,1)S(1)} %add_convert_fusion), channel_id=1, source_target_pairs={{0,8},{1,9},{2,10},{3,11},{4,12},{5,13},{6,14},{7,15},{8,0},{9,1},... | collective-permute-start | bytes 884744 | tf_op jit(solution)/shard_map/ppermute | solution.py:115
  108.5 4.7 %collective-permute-done.29.refs_24_ = bf16[128,1024]{1,0:T(8,128)(2,1)S(1)} collective-permute-done((bf16[128,1024]{1,0:T(8,128)(2,1)S(1)}, bf16[128,1024]{1,0:T(8,128)(2,1)S(1)}, u32[]{:S(2)}, u32[]{:S(2)}) %collective-permute-start.29) | collective-permute-done | bytes 262176 | tf_op jit(solution)/shard_map/ppermute | solution.py:115
  114.8 8.5 %shard_map.121 = (bf16[1024,512]{1,0:T(8,128)(2,1)}, bf16[1024,512]{1,0:T(8,128)(2,1)}, bf16[512,1024]{1,0:T(8,128)(2,1)}, bf16[128,1024]{1,0:T(8,128)(2,1)}, bf16[128,1024]{1,0:T(8,128)(2,1)}) custom-call(bf16[144,1024]{1,0:T(8,128)(2,1)} %copy-done.1, bf16[144,1024]{1,0:T(8,128)(2,1)} %copy-done.5, bf16[144,1024]{1,0:T(8,128)(2,1)} %copy-done.3, ...), custom_call_target="tpu_custom_call" | custom-call | flops 3221225472 | bytes 18612224 | tf_op jit(solution)/shard_map/pallas_call | solution.py:162
  123.3 1.5 %collective-permute-done.24 = bf16[144,1024]{1,0:T(8,128)(2,1)S(1)} collective-permute-done((bf16[144,1024]{1,0:T(8,128)(2,1)S(1)}, bf16[144,1024]{1,0:T(8,128)(2,1)S(1)}, u32[]{:S(2)}, u32[]{:S(2)}) %collective-permute-start.24) | collective-permute-done | bytes 294944 | tf_op jit(solution)/shard_map/ppermute | solution.py:115
  (114 shorter events, 12.7 us)
Async XLA Ops:
  0.6 3.0 %collective-permute-start = (bf16[1024,512]{1,0:T(8,128)(2,1)}, bf16[1024,512]{1,0:T(8,128)(2,1)S(1)}, u32[]{:S(2)}, u32[]{:S(2)}) collective-permute-start(bf16[1024,512]{1,0:T(8,128)(2,1)} %bitcast.20), channel_id=1, source_target_pairs={{0,1},{1,0},{2,3},{3,2},{4,5},{5,4},{6,7},{7,6},{8,9},{9,8},{10,11... | collective-permute-start | bytes 3145736 | tf_op jit(solution)/shard_map/ppermute | solution.py:115
  3.1 63.1 %copy-start.2 = (bf16[128,1024]{1,0:T(8,128)(2,1)}, bf16[128,1024]{1,0:T(8,128)(2,1)S(1)}, u32[]{:S(2)}) copy-start(bf16[128,1024]{1,0:T(8,128)(2,1)S(1)} %pad_maximum_fusion.refs_0_.refs_8_) | copy-start | bytes 786436
  3.2 51.4 %copy-start.1 = (bf16[144,1024]{1,0:T(8,128)(2,1)}, bf16[144,1024]{1,0:T(8,128)(2,1)S(1)}, u32[]{:S(2)}) copy-start(bf16[144,1024]{1,0:T(8,128)(2,1)S(1)} %fusion.1.refs_0_) | copy-start | bytes 884740
  4.6 19.5 %collective-permute-start.5 = (bf16[1024,512]{1,0:T(8,128)(2,1)}, bf16[1024,512]{1,0:T(8,128)(2,1)S(1)}, u32[]{:S(2)}, u32[]{:S(2)}) collective-permute-start(bf16[1024,512]{1,0:T(8,128)(2,1)} %bitcast.23), channel_id=1, source_target_pairs={{0,1},{1,0},{2,3},{3,2},{4,5},{5,4},{6,7},{7,6},{8,9},{9,8},{10,11... | collective-permute-start | bytes 3145736 | tf_op jit(solution)/shard_map/ppermute | solution.py:115
  5.0 18.4 %collective-permute-start.3 = (bf16[144,1024]{1,0:T(8,128)(2,1)S(1)}, bf16[144,1024]{1,0:T(8,128)(2,1)S(1)}, u32[]{:S(2)}, u32[]{:S(2)}) collective-permute-start(bf16[144,1024]{1,0:T(8,128)(2,1)S(1)} %fusion.1.refs_0_), channel_id=1, source_target_pairs={{0,8},{1,9},{2,10},{3,11},{4,12},{5,13},{6,14},{7,15},{8,0},{9,1},... | collective-permute-start | bytes 884744 | tf_op jit(solution)/shard_map/ppermute | solution.py:115
  8.7 14.6 %collective-permute-start.2 = (bf16[144,1024]{1,0:T(8,128)(2,1)S(1)}, bf16[144,1024]{1,0:T(8,128)(2,1)S(1)}, u32[]{:S(2)}, u32[]{:S(2)}) collective-permute-start(bf16[144,1024]{1,0:T(8,128)(2,1)S(1)} %fusion.1.refs_0_), channel_id=1, source_target_pairs={{0,2},{1,3},{2,0},{3,1},{4,6},{5,7},{6,4},{7,5},{8,10},{9,11},{10,... | collective-permute-start | bytes 884744 | tf_op jit(solution)/shard_map/ppermute | solution.py:115
  10.2 13.9 %collective-permute-start.1 = (bf16[144,1024]{1,0:T(8,128)(2,1)S(1)}, bf16[144,1024]{1,0:T(8,128)(2,1)S(1)}, u32[]{:S(2)}, u32[]{:S(2)}) collective-permute-start(bf16[144,1024]{1,0:T(8,128)(2,1)S(1)} %fusion.1.refs_0_), channel_id=1, source_target_pairs={{0,4},{1,5},{2,6},{3,7},{4,0},{5,1},{6,2},{7,3},{8,12},{9,13},{10,... | collective-permute-start | bytes 884744 | tf_op jit(solution)/shard_map/ppermute | solution.py:115
  11.8 11.5 %collective-permute-start.4 = (bf16[128,1024]{1,0:T(8,128)(2,1)S(1)}, bf16[128,1024]{1,0:T(8,128)(2,1)S(1)}, u32[]{:S(2)}, u32[]{:S(2)}) collective-permute-start(bf16[128,1024]{1,0:T(8,128)(2,1)S(1)} %pad_maximum_fusion.refs_0_.refs_8_), channel_id=1, source_target_pairs={{0,2},{1,3},{2,0},{3,1},{4,6},{5,7},{6,4},{7,5},{8,10},{9,11},{10,... | collective-permute-start | bytes 786440 | tf_op jit(solution)/shard_map/ppermute | solution.py:115
  24.1 30.4 %collective-permute-start.14 = (bf16[512,1024]{1,0:T(8,128)(2,1)}, bf16[512,1024]{1,0:T(8,128)(2,1)}, u32[]{:S(2)}, u32[]{:S(2)}) collective-permute-start(bf16[512,1024]{1,0:T(8,128)(2,1)} %bitcast.26), channel_id=1, source_target_pairs={{0,1},{1,0},{2,3},{3,2},{4,5},{5,4},{6,7},{7,6},{8,9},{9,8},{10,11... | collective-permute-start | bytes 3145736 | tf_op jit(solution)/shard_map/ppermute | solution.py:115
  24.2 13.5 %collective-permute-start.6 = (bf16[144,1024]{1,0:T(8,128)(2,1)S(1)}, bf16[144,1024]{1,0:T(8,128)(2,1)S(1)}, u32[]{:S(2)}, u32[]{:S(2)}) collective-permute-start(bf16[144,1024]{1,0:T(8,128)(2,1)S(1)} %collective-permute-done.3.refs_2_), channel_id=1, source_target_pairs={{0,4},{1,5},{2,6},{3,7},{4,0},{5,1},{6,2},{7,3},{8,12},{9,13},{10,... | collective-permute-start | bytes 884744 | tf_op jit(solution)/shard_map/ppermute | solution.py:115
  25.1 16.4 %collective-permute-start.10 = (bf16[144,1024]{1,0:T(8,128)(2,1)S(1)}, bf16[144,1024]{1,0:T(8,128)(2,1)S(1)}, u32[]{:S(2)}, u32[]{:S(2)}) collective-permute-start(bf16[144,1024]{1,0:T(8,128)(2,1)S(1)} %collective-permute-done.1.refs_1_), channel_id=1, source_target_pairs={{0,2},{1,3},{2,0},{3,1},{4,6},{5,7},{6,4},{7,5},{8,10},{9,11},{10,... | collective-permute-start | bytes 884744 | tf_op jit(solution)/shard_map/ppermute | solution.py:115
  26.6 15.0 %collective-permute-start.11 = (bf16[144,1024]{1,0:T(8,128)(2,1)S(1)}, bf16[144,1024]{1,0:T(8,128)(2,1)S(1)}, u32[]{:S(2)}, u32[]{:S(2)}) collective-permute-start(bf16[144,1024]{1,0:T(8,128)(2,1)S(1)} %collective-permute-done.3.refs_2_), channel_id=1, source_target_pairs={{0,2},{1,3},{2,0},{3,1},{4,6},{5,7},{6,4},{7,5},{8,10},{9,11},{10,... | collective-permute-start | bytes 884744 | tf_op jit(solution)/shard_map/ppermute | solution.py:115
  27.2 14.4 %collective-permute-start.9 = (bf16[128,1024]{1,0:T(8,128)(2,1)S(1)}, bf16[128,1024]{1,0:T(8,128)(2,1)S(1)}, u32[]{:S(2)}, u32[]{:S(2)}) collective-permute-start(bf16[128,1024]{1,0:T(8,128)(2,1)S(1)} %pad_maximum_fusion.refs_0_.refs_8_), channel_id=1, source_target_pairs={{0,8},{1,9},{2,10},{3,11},{4,12},{5,13},{6,14},{7,15},{8,0},{9,1},... | collective-permute-start | bytes 786440 | tf_op jit(solution)/shard_map/ppermute | solution.py:115
  37.7 14.9 %collective-permute-start.7 = (bf16[144,1024]{1,0:T(8,128)(2,1)S(1)}, bf16[144,1024]{1,0:T(8,128)(2,1)S(1)}, u32[]{:S(2)}, u32[]{:S(2)}) collective-permute-start(bf16[144,1024]{1,0:T(8,128)(2,1)S(1)} %collective-permute-done.6.refs_3_), channel_id=1, source_target_pairs={{0,2},{1,3},{2,0},{3,1},{4,6},{5,7},{6,4},{7,5},{8,10},{9,11},{10,... | collective-permute-start | bytes 884744 | tf_op jit(solution)/shard_map/ppermute | solution.py:115
  41.6 9.2 %collective-permute-start.8 = (bf16[128,1024]{1,0:T(8,128)(2,1)S(1)}, bf16[128,1024]{1,0:T(8,128)(2,1)S(1)}, u32[]{:S(2)}, u32[]{:S(2)}) collective-permute-start(bf16[128,1024]{1,0:T(8,128)(2,1)S(1)} %pad_maximum_fusion.refs_0_.refs_8_), channel_id=1, source_target_pairs={{0,4},{1,5},{2,6},{3,7},{4,0},{5,1},{6,2},{7,3},{8,12},{9,13},{10,... | collective-permute-start | bytes 786440 | tf_op jit(solution)/shard_map/ppermute | solution.py:115
  41.6 11.0 %collective-permute-start.12 = (bf16[128,1024]{1,0:T(8,128)(2,1)S(1)}, bf16[128,1024]{1,0:T(8,128)(2,1)}, u32[]{:S(2)}, u32[]{:S(2)}) collective-permute-start(bf16[128,1024]{1,0:T(8,128)(2,1)S(1)} %collective-permute-done.9.refs_2_.refs_10_), channel_id=1, source_target_pairs={{0,2},{1,3},{2,0},{3,1},{4,6},{5,7},{6,4},{7,5},{8,10},{9,11},{10,... | collective-permute-start | bytes 786440 | tf_op jit(solution)/shard_map/ppermute | solution.py:115
  43.1 25.4 %collective-permute-start.13 = (bf16[128,1024]{1,0:T(8,128)(2,1)S(1)}, bf16[128,1024]{1,0:T(8,128)(2,1)S(1)}, u32[]{:S(2)}, u32[]{:S(2)}) collective-permute-start(bf16[128,1024]{1,0:T(8,128)(2,1)S(1)} %collective-permute-done.9.refs_2_.refs_10_), channel_id=1, source_target_pairs={{0,4},{1,5},{2,6},{3,7},{4,0},{5,1},{6,2},{7,3},{8,12},{9,13},{10,... | collective-permute-start | bytes 786440 | tf_op jit(solution)/shard_map/ppermute | solution.py:115
  52.6 13.7 %collective-permute-start.15 = (bf16[128,1024]{1,0:T(8,128)(2,1)S(1)}, bf16[128,1024]{1,0:T(8,128)(2,1)S(1)}, u32[]{:S(2)}, u32[]{:S(2)}) collective-permute-start(bf16[128,1024]{1,0:T(8,128)(2,1)S(1)} %collective-permute-done.8.refs_1_.refs_9_), channel_id=1, source_target_pairs={{0,2},{1,3},{2,0},{3,1},{4,6},{5,7},{6,4},{7,5},{8,10},{9,11},{10,... | collective-permute-start | bytes 786440 | tf_op jit(solution)/shard_map/ppermute | solution.py:115
  54.1 12.3 %collective-permute-start.16 = (bf16[128,1024]{1,0:T(8,128)(2,1)}, bf16[128,1024]{1,0:T(8,128)(2,1)S(1)}, u32[]{:S(2)}, u32[]{:S(2)}) collective-permute-start(bf16[128,1024]{1,0:T(8,128)(2,1)} %collective-permute-done.12.refs_6_.refs_14_), channel_id=1, source_target_pairs={{0,4},{1,5},{2,6},{3,7},{4,0},{5,1},{6,2},{7,3},{8,12},{9,13},{10,... | collective-permute-start | bytes 786440 | tf_op jit(solution)/shard_map/ppermute | solution.py:115
  66.4 14.8 %collective-permute-start.18 = (bf16[128,1024]{1,0:T(8,128)(2,1)}, bf16[128,1024]{1,0:T(8,128)(2,1)S(1)}, u32[]{:S(2)}, u32[]{:S(2)}) collective-permute-start(bf16[128,1024]{1,0:T(8,128)(2,1)} %get-tuple-element.127), channel_id=1, source_target_pairs={{0,2},{1,3},{2,0},{3,1},{4,6},{5,7},{6,4},{7,5},{8,10},{9,11},{10,... | collective-permute-start | bytes 786440 | tf_op jit(solution)/shard_map/ppermute | solution.py:115
  67.6 13.6 %collective-permute-start.17 = (bf16[256,1024]{1,0:T(8,128)(2,1)}, bf16[256,1024]{1,0:T(8,128)(2,1)S(1)}, u32[]{:S(2)}, u32[]{:S(2)}) collective-permute-start(bf16[256,1024]{1,0:T(8,128)(2,1)} %get-tuple-element.126), channel_id=1, source_target_pairs={{0,4},{1,5},{2,6},{3,7},{4,0},{5,1},{6,2},{7,3},{8,12},{9,13},{10,... | collective-permute-start | bytes 1572872 | tf_op jit(solution)/shard_map/ppermute | solution.py:115
  81.4 13.8 %collective-permute-start.19 = (bf16[288,1024]{1,0:T(8,128)(2,1)}, bf16[288,1024]{1,0:T(8,128)(2,1)S(1)}, u32[]{:S(2)}, u32[]{:S(2)}) collective-permute-start(bf16[288,1024]{1,0:T(8,128)(2,1)} %get-tuple-element.143), channel_id=1, source_target_pairs={{0,4},{1,5},{2,6},{3,7},{4,0},{5,1},{6,2},{7,3},{8,12},{9,13},{10,... | collective-permute-start | bytes 1769480 | tf_op jit(solution)/shard_map/ppermute | solution.py:115
  82.6 9.5 %collective-permute-start.20 = (bf16[128,1024]{1,0:T(8,128)(2,1)S(1)}, bf16[128,1024]{1,0:T(8,128)(2,1)S(1)}, u32[]{:S(2)}, u32[]{:S(2)}) collective-permute-start(bf16[128,1024]{1,0:T(8,128)(2,1)S(1)} %add_convert_fusion.5), channel_id=1, source_target_pairs={{0,2},{1,3},{2,0},{3,1},{4,6},{5,7},{6,4},{7,5},{8,10},{9,11},{10,... | collective-permute-start | bytes 786440 | tf_op jit(solution)/shard_map/ppermute | solution.py:115
  83.4 11.6 %collective-permute-start.21 = (bf16[144,1024]{1,0:T(8,128)(2,1)}, bf16[144,1024]{1,0:T(8,128)(2,1)S(1)}, u32[]{:S(2)}, u32[]{:S(2)}) collective-permute-start(bf16[144,1024]{1,0:T(8,128)(2,1)} %get-tuple-element.145), channel_id=1, source_target_pairs={{0,2},{1,3},{2,0},{3,1},{4,6},{5,7},{6,4},{7,5},{8,10},{9,11},{10,... | collective-permute-start | bytes 884744 | tf_op jit(solution)/shard_map/ppermute | solution.py:115
  95.2 10.1 %collective-permute-start.23 = (bf16[1536,1024]{1,0:T(8,128)(2,1)}, bf16[1536,1024]{1,0:T(8,128)(2,1)S(1)}, u32[]{:S(2)}, u32[]{:S(2)}) collective-permute-start(bf16[1536,1024]{1,0:T(8,128)(2,1)} %shard_map.120), channel_id=1, source_target_pairs={{0,1},{1,0},{2,3},{3,2},{4,5},{5,4},{6,7},{7,6},{8,9},{9,8},{10,11... | collective-permute-start | bytes 9437192 | tf_op jit(solution)/shard_map/ppermute | solution.py:115
  95.3 9.9 %collective-permute-start.22 = (bf16[144,1024]{1,0:T(8,128)(2,1)S(1)}, bf16[144,1024]{1,0:T(8,128)(2,1)S(1)}, u32[]{:S(2)}, u32[]{:S(2)}) collective-permute-start(bf16[144,1024]{1,0:T(8,128)(2,1)S(1)} %add_convert_fusion.1), channel_id=1, source_target_pairs={{0,2},{1,3},{2,0},{3,1},{4,6},{5,7},{6,4},{7,5},{8,10},{9,11},{10,... | collective-permute-start | bytes 884744 | tf_op jit(solution)/shard_map/ppermute | solution.py:115
  97.0 16.2 %collective-permute-start.29 = (bf16[128,1024]{1,0:T(8,128)(2,1)S(1)}, bf16[128,1024]{1,0:T(8,128)(2,1)S(1)}, u32[]{:S(2)}, u32[]{:S(2)}) collective-permute-start(bf16[128,1024]{1,0:T(8,128)(2,1)S(1)} %add_convert_fusion.3), channel_id=1, source_target_pairs={{0,8},{1,9},{2,10},{3,11},{4,12},{5,13},{6,14},{7,15},{8,0},{9,1},... | collective-permute-start | bytes 786440 | tf_op jit(solution)/shard_map/ppermute | solution.py:115
  98.8 15.2 %collective-permute-start.27 = (bf16[128,1024]{1,0:T(8,128)(2,1)S(1)}, bf16[128,1024]{1,0:T(8,128)(2,1)S(1)}, u32[]{:S(2)}, u32[]{:S(2)}) collective-permute-start(bf16[128,1024]{1,0:T(8,128)(2,1)S(1)} %copy-done.30), channel_id=1, source_target_pairs={{0,2},{1,3},{2,0},{3,1},{4,6},{5,7},{6,4},{7,5},{8,10},{9,11},{10,... | collective-permute-start | bytes 786440 | tf_op jit(solution)/shard_map/ppermute | solution.py:115
  99.7 14.2 %collective-permute-start.28 = (bf16[128,1024]{1,0:T(8,128)(2,1)S(1)}, bf16[128,1024]{1,0:T(8,128)(2,1)S(1)}, u32[]{:S(2)}, u32[]{:S(2)}) collective-permute-start(bf16[128,1024]{1,0:T(8,128)(2,1)S(1)} %add_convert_fusion.4), channel_id=1, source_target_pairs={{0,4},{1,5},{2,6},{3,7},{4,0},{5,1},{6,2},{7,3},{8,12},{9,13},{10,... | collective-permute-start | bytes 786440 | tf_op jit(solution)/shard_map/ppermute | solution.py:115
  105.4 19.4 %collective-permute-start.24 = (bf16[144,1024]{1,0:T(8,128)(2,1)S(1)}, bf16[144,1024]{1,0:T(8,128)(2,1)S(1)}, u32[]{:S(2)}, u32[]{:S(2)}) collective-permute-start(bf16[144,1024]{1,0:T(8,128)(2,1)S(1)} %add_convert_fusion), channel_id=1, source_target_pairs={{0,8},{1,9},{2,10},{3,11},{4,12},{5,13},{6,14},{7,15},{8,0},{9,1},... | collective-permute-start | bytes 884744 | tf_op jit(solution)/shard_map/ppermute | solution.py:115
  107.5 17.8 %collective-permute-start.25 = (bf16[144,1024]{1,0:T(8,128)(2,1)S(1)}, bf16[144,1024]{1,0:T(8,128)(2,1)S(1)}, u32[]{:S(2)}, u32[]{:S(2)}) collective-permute-start(bf16[144,1024]{1,0:T(8,128)(2,1)S(1)} %add_convert_fusion.2), channel_id=1, source_target_pairs={{0,4},{1,5},{2,6},{3,7},{4,0},{5,1},{6,2},{7,3},{8,12},{9,13},{10,... | collective-permute-start | bytes 884744 | tf_op jit(solution)/shard_map/ppermute | solution.py:115
  113.2 12.1 %collective-permute-start.26 = (bf16[144,1024]{1,0:T(8,128)(2,1)S(1)}, bf16[144,1024]{1,0:T(8,128)(2,1)S(1)}, u32[]{:S(2)}, u32[]{:S(2)}) collective-permute-start(bf16[144,1024]{1,0:T(8,128)(2,1)S(1)} %copy-done.29), channel_id=1, source_target_pairs={{0,2},{1,3},{2,0},{3,1},{4,6},{5,7},{6,4},{7,5},{8,10},{9,11},{10,... | collective-permute-start | bytes 884744 | tf_op jit(solution)/shard_map/ppermute | solution.py:115
  (29 other events, 395.6 us)

commit v16 on v15

--- a/solution.py
+++ b/solution.py
@@ -293,10 +293,12 @@
         for b in range(count):
             at = pl.ds(b * tok_count, tok_count)
             fetch.start(("y", b), y_buf.at[at], returned(b, 0, tok_count))
-        g_buf[...] = dot(factor_buf[...], wide_w[...], ((1,), (1,))).astype(bf16)
-        for b in range(count):
-            at = pl.ds(b * tok_count, tok_count)
-            fetch.start(("g", b), g_buf.at[at], returned(b, tok_count, tok_count))
+        for first in (0, count // 2):
+            rows = slice(first * tok_count, (first + count // 2) * tok_count)
+            g_buf[rows, :] = dot(factor_buf[rows, :], wide_w[...], ((1,), (1,))).astype(bf16)
+            for b in range(first, first + count // 2):
+                at = pl.ds(b * tok_count, tok_count)
+                fetch.start(("g", b), g_buf.at[at], returned(b, tok_count, tok_count))
         if last:
             wide_buf[...] = jnp.zeros((count, EXTRA, width), f32)
             inner_buf[...] = inner_buf[...].T

time: 127 us -> 127 us (level)
  no operation moved by 1% of the time
where the time goes in v16:
time: 127 us
  waiting for transfers between devices  45.8 us (36%)
  Pallas kernels  39.1 us (31%)
  starting transfers between devices  33.9 us (27%)
  local copies, waits for them, and re-layouts  4.49 us (4%)
  other arithmetic  2.15 us (2%)
    ppermute x30, waiting for transfers between devices, swap(): return lax.ppermute(value, 'ep', pairs)  45.8 us
    pallas_call x4, Pallas kernels, kernel(): pl.pallas_call(body, out_shape=outs, in_specs=in_specs, out_specs=[pl.Blo...  39.1 us
    ppermute x30, starting transfers between devices, swap(): return lax.ppermute(value, 'ep', pairs)  33.9 us
    unnamed x62, local copies, waits for them, and re-layouts  2.59 us
  transfers between devices with their start and end apart: 30, of which 12 were waited for; matrix products, arithmetic and copies ran while one was open for 2% of the time, Pallas kernels for 31%

profile of v16, /device:TPU:0, one launch (start us, length us, event | category | flops | bytes accessed | tf_op | source)
XLA Modules:
  0.0 126.5 jit_solution(72823018146159879)
XLA Ops:
  2.0 1.1 fusion.4
  3.6 1.0 copy-done.27
  5.0 3.7 %collective-permute-start.3 = (bf16[144,1024]{1,0:T(8,128)(2,1)S(1)}, bf16[144,1024]{1,0:T(8,128)(2,1)S(1)}, u32[]{:S(2)}, u32[]{:S(2)}) collective-permute-start(bf16[144,1024]{1,0:T(8,128)(2,1)S(1)} %fusion.1.refs_0_), channel_id=1, source_target_pairs={{0,8},{1,9},{2,10},{3,11},{4,12},{5,13},{6,14},{7,15},{8,0},{9,1},... | collective-permute-start | bytes 884744 | tf_op jit(solution)/shard_map/ppermute | solution.py:115
  8.7 1.5 %collective-permute-start.2 = (bf16[144,1024]{1,0:T(8,128)(2,1)S(1)}, bf16[144,1024]{1,0:T(8,128)(2,1)S(1)}, u32[]{:S(2)}, u32[]{:S(2)}) collective-permute-start(bf16[144,1024]{1,0:T(8,128)(2,1)S(1)} %fusion.1.refs_0_), channel_id=1, source_target_pairs={{0,2},{1,3},{2,0},{3,1},{4,6},{5,7},{6,4},{7,5},{8,10},{9,11},{10,... | collective-permute-start | bytes 884744 | tf_op jit(solution)/shard_map/ppermute | solution.py:115
  10.2 1.6 %collective-permute-start.1 = (bf16[144,1024]{1,0:T(8,128)(2,1)S(1)}, bf16[144,1024]{1,0:T(8,128)(2,1)S(1)}, u32[]{:S(2)}, u32[]{:S(2)}) collective-permute-start(bf16[144,1024]{1,0:T(8,128)(2,1)S(1)} %fusion.1.refs_0_), channel_id=1, source_target_pairs={{0,4},{1,5},{2,6},{3,7},{4,0},{5,1},{6,2},{7,3},{8,12},{9,13},{10,... | collective-permute-start | bytes 884744 | tf_op jit(solution)/shard_map/ppermute | solution.py:115
  12.3 11.0 %collective-permute-done.4.refs_4_.refs_12_ = bf16[128,1024]{1,0:T(8,128)(2,1)S(1)} collective-permute-done((bf16[128,1024]{1,0:T(8,128)(2,1)S(1)}, bf16[128,1024]{1,0:T(8,128)(2,1)S(1)}, u32[]{:S(2)}, u32[]{:S(2)}) %collective-permute-start.4) | collective-permute-done | bytes 262176 | tf_op jit(solution)/shard_map/ppermute | solution.py:115
  24.2 1.0 collective-permute-start.6
  25.1 1.5 %collective-permute-start.10 = (bf16[144,1024]{1,0:T(8,128)(2,1)S(1)}, bf16[144,1024]{1,0:T(8,128)(2,1)S(1)}, u32[]{:S(2)}, u32[]{:S(2)}) collective-permute-start(bf16[144,1024]{1,0:T(8,128)(2,1)S(1)} %collective-permute-done.1.refs_1_), channel_id=1, source_target_pairs={{0,2},{1,3},{2,0},{3,1},{4,6},{5,7},{6,4},{7,5},{8,10},{9,11},{10,... | collective-permute-start | bytes 884744 | tf_op jit(solution)/shard_map/ppermute | solution.py:115
  27.2 2.2 %collective-permute-start.9 = (bf16[128,1024]{1,0:T(8,128)(2,1)S(1)}, bf16[128,1024]{1,0:T(8,128)(2,1)S(1)}, u32[]{:S(2)}, u32[]{:S(2)}) collective-permute-start(bf16[128,1024]{1,0:T(8,128)(2,1)S(1)} %pad_maximum_fusion.refs_0_.refs_8_), channel_id=1, source_target_pairs={{0,8},{1,9},{2,10},{3,11},{4,12},{5,13},{6,14},{7,15},{8,0},{9,1},... | collective-permute-start | bytes 786440 | tf_op jit(solution)/shard_map/ppermute | solution.py:115
  29.3 8.4 %collective-permute-done.6.refs_3_ = bf16[144,1024]{1,0:T(8,128)(2,1)S(1)} collective-permute-done((bf16[144,1024]{1,0:T(8,128)(2,1)S(1)}, bf16[144,1024]{1,0:T(8,128)(2,1)S(1)}, u32[]{:S(2)}, u32[]{:S(2)}) %collective-permute-start.6) | collective-permute-done | bytes 294944 | tf_op jit(solution)/shard_map/ppermute | solution.py:115
  38.1 3.4 %collective-permute-done.9.refs_2_.refs_10_ = bf16[128,1024]{1,0:T(8,128)(2,1)S(1)} collective-permute-done((bf16[128,1024]{1,0:T(8,128)(2,1)S(1)}, bf16[128,1024]{1,0:T(8,128)(2,1)S(1)}, u32[]{:S(2)}, u32[]{:S(2)}) %collective-permute-start.9) | collective-permute-done | bytes 262176 | tf_op jit(solution)/shard_map/ppermute | solution.py:115
  41.6 1.5 %collective-permute-start.12 = (bf16[128,1024]{1,0:T(8,128)(2,1)S(1)}, bf16[128,1024]{1,0:T(8,128)(2,1)}, u32[]{:S(2)}, u32[]{:S(2)}) collective-permute-start(bf16[128,1024]{1,0:T(8,128)(2,1)S(1)} %collective-permute-done.9.refs_2_.refs_10_), channel_id=1, source_target_pairs={{0,2},{1,3},{2,0},{3,1},{4,6},{5,7},{6,4},{7,5},{8,10},{9,11},{10,... | collective-permute-start | bytes 786440 | tf_op jit(solution)/shard_map/ppermute | solution.py:115
  43.1 2.0 %collective-permute-start.13 = (bf16[128,1024]{1,0:T(8,128)(2,1)S(1)}, bf16[128,1024]{1,0:T(8,128)(2,1)S(1)}, u32[]{:S(2)}, u32[]{:S(2)}) collective-permute-start(bf16[128,1024]{1,0:T(8,128)(2,1)S(1)} %collective-permute-done.9.refs_2_.refs_10_), channel_id=1, source_target_pairs={{0,4},{1,5},{2,6},{3,7},{4,0},{5,1},{6,2},{7,3},{8,12},{9,13},{10,... | collective-permute-start | bytes 786440 | tf_op jit(solution)/shard_map/ppermute | solution.py:115
  45.1 5.6 %collective-permute-done.8.refs_1_.refs_9_ = bf16[128,1024]{1,0:T(8,128)(2,1)S(1)} collective-permute-done((bf16[128,1024]{1,0:T(8,128)(2,1)S(1)}, bf16[128,1024]{1,0:T(8,128)(2,1)S(1)}, u32[]{:S(2)}, u32[]{:S(2)}) %collective-permute-start.8) | collective-permute-done | bytes 262176 | tf_op jit(solution)/shard_map/ppermute | solution.py:115
  50.8 1.8 %collective-permute-done.12.refs_6_.refs_14_ = bf16[128,1024]{1,0:T(8,128)(2,1)} collective-permute-done((bf16[128,1024]{1,0:T(8,128)(2,1)S(1)}, bf16[128,1024]{1,0:T(8,128)(2,1)}, u32[]{:S(2)}, u32[]{:S(2)}) %collective-permute-start.12) | collective-permute-done | bytes 262176 | tf_op jit(solution)/shard_map/ppermute | solution.py:115
  52.6 1.5 %collective-permute-start.15 = (bf16[128,1024]{1,0:T(8,128)(2,1)S(1)}, bf16[128,1024]{1,0:T(8,128)(2,1)S(1)}, u32[]{:S(2)}, u32[]{:S(2)}) collective-permute-start(bf16[128,1024]{1,0:T(8,128)(2,1)S(1)} %collective-permute-done.8.refs_1_.refs_9_), channel_id=1, source_target_pairs={{0,2},{1,3},{2,0},{3,1},{4,6},{5,7},{6,4},{7,5},{8,10},{9,11},{10,... | collective-permute-start | bytes 786440 | tf_op jit(solution)/shard_map/ppermute | solution.py:115
  54.6 11.6 %shard_map.118 = (bf16[128,1024]{1,0:T(8,128)(2,1)}, bf16[128,1024]{1,0:T(8,128)(2,1)}, bf16[128,1024]{1,0:T(8,128)(2,1)}, bf16[128,1024]{1,0:T(8,128)(2,1)}, bf...) custom-call(s32[1]{0:T(128)} %bitcast.me_ref, ...), custom_call_target="tpu_custom_call" | custom-call | flops 6442450944 | bytes 14024704 | tf_op jit(solution)/shard_map/pallas_call | solution.py:162
  66.3 1.3 %collective-permute-start.18 = (bf16[128,1024]{1,0:T(8,128)(2,1)}, bf16[128,1024]{1,0:T(8,128)(2,1)S(1)}, u32[]{:S(2)}, u32[]{:S(2)}) collective-permute-start(bf16[128,1024]{1,0:T(8,128)(2,1)} %get-tuple-element.127), channel_id=1, source_target_pairs={{0,2},{1,3},{2,0},{3,1},{4,6},{5,7},{6,4},{7,5},{8,10},{9,11},{10,... | collective-permute-start | bytes 786440 | tf_op jit(solution)/shard_map/ppermute | solution.py:115
  69.2 11.6 %shard_map.119 = (bf16[144,1024]{1,0:T(8,128)(2,1)}, bf16[144,1024]{1,0:T(8,128)(2,1)}, bf16[144,1024]{1,0:T(8,128)(2,1)}, bf16[144,1024]{1,0:T(8,128)(2,1)}, bf...) custom-call(s32[1]{0:T(128)} %bitcast.me_ref, ...), custom_call_target="tpu_custom_call" | custom-call | flops 6442450944 | bytes 14024704 | tf_op jit(solution)/shard_map/pallas_call | solution.py:162
  81.0 1.2 collective-permute-start.19
  83.0 1.2 collective-permute-start.21
  84.2 7.4 %shard_map.120 = bf16[1536,1024]{1,0:T(8,128)(2,1)} custom-call(bf16[144,1024]{1,0:T(8,128)(2,1)} %copy-done.1, bf16[144,1024]{1,0:T(8,128)(2,1)} %copy-done.5, bf16[144,1024]{1,0:T(8,128)(2,1)} %copy-done.3, bf16[144,1024]{1,0:T(8,128)(2,1)} %copy-done.6, bf16[144,1024]{1,0:T(8,128)(2,1)} %copy-done.4, bf16[144,1024]{1,0:T(8,128)(2,1)} %copy-done.7, ...), custom_call_target="tpu_custom_call" | custom-call | flops 3221225472 | bytes 13893632 | tf_op jit(solution)/shard_map/pallas_call | solution.py:162
  91.7 3.0 %collective-permute-done.21 = bf16[144,1024]{1,0:T(8,128)(2,1)S(1)} collective-permute-done((bf16[144,1024]{1,0:T(8,128)(2,1)}, bf16[144,1024]{1,0:T(8,128)(2,1)S(1)}, u32[]{:S(2)}, u32[]{:S(2)}) %collective-permute-start.21) | collective-permute-done | bytes 294944 | tf_op jit(solution)/shard_map/ppermute | solution.py:115
  94.9 1.5 %collective-permute-start.22 = (bf16[144,1024]{1,0:T(8,128)(2,1)S(1)}, bf16[144,1024]{1,0:T(8,128)(2,1)S(1)}, u32[]{:S(2)}, u32[]{:S(2)}) collective-permute-start(bf16[144,1024]{1,0:T(8,128)(2,1)S(1)} %add_convert_fusion.1), channel_id=1, source_target_pairs={{0,2},{1,3},{2,0},{3,1},{4,6},{5,7},{6,4},{7,5},{8,10},{9,11},{10,... | collective-permute-start | bytes 884744 | tf_op jit(solution)/shard_map/ppermute | solution.py:115
  96.6 1.8 %collective-permute-start.29 = (bf16[128,1024]{1,0:T(8,128)(2,1)S(1)}, bf16[128,1024]{1,0:T(8,128)(2,1)S(1)}, u32[]{:S(2)}, u32[]{:S(2)}) collective-permute-start(bf16[128,1024]{1,0:T(8,128)(2,1)S(1)} %add_convert_fusion.3), channel_id=1, source_target_pairs={{0,8},{1,9},{2,10},{3,11},{4,12},{5,13},{6,14},{7,15},{8,0},{9,1},... | collective-permute-start | bytes 786440 | tf_op jit(solution)/shard_map/ppermute | solution.py:115
  98.4 0.9 collective-permute-start.27
  99.3 0.9 collective-permute-start.28
  100.3 4.5 %collective-permute-done.22 = bf16[144,1024]{1,0:T(8,128)(2,1)S(1)} collective-permute-done((bf16[144,1024]{1,0:T(8,128)(2,1)S(1)}, bf16[144,1024]{1,0:T(8,128)(2,1)S(1)}, u32[]{:S(2)}, u32[]{:S(2)}) %collective-permute-start.22) | collective-permute-done | bytes 294944 | tf_op jit(solution)/shard_map/ppermute | solution.py:115
  105.0 2.2 %collective-permute-start.24 = (bf16[144,1024]{1,0:T(8,128)(2,1)S(1)}, bf16[144,1024]{1,0:T(8,128)(2,1)S(1)}, u32[]{:S(2)}, u32[]{:S(2)}) collective-permute-start(bf16[144,1024]{1,0:T(8,128)(2,1)S(1)} %add_convert_fusion), channel_id=1, source_target_pairs={{0,8},{1,9},{2,10},{3,11},{4,12},{5,13},{6,14},{7,15},{8,0},{9,1},... | collective-permute-start | bytes 884744 | tf_op jit(solution)/shard_map/ppermute | solution.py:115
  108.1 4.7 %collective-permute-done.29.refs_24_ = bf16[128,1024]{1,0:T(8,128)(2,1)S(1)} collective-permute-done((bf16[128,1024]{1,0:T(8,128)(2,1)S(1)}, bf16[128,1024]{1,0:T(8,128)(2,1)S(1)}, u32[]{:S(2)}, u32[]{:S(2)}) %collective-permute-start.29) | collective-permute-done | bytes 262176 | tf_op jit(solution)/shard_map/ppermute | solution.py:115
  114.4 8.5 %shard_map.121 = (bf16[1024,512]{1,0:T(8,128)(2,1)}, bf16[1024,512]{1,0:T(8,128)(2,1)}, bf16[512,1024]{1,0:T(8,128)(2,1)}, bf16[128,1024]{1,0:T(8,128)(2,1)}, bf16[128,1024]{1,0:T(8,128)(2,1)}) custom-call(bf16[144,1024]{1,0:T(8,128)(2,1)} %copy-done.1, bf16[144,1024]{1,0:T(8,128)(2,1)} %copy-done.5, bf16[144,1024]{1,0:T(8,128)(2,1)} %copy-done.3, ...), custom_call_target="tpu_custom_call" | custom-call | flops 3221225472 | bytes 18612224 | tf_op jit(solution)/shard_map/pallas_call | solution.py:162
  122.9 1.4 %collective-permute-done.24 = bf16[144,1024]{1,0:T(8,128)(2,1)S(1)} collective-permute-done((bf16[144,1024]{1,0:T(8,128)(2,1)S(1)}, bf16[144,1024]{1,0:T(8,128)(2,1)S(1)}, u32[]{:S(2)}, u32[]{:S(2)}) %collective-permute-start.24) | collective-permute-done | bytes 294944 | tf_op jit(solution)/shard_map/ppermute | solution.py:115
  (114 shorter events, 12.7 us)
Async XLA Ops:
  0.6 3.0 %collective-permute-start = (bf16[1024,512]{1,0:T(8,128)(2,1)}, bf16[1024,512]{1,0:T(8,128)(2,1)S(1)}, u32[]{:S(2)}, u32[]{:S(2)}) collective-permute-start(bf16[1024,512]{1,0:T(8,128)(2,1)} %bitcast.20), channel_id=1, source_target_pairs={{0,1},{1,0},{2,3},{3,2},{4,5},{5,4},{6,7},{7,6},{8,9},{9,8},{10,11... | collective-permute-start | bytes 3145736 | tf_op jit(solution)/shard_map/ppermute | solution.py:115
  3.1 63.0 %copy-start.2 = (bf16[128,1024]{1,0:T(8,128)(2,1)}, bf16[128,1024]{1,0:T(8,128)(2,1)S(1)}, u32[]{:S(2)}) copy-start(bf16[128,1024]{1,0:T(8,128)(2,1)S(1)} %pad_maximum_fusion.refs_0_.refs_8_) | copy-start | bytes 786436
  3.2 51.4 %copy-start.1 = (bf16[144,1024]{1,0:T(8,128)(2,1)}, bf16[144,1024]{1,0:T(8,128)(2,1)S(1)}, u32[]{:S(2)}) copy-start(bf16[144,1024]{1,0:T(8,128)(2,1)S(1)} %fusion.1.refs_0_) | copy-start | bytes 884740
  4.6 19.5 %collective-permute-start.5 = (bf16[1024,512]{1,0:T(8,128)(2,1)}, bf16[1024,512]{1,0:T(8,128)(2,1)S(1)}, u32[]{:S(2)}, u32[]{:S(2)}) collective-permute-start(bf16[1024,512]{1,0:T(8,128)(2,1)} %bitcast.23), channel_id=1, source_target_pairs={{0,1},{1,0},{2,3},{3,2},{4,5},{5,4},{6,7},{7,6},{8,9},{9,8},{10,11... | collective-permute-start | bytes 3145736 | tf_op jit(solution)/shard_map/ppermute | solution.py:115
  5.0 18.4 %collective-permute-start.3 = (bf16[144,1024]{1,0:T(8,128)(2,1)S(1)}, bf16[144,1024]{1,0:T(8,128)(2,1)S(1)}, u32[]{:S(2)}, u32[]{:S(2)}) collective-permute-start(bf16[144,1024]{1,0:T(8,128)(2,1)S(1)} %fusion.1.refs_0_), channel_id=1, source_target_pairs={{0,8},{1,9},{2,10},{3,11},{4,12},{5,13},{6,14},{7,15},{8,0},{9,1},... | collective-permute-start | bytes 884744 | tf_op jit(solution)/shard_map/ppermute | solution.py:115
  8.7 14.6 %collective-permute-start.2 = (bf16[144,1024]{1,0:T(8,128)(2,1)S(1)}, bf16[144,1024]{1,0:T(8,128)(2,1)S(1)}, u32[]{:S(2)}, u32[]{:S(2)}) collective-permute-start(bf16[144,1024]{1,0:T(8,128)(2,1)S(1)} %fusion.1.refs_0_), channel_id=1, source_target_pairs={{0,2},{1,3},{2,0},{3,1},{4,6},{5,7},{6,4},{7,5},{8,10},{9,11},{10,... | collective-permute-start | bytes 884744 | tf_op jit(solution)/shard_map/ppermute | solution.py:115
  10.2 13.9 %collective-permute-start.1 = (bf16[144,1024]{1,0:T(8,128)(2,1)S(1)}, bf16[144,1024]{1,0:T(8,128)(2,1)S(1)}, u32[]{:S(2)}, u32[]{:S(2)}) collective-permute-start(bf16[144,1024]{1,0:T(8,128)(2,1)S(1)} %fusion.1.refs_0_), channel_id=1, source_target_pairs={{0,4},{1,5},{2,6},{3,7},{4,0},{5,1},{6,2},{7,3},{8,12},{9,13},{10,... | collective-permute-start | bytes 884744 | tf_op jit(solution)/shard_map/ppermute | solution.py:115
  11.8 11.5 %collective-permute-start.4 = (bf16[128,1024]{1,0:T(8,128)(2,1)S(1)}, bf16[128,1024]{1,0:T(8,128)(2,1)S(1)}, u32[]{:S(2)}, u32[]{:S(2)}) collective-permute-start(bf16[128,1024]{1,0:T(8,128)(2,1)S(1)} %pad_maximum_fusion.refs_0_.refs_8_), channel_id=1, source_target_pairs={{0,2},{1,3},{2,0},{3,1},{4,6},{5,7},{6,4},{7,5},{8,10},{9,11},{10,... | collective-permute-start | bytes 786440 | tf_op jit(solution)/shard_map/ppermute | solution.py:115
  24.1 30.4 %collective-permute-start.14 = (bf16[512,1024]{1,0:T(8,128)(2,1)}, bf16[512,1024]{1,0:T(8,128)(2,1)}, u32[]{:S(2)}, u32[]{:S(2)}) collective-permute-start(bf16[512,1024]{1,0:T(8,128)(2,1)} %bitcast.26), channel_id=1, source_target_pairs={{0,1},{1,0},{2,3},{3,2},{4,5},{5,4},{6,7},{7,6},{8,9},{9,8},{10,11... | collective-permute-start | bytes 3145736 | tf_op jit(solution)/shard_map/ppermute | solution.py:115
  24.2 13.5 %collective-permute-start.6 = (bf16[144,1024]{1,0:T(8,128)(2,1)S(1)}, bf16[144,1024]{1,0:T(8,128)(2,1)S(1)}, u32[]{:S(2)}, u32[]{:S(2)}) collective-permute-start(bf16[144,1024]{1,0:T(8,128)(2,1)S(1)} %collective-permute-done.3.refs_2_), channel_id=1, source_target_pairs={{0,4},{1,5},{2,6},{3,7},{4,0},{5,1},{6,2},{7,3},{8,12},{9,13},{10,... | collective-permute-start | bytes 884744 | tf_op jit(solution)/shard_map/ppermute | solution.py:115
  25.1 16.4 %collective-permute-start.10 = (bf16[144,1024]{1,0:T(8,128)(2,1)S(1)}, bf16[144,1024]{1,0:T(8,128)(2,1)S(1)}, u32[]{:S(2)}, u32[]{:S(2)}) collective-permute-start(bf16[144,1024]{1,0:T(8,128)(2,1)S(1)} %collective-permute-done.1.refs_1_), channel_id=1, source_target_pairs={{0,2},{1,3},{2,0},{3,1},{4,6},{5,7},{6,4},{7,5},{8,10},{9,11},{10,... | collective-permute-start | bytes 884744 | tf_op jit(solution)/shard_map/ppermute | solution.py:115
  26.6 15.0 %collective-permute-start.11 = (bf16[144,1024]{1,0:T(8,128)(2,1)S(1)}, bf16[144,1024]{1,0:T(8,128)(2,1)S(1)}, u32[]{:S(2)}, u32[]{:S(2)}) collective-permute-start(bf16[144,1024]{1,0:T(8,128)(2,1)S(1)} %collective-permute-done.3.refs_2_), channel_id=1, source_target_pairs={{0,2},{1,3},{2,0},{3,1},{4,6},{5,7},{6,4},{7,5},{8,10},{9,11},{10,... | collective-permute-start | bytes 884744 | tf_op jit(solution)/shard_map/ppermute | solution.py:115
  27.2 14.4 %collective-permute-start.9 = (bf16[128,1024]{1,0:T(8,128)(2,1)S(1)}, bf16[128,1024]{1,0:T(8,128)(2,1)S(1)}, u32[]{:S(2)}, u32[]{:S(2)}) collective-permute-start(bf16[128,1024]{1,0:T(8,128)(2,1)S(1)} %pad_maximum_fusion.refs_0_.refs_8_), channel_id=1, source_target_pairs={{0,8},{1,9},{2,10},{3,11},{4,12},{5,13},{6,14},{7,15},{8,0},{9,1},... | collective-permute-start | bytes 786440 | tf_op jit(solution)/shard_map/ppermute | solution.py:115
  37.7 14.9 %collective-permute-start.7 = (bf16[144,1024]{1,0:T(8,128)(2,1)S(1)}, bf16[144,1024]{1,0:T(8,128)(2,1)S(1)}, u32[]{:S(2)}, u32[]{:S(2)}) collective-permute-start(bf16[144,1024]{1,0:T(8,128)(2,1)S(1)} %collective-permute-done.6.refs_3_), channel_id=1, source_target_pairs={{0,2},{1,3},{2,0},{3,1},{4,6},{5,7},{6,4},{7,5},{8,10},{9,11},{10,... | collective-permute-start | bytes 884744 | tf_op jit(solution)/shard_map/ppermute | solution.py:115
  41.6 9.2 %collective-permute-start.8 = (bf16[128,1024]{1,0:T(8,128)(2,1)S(1)}, bf16[128,1024]{1,0:T(8,128)(2,1)S(1)}, u32[]{:S(2)}, u32[]{:S(2)}) collective-permute-start(bf16[128,1024]{1,0:T(8,128)(2,1)S(1)} %pad_maximum_fusion.refs_0_.refs_8_), channel_id=1, source_target_pairs={{0,4},{1,5},{2,6},{3,7},{4,0},{5,1},{6,2},{7,3},{8,12},{9,13},{10,... | collective-permute-start | bytes 786440 | tf_op jit(solution)/shard_map/ppermute | solution.py:115
  41.6 11.0 %collective-permute-start.12 = (bf16[128,1024]{1,0:T(8,128)(2,1)S(1)}, bf16[128,1024]{1,0:T(8,128)(2,1)}, u32[]{:S(2)}, u32[]{:S(2)}) collective-permute-start(bf16[128,1024]{1,0:T(8,128)(2,1)S(1)} %collective-permute-done.9.refs_2_.refs_10_), channel_id=1, source_target_pairs={{0,2},{1,3},{2,0},{3,1},{4,6},{5,7},{6,4},{7,5},{8,10},{9,11},{10,... | collective-permute-start | bytes 786440 | tf_op jit(solution)/shard_map/ppermute | solution.py:115
  43.1 25.3 %collective-permute-start.13 = (bf16[128,1024]{1,0:T(8,128)(2,1)S(1)}, bf16[128,1024]{1,0:T(8,128)(2,1)S(1)}, u32[]{:S(2)}, u32[]{:S(2)}) collective-permute-start(bf16[128,1024]{1,0:T(8,128)(2,1)S(1)} %collective-permute-done.9.refs_2_.refs_10_), channel_id=1, source_target_pairs={{0,4},{1,5},{2,6},{3,7},{4,0},{5,1},{6,2},{7,3},{8,12},{9,13},{10,... | collective-permute-start | bytes 786440 | tf_op jit(solution)/shard_map/ppermute | solution.py:115
  52.6 13.6 %collective-permute-start.15 = (bf16[128,1024]{1,0:T(8,128)(2,1)S(1)}, bf16[128,1024]{1,0:T(8,128)(2,1)S(1)}, u32[]{:S(2)}, u32[]{:S(2)}) collective-permute-start(bf16[128,1024]{1,0:T(8,128)(2,1)S(1)} %collective-permute-done.8.refs_1_.refs_9_), channel_id=1, source_target_pairs={{0,2},{1,3},{2,0},{3,1},{4,6},{5,7},{6,4},{7,5},{8,10},{9,11},{10,... | collective-permute-start | bytes 786440 | tf_op jit(solution)/shard_map/ppermute | solution.py:115
  54.1 12.2 %collective-permute-start.16 = (bf16[128,1024]{1,0:T(8,128)(2,1)}, bf16[128,1024]{1,0:T(8,128)(2,1)S(1)}, u32[]{:S(2)}, u32[]{:S(2)}) collective-permute-start(bf16[128,1024]{1,0:T(8,128)(2,1)} %collective-permute-done.12.refs_6_.refs_14_), channel_id=1, source_target_pairs={{0,4},{1,5},{2,6},{3,7},{4,0},{5,1},{6,2},{7,3},{8,12},{9,13},{10,... | collective-permute-start | bytes 786440 | tf_op jit(solution)/shard_map/ppermute | solution.py:115
  66.3 14.5 %collective-permute-start.18 = (bf16[128,1024]{1,0:T(8,128)(2,1)}, bf16[128,1024]{1,0:T(8,128)(2,1)S(1)}, u32[]{:S(2)}, u32[]{:S(2)}) collective-permute-start(bf16[128,1024]{1,0:T(8,128)(2,1)} %get-tuple-element.127), channel_id=1, source_target_pairs={{0,2},{1,3},{2,0},{3,1},{4,6},{5,7},{6,4},{7,5},{8,10},{9,11},{10,... | collective-permute-start | bytes 786440 | tf_op jit(solution)/shard_map/ppermute | solution.py:115
  67.5 13.3 %collective-permute-start.17 = (bf16[256,1024]{1,0:T(8,128)(2,1)}, bf16[256,1024]{1,0:T(8,128)(2,1)S(1)}, u32[]{:S(2)}, u32[]{:S(2)}) collective-permute-start(bf16[256,1024]{1,0:T(8,128)(2,1)} %get-tuple-element.126), channel_id=1, source_target_pairs={{0,4},{1,5},{2,6},{3,7},{4,0},{5,1},{6,2},{7,3},{8,12},{9,13},{10,... | collective-permute-start | bytes 1572872 | tf_op jit(solution)/shard_map/ppermute | solution.py:115
  81.0 13.8 %collective-permute-start.19 = (bf16[288,1024]{1,0:T(8,128)(2,1)}, bf16[288,1024]{1,0:T(8,128)(2,1)S(1)}, u32[]{:S(2)}, u32[]{:S(2)}) collective-permute-start(bf16[288,1024]{1,0:T(8,128)(2,1)} %get-tuple-element.143), channel_id=1, source_target_pairs={{0,4},{1,5},{2,6},{3,7},{4,0},{5,1},{6,2},{7,3},{8,12},{9,13},{10,... | collective-permute-start | bytes 1769480 | tf_op jit(solution)/shard_map/ppermute | solution.py:115
  82.2 9.5 %collective-permute-start.20 = (bf16[128,1024]{1,0:T(8,128)(2,1)S(1)}, bf16[128,1024]{1,0:T(8,128)(2,1)S(1)}, u32[]{:S(2)}, u32[]{:S(2)}) collective-permute-start(bf16[128,1024]{1,0:T(8,128)(2,1)S(1)} %add_convert_fusion.5), channel_id=1, source_target_pairs={{0,2},{1,3},{2,0},{3,1},{4,6},{5,7},{6,4},{7,5},{8,10},{9,11},{10,... | collective-permute-start | bytes 786440 | tf_op jit(solution)/shard_map/ppermute | solution.py:115
  83.0 11.7 %collective-permute-start.21 = (bf16[144,1024]{1,0:T(8,128)(2,1)}, bf16[144,1024]{1,0:T(8,128)(2,1)S(1)}, u32[]{:S(2)}, u32[]{:S(2)}) collective-permute-start(bf16[144,1024]{1,0:T(8,128)(2,1)} %get-tuple-element.145), channel_id=1, source_target_pairs={{0,2},{1,3},{2,0},{3,1},{4,6},{5,7},{6,4},{7,5},{8,10},{9,11},{10,... | collective-permute-start | bytes 884744 | tf_op jit(solution)/shard_map/ppermute | solution.py:115
  94.8 10.1 %collective-permute-start.23 = (bf16[1536,1024]{1,0:T(8,128)(2,1)}, bf16[1536,1024]{1,0:T(8,128)(2,1)S(1)}, u32[]{:S(2)}, u32[]{:S(2)}) collective-permute-start(bf16[1536,1024]{1,0:T(8,128)(2,1)} %shard_map.120), channel_id=1, source_target_pairs={{0,1},{1,0},{2,3},{3,2},{4,5},{5,4},{6,7},{7,6},{8,9},{9,8},{10,11... | collective-permute-start | bytes 9437192 | tf_op jit(solution)/shard_map/ppermute | solution.py:115
  94.9 9.9 %collective-permute-start.22 = (bf16[144,1024]{1,0:T(8,128)(2,1)S(1)}, bf16[144,1024]{1,0:T(8,128)(2,1)S(1)}, u32[]{:S(2)}, u32[]{:S(2)}) collective-permute-start(bf16[144,1024]{1,0:T(8,128)(2,1)S(1)} %add_convert_fusion.1), channel_id=1, source_target_pairs={{0,2},{1,3},{2,0},{3,1},{4,6},{5,7},{6,4},{7,5},{8,10},{9,11},{10,... | collective-permute-start | bytes 884744 | tf_op jit(solution)/shard_map/ppermute | solution.py:115
  96.6 16.2 %collective-permute-start.29 = (bf16[128,1024]{1,0:T(8,128)(2,1)S(1)}, bf16[128,1024]{1,0:T(8,128)(2,1)S(1)}, u32[]{:S(2)}, u32[]{:S(2)}) collective-permute-start(bf16[128,1024]{1,0:T(8,128)(2,1)S(1)} %add_convert_fusion.3), channel_id=1, source_target_pairs={{0,8},{1,9},{2,10},{3,11},{4,12},{5,13},{6,14},{7,15},{8,0},{9,1},... | collective-permute-start | bytes 786440 | tf_op jit(solution)/shard_map/ppermute | solution.py:115
  98.4 15.2 %collective-permute-start.27 = (bf16[128,1024]{1,0:T(8,128)(2,1)S(1)}, bf16[128,1024]{1,0:T(8,128)(2,1)S(1)}, u32[]{:S(2)}, u32[]{:S(2)}) collective-permute-start(bf16[128,1024]{1,0:T(8,128)(2,1)S(1)} %copy-done.30), channel_id=1, source_target_pairs={{0,2},{1,3},{2,0},{3,1},{4,6},{5,7},{6,4},{7,5},{8,10},{9,11},{10,... | collective-permute-start | bytes 786440 | tf_op jit(solution)/shard_map/ppermute | solution.py:115
  99.3 14.2 %collective-permute-start.28 = (bf16[128,1024]{1,0:T(8,128)(2,1)S(1)}, bf16[128,1024]{1,0:T(8,128)(2,1)S(1)}, u32[]{:S(2)}, u32[]{:S(2)}) collective-permute-start(bf16[128,1024]{1,0:T(8,128)(2,1)S(1)} %add_convert_fusion.4), channel_id=1, source_target_pairs={{0,4},{1,5},{2,6},{3,7},{4,0},{5,1},{6,2},{7,3},{8,12},{9,13},{10,... | collective-permute-start | bytes 786440 | tf_op jit(solution)/shard_map/ppermute | solution.py:115
  105.0 19.4 %collective-permute-start.24 = (bf16[144,1024]{1,0:T(8,128)(2,1)S(1)}, bf16[144,1024]{1,0:T(8,128)(2,1)S(1)}, u32[]{:S(2)}, u32[]{:S(2)}) collective-permute-start(bf16[144,1024]{1,0:T(8,128)(2,1)S(1)} %add_convert_fusion), channel_id=1, source_target_pairs={{0,8},{1,9},{2,10},{3,11},{4,12},{5,13},{6,14},{7,15},{8,0},{9,1},... | collective-permute-start | bytes 884744 | tf_op jit(solution)/shard_map/ppermute | solution.py:115
  107.2 17.8 %collective-permute-start.25 = (bf16[144,1024]{1,0:T(8,128)(2,1)S(1)}, bf16[144,1024]{1,0:T(8,128)(2,1)S(1)}, u32[]{:S(2)}, u32[]{:S(2)}) collective-permute-start(bf16[144,1024]{1,0:T(8,128)(2,1)S(1)} %add_convert_fusion.2), channel_id=1, source_target_pairs={{0,4},{1,5},{2,6},{3,7},{4,0},{5,1},{6,2},{7,3},{8,12},{9,13},{10,... | collective-permute-start | bytes 884744 | tf_op jit(solution)/shard_map/ppermute | solution.py:115
  112.8 12.1 %collective-permute-start.26 = (bf16[144,1024]{1,0:T(8,128)(2,1)S(1)}, bf16[144,1024]{1,0:T(8,128)(2,1)S(1)}, u32[]{:S(2)}, u32[]{:S(2)}) collective-permute-start(bf16[144,1024]{1,0:T(8,128)(2,1)S(1)} %copy-done.29), channel_id=1, source_target_pairs={{0,2},{1,3},{2,0},{3,1},{4,6},{5,7},{6,4},{7,5},{8,10},{9,11},{10,... | collective-permute-start | bytes 884744 | tf_op jit(solution)/shard_map/ppermute | solution.py:115
  (29 other events, 394.7 us)
